TPU v7x, 512 devices: a whole 4x4x16 slice. The times are simulated.
512 devices in a mesh: seq: 64 (over z, x_hi, core), row: 8 (over y, x_lo).
Axes of the slice: x: 4 (x_hi: 2, x_lo: 2; x = x_hi * 2 + x_lo), y: 4, z: 16, core: 2. Of those that a mesh axis runs over, the one named last changes fastest.
Arguments:
- patch_queries: bfloat16 [8192, 2048], P('seq', 'row'), may hold values from -15 to 15
- patch_keys: bfloat16 [8192, 2048], P('seq', 'row'), may hold values from -15 to 15
- patch_values: bfloat16 [8192, 2048], P('seq', 'row'), may hold values from -6 to 6
- patch_tasks: int32 [8192], P('seq'), may hold values from 0 to 7
- residual: bfloat16 [8192, 2048], P('seq', 'row'), may hold values from -6 to 6
- output_weight: bfloat16 [2048, 2048], P('row'), may hold values from -0.5 to 0.5
- global_down: bfloat16 [2048, 16], P('row'), may hold values from -0.5 to 0.5
- global_up: bfloat16 [16, 2048], P(None, 'row'), may hold values from -1.5 to 1.5
- global_scales: float32 [8, 16], replicated, may hold values from 0.25 to 4
- local_weight: bfloat16 [2048, 512], P('row'), may hold values from -0.125 to 0.125
- byte_ids: int32 [65536], P('seq'), may hold values from 0 to 255
- byte_table: bfloat16 [256, 512], replicated, may hold values from -6 to 6
- position_table: bfloat16 [8, 512], replicated, may hold values from -6 to 6
- norm_gain: float32 [512], replicated, may hold values from 0.5 to 1.5
- hidden_in: bfloat16 [2048, 512], P('row', 'seq'), may hold values from -0.25 to 0.25
- hidden_out: bfloat16 [2048, 512], P('row', 'seq'), may hold values from -0.125 to 0.125
- local_down: bfloat16 [512, 16], replicated, may hold values from -0.25 to 0.25
- local_up: bfloat16 [16, 2048], P(None, 'row'), may hold values from -1.5 to 1.5
- local_scales: float32 [8, 16], replicated, may hold values from 0.25 to 4
- cotangent: bfloat16 [65536, 512], P(('seq', 'row')), may hold values from -6 to 6
Outputs:
- grad_global_down: float32 [2048, 16], P('row')
- grad_global_up: float32 [16, 2048], P(None, 'row')
- grad_global_scales: float32 [8, 16], replicated
- grad_local_down: float32 [512, 16], replicated
- grad_local_up: float32 [16, 2048], P(None, 'row')
- grad_local_scales: float32 [8, 16], replicated
All inputs are finite; a program needn't handle non-finite values.
Results may differ from a plain program's by a relative error of at most 0.028.
Values may be sent and summed in bfloat16 or wider, within the bound.
No kernel may reach another device: no remote copies, remote signals or barrier semaphores. Data moves between devices by JAX's collectives and lax.ppermute only.
A program may use at most 64 MiB of HBM per device.

v0:
```python
import functools
import math

import jax
import jax.numpy as jnp
from jax import lax
from jax.sharding import Mesh
from jax.sharding import PartitionSpec as P

HEAD = 128
VOCAB = 256
PATCH = 8
TASKS = 8
ROW = ("row_0", "row_1")
SEQ = ("seq_0", "seq_1", "seq_2")
SEQ_ROW = ("seq_0", "seq_1", "seq_2", "row_0", "row_1")


def in_one_piece(arrays, axis, dim, along):
    widths = [a.shape[along] for a in arrays]
    both = jnp.concatenate(arrays, axis=along)
    out = lax.all_gather(both, axis, axis=dim, tiled=True)
    return tuple(jnp.split(out, [sum(widths[:k]) for k in range(1, len(widths))], axis=along))


def from_everyone(array, axis):
    size = lax.axis_size(axis)
    return lax.all_to_all(
        jnp.broadcast_to(array[None], (size, *array.shape)), axis, 0, 0, tiled=True
    )


def over_copies(array, axis):
    return from_everyone(array, axis).sum(axis=0)


def in_blocks(array, dim, size):
    before, after = (array.shape[:dim], array.shape[dim + 1 :])
    return jnp.moveaxis(array.reshape(*before, size, -1, *after), dim, 0)


def summed_on_arrival(array, axis, dim):
    pieces = in_blocks(array, dim, lax.axis_size(axis))
    arrived = lax.all_to_all(pieces, axis, split_axis=0, concat_axis=0, tiled=True)
    return arrived.astype(jnp.float32).sum(axis=0)


def gather_turned(arrays, axis, dims):
    turned = [jnp.moveaxis(a, dim, 0) for a, dim in zip(arrays, dims)]
    both = jnp.concatenate([t.reshape(len(t), -1) for t in turned], axis=1)
    out, at, finished = (lax.all_gather(both, axis, axis=0, tiled=True), 0, [])
    for t, dim in zip(turned, dims):
        share = out[:, at : at + t[0].size].reshape(-1, *t.shape[1:])
        finished.append(jnp.moveaxis(share, 0, dim))
        at += t[0].size
    return tuple(finished)


def in_one_piece_2(arrays, axis, dim, along):
    both = jnp.concatenate(arrays, axis=along)
    out, at, finished = (summed_on_arrival(both, axis, dim), 0, [])
    for a in arrays:
        finished.append(lax.slice_in_dim(out, at, at + a.shape[along], axis=along))
        at += a.shape[along]
    return tuple(finished)


def in_order(pieces, dim):
    pieces = jnp.moveaxis(pieces, 0, dim)
    lengths = pieces.shape
    return pieces.reshape(*lengths[:dim], lengths[dim] * lengths[dim + 1], *lengths[dim + 2 :])


def gather_directly(array, axis, dim):
    return in_order(from_everyone(array, axis), dim)


def sent_and_summed(array, axis, dim):
    pieces = in_blocks(array, dim, lax.axis_size(axis))
    arrived = lax.all_to_all(pieces, axis, split_axis=0, concat_axis=0, tiled=True)
    return arrived.sum(axis=0)


def padded_to(lines, size):
    spare = -len(lines) % size
    return jnp.pad(lines, [(0, spare)] + [(0, 0)] * (lines.ndim - 1))


def nested_sum(array, axes):
    own = sent_and_summed(padded_to(array, lax.axis_size(axes)), axes, 0)
    whole = gather_directly(own, axes, 0)
    return whole[: len(array)].reshape(array.shape)


def packed_total(arrays, axis):
    ends = [0]
    for a in arrays:
        ends.append(ends[-1] + a.size)
    so_far = nested_sum(jnp.concatenate([a.ravel() for a in arrays]), axis)
    return tuple((so_far[b:e].reshape(a.shape) for a, b, e in zip(arrays, ends, ends[1:])))


def one_axis_at_a_time(array, axes):
    return functools.reduce(lax.psum, axes, array)


def contract(left, right, left_dim, right_dim):
    return lax.dot_general(
        left, right, (((left_dim,), (right_dim,)), ((), ())), preferred_element_type=jnp.float32
    )


def select_rows(table, tasks):
    picks = (tasks[:, None] == jnp.arange(table.shape[0], dtype=jnp.int32)[None, :]).astype(
        jnp.float32
    )
    return jnp.dot(picks, table, precision=lax.Precision.HIGHEST)


def task_totals(tasks, values):
    picks = (tasks[:, None] == jnp.arange(TASKS, dtype=jnp.int32)[None, :]).astype(jnp.float32)
    return lax.dot_general(picks, values, (((0,), (0,)), ((), ())), precision=lax.Precision.HIGHEST)


def gelu_slope(upper):
    cumulative = 0.5 * (1.0 + lax.erf(upper * 0.7071067811865476))
    density = jnp.exp(-0.5 * upper * upper) * 0.3989422804014327
    return cumulative + upper * density


def local_inputs(
    identities, projected, tasks, byte_table, position_table, norm_gain, local_down, local_scales
):
    count = identities.shape[0]
    picks = (identities[:, None] == jnp.arange(VOCAB, dtype=jnp.int32)[None, :]).astype(
        jnp.bfloat16
    )
    embedded = jnp.dot(picks, byte_table, preferred_element_type=jnp.float32)
    patches = count // PATCH
    inputs = (
        embedded.reshape(patches, PATCH, -1)
        + position_table.astype(jnp.float32)[None]
        + projected.astype(jnp.float32)[:, None, :]
    )
    inputs = inputs.reshape(count, -1)
    inverse = lax.rsqrt(jnp.mean(inputs * inputs, axis=1, keepdims=True) + 1e-06)
    normed = (inputs * inverse * norm_gain).astype(jnp.bfloat16)
    lowered = jnp.dot(normed, local_down, preferred_element_type=jnp.float32)
    byte_tasks = jnp.repeat(tasks, PATCH)
    scales = select_rows(local_scales, byte_tasks)
    shrunk = (lowered * scales).astype(jnp.bfloat16)
    return (inputs, inverse, normed, lowered, scales, shrunk, byte_tasks)


def update_state(state, query_rows, first, key_heads, value_heads, key_places, scale):
    running_max, running_sum, running_out = state
    count = query_rows.shape[0]
    heads = key_heads.shape[1]
    query_heads = query_rows.reshape(count, heads, HEAD)
    scores = (
        jnp.einsum("qhd,khd->hqk", query_heads, key_heads, preferred_element_type=jnp.float32)
        * scale
    )
    query_places = first + jnp.arange(count, dtype=jnp.int32)
    allowed = key_places[None, :] <= query_places[:, None]
    scores = jnp.where(allowed[None], scores, -1e30)
    new_max = jnp.maximum(running_max, jnp.max(scores, axis=2))
    weights = jnp.where(allowed[None], jnp.exp(scores - new_max[:, :, None]), 0.0)
    shrink = jnp.exp(running_max - new_max)
    running_sum = running_sum * shrink + jnp.sum(weights, axis=2)
    mixed = jnp.einsum(
        "hqk,khd->qhd",
        weights.astype(jnp.bfloat16),
        value_heads,
        preferred_element_type=jnp.float32,
    )
    running_out = running_out * jnp.transpose(shrink)[:, :, None] + mixed
    return (new_max, running_sum, running_out)


def finish_state(state):
    running_max, running_sum, running_out = state
    result = running_out / jnp.transpose(running_sum)[:, :, None]
    return result.reshape(result.shape[0], -1).astype(jnp.bfloat16)


def body(
    patch_queries,
    patch_keys,
    patch_values,
    patch_tasks,
    residual,
    output_weight,
    global_down,
    global_up,
    global_scales,
    local_weight,
    byte_ids,
    byte_table,
    position_table,
    norm_gain,
    hidden_in,
    hidden_out,
    local_down,
    local_up,
    local_scales,
    cotangent,
):
    rows = patch_queries.shape[0]
    width = patch_queries.shape[1]
    heads = width // HEAD
    row_count = lax.axis_size(ROW)
    seq_index = lax.axis_index(SEQ)
    row_index = lax.axis_index(ROW)
    scale = 1.0 / math.sqrt(HEAD)
    own_first = seq_index * rows
    groups = [(patch_queries, own_first)]

    def visit(state, query_rows, first, key_heads, value_heads, key_places):
        return update_state(state, query_rows, first, key_heads, value_heads, key_places, scale)

    initial = tuple(
        (
            (
                jnp.full((heads, query_rows.shape[0]), -1e30, jnp.float32),
                jnp.zeros((heads, query_rows.shape[0]), jnp.float32),
                jnp.zeros((query_rows.shape[0], heads, HEAD), jnp.float32),
            )
            for query_rows, first in groups
        )
    )
    key_piece, value_piece = in_one_piece((patch_keys, patch_values), SEQ, 0, 1)
    count = key_piece.shape[0]
    span = math.gcd(count, 1024)

    def one_span(index, states):
        offset = index * span
        key_heads = lax.dynamic_slice_in_dim(key_piece, offset, span, 0).reshape(span, heads, HEAD)
        value_heads = lax.dynamic_slice_in_dim(value_piece, offset, span, 0).reshape(
            span, heads, HEAD
        )
        key_places = offset + jnp.arange(span, dtype=jnp.int32)
        updated = []
        for (query_rows, first), state in zip(groups, states):
            updated.append(visit(state, query_rows, first, key_heads, value_heads, key_places))
        return tuple(updated)

    states = lax.fori_loop(0, count // span, one_span, initial)
    outputs = [finish_state(state) for state in states]
    attended = outputs[0]
    reduced = over_copies(jnp.dot(attended, global_down, preferred_element_type=jnp.float32), ROW)
    task_scales = select_rows(global_scales, patch_tasks)
    scaled = (reduced * task_scales).astype(jnp.bfloat16)
    mixed = summed_on_arrival(contract(output_weight, attended, 0, 1).astype(jnp.bfloat16), ROW, 0)
    mixed = mixed + jnp.transpose(residual.astype(jnp.float32)) + contract(global_up, scaled, 0, 1)
    mixed_b = mixed.astype(jnp.bfloat16)
    own_patches = rows // row_count
    own_bytes = own_patches * PATCH
    own_tasks = lax.dynamic_slice_in_dim(patch_tasks, row_index * own_patches, own_patches)
    own_ids = lax.dynamic_slice_in_dim(byte_ids, row_index * own_bytes, own_bytes)
    rows_in, rows_out = gather_turned((hidden_in, hidden_out), SEQ, (1, 1))
    projected = summed_on_arrival(
        contract(mixed_b, local_weight, 0, 0).astype(jnp.bfloat16), ROW, 0
    ).astype(jnp.bfloat16)
    inputs, inverse, normed, lowered, scales, shrunk, byte_tasks = local_inputs(
        own_ids,
        projected,
        own_tasks,
        byte_table,
        position_table,
        norm_gain,
        local_down,
        local_scales,
    )
    normed_all, shrunk_all, cotangent_all = in_one_piece((normed, shrunk, cotangent), ROW, 0, 1)
    upper = contract(normed_all, rows_in, 1, 1) + jnp.dot(
        shrunk_all, local_up, preferred_element_type=jnp.float32
    )
    through = contract(cotangent_all, rows_out, 1, 1)
    grown = (through * gelu_slope(upper)).astype(jnp.bfloat16)
    grad_local_up = contract(shrunk_all, grown, 0, 0)
    back_norm, back_rank = in_one_piece_2(
        (
            jnp.dot(grown, rows_in, preferred_element_type=jnp.float32).astype(jnp.bfloat16),
            contract(grown, local_up, 1, 1).astype(jnp.bfloat16),
        ),
        ROW,
        0,
        1,
    )
    grad_local_scales = task_totals(byte_tasks, back_rank * lowered)
    moved = (back_rank * scales).astype(jnp.bfloat16)
    grad_local_down = contract(normed, moved, 0, 0)
    back_total = back_norm + contract(moved, local_down, 1, 1)
    gained = back_total * norm_gain
    average = jnp.mean(gained * inputs, axis=1, keepdims=True)
    back_inputs = cotangent.astype(jnp.float32) + inverse * (
        gained - inputs * inverse * inverse * average
    )
    patch_grad = back_inputs.reshape(own_patches, PATCH, -1).sum(axis=1).astype(jnp.bfloat16)
    back_mixed = contract(gather_directly(patch_grad, ROW, 0), local_weight, 1, 1).astype(
        jnp.bfloat16
    )
    grad_global_up = contract(scaled, back_mixed, 0, 0)
    back_scaled = over_copies(contract(back_mixed, global_up, 1, 1), ROW)
    grad_global_scales = task_totals(patch_tasks, back_scaled * reduced)
    back_reduced = (back_scaled * task_scales).astype(jnp.bfloat16)
    grad_global_down = contract(attended, back_reduced, 0, 0)
    grad_global_down, grad_global_up, grad_global_scales, grad_local_up = packed_total(
        (grad_global_down, grad_global_up, grad_global_scales, grad_local_up), SEQ
    )
    grad_local_down, grad_local_scales = (
        one_axis_at_a_time(grad_local_down, SEQ_ROW),
        one_axis_at_a_time(grad_local_scales, SEQ_ROW),
    )
    return (
        grad_global_down,
        grad_global_up,
        grad_global_scales,
        grad_local_down,
        grad_local_up,
        grad_local_scales,
    )


def solution(mesh):
    torus = Mesh(
        mesh.devices.reshape(16, 2, 2, 4, 2), ("seq_0", "seq_1", "seq_2", "row_0", "row_1")
    )
    placed = (
        P(SEQ, ROW),
        P(SEQ, ROW),
        P(SEQ, ROW),
        P(SEQ),
        P(SEQ, ROW),
        P(ROW, None),
        P(ROW, None),
        P(None, ROW),
        P(),
        P(ROW, None),
        P(SEQ),
        P(),
        P(),
        P(),
        P(ROW, SEQ),
        P(ROW, SEQ),
        P(),
        P(None, ROW),
        P(),
        P(SEQ_ROW, None),
    )
    return jax.shard_map(
        body,
        mesh=torus,
        in_specs=placed,
        out_specs=(P(ROW, None), P(None, ROW), P(), P(), P(None, ROW), P()),
        check_vma=False,
    )
```

profile of v0, /device:TPU:1, one launch (start us, length us, event | category | flops | bytes accessed | tf_op | source)
XLA Modules:
  0.0 503.0 jit_solution(2075707168768046203)
XLA Ops:
  7.2 1.0 copy.94
  8.3 1.0 copy.95
  9.2 0.7 pad_maximum_fusion
  10.0 176.1 %all-gather.3.cloned.1.call-done = bf16[8192,512]{0,1:T(8,128)(2,1)} async-done(((bf16[128,512]{0,1:T(8,128)(2,1)}), bf16[8192,512]{0,1:T(8,128)(2,1)}) %all-gather.3.cloned.1.call-update) | async-done | bytes 8388624 | tf_op jit(solution)/shard_map/all_gather | solution.py:22
  186.0 5.9 %fusion.52 = (bf16[8192,256]{0,1:T(8,128)(2,1)}, bf16[8192,256]{0,1:T(8,128)(2,1)}) fusion(bf16[8192,512]{0,1:T(8,128)(2,1)} %all-gather.3.cloned.1.call-done), kind=kLoop, calls=%fused_computation.96 | loop fusion | bytes 16777216 | tf_op jit(solution)/shard_map/split | solution.py:23
  191.9 20.6 %while.18 = (s32[]{:T(128)}, f32[2,128]{1,0:T(2,128)S(1)}, f32[2,128]{1,0:T(2,128)S(1)}, f32[128,2,128]{0,2,1:T(8,128)S(1)}, s32[]{:T(128)}, /*index=5*/bf16[819...) while((s32[]{:T(128)}, f32[2,128]{1,0:T(2,128)S(1)}, ...), condition=%wide.region_3.4_spmd.clone, body=%wide.region_0.3_spmd.clone.sunk | while | flops 136809088 | bytes 7169211 | solution.py:248
  191.9 1.3 constant_dynamic-slice_fusion.3
  193.4 0.4 fusion.99
  193.8 0.4 fusion.103
  194.5 1.3 constant_dynamic-slice_fusion.3
  196.0 0.4 fusion.99
  196.4 0.4 fusion.103
  197.1 1.3 constant_dynamic-slice_fusion.3
  198.6 0.4 fusion.99
  199.0 0.4 fusion.103
  199.7 1.3 constant_dynamic-slice_fusion.3
  201.6 0.4 fusion.103
  202.2 1.3 constant_dynamic-slice_fusion.3
  203.8 0.4 fusion.99
  204.2 0.4 fusion.103
  204.8 1.3 constant_dynamic-slice_fusion.3
  206.7 0.4 fusion.103
  207.4 1.3 constant_dynamic-slice_fusion.3
  209.3 0.4 fusion.103
  210.0 1.3 constant_dynamic-slice_fusion.3
  211.5 0.4 fusion.99
  211.9 0.4 fusion.103
  212.8 0.6 broadcast_in_dim.106
  213.4 4.1 all-to-all-start.1
  217.9 0.8 copy.123
  218.8 4.0 all-to-all-done.1
  222.8 3.6 all-to-all-start
  226.7 0.8 dynamic_slice.20
  227.7 7.1 %all-to-all-done = bf16[8,256,128]{1,2,0:T(8,128)(2,1)S(1)} async-done(((bf16[8,256,128]{1,2,0:T(8,128)(2,1)}), bf16[8,256,128]{1,2,0:T(8,128)(2,1)S(1)}, u32[]{:S(2)}, u32[]{:S(2)}) %all-to-all-start) | async-done | bytes 524320 | tf_op jit(solution)/shard_map/all_to_all | solution.py:44
  234.9 1.0 convolution_convert_fusion.2
  235.8 3.4 all-to-all-start.2
  239.5 5.2 %all-to-all-done.2 = bf16[8,16,512]{2,1,0:T(8,128)(2,1)S(1)} async-done(((bf16[8,16,512]{2,1,0:T(8,128)(2,1)}), bf16[8,16,512]{2,1,0:T(8,128)(2,1)S(1)}, u32[]{:S(2)}, u32[]{:S(2)}) %all-to-all-start.2) | async-done | bytes 131104 | tf_op jit(solution)/shard_map/all_to_all | solution.py:44
  245.5 0.9 concatenate.16
  246.4 81.0 %all_gather.11 = bf16[512,512]{1,0:T(8,128)(2,1)S(1)} all-gather(bf16[8,512]{1,0:T(8,128)(2,1)S(1)} %pad_maximum_fusion.2), channel_id=1, replica_groups=mesh['seq_0'=16,'seq_1'=2,'seq_2'=2,'row_0'=4,'row_1'=2] {'seq_0','seq_1..., dimensions={0}, use_global_device_ids=true | all-gather | bytes 532480 | tf_op jit(solution)/shard_map/all_gather | solution.py:51
  327.4 1.8 fusion.24
  329.7 0.8 fusion.15
  330.5 0.5 convolution_convert_fusion.1
  331.4 18.3 %all_to_all.45 = bf16[8,128,528]{1,2,0:T(8,128)(2,1)S(1)} all-to-all(bf16[8,128,528]{1,2,0:T(8,128)(2,1)S(1)} %copy_bitcast_fusion), channel_id=1, replica_groups=mesh['seq_0'=16,'seq_1'=2,'seq_2'=2,'row_0'=4,'row_1'=2] {'row_0','row_1'}, dimensions={0} | all-to-all | bytes 2162688 | tf_op jit(solution)/shard_map/all_to_all | solution.py:44
  350.5 0.7 broadcast_in_dim.108
  351.2 3.4 all-to-all-start.4
  354.6 1.2 convolution_bitcast_fusion.2
  355.8 4.3 all-to-all-done.4
  360.4 0.6 broadcast_in_dim.109
  361.0 3.3 all-to-all-start.5
  364.5 5.0 all-to-all-done.5
  370.1 0.9 all_to_all.34
  371.0 11.0 %all-to-all-start.6 = ((f32[64,1,194]{2,1,0:T(1,128)}), f32[64,1,194]{2,1,0:T(1,128)S(1)}, u32[]{:S(2)}, u32[]{:S(2)}) async-start(f32[64,1,194]{2,1,0:T(1,128)} %all_to_all.34), calls=%async_computation.6 | async-start | bytes 131072 | tf_op jit(solution)/shard_map/all_to_all | solution.py:80
  382.1 15.8 %all-to-all-done.6 = f32[64,1,194]{2,1,0:T(1,128)S(1)} async-done(((f32[64,1,194]{2,1,0:T(1,128)}), f32[64,1,194]{2,1,0:T(1,128)S(1)}, u32[]{:S(2)}, u32[]{:S(2)}) %all-to-all-start.6) | async-done | bytes 49696 | tf_op jit(solution)/shard_map/all_to_all | solution.py:80
  398.0 0.7 broadcast_in_dim.110
  398.7 4.4 all-to-all-start.7
  403.3 43.6 %all-reduce = (f32[512,16]{0,1:T(8,128)S(1)}, f32[8,16]{1,0:T(8,128)S(1)}) all-reduce(f32[512,16]{0,1:T(8,128)S(1)} %fusion.54, f32[8,16]{1,0:T(8,128)S(1)} %fusion.40), channel_id=1, replica_groups=mesh['seq_0'=16,'seq_1'=2,'seq_2'=2,'row_0'=4,'row_1'=2] {'seq_0'}, use_global_device_ids=true, to_apply=%region_13.14 | all-reduce | flops 8320 | bytes 66560 | tf_op jit(solution)/shard_map/psum | solution.py:104
  446.9 9.0 %all-reduce.4 = (f32[512,16]{0,1:T(8,128)S(1)}, f32[8,16]{1,0:T(8,128)S(1)}) all-reduce(f32[512,16]{0,1:T(8,128)S(1)} %get-tuple-element.235, f32[8,16]{1,0:T(8,128)S(1)} %get-tuple-element.236), channel_id=1, replica_groups=mesh['seq_0'=16,'seq_1'=2,'seq_2'=2,'row_0'=4,'row_1'=2] {'seq_1'}, use_global_device_ids=true, to_apply=%region_14.15 | all-reduce | flops 8320 | bytes 66560 | tf_op jit(solution)/shard_map/psum | solution.py:104
  455.9 19.0 %all-reduce.3 = (f32[512,16]{0,1:T(8,128)S(1)}, f32[8,16]{1,0:T(8,128)S(1)}) all-reduce(f32[512,16]{0,1:T(8,128)S(1)} %get-tuple-element.243, f32[8,16]{1,0:T(8,128)S(1)} %get-tuple-element.244), channel_id=1, replica_groups=mesh['seq_0'=16,'seq_1'=2,'seq_2'=2,'row_0'=4,'row_1'=2] {'seq_2'}, use_global_device_ids=true, to_apply=%region_15.16 | all-reduce | flops 8320 | bytes 66560 | tf_op jit(solution)/shard_map/psum | solution.py:104
  474.9 12.0 %all-reduce.1 = (f32[512,16]{0,1:T(8,128)S(1)}, f32[8,16]{1,0:T(8,128)S(1)}) all-reduce(f32[512,16]{0,1:T(8,128)S(1)} %get-tuple-element.241, f32[8,16]{1,0:T(8,128)S(1)} %get-tuple-element.242), channel_id=1, replica_groups=mesh['seq_0'=16,'seq_1'=2,'seq_2'=2,'row_0'=4,'row_1'=2] {'row_0'}, use_global_device_ids=true, to_apply=%region_16.17 | all-reduce | flops 8320 | bytes 66560 | tf_op jit(solution)/shard_map/psum | solution.py:104
  486.9 6.3 %all-reduce.2 = (f32[512,16]{0,1:T(8,128)}, f32[8,16]{1,0:T(8,128)}) all-reduce(f32[512,16]{0,1:T(8,128)S(1)} %get-tuple-element.237, f32[8,16]{1,0:T(8,128)S(1)} %get-tuple-element.238), channel_id=1, replica_groups=mesh['seq_0'=16,'seq_1'=2,'seq_2'=2,'row_0'=4,'row_1'=2] {'row_1'}, use_global_device_ids=true, to_apply=%region_17.18 | all-reduce | flops 8320 | bytes 66560 | tf_op jit(solution)/shard_map/psum | solution.py:104
  493.5 0.6 slice.43
  494.3 0.7 copy.103
  495.0 0.6 reshape.169
  495.6 0.6 reshape.170
  (151 shorter events, 10.8 us)
Async XLA Ops:
  7.2 210.4 %copy-start = (bf16[256,2048]{1,0:T(8,128)(2,1)S(1)}, bf16[256,2048]{1,0:T(8,128)(2,1)}, u32[]{:S(2)}) copy-start(bf16[256,2048]{1,0:T(8,128)(2,1)} %param.27) | copy-start | bytes 3145732
  7.2 178.9 %all-gather.3.cloned.1.call-start = ((), (), s32[]{:S(2)}) async-start(), calls=%async_computation.8 | async-start | bytes 8519680 | tf_op jit(solution)/shard_map/all_gather | solution.py:22
  10.0 181.9 %copy-start.1 = (bf16[128,256]{1,0:T(8,128)(2,1)S(1)}, bf16[128,256]{1,0:T(8,128)(2,1)}, u32[]{:S(2)}) copy-start(bf16[128,256]{1,0:T(8,128)(2,1)} %param.22) | copy-start | bytes 196612
  191.9 20.7 %copy-start.11 = (bf16[256,16]{0,1:T(8,128)(2,1)S(1)}, bf16[256,16]{0,1:T(8,128)(2,1)}, u32[]{:S(2)}) copy-start(bf16[256,16]{0,1:T(8,128)(2,1)} %param.28) | copy-start | bytes 24580
  212.6 13.8 %copy-start.12 = (bf16[8,512]{1,0:T(8,128)(2,1)S(1)}, bf16[8,512]{1,0:T(8,128)(2,1)}, u32[]{:S(2)}) copy-start(bf16[8,512]{1,0:T(8,128)(2,1)} %param.34) | copy-start | bytes 24580
  212.6 13.9 %copy-start.17 = (s32[128]{0:T(128)S(1)}, s32[128]{0:T(128)}, u32[]{:S(2)}) copy-start(s32[128]{0:T(128)} %param.25) | copy-start | bytes 1540
  212.6 14.9 %copy-start.15 = (f32[8,16]{1,0:T(8,128)S(1)}, f32[8,16]{1,0:T(8,128)}, u32[]{:S(2)}) copy-start(f32[8,16]{1,0:T(8,128)} %param.30) | copy-start | bytes 1540
  213.4 21.4 %copy-start.2 = (bf16[256,512]{1,0:T(8,128)(2,1)S(1)}, bf16[256,512]{1,0:T(8,128)(2,1)}, u32[]{:S(2)}) copy-start(bf16[256,512]{1,0:T(8,128)(2,1)} %param.31) | copy-start | bytes 786436
  213.4 21.5 %copy-start.6 = (bf16[128,256]{1,0:T(8,128)(2,1)S(1)}, bf16[128,256]{1,0:T(8,128)(2,1)}, u32[]{:S(2)}) copy-start(bf16[128,256]{1,0:T(8,128)(2,1)} %param.26) | copy-start | bytes 196612
  213.4 21.5 %copy-start.9 = (bf16[16,256]{1,0:T(8,128)(2,1)S(1)}, bf16[16,256]{1,0:T(8,128)(2,1)}, u32[]{:S(2)}) copy-start(bf16[16,256]{1,0:T(8,128)(2,1)} %param.29) | copy-start | bytes 24580
  213.4 9.3 %all-to-all-start.1 = ((f32[8,128,16]{1,2,0:T(8,128)}), f32[8,128,16]{1,2,0:T(8,128)S(1)}, u32[]{:S(2)}, u32[]{:S(2)}) async-start(f32[8,128,16]{1,2,0:T(8,128)} %broadcast_in_dim.106), calls=%async_computation.1 | async-start | bytes 131072 | tf_op jit(solution)/shard_map/all_to_all | solution.py:28
  217.6 21.7 %copy-start.16 = (f32[8,16]{1,0:T(8,128)S(1)}, f32[8,16]{1,0:T(8,128)}, u32[]{:S(2)}) copy-start(f32[8,16]{1,0:T(8,128)} %param.40) | copy-start | bytes 1540
  217.9 26.8 %copy-start.5 = (bf16[256,512]{1,0:T(8,128)(2,1)S(1)}, bf16[256,512]{1,0:T(8,128)(2,1)}, u32[]{:S(2)}) copy-start(bf16[256,512]{1,0:T(8,128)(2,1)} %param.33) | copy-start | bytes 786436
  217.9 27.2 %copy-start.10 = (f32[512]{0:T(512)S(1)}, f32[512]{0:T(512)}, u32[]{:S(2)}) copy-start(f32[512]{0:T(512)} %param.35) | copy-start | bytes 6148
  217.9 27.3 %copy-start.7 = (bf16[512,16]{0,1:T(8,128)(2,1)S(1)}, bf16[512,16]{0,1:T(8,128)(2,1)}, u32[]{:S(2)}) copy-start(bf16[512,16]{0,1:T(8,128)(2,1)} %param.38) | copy-start | bytes 49156
  218.8 26.7 %copy-start.4 = (bf16[128,512]{1,0:T(8,128)(2,1)S(1)}, bf16[128,512]{1,0:T(8,128)(2,1)}, u32[]{:S(2)}) copy-start(bf16[128,512]{1,0:T(8,128)(2,1)} %param.41) | copy-start | bytes 393220
  222.8 23.6 %copy-start.13 = (bf16[256,8]{0,1:T(8,128)(2,1)S(1)}, bf16[256,8]{0,1:T(8,128)(2,1)}, u32[]{:S(2)}) copy-start(bf16[256,8]{0,1:T(8,128)(2,1)} %param.37) | copy-start | bytes 12292
  222.8 23.6 %copy-start.14 = (bf16[256,8]{0,1:T(8,128)(2,1)S(1)}, bf16[256,8]{0,1:T(8,128)(2,1)}, u32[]{:S(2)}) copy-start(bf16[256,8]{0,1:T(8,128)(2,1)} %param.36) | copy-start | bytes 12292
  222.8 12.0 %all-to-all-start = ((bf16[8,256,128]{1,2,0:T(8,128)(2,1)}), bf16[8,256,128]{1,2,0:T(8,128)(2,1)S(1)}, u32[]{:S(2)}, u32[]{:S(2)}) async-start(bf16[8,256,128]{1,2,0:T(8,128)(2,1)} %bitcast.89), calls=%async_computation | async-start | bytes 1048576 | tf_op jit(solution)/shard_map/all_to_all | solution.py:44
  235.8 8.8 %all-to-all-start.2 = ((bf16[8,16,512]{2,1,0:T(8,128)(2,1)}), bf16[8,16,512]{2,1,0:T(8,128)(2,1)S(1)}, u32[]{:S(2)}, u32[]{:S(2)}) async-start(bf16[8,16,512]{2,1,0:T(8,128)(2,1)} %bitcast.6), calls=%async_computation.2 | async-start | bytes 262144 | tf_op jit(solution)/shard_map/all_to_all | solution.py:44
  239.2 88.2 %all-gather.5.cloned.1.call-start = ((), (), s32[]{:S(2)}) async-start(), calls=%async_computation.9 | async-start | bytes 2654208 | tf_op jit(solution)/shard_map/all_gather | solution.py:22
  244.7 84.5 %copy-start.8 = (bf16[16,256]{1,0:T(8,128)(2,1)S(1)}, bf16[16,256]{1,0:T(8,128)(2,1)}, u32[]{:S(2)}) copy-start(bf16[16,256]{1,0:T(8,128)(2,1)} %param.39) | copy-start | bytes 24580
  327.4 2.0 copy-start.3
  351.2 8.8 %all-to-all-start.4 = ((bf16[8,16,512]{2,1,0:T(8,128)(2,1)}), bf16[8,16,512]{2,1,0:T(8,128)(2,1)S(1)}, u32[]{:S(2)}, u32[]{:S(2)}) async-start(bf16[8,16,512]{2,1,0:T(8,128)(2,1)} %broadcast_in_dim.108), calls=%async_computation.4 | async-start | bytes 262144 | tf_op jit(solution)/shard_map/all_to_all | solution.py:28
  361.0 8.5 %all-to-all-start.5 = ((f32[8,128,16]{1,2,0:T(8,128)}), f32[8,128,16]{1,2,0:T(8,128)S(1)}, u32[]{:S(2)}, u32[]{:S(2)}) async-start(f32[8,128,16]{1,2,0:T(8,128)} %broadcast_in_dim.109), calls=%async_computation.5 | async-start | bytes 131072 | tf_op jit(solution)/shard_map/all_to_all | solution.py:28
  371.0 26.9 %all-to-all-start.6 = ((f32[64,1,194]{2,1,0:T(1,128)}), f32[64,1,194]{2,1,0:T(1,128)S(1)}, u32[]{:S(2)}, u32[]{:S(2)}) async-start(f32[64,1,194]{2,1,0:T(1,128)} %all_to_all.34), calls=%async_computation.6 | async-start | bytes 131072 | tf_op jit(solution)/shard_map/all_to_all | solution.py:80
  398.7 94.5 %all-to-all-start.7 = ((f32[64,1,194]{2,1,0:T(1,128)}), f32[64,1,194]{2,1,0:T(1,128)S(1)}, u32[]{:S(2)}, u32[]{:S(2)}) async-start(f32[64,1,194]{2,1,0:T(1,128)} %broadcast_in_dim.110), calls=%async_computation.7 | async-start | bytes 131072 | tf_op jit(solution)/shard_map/all_to_all | solution.py:28
Sparse Core Ops, SparseCore 0:
  11.0 174.9 all-gather.2
  246.5 63.9 all-gather.4
where the time goes:
time: 508 us; the launch traced here: 503 us
  waiting for transfers between devices  217 us (43%)
  blocking collectives  189 us (37%)
  starting transfers between devices  33.3 us (7%)
  local copies, waits for them, and re-layouts  27.9 us (5%)
  matrix products  14.6 us (3%)
  between operations  14.6 us (3%)
  other arithmetic  5.48 us (1%)
    all_gather x2, waiting for transfers between devices, in_one_piece(): out = lax.all_gather(both, axis, axis=dim, tiled=True)  176 us
    psum x5, blocking collectives, one_axis_at_a_time(): return functools.reduce(lax.psum, axes, array)  89.8 us
    all_gather x1, blocking collectives, gather_turned(): out, at, finished = (lax.all_gather(both, axis, axis=0, tiled=True), 0, [])  81 us
    all_to_all x1, blocking collectives, summed_on_arrival(): lax.all_to_all(pieces, axis, split_axis=0, concat_axis=0, tiled=True)  18.3 us
    all_to_all x1, waiting for transfers between devices, sent_and_summed(): lax.all_to_all(pieces, axis, split_axis=0, concat_axis=0, tiled=True)  15.8 us
    all_to_all x4, starting transfers between devices, from_everyone(): lax.all_to_all(jnp.broadcast_to(array[None], (size, *array.shape)), axis,...  15.3 us
    all_to_all x4, waiting for transfers between devices, from_everyone(): lax.all_to_all(jnp.broadcast_to(array[None], (size, *array.shape)), axis,...  13.2 us
    all_to_all x2, waiting for transfers between devices, summed_on_arrival(): lax.all_to_all(pieces, axis, split_axis=0, concat_axis=0, tiled=True)  12.3 us
  transfers between devices with their start and end apart: 9, of which 7 were waited for; matrix products, arithmetic and copies ran while one was open for 1% of the time, Pallas kernels for 0%

commit v1 on v0

v1 whole, which is shorter than its diff:
```python
import math

import jax
import jax.numpy as jnp
from jax import lax
from jax.sharding import Mesh
from jax.sharding import PartitionSpec as P

HEAD = 128
VOCAB = 256
PATCH = 8
TASKS = 8
RANK = 16
ROW = ("row_0", "row_1")
SEQ = ("seq_0", "seq_1", "seq_2")
Z, FAR, CORE = SEQ
SEQ_ROW = SEQ + ROW
SWAP = [(0, 1), (1, 0)]
BF = jnp.bfloat16
F32 = jnp.float32


def exchange(pieces, axis):
    return lax.all_to_all(pieces, axis, split_axis=0, concat_axis=0, tiled=True)


def to_everyone(array, axis):
    size = lax.axis_size(axis)
    return exchange(jnp.broadcast_to(array[None], (size, *array.shape)), axis)


def contract(left, right, left_dim, right_dim):
    return lax.dot_general(
        left, right, (((left_dim,), (right_dim,)), ((), ())), preferred_element_type=F32
    )


def select_rows(table, tasks):
    picks = (tasks[:, None] == jnp.arange(table.shape[0], dtype=jnp.int32)[None, :]).astype(F32)
    return jnp.dot(picks, table, precision=lax.Precision.HIGHEST)


def task_totals(tasks, values):
    picks = (tasks[:, None] == jnp.arange(TASKS, dtype=jnp.int32)[None, :]).astype(F32)
    return lax.dot_general(picks, values, (((0,), (0,)), ((), ())), precision=lax.Precision.HIGHEST)


def gelu_slope(upper):
    cumulative = 0.5 * (1.0 + lax.erf(upper * 0.7071067811865476))
    density = jnp.exp(-0.5 * upper * upper) * 0.3989422804014327
    return cumulative + upper * density


def in_pair_order(mine, other, place, axis):
    first = jnp.where(place == 0, mine, other)
    second = jnp.where(place == 0, other, mine)
    return jnp.concatenate([first, second], axis=axis)


def attend(state, queries, query_places, keys, values, key_places):
    top, mass, out = state
    scores = contract(queries, keys, 1, 1) * (1.0 / math.sqrt(HEAD))
    allowed = key_places[None, :] <= query_places[:, None]
    scores = jnp.where(allowed, scores, -1e30)
    new_top = jnp.maximum(top, jnp.max(scores, axis=1, keepdims=True))
    weights = jnp.where(allowed, jnp.exp(scores - new_top), 0.0)
    shrink = jnp.exp(top - new_top)
    mass = mass * shrink + jnp.sum(weights, axis=1, keepdims=True)
    out = out * shrink + jnp.dot(weights.astype(BF), values, preferred_element_type=F32)
    return (new_top, mass, out)


def body(
    patch_queries,
    patch_keys,
    patch_values,
    patch_tasks,
    residual,
    output_weight,
    global_down,
    global_up,
    global_scales,
    local_weight,
    byte_ids,
    byte_table,
    position_table,
    norm_gain,
    hidden_in,
    hidden_out,
    local_down,
    local_up,
    local_scales,
    cotangent,
):
    rows, width = patch_queries.shape
    ring = lax.axis_size(Z)
    row_count = lax.axis_size(ROW)
    z = lax.axis_index(Z)
    far = lax.axis_index(FAR)
    core = lax.axis_index(CORE)
    row_index = lax.axis_index(ROW)
    columns = local_weight.shape[1]
    units = hidden_in.shape[0]
    share = hidden_in.shape[1]

    def head(array, which):
        return lax.dynamic_slice_in_dim(array, which * HEAD, HEAD, 1)

    trio = (patch_queries, patch_keys, patch_values)
    mine = jnp.concatenate([head(a, core) for a in trio], axis=1)
    other = jnp.concatenate([head(a, 1 - core) for a in trio], axis=1)
    both = jnp.concatenate([mine, lax.ppermute(other, CORE, SWAP)], axis=0)
    queries = both[:, :HEAD]
    hidden = jnp.concatenate([hidden_in.T, hidden_out.T], axis=0)
    halves = [hidden[:, k * HEAD : (k + 1) * HEAD] for k in range(units // HEAD)]
    arrived = lax.ppermute(jnp.concatenate([queries, *halves], axis=0), FAR, SWAP)
    chip_rows = 2 * rows
    tall = 2 * share
    far_hidden = jnp.concatenate(
        [
            arrived[chip_rows + k * tall : chip_rows + (k + 1) * tall]
            for k in range(units // HEAD)
        ],
        axis=1,
    )
    queries = jnp.concatenate([queries, arrived[:chip_rows]], axis=0)
    packet = jnp.concatenate([both[:, HEAD:], hidden, far_hidden], axis=0)

    def places(z_index, far_index):
        start = (z_index * 4 + far_index * 2) * rows
        count = jnp.arange(rows, dtype=jnp.int32)
        return jnp.concatenate([start + core * rows + count, start + (1 - core) * rows + count])

    query_places = jnp.concatenate([places(z, far), places(z, 1 - far)])
    total = 2 * chip_rows
    state = (
        jnp.full((total, 1), -1e30, F32),
        jnp.zeros((total, 1), F32),
        jnp.zeros((total, HEAD), F32),
    )
    up = [(i, (i + 1) % ring) for i in range(ring)]
    down = [(i, (i - 1) % ring) for i in range(ring)]

    def visit(state, packets, indices):
        keys = jnp.concatenate([p[:chip_rows, :HEAD] for p in packets])
        values = jnp.concatenate([p[:chip_rows, HEAD:] for p in packets])
        key_places = jnp.concatenate([places(i, far) for i in indices])
        return attend(state, queries, query_places, keys, values, key_places)

    riders = [None] * ring
    riders[0] = packet[chip_rows:]
    rising = falling = packet
    now, at = [packet], [z]
    for step in range(1, ring // 2 + 1):
        rising = lax.ppermute(rising, Z, up)
        riders[-step % ring] = rising[chip_rows:]
        later, then = [rising], [(z - step) % ring]
        if step < ring // 2:
            falling = lax.ppermute(falling, Z, down)
            riders[step] = falling[chip_rows:]
            later.append(falling)
            then.append((z + step) % ring)
        state = visit(state, now, at)
        now, at = later, then
    state = visit(state, now, at)

    top, mass, out = state
    level = jnp.where(mass > 0, top + jnp.log(jnp.where(mass > 0, mass, 1.0)), -1e30)
    out = out / jnp.where(mass > 0, mass, 1.0)
    sent = level[chip_rows:]
    high = sent.astype(BF)
    middle = (sent - high.astype(F32)).astype(BF)
    low = (sent - high.astype(F32) - middle.astype(F32)).astype(BF)
    wide = [jnp.broadcast_to(a, (chip_rows, n)) for a, n in ((high, 32), (middle, 32), (low, 64))]
    met = lax.ppermute(jnp.concatenate([out[chip_rows:].astype(BF), *wide], axis=1), FAR, SWAP)
    met = met.astype(F32)
    far_level = met[:, 128:129] + met[:, 160:161] + met[:, 192:193]
    own_level = level[:chip_rows]
    peak = jnp.maximum(own_level, far_level)
    own_part = jnp.exp(own_level - peak)
    far_part = jnp.exp(far_level - peak)
    merged = (own_part * out[:chip_rows] + far_part * met[:, :HEAD]) / (own_part + far_part)
    merged = merged.astype(BF)
    partner = lax.ppermute(merged[rows:], CORE, SWAP)
    attended = in_pair_order(merged[:rows], partner, core, 1)

    riders = jnp.stack(riders)
    riders = jnp.roll(riders, z, axis=0)
    riders = riders.reshape(ring, 2, tall, units)
    riders = in_pair_order(riders[:, 0:1], riders[:, 1:2], far, 1)
    rest = lax.ppermute(riders, CORE, SWAP)
    riders = in_pair_order(riders[:, :, None], rest[:, :, None], core, 2)
    riders = riders.reshape(ring, 2, 2, 2, share, units)
    rows_in = riders[:, :, :, 0].reshape(columns, units)
    rows_out = riders[:, :, :, 1].reshape(columns, units)
    lanes = 128
    stacked = jnp.concatenate(
        [rows_in, local_up, jnp.zeros((lanes - RANK, units), BF)], axis=0
    )

    up_rows = jnp.concatenate([global_up[:, :128], global_up[:, 128:]], axis=0)
    up_rows = jnp.concatenate([up_rows[8 * k : 8 * k + 8] for k in range(4)], axis=1)
    weights = jnp.concatenate([local_weight, up_rows], axis=0)
    weights = lax.all_gather(weights, ROW, axis=0, tiled=False)
    local_whole = weights[:, :width].reshape(-1, columns)
    up_rows = weights[:, width:]
    up_rows = jnp.concatenate([up_rows[:, :, 128 * k : 128 * k + 128] for k in range(4)], axis=1)
    up_whole = jnp.concatenate([up_rows[:, :RANK], up_rows[:, RANK:]], axis=2)
    cotangent_all = lax.all_gather(cotangent, ROW, axis=0, tiled=True)
    through = contract(cotangent_all, rows_out, 1, 0)

    task_scales = select_rows(global_scales, patch_tasks)
    part = contract(output_weight, attended, 0, 1).astype(BF).reshape(row_count, width, rows)
    low_part = contract(global_down, attended, 0, 1).astype(BF)
    low_part = jnp.broadcast_to(low_part[None], (row_count, RANK, rows))
    arrived = exchange(jnp.concatenate([part, low_part], axis=1), ROW)
    arrived = arrived.astype(F32).sum(axis=0)
    reduced = jnp.transpose(arrived[width:])
    scaled = (reduced * task_scales).astype(BF)
    mixed = arrived[:width] + jnp.transpose(residual.astype(F32)) + contract(global_up, scaled, 0, 1)
    mixed_b = mixed.astype(BF)
    own_patches = rows // row_count
    own_bytes = own_patches * PATCH
    own_tasks = lax.dynamic_slice_in_dim(patch_tasks, row_index * own_patches, own_patches)
    own_ids = lax.dynamic_slice_in_dim(byte_ids, row_index * own_bytes, own_bytes)
    projected = contract(mixed_b, local_weight, 0, 0).astype(BF)
    projected = exchange(projected.reshape(row_count, own_patches, columns), ROW)
    projected = projected.astype(F32).sum(axis=0).astype(BF)

    picks = (own_ids[:, None] == jnp.arange(VOCAB, dtype=jnp.int32)[None, :]).astype(BF)
    embedded = jnp.dot(picks, byte_table, preferred_element_type=F32)
    embedded = embedded.reshape(own_patches, PATCH, -1) + position_table.astype(F32)[None]
    inputs = (embedded + projected.astype(F32)[:, None, :]).reshape(own_bytes, columns)
    inverse = lax.rsqrt(jnp.mean(inputs * inputs, axis=1, keepdims=True) + 1e-06)
    normed = (inputs * inverse * norm_gain).astype(BF)
    lowered = jnp.dot(normed, local_down, preferred_element_type=F32)
    byte_tasks = jnp.repeat(own_tasks, PATCH)
    scales = select_rows(local_scales, byte_tasks)
    shrunk = (lowered * scales).astype(BF)
    joined = jnp.concatenate(
        [normed, shrunk, jnp.zeros((own_bytes, lanes - RANK), BF)], axis=1
    )
    joined = to_everyone(joined, ROW).reshape(row_count * own_bytes, columns + lanes)
    upper = contract(joined, stacked, 1, 0)
    grown = (through * gelu_slope(upper)).astype(BF)
    grad_local_up = contract(joined[:, columns:], grown, 0, 0)[:RANK]
    back = contract(grown, stacked, 1, 1).astype(BF)
    back = exchange(back.reshape(row_count, own_bytes, columns + lanes), ROW)
    back = back.astype(F32).sum(axis=0)
    back_norm = back[:, :columns]
    back_rank = back[:, columns : columns + RANK]
    grad_local_scales = task_totals(byte_tasks, back_rank * lowered)
    moved = (back_rank * scales).astype(BF)
    grad_local_down = contract(moved, normed, 0, 0)
    back_total = back_norm + contract(moved, local_down, 1, 1)
    gained = back_total * norm_gain
    average = jnp.mean(gained * inputs, axis=1, keepdims=True)
    back_inputs = cotangent.astype(F32) + inverse * (
        gained - inputs * inverse * inverse * average
    )
    patch_grad = back_inputs.reshape(own_patches, PATCH, -1).sum(axis=1).astype(BF)

    spare = jnp.zeros((TASKS, columns - RANK), F32)
    local_rows = jnp.concatenate([grad_local_scales, spare], axis=1)
    local_rows = jnp.concatenate([grad_local_down, local_rows, jnp.zeros_like(local_rows)])
    row_pack = jnp.concatenate([patch_grad, local_rows.astype(BF)], axis=0)
    row_pack = to_everyone(row_pack, ROW)
    patch_grads = row_pack[:, :own_patches].reshape(rows, columns)
    local_sums = row_pack[:, own_patches:].astype(F32).sum(axis=0)
    back_mixed = contract(patch_grads, local_weight, 1, 1).astype(BF)
    back_whole = contract(patch_grads, local_whole, 1, 1).astype(BF)
    up_flat = jnp.transpose(up_whole, (1, 0, 2)).reshape(RANK, -1)
    back_scaled = contract(back_whole, up_flat, 1, 1)
    grad_global_up = contract(scaled, back_mixed, 0, 0)
    grad_global_scales = task_totals(patch_tasks, back_scaled * reduced)
    back_reduced = (back_scaled * task_scales).astype(BF)
    grad_global_down = contract(back_reduced, attended, 0, 0)

    small = jnp.concatenate([grad_global_scales, jnp.zeros((TASKS, width - RANK), F32)], axis=1)
    small_local = local_sums[RANK : RANK + TASKS, :width]
    packed = jnp.concatenate(
        [
            grad_global_down,
            grad_global_up,
            grad_local_up,
            local_sums[:RANK, :width],
            local_sums[:RANK, width:],
            small,
            small_local,
        ]
    ).astype(BF)
    shape = packed.shape
    pieces = packed.reshape(lax.axis_size(SEQ), -1)
    pieces = exchange(pieces, SEQ).astype(F32).sum(axis=0).astype(BF)
    packed = to_everyone(pieces, SEQ).reshape(shape).astype(F32)
    return (
        jnp.transpose(packed[:16]),
        packed[16:32],
        packed[80:88, :RANK],
        jnp.transpose(jnp.concatenate([packed[48:64], packed[64:80]], axis=1)),
        packed[32:48],
        packed[88:96, :RANK],
    )


def solution(mesh):
    torus = Mesh(mesh.devices.reshape(16, 2, 2, 4, 2), SEQ_ROW)
    placed = (
        P(SEQ, ROW),
        P(SEQ, ROW),
        P(SEQ, ROW),
        P(SEQ),
        P(SEQ, ROW),
        P(ROW, None),
        P(ROW, None),
        P(None, ROW),
        P(),
        P(ROW, None),
        P(SEQ),
        P(),
        P(),
        P(),
        P(ROW, SEQ),
        P(ROW, SEQ),
        P(),
        P(None, ROW),
        P(),
        P(SEQ_ROW, None),
    )
    return jax.shard_map(
        body,
        mesh=torus,
        in_specs=placed,
        out_specs=(P(ROW, None), P(None, ROW), P(), P(), P(None, ROW), P()),
        check_vma=False,
    )
```

time: 508 us -> 321 us (0.63)
  blocking collectives: 189 us -> 53.1 us
  waiting for transfers between devices: 217 us -> 94.5 us
  starting transfers between devices: 33.3 us -> 107 us
  local copies, waits for them, and re-layouts: 27.9 us -> 15.5 us
  matrix products: 14.6 us -> 21.6 us
  other arithmetic: 5.48 us -> 11.1 us
    all_gather x2, waiting for transfers between devices: 176 us -> 10.8 us  [the longest x1 10.8 us: body(): weights = lax.all_gather(weights, ROW, axis=0, tiled=False)]
    psum x5 -> x0, blocking collectives: 89.8 us -> none  [one_axis_at_a_time(): return functools.reduce(lax.psum, axes, array)]
    ppermute x0 -> x20, starting transfers between devices: none -> 86.4 us  [the longest x7 30.8 us: body(): falling = lax.ppermute(falling, Z, down)]
    all_gather x1 -> x0, blocking collectives: 81 us -> none  [gather_turned(): out, at, finished = (lax.all_gather(both, axis, axis=0, tiled=True), 0, [])]
    all_to_all x1 -> x2, blocking collectives: 18.3 us -> 53.1 us  [exchange(): return lax.all_to_all(pieces, axis, split_axis=0, concat_axis=0, tiled=True)]
    ppermute x0 -> x20, waiting for transfers between devices: none -> 29.7 us  [the longest x7 11.4 us: body(): falling = lax.ppermute(falling, Z, down)]
    all_to_all x7 -> x5, waiting for transfers between devices: 41.4 us -> 54 us  [exchange(): return lax.all_to_all(pieces, axis, split_axis=0, concat_axis=0, tiled=True)]
    all_to_all x7 -> x5, starting transfers between devices: 33.3 us -> 20.9 us  [exchange(): return lax.all_to_all(pieces, axis, split_axis=0, concat_axis=0, tiled=True)]
  transfers between devices with their start and end apart: 9 -> 27, of which waited for: 7 -> 24; matrix products, arithmetic and copies ran while one was open for 1% -> 11% of each run, Pallas kernels for 0% -> 0%
where the time goes in v1:
time: 321 us; the launch traced here: 319 us
  starting transfers between devices  107 us (33%)
  waiting for transfers between devices  94.5 us (29%)
  blocking collectives  53.1 us (17%)
  matrix products  21.6 us (7%)
  between operations  16 us (5%)
  local copies, waits for them, and re-layouts  15.5 us (5%)
  other arithmetic  11.1 us (3%)
    all_to_all x5, waiting for transfers between devices, exchange(): return lax.all_to_all(pieces, axis, split_axis=0, concat_axis=0, tiled=True)  54 us
    all_to_all x2, blocking collectives, exchange(): return lax.all_to_all(pieces, axis, split_axis=0, concat_axis=0, tiled=True)  53.1 us
    ppermute x7, starting transfers between devices, body(): falling = lax.ppermute(falling, Z, down)  30.8 us
    ppermute x8, starting transfers between devices, body(): rising = lax.ppermute(rising, Z, up)  22.1 us
    all_to_all x5, starting transfers between devices, exchange(): return lax.all_to_all(pieces, axis, split_axis=0, concat_axis=0, tiled=True)  20.9 us
    dot_general x21, matrix products, contract(): lax.dot_general(left, right, (((left_dim,), (right_dim,)), ((), ())), pre...  15.1 us
    ppermute x1, starting transfers between devices, body(): partner = lax.ppermute(merged[rows:], CORE, SWAP)  13.3 us
    ppermute x7, waiting for transfers between devices, body(): falling = lax.ppermute(falling, Z, down)  11.4 us
  transfers between devices with their start and end apart: 27, of which 24 were waited for; matrix products, arithmetic and copies ran while one was open for 11% of the time, Pallas kernels for 0%

profile of v1, /device:TPU:1, one launch (start us, length us, event | category | flops | bytes accessed | tf_op | source)
XLA Modules:
  0.0 319.1 jit_solution(4226346698423121856)
XLA Ops:
  7.3 0.9 constant_dynamic-slice_fusion.6
  9.0 8.8 %collective-permute-start = (bf16[128,384]{1,0:T(8,128)(2,1)S(1)}, bf16[128,384]{1,0:T(8,128)(2,1)S(1)}, u32[]{:S(2)}, u32[]{:S(2)}) collective-permute-start(bf16[128,384]{1,0:T(8,128)(2,1)S(1)} %pad_maximum_fusion.6), channel_id=1, source_target_pairs={{0,8},{8,0},{1,9},{9,1},{2,10},{10,2},{3,11},{11,3},{4,12},{12,4},... | collective-permute-start | bytes 294920 | tf_op jit(solution)/shard_map/ppermute | solution.py:112
  18.6 1.3 dynamic_slice.28
  21.1 1.9 collective-permute-start.1
  23.0 5.3 %collective-permute-done.1 = bf16[288,128]{1,0:T(8,128)(2,1)S(1)} collective-permute-done((bf16[288,128]{1,0:T(8,128)(2,1)S(1)}, bf16[288,128]{1,0:T(8,128)(2,1)S(1)}, u32[]{:S(2)}, u32[]{:S(2)}) %collective-permute-start.1) | collective-permute-done | bytes 73760 | tf_op jit(solution)/shard_map/ppermute | solution.py:116
  28.4 1.9 collective-permute-start.2
  30.3 5.7 %collective-permute-start.3 = (bf16[288,256]{1,0:T(8,128)(2,1)S(1)}, bf16[288,256]{1,0:T(8,128)(2,1)S(1)}, u32[]{:S(2)}, u32[]{:S(2)}) collective-permute-start(bf16[288,256]{1,0:T(8,128)(2,1)S(1)} %maximum_maximum_fusion.5), channel_id=1, source_target_pairs={{0,480},{32,0},{64,32},{96,64},{128,96},{160,128},{192,160},{224,1... | collective-permute-start | bytes 442376 | tf_op jit(solution)/shard_map/ppermute | solution.py:159
  36.3 1.3 collective-permute-done.2
  38.7 1.9 collective-permute-start.4
  40.7 5.4 %collective-permute-start.5 = (bf16[288,256]{1,0:T(8,128)(2,1)S(1)}, bf16[288,256]{1,0:T(8,128)(2,1)S(1)}, u32[]{:S(2)}, u32[]{:S(2)}) collective-permute-start(bf16[288,256]{1,0:T(8,128)(2,1)S(1)} %collective-permute-done.3), channel_id=1, source_target_pairs={{0,480},{32,0},{64,32},{96,64},{128,96},{160,128},{192,160},{224,1... | collective-permute-start | bytes 442376 | tf_op jit(solution)/shard_map/ppermute | solution.py:159
  46.1 0.9 collective-permute-done.4
  47.1 1.1 collective-permute-done.5
  48.5 1.9 collective-permute-start.6
  50.4 5.3 %collective-permute-start.7 = (bf16[288,256]{1,0:T(8,128)(2,1)S(1)}, bf16[288,256]{1,0:T(8,128)(2,1)S(1)}, u32[]{:S(2)}, u32[]{:S(2)}) collective-permute-start(bf16[288,256]{1,0:T(8,128)(2,1)S(1)} %collective-permute-done.5), channel_id=1, source_target_pairs={{0,480},{32,0},{64,32},{96,64},{128,96},{160,128},{192,160},{224,1... | collective-permute-start | bytes 442376 | tf_op jit(solution)/shard_map/ppermute | solution.py:159
  55.8 1.0 collective-permute-done.6
  56.8 1.1 collective-permute-done.7
  58.2 1.9 collective-permute-start.8
  60.1 5.4 %collective-permute-start.9 = (bf16[288,256]{1,0:T(8,128)(2,1)S(1)}, bf16[288,256]{1,0:T(8,128)(2,1)S(1)}, u32[]{:S(2)}, u32[]{:S(2)}) collective-permute-start(bf16[288,256]{1,0:T(8,128)(2,1)S(1)} %collective-permute-done.7), channel_id=1, source_target_pairs={{0,480},{32,0},{64,32},{96,64},{128,96},{160,128},{192,160},{224,1... | collective-permute-start | bytes 442376 | tf_op jit(solution)/shard_map/ppermute | solution.py:159
  66.2 1.5 collective-permute-done.9
  68.0 3.3 %collective-permute-start.10 = (bf16[288,256]{1,0:T(8,128)(2,1)S(1)}, bf16[288,256]{1,0:T(8,128)(2,1)S(1)}, u32[]{:S(2)}, u32[]{:S(2)}) collective-permute-start(bf16[288,256]{1,0:T(8,128)(2,1)S(1)} %collective-permute-done.8), channel_id=1, source_target_pairs={{0,32},{32,64},{64,96},{96,128},{128,160},{160,192},{192,224},{224... | collective-permute-start | bytes 442376 | tf_op jit(solution)/shard_map/ppermute | solution.py:155
  71.3 3.6 %collective-permute-start.11 = (bf16[288,256]{1,0:T(8,128)(2,1)S(1)}, bf16[288,256]{1,0:T(8,128)(2,1)S(1)}, u32[]{:S(2)}, u32[]{:S(2)}) collective-permute-start(bf16[288,256]{1,0:T(8,128)(2,1)S(1)} %collective-permute-done.9), channel_id=1, source_target_pairs={{0,480},{32,0},{64,32},{96,64},{128,96},{160,128},{192,160},{224,1... | collective-permute-start | bytes 442376 | tf_op jit(solution)/shard_map/ppermute | solution.py:159
  75.5 1.7 collective-permute-done.11
  77.6 4.6 %collective-permute-start.12 = (bf16[288,256]{1,0:T(8,128)(2,1)S(1)}, bf16[288,256]{1,0:T(8,128)(2,1)S(1)}, u32[]{:S(2)}, u32[]{:S(2)}) collective-permute-start(bf16[288,256]{1,0:T(8,128)(2,1)S(1)} %collective-permute-done.10), channel_id=1, source_target_pairs={{0,32},{32,64},{64,96},{96,128},{128,160},{160,192},{192,224},{224... | collective-permute-start | bytes 442376 | tf_op jit(solution)/shard_map/ppermute | solution.py:155
  82.1 2.1 collective-permute-start.13
  84.9 3.1 collective-permute-done.13
  88.4 3.4 %collective-permute-start.14 = (bf16[288,256]{1,0:T(8,128)(2,1)S(1)}, bf16[288,256]{1,0:T(8,128)(2,1)S(1)}, u32[]{:S(2)}, u32[]{:S(2)}) collective-permute-start(bf16[288,256]{1,0:T(8,128)(2,1)S(1)} %collective-permute-done.12), channel_id=1, source_target_pairs={{0,32},{32,64},{64,96},{96,128},{128,160},{160,192},{192,224},{224... | collective-permute-start | bytes 442376 | tf_op jit(solution)/shard_map/ppermute | solution.py:155
  91.7 3.1 collective-permute-start.15
  95.5 2.1 collective-permute-done.15
  98.0 3.1 collective-permute-start.16
  101.1 3.9 %collective-permute-done.16 = bf16[288,256]{1,0:T(8,128)(2,1)S(1)} collective-permute-done((bf16[288,256]{1,0:T(8,128)(2,1)S(1)}, bf16[288,256]{1,0:T(8,128)(2,1)S(1)}, u32[]{:S(2)}, u32[]{:S(2)}) %collective-permute-start.16) | collective-permute-done | bytes 147488 | tf_op jit(solution)/shard_map/ppermute | solution.py:155
  105.8 1.5 fusion.36
  110.7 4.7 %collective-permute-start.17 = (bf16[256,256]{0,1:T(8,128)(2,1)S(1)}, bf16[256,256]{0,1:T(8,128)(2,1)S(1)}, u32[]{:S(2)}, u32[]{:S(2)}) collective-permute-start(bf16[256,256]{0,1:T(8,128)(2,1)S(1)} %pad_maximum_fusion.5), channel_id=1, source_target_pairs={{0,16},{16,0},{1,17},{17,1},{2,18},{18,2},{3,19},{19,3},{4,20},{20... | collective-permute-start | bytes 393224 | tf_op jit(solution)/shard_map/ppermute | solution.py:175
  115.6 2.3 collective-permute-done.17
  118.0 13.3 %collective-permute-start.18 = (bf16[128,128]{0,1:T(8,128)(2,1)S(1)}, bf16[128,128]{0,1:T(8,128)(2,1)S(1)}, u32[]{:S(2)}, u32[]{:S(2)}) collective-permute-start(bf16[128,128]{0,1:T(8,128)(2,1)S(1)} %slice.452), channel_id=1, source_target_pairs={{0,8},{8,0},{1,9},{9,1},{2,10},{10,2},{3,11},{11,3},{4,12},{12,4},... | collective-permute-start | bytes 98312 | tf_op jit(solution)/shard_map/ppermute | solution.py:184
  133.9 5.3 %all-to-all-start = ((bf16[8,272,128]{2,1,0:T(8,128)(2,1)}), bf16[8,272,128]{2,1,0:T(8,128)(2,1)S(1)}, u32[]{:S(2)}, u32[]{:S(2)}) async-start(bf16[8,272,128]{2,1,0:T(8,128)(2,1)} %pad_maximum_fusion), calls=%async_computation | async-start | bytes 1114112 | tf_op jit(solution)/shard_map/all_to_all | solution.py:24
  139.3 9.5 %all-to-all-done = bf16[8,272,128]{2,1,0:T(8,128)(2,1)S(1)} async-done(((bf16[8,272,128]{2,1,0:T(8,128)(2,1)}), bf16[8,272,128]{2,1,0:T(8,128)(2,1)S(1)}, u32[]{:S(2)}, u32[]{:S(2)}) %all-to-all-start) | async-done | bytes 557088 | tf_op jit(solution)/shard_map/all_to_all | solution.py:24
  149.0 0.9 multiply_convert_fusion.4
  149.9 1.0 convolution_convert_fusion.3
  150.9 3.5 %all-to-all-start.1 = ((bf16[8,16,512]{2,1,0:T(8,128)(2,1)}), bf16[8,16,512]{2,1,0:T(8,128)(2,1)S(1)}, u32[]{:S(2)}, u32[]{:S(2)}) async-start(bf16[8,16,512]{2,1,0:T(8,128)(2,1)} %bitcast.30), calls=%async_computation.1 | async-start | bytes 262144 | tf_op jit(solution)/shard_map/all_to_all | solution.py:24
  154.4 5.5 %all-to-all-done.1 = bf16[8,16,512]{2,1,0:T(8,128)(2,1)S(1)} async-done(((bf16[8,16,512]{2,1,0:T(8,128)(2,1)}), bf16[8,16,512]{2,1,0:T(8,128)(2,1)S(1)}, u32[]{:S(2)}, u32[]{:S(2)}) %all-to-all-start.1) | async-done | bytes 131104 | tf_op jit(solution)/shard_map/all_to_all | solution.py:24
  161.3 1.2 broadcast_in_dim.88
  162.5 3.6 %all-to-all-start.2 = ((bf16[8,128,640]{2,1,0:T(8,128)(2,1)}), bf16[8,128,640]{2,1,0:T(8,128)(2,1)S(1)}, u32[]{:S(2)}, u32[]{:S(2)}) async-start(bf16[8,128,640]{2,1,0:T(8,128)(2,1)} %broadcast_in_dim.88), calls=%async_computation.2 | async-start | bytes 2621440 | tf_op jit(solution)/shard_map/all_to_all | solution.py:24
  166.2 4.8 %collective-permute-start.19 = (bf16[16,2,16,256]{3,2,1,0:T(8,128)(2,1)S(1)}, bf16[16,2,16,256]{3,2,1,0:T(8,128)(2,1)}, u32[]{:S(2)}, u32[]{:S(2)}) collective-permute-start(bf16[16,2,16,256]{3,2,1,0:T(8,128)(2,1)S(1)} %pad_maximum_fusion.2), channel_id=1, source_target_pairs={{0,8},{8,0},{1,9},{9,1},{2,10},{10,2},{3,11},{11,3},{4,12},{12,4},... | collective-permute-start | bytes 786440 | tf_op jit(solution)/shard_map/ppermute | solution.py:191
  172.2 1.0 select_bitcast_fusion
  173.3 8.6 %all-to-all-done.2 = bf16[8,128,640]{2,1,0:T(8,128)(2,1)S(1)} async-done(((bf16[8,128,640]{2,1,0:T(8,128)(2,1)}), bf16[8,128,640]{2,1,0:T(8,128)(2,1)S(1)}, u32[]{:S(2)}, u32[]{:S(2)}) %all-to-all-start.2) | async-done | bytes 1310752 | tf_op jit(solution)/shard_map/all_to_all | solution.py:24
  181.9 2.4 fusion.101
  184.3 2.2 fusion.9
  186.5 1.8 convolution_convert_fusion.2
  188.3 4.4 %all-to-all-start.3 = ((bf16[8,128,640]{2,1,0:T(8,128)(2,1)}), bf16[8,128,640]{2,1,0:T(8,128)(2,1)}, u32[]{:S(2)}, u32[]{:S(2)}) async-start(bf16[8,128,640]{2,1,0:T(8,128)(2,1)} %bitcast.204), calls=%async_computation.3 | async-start | bytes 2621440 | tf_op jit(solution)/shard_map/all_to_all | solution.py:24
  194.2 30.3 %all-to-all-done.3 = bf16[8,128,640]{2,1,0:T(8,128)(2,1)} async-done(((bf16[8,128,640]{2,1,0:T(8,128)(2,1)}), bf16[8,128,640]{2,1,0:T(8,128)(2,1)}, u32[]{:S(2)}, u32[]{:S(2)}) %all-to-all-start.3) | async-done | bytes 1310752 | tf_op jit(solution)/shard_map/all_to_all | solution.py:24
  224.5 1.6 convert_reduce_fusion
  227.9 4.1 %all-to-all-start.4 = ((bf16[8,48,512]{2,1,0:T(8,128)(2,1)}), bf16[8,48,512]{2,1,0:T(8,128)(2,1)}, u32[]{:S(2)}, u32[]{:S(2)}) async-start(bf16[8,48,512]{2,1,0:T(8,128)(2,1)} %broadcast_in_dim.176), calls=%async_computation.4 | async-start | bytes 786432 | tf_op jit(solution)/shard_map/all_to_all | solution.py:24
  232.1 0.9 fusion.91
  233.0 10.8 %all-gather.6.cloned.1.call-done = bf16[2112,512]{1,0:T(8,128)(2,1)} async-done(((bf16[264,512]{1,0:T(8,128)(2,1)}), bf16[2112,512]{1,0:T(8,128)(2,1)}) %all-gather.6.cloned.1.call-update) | async-done | bytes 2162704 | tf_op jit(solution)/shard_map/all_gather | solution.py:204
  243.8 1.8 slice.477
  247.1 0.9 slice.476
  248.0 1.9 fusion.10
  249.9 0.9 convolution_convert_fusion.8
  250.8 0.9 fusion.27
  252.9 1.0 slice_reduce_fusion
  254.4 0.9 reduce.13
  255.5 33.4 %all_to_all.37 = bf16[64,2,192]{2,1,0:T(2,128)(2,1)S(1)} all-to-all(bf16[64,2,192]{2,1,0:T(2,128)(2,1)S(1)} %reshape.613), channel_id=1, replica_groups=mesh['seq_0'=16,'seq_1'=2,'seq_2'=2,'row_0'=4,'row_1'=2] {'seq_0','seq_1..., dimensions={0} | all-to-all | bytes 98304 | tf_op jit(solution)/shard_map/all_to_all | solution.py:24
  289.2 0.9 reduce.14
  290.2 19.7 %all_to_all.38 = bf16[64,2,192]{2,1,0:T(2,128)(2,1)S(1)} all-to-all(bf16[64,2,192]{2,1,0:T(2,128)(2,1)S(1)} %reshape.615), channel_id=1, replica_groups=mesh['seq_0'=16,'seq_1'=2,'seq_2'=2,'row_0'=4,'row_1'=2] {'seq_0','seq_1..., dimensions={0} | all-to-all | bytes 98304 | tf_op jit(solution)/shard_map/all_to_all | solution.py:24
  (278 shorter events, 26.6 us)
Async XLA Ops:
  7.2 125.0 %copy-start = (bf16[256,2048]{1,0:T(8,128)(2,1)S(1)}, bf16[256,2048]{1,0:T(8,128)(2,1)}, u32[]{:S(2)}) copy-start(bf16[256,2048]{1,0:T(8,128)(2,1)} %param.25) | copy-start | bytes 3145732
  7.2 10.9 %copy-start.26 = (bf16[8,512]{1,0:T(8,128)(2,1)S(1)}, bf16[8,512]{1,0:T(8,128)(2,1)}, u32[]{:S(2)}) copy-start(bf16[8,512]{1,0:T(8,128)(2,1)} %param.32) | copy-start | bytes 24580
  7.2 10.9 %copy-start.36 = (s32[128]{0:T(128)S(1)}, s32[128]{0:T(128)}, u32[]{:S(2)}) copy-start(s32[128]{0:T(128)} %param.23) | copy-start | bytes 1540
  7.2 11.2 %copy-start.11 = (bf16[256,8]{0,1:T(8,128)(2,1)S(1)}, bf16[256,8]{0,1:T(8,128)(2,1)}, u32[]{:S(2)}) copy-start(bf16[256,8]{0,1:T(8,128)(2,1)} %param.34) | copy-start | bytes 12292
  7.2 11.2 %copy-start.10 = (bf16[256,8]{0,1:T(8,128)(2,1)S(1)}, bf16[256,8]{0,1:T(8,128)(2,1)}, u32[]{:S(2)}) copy-start(bf16[256,8]{0,1:T(8,128)(2,1)} %param.35) | copy-start | bytes 12292
  7.2 12.7 %copy-start.34 = (f32[8,16]{1,0:T(8,128)S(1)}, f32[8,16]{1,0:T(8,128)}, u32[]{:S(2)}) copy-start(f32[8,16]{1,0:T(8,128)} %param.38) | copy-start | bytes 1540
  7.2 177.0 %all-gather.4.cloned.1.call-start = ((), (), s32[]{:S(2)}) async-start(), calls=%async_computation.7 | async-start | bytes 1179648 | tf_op jit(solution)/shard_map/all_gather | solution.py:209
  9.0 12.0 %collective-permute-start = (bf16[128,384]{1,0:T(8,128)(2,1)S(1)}, bf16[128,384]{1,0:T(8,128)(2,1)S(1)}, u32[]{:S(2)}, u32[]{:S(2)}) collective-permute-start(bf16[128,384]{1,0:T(8,128)(2,1)S(1)} %pad_maximum_fusion.6), channel_id=1, source_target_pairs={{0,8},{8,0},{1,9},{9,1},{2,10},{10,2},{3,11},{11,3},{4,12},{12,4},... | collective-permute-start | bytes 294920 | tf_op jit(solution)/shard_map/ppermute | solution.py:112
  18.4 2.5 copy-start.27
  20.9 140.4 %copy-start.20 = (bf16[640]{0:T(1024)(128)(2,1)}, bf16[640]{0:T(1024)(128)(2,1)S(1)}, u32[]{:S(2)}) copy-start(bf16[640]{0:T(1024)(128)(2,1)S(1)} %pad.24.clone) | copy-start | bytes 3844
  21.1 7.3 %collective-permute-start.1 = (bf16[288,128]{1,0:T(8,128)(2,1)S(1)}, bf16[288,128]{1,0:T(8,128)(2,1)S(1)}, u32[]{:S(2)}, u32[]{:S(2)}) collective-permute-start(bf16[288,128]{1,0:T(8,128)(2,1)S(1)} %fusion.152), channel_id=1, source_target_pairs={{0,16},{16,0},{1,17},{17,1},{2,18},{18,2},{3,19},{19,3},{4,20},{20... | collective-permute-start | bytes 221192 | tf_op jit(solution)/shard_map/ppermute | solution.py:116
  28.4 9.3 %collective-permute-start.2 = (bf16[288,256]{1,0:T(8,128)(2,1)S(1)}, bf16[288,256]{1,0:T(8,128)(2,1)S(1)}, u32[]{:S(2)}, u32[]{:S(2)}) collective-permute-start(bf16[288,256]{1,0:T(8,128)(2,1)S(1)} %maximum_maximum_fusion.5), channel_id=1, source_target_pairs={{0,32},{32,64},{64,96},{96,128},{128,160},{160,192},{192,224},{224... | collective-permute-start | bytes 442376 | tf_op jit(solution)/shard_map/ppermute | solution.py:155
  30.3 8.1 %collective-permute-start.3 = (bf16[288,256]{1,0:T(8,128)(2,1)S(1)}, bf16[288,256]{1,0:T(8,128)(2,1)S(1)}, u32[]{:S(2)}, u32[]{:S(2)}) collective-permute-start(bf16[288,256]{1,0:T(8,128)(2,1)S(1)} %maximum_maximum_fusion.5), channel_id=1, source_target_pairs={{0,480},{32,0},{64,32},{96,64},{128,96},{160,128},{192,160},{224,1... | collective-permute-start | bytes 442376 | tf_op jit(solution)/shard_map/ppermute | solution.py:159
  38.7 8.3 %collective-permute-start.4 = (bf16[288,256]{1,0:T(8,128)(2,1)S(1)}, bf16[288,256]{1,0:T(8,128)(2,1)S(1)}, u32[]{:S(2)}, u32[]{:S(2)}) collective-permute-start(bf16[288,256]{1,0:T(8,128)(2,1)S(1)} %collective-permute-done.2), channel_id=1, source_target_pairs={{0,32},{32,64},{64,96},{96,128},{128,160},{160,192},{192,224},{224... | collective-permute-start | bytes 442376 | tf_op jit(solution)/shard_map/ppermute | solution.py:155
  40.7 7.5 %collective-permute-start.5 = (bf16[288,256]{1,0:T(8,128)(2,1)S(1)}, bf16[288,256]{1,0:T(8,128)(2,1)S(1)}, u32[]{:S(2)}, u32[]{:S(2)}) collective-permute-start(bf16[288,256]{1,0:T(8,128)(2,1)S(1)} %collective-permute-done.3), channel_id=1, source_target_pairs={{0,480},{32,0},{64,32},{96,64},{128,96},{160,128},{192,160},{224,1... | collective-permute-start | bytes 442376 | tf_op jit(solution)/shard_map/ppermute | solution.py:159
  48.5 8.3 %collective-permute-start.6 = (bf16[288,256]{1,0:T(8,128)(2,1)S(1)}, bf16[288,256]{1,0:T(8,128)(2,1)S(1)}, u32[]{:S(2)}, u32[]{:S(2)}) collective-permute-start(bf16[288,256]{1,0:T(8,128)(2,1)S(1)} %collective-permute-done.4), channel_id=1, source_target_pairs={{0,32},{32,64},{64,96},{96,128},{128,160},{160,192},{192,224},{224... | collective-permute-start | bytes 442376 | tf_op jit(solution)/shard_map/ppermute | solution.py:155
  50.4 7.4 %collective-permute-start.7 = (bf16[288,256]{1,0:T(8,128)(2,1)S(1)}, bf16[288,256]{1,0:T(8,128)(2,1)S(1)}, u32[]{:S(2)}, u32[]{:S(2)}) collective-permute-start(bf16[288,256]{1,0:T(8,128)(2,1)S(1)} %collective-permute-done.5), channel_id=1, source_target_pairs={{0,480},{32,0},{64,32},{96,64},{128,96},{160,128},{192,160},{224,1... | collective-permute-start | bytes 442376 | tf_op jit(solution)/shard_map/ppermute | solution.py:159
  58.2 7.9 %collective-permute-start.8 = (bf16[288,256]{1,0:T(8,128)(2,1)S(1)}, bf16[288,256]{1,0:T(8,128)(2,1)S(1)}, u32[]{:S(2)}, u32[]{:S(2)}) collective-permute-start(bf16[288,256]{1,0:T(8,128)(2,1)S(1)} %collective-permute-done.6), channel_id=1, source_target_pairs={{0,32},{32,64},{64,96},{96,128},{128,160},{160,192},{192,224},{224... | collective-permute-start | bytes 442376 | tf_op jit(solution)/shard_map/ppermute | solution.py:155
  60.1 7.5 %collective-permute-start.9 = (bf16[288,256]{1,0:T(8,128)(2,1)S(1)}, bf16[288,256]{1,0:T(8,128)(2,1)S(1)}, u32[]{:S(2)}, u32[]{:S(2)}) collective-permute-start(bf16[288,256]{1,0:T(8,128)(2,1)S(1)} %collective-permute-done.7), channel_id=1, source_target_pairs={{0,480},{32,0},{64,32},{96,64},{128,96},{160,128},{192,160},{224,1... | collective-permute-start | bytes 442376 | tf_op jit(solution)/shard_map/ppermute | solution.py:159
  68.0 7.5 %collective-permute-start.10 = (bf16[288,256]{1,0:T(8,128)(2,1)S(1)}, bf16[288,256]{1,0:T(8,128)(2,1)S(1)}, u32[]{:S(2)}, u32[]{:S(2)}) collective-permute-start(bf16[288,256]{1,0:T(8,128)(2,1)S(1)} %collective-permute-done.8), channel_id=1, source_target_pairs={{0,32},{32,64},{64,96},{96,128},{128,160},{160,192},{192,224},{224... | collective-permute-start | bytes 442376 | tf_op jit(solution)/shard_map/ppermute | solution.py:155
  71.3 5.9 %collective-permute-start.11 = (bf16[288,256]{1,0:T(8,128)(2,1)S(1)}, bf16[288,256]{1,0:T(8,128)(2,1)S(1)}, u32[]{:S(2)}, u32[]{:S(2)}) collective-permute-start(bf16[288,256]{1,0:T(8,128)(2,1)S(1)} %collective-permute-done.9), channel_id=1, source_target_pairs={{0,480},{32,0},{64,32},{96,64},{128,96},{160,128},{192,160},{224,1... | collective-permute-start | bytes 442376 | tf_op jit(solution)/shard_map/ppermute | solution.py:159
  77.6 7.3 %collective-permute-start.12 = (bf16[288,256]{1,0:T(8,128)(2,1)S(1)}, bf16[288,256]{1,0:T(8,128)(2,1)S(1)}, u32[]{:S(2)}, u32[]{:S(2)}) collective-permute-start(bf16[288,256]{1,0:T(8,128)(2,1)S(1)} %collective-permute-done.10), channel_id=1, source_target_pairs={{0,32},{32,64},{64,96},{96,128},{128,160},{160,192},{192,224},{224... | collective-permute-start | bytes 442376 | tf_op jit(solution)/shard_map/ppermute | solution.py:155
  82.1 5.9 %collective-permute-start.13 = (bf16[288,256]{1,0:T(8,128)(2,1)S(1)}, bf16[288,256]{1,0:T(8,128)(2,1)S(1)}, u32[]{:S(2)}, u32[]{:S(2)}) collective-permute-start(bf16[288,256]{1,0:T(8,128)(2,1)S(1)} %collective-permute-done.11), channel_id=1, source_target_pairs={{0,480},{32,0},{64,32},{96,64},{128,96},{160,128},{192,160},{224,1... | collective-permute-start | bytes 442376 | tf_op jit(solution)/shard_map/ppermute | solution.py:159
  88.4 7.1 %collective-permute-start.14 = (bf16[288,256]{1,0:T(8,128)(2,1)S(1)}, bf16[288,256]{1,0:T(8,128)(2,1)S(1)}, u32[]{:S(2)}, u32[]{:S(2)}) collective-permute-start(bf16[288,256]{1,0:T(8,128)(2,1)S(1)} %collective-permute-done.12), channel_id=1, source_target_pairs={{0,32},{32,64},{64,96},{96,128},{128,160},{160,192},{192,224},{224... | collective-permute-start | bytes 442376 | tf_op jit(solution)/shard_map/ppermute | solution.py:155
  91.7 5.9 %collective-permute-start.15 = (bf16[288,256]{1,0:T(8,128)(2,1)S(1)}, bf16[288,256]{1,0:T(8,128)(2,1)S(1)}, u32[]{:S(2)}, u32[]{:S(2)}) collective-permute-start(bf16[288,256]{1,0:T(8,128)(2,1)S(1)} %collective-permute-done.13), channel_id=1, source_target_pairs={{0,480},{32,0},{64,32},{96,64},{128,96},{160,128},{192,160},{224,1... | collective-permute-start | bytes 442376 | tf_op jit(solution)/shard_map/ppermute | solution.py:159
  98.0 7.1 %collective-permute-start.16 = (bf16[288,256]{1,0:T(8,128)(2,1)S(1)}, bf16[288,256]{1,0:T(8,128)(2,1)S(1)}, u32[]{:S(2)}, u32[]{:S(2)}) collective-permute-start(bf16[288,256]{1,0:T(8,128)(2,1)S(1)} %collective-permute-done.14), channel_id=1, source_target_pairs={{0,32},{32,64},{64,96},{96,128},{128,160},{160,192},{192,224},{224... | collective-permute-start | bytes 442376 | tf_op jit(solution)/shard_map/ppermute | solution.py:155
  110.7 7.2 %collective-permute-start.17 = (bf16[256,256]{0,1:T(8,128)(2,1)S(1)}, bf16[256,256]{0,1:T(8,128)(2,1)S(1)}, u32[]{:S(2)}, u32[]{:S(2)}) collective-permute-start(bf16[256,256]{0,1:T(8,128)(2,1)S(1)} %pad_maximum_fusion.5), channel_id=1, source_target_pairs={{0,16},{16,0},{1,17},{17,1},{2,18},{18,2},{3,19},{19,3},{4,20},{20... | collective-permute-start | bytes 393224 | tf_op jit(solution)/shard_map/ppermute | solution.py:175
  118.0 14.1 %collective-permute-start.18 = (bf16[128,128]{0,1:T(8,128)(2,1)S(1)}, bf16[128,128]{0,1:T(8,128)(2,1)S(1)}, u32[]{:S(2)}, u32[]{:S(2)}) collective-permute-start(bf16[128,128]{0,1:T(8,128)(2,1)S(1)} %slice.452), channel_id=1, source_target_pairs={{0,8},{8,0},{1,9},{9,1},{2,10},{10,2},{3,11},{11,3},{4,12},{12,4},... | collective-permute-start | bytes 98312 | tf_op jit(solution)/shard_map/ppermute | solution.py:184
  132.2 0.7 copy-start.8
  132.2 0.7 copy-start.33
  133.9 15.1 %copy-start.35 = (f32[8,16]{1,0:T(8,128)S(1)}, f32[8,16]{1,0:T(8,128)}, u32[]{:S(2)}) copy-start(f32[8,16]{1,0:T(8,128)} %param.28) | copy-start | bytes 1540
  133.9 15.1 %copy-start.37 = (s32[128]{0:T(128)S(1)}, s32[128]{0:T(128)}, u32[]{:S(2)}) copy-start(s32[128]{0:T(128)} %param.23) | copy-start | bytes 1540
  133.9 16.0 %copy-start.1 = (bf16[256,512]{1,0:T(8,128)(2,1)S(1)}, bf16[256,512]{1,0:T(8,128)(2,1)}, u32[]{:S(2)}) copy-start(bf16[256,512]{1,0:T(8,128)(2,1)} %param.29) | copy-start | bytes 786436
  133.9 16.0 %copy-start.12 = (bf16[128,256]{1,0:T(8,128)(2,1)S(1)}, bf16[128,256]{1,0:T(8,128)(2,1)}, u32[]{:S(2)}) copy-start(bf16[128,256]{1,0:T(8,128)(2,1)} %param.24) | copy-start | bytes 196612
  133.9 16.0 %copy-start.16 = (bf16[16,256]{1,0:T(8,128)(2,1)S(1)}, bf16[16,256]{1,0:T(8,128)(2,1)}, u32[]{:S(2)}) copy-start(bf16[16,256]{1,0:T(8,128)(2,1)} %param.27) | copy-start | bytes 24580
  133.9 14.9 %all-to-all-start = ((bf16[8,272,128]{2,1,0:T(8,128)(2,1)}), bf16[8,272,128]{2,1,0:T(8,128)(2,1)S(1)}, u32[]{:S(2)}, u32[]{:S(2)}) async-start(bf16[8,272,128]{2,1,0:T(8,128)(2,1)} %pad_maximum_fusion), calls=%async_computation | async-start | bytes 1114112 | tf_op jit(solution)/shard_map/all_to_all | solution.py:24
  139.2 20.8 %copy-start.6 = (bf16[256,512]{1,0:T(8,128)(2,1)S(1)}, bf16[256,512]{1,0:T(8,128)(2,1)}, u32[]{:S(2)}) copy-start(bf16[256,512]{1,0:T(8,128)(2,1)} %param.31) | copy-start | bytes 786436
  139.2 20.8 %copy-start.31 = (s32[128]{0:T(128)S(1)}, s32[128]{0:T(128)}, u32[]{:S(2)}) copy-start(s32[128]{0:T(128)} %dynamic_slice.28) | copy-start | bytes 1540
  139.2 21.6 %copy-start.24 = (f32[512]{0:T(512)S(1)}, f32[512]{0:T(512)}, u32[]{:S(2)}) copy-start(f32[512]{0:T(512)} %param.33) | copy-start | bytes 6148
  148.9 12.1 %copy-start.4 = (f32[272,128]{1,0:T(8,128)}, f32[272,128]{1,0:T(8,128)S(1)}, u32[]{:S(2)}) copy-start(f32[272,128]{1,0:T(8,128)S(1)} %convert_reduce_fusion.1) | copy-start | bytes 417796
  148.9 12.1 %copy-start.13 = (bf16[512,16]{0,1:T(8,128)(2,1)S(1)}, bf16[512,16]{0,1:T(8,128)(2,1)}, u32[]{:S(2)}) copy-start(bf16[512,16]{0,1:T(8,128)(2,1)} %param.36) | copy-start | bytes 49156
  148.9 12.1 %copy-start.18 = (f32[128,16]{0,1:T(8,128)S(1)}, f32[128,16]{0,1:T(8,128)}, u32[]{:S(2)}) copy-start(f32[128,16]{0,1:T(8,128)} %fusion.158) | copy-start | bytes 24580
  149.9 12.6 %copy-start.22 = (bf16[128,16]{0,1:T(8,128)(2,1)}, bf16[128,16]{0,1:T(8,128)(2,1)S(1)}, u32[]{:S(2)}) copy-start(bf16[128,16]{0,1:T(8,128)(2,1)S(1)} %get-tuple-element.116) | copy-start | bytes 12292
  150.9 9.1 %all-to-all-start.1 = ((bf16[8,16,512]{2,1,0:T(8,128)(2,1)}), bf16[8,16,512]{2,1,0:T(8,128)(2,1)S(1)}, u32[]{:S(2)}, u32[]{:S(2)}) async-start(bf16[8,16,512]{2,1,0:T(8,128)(2,1)} %bitcast.30), calls=%async_computation.1 | async-start | bytes 262144 | tf_op jit(solution)/shard_map/all_to_all | solution.py:24
  162.5 19.4 %all-to-all-start.2 = ((bf16[8,128,640]{2,1,0:T(8,128)(2,1)}), bf16[8,128,640]{2,1,0:T(8,128)(2,1)S(1)}, u32[]{:S(2)}, u32[]{:S(2)}) async-start(bf16[8,128,640]{2,1,0:T(8,128)(2,1)} %broadcast_in_dim.88), calls=%async_computation.2 | async-start | bytes 2621440 | tf_op jit(solution)/shard_map/all_to_all | solution.py:24
  166.1 5.0 %copy-start.17 = (bf16[16,256]{1,0:T(8,128)(2,1)S(1)}, bf16[16,256]{1,0:T(8,128)(2,1)}, u32[]{:S(2)}) copy-start(bf16[16,256]{1,0:T(8,128)(2,1)} %param.27) | copy-start | bytes 24580
  166.1 77.7 %all-gather.6.cloned.1.call-start = ((), (), s32[]{:S(2)}) async-start(), calls=%async_computation.8 | async-start | bytes 2433024 | tf_op jit(solution)/shard_map/all_gather | solution.py:204
  166.2 5.9 %collective-permute-start.19 = (bf16[16,2,16,256]{3,2,1,0:T(8,128)(2,1)S(1)}, bf16[16,2,16,256]{3,2,1,0:T(8,128)(2,1)}, u32[]{:S(2)}, u32[]{:S(2)}) collective-permute-start(bf16[16,2,16,256]{3,2,1,0:T(8,128)(2,1)S(1)} %pad_maximum_fusion.2), channel_id=1, source_target_pairs={{0,8},{8,0},{1,9},{9,1},{2,10},{10,2},{3,11},{11,3},{4,12},{12,4},... | collective-permute-start | bytes 786440 | tf_op jit(solution)/shard_map/ppermute | solution.py:191
  173.2 8.8 %copy-start.15 = (bf16[16,256]{1,0:T(8,128)(2,1)S(1)}, bf16[16,256]{1,0:T(8,128)(2,1)}, u32[]{:S(2)}) copy-start(bf16[16,256]{1,0:T(8,128)(2,1)} %param.37) | copy-start | bytes 24580
  184.3 2.2 copy-start.21
  186.5 1.8 copy-start.2
  188.3 4.4 %copy-start.19 = (f32[128,16]{0,1:T(8,128)S(1)}, f32[128,16]{0,1:T(8,128)}, u32[]{:S(2)}) copy-start(f32[128,16]{0,1:T(8,128)} %fusion.158) | copy-start | bytes 24580
  188.3 36.1 %all-to-all-start.3 = ((bf16[8,128,640]{2,1,0:T(8,128)(2,1)}), bf16[8,128,640]{2,1,0:T(8,128)(2,1)}, u32[]{:S(2)}, u32[]{:S(2)}) async-start(bf16[8,128,640]{2,1,0:T(8,128)(2,1)} %bitcast.204), calls=%async_computation.3 | async-start | bytes 2621440 | tf_op jit(solution)/shard_map/all_to_all | solution.py:24
  192.8 33.3 %copy-start.14 = (bf16[512,16]{0,1:T(8,128)(2,1)S(1)}, bf16[512,16]{0,1:T(8,128)(2,1)}, u32[]{:S(2)}) copy-start(bf16[512,16]{0,1:T(8,128)(2,1)} %param.36) | copy-start | bytes 49156
  192.8 33.3 %copy-start.25 = (f32[512]{0:T(512)S(1)}, f32[512]{0:T(512)}, u32[]{:S(2)}) copy-start(f32[512]{0:T(512)} %param.33) | copy-start | bytes 6148
  194.2 32.2 %copy-start.30 = (f32[128]{0:T(128)S(1)}, f32[128]{0:T(128)}, u32[]{:S(2)}) copy-start(f32[128]{0:T(128)} %copy-done.29) | copy-start | bytes 1540
  194.2 32.4 %copy-start.28 = (s32[128]{0:T(128)S(1)}, s32[128]{0:T(128)}, u32[]{:S(2)}) copy-start(s32[128]{0:T(128)} %copy-done.27) | copy-start | bytes 1540
  224.5 1.9 copy-start.5
  224.5 2.1 copy-start.7
  226.0 1.0 copy-start.32
  226.3 5.7 %copy-start.3 = (bf16[1024,256]{0,1:T(8,128)(2,1)S(1)}, bf16[1024,256]{0,1:T(8,128)(2,1)}, u32[]{:S(2)}) copy-start(bf16[1024,256]{0,1:T(8,128)(2,1)} %copy-done.2) | copy-start | bytes 1572868
  227.9 19.1 %all-to-all-start.4 = ((bf16[8,48,512]{2,1,0:T(8,128)(2,1)}), bf16[8,48,512]{2,1,0:T(8,128)(2,1)}, u32[]{:S(2)}, u32[]{:S(2)}) async-start(bf16[8,48,512]{2,1,0:T(8,128)(2,1)} %broadcast_in_dim.176), calls=%async_computation.4 | async-start | bytes 786432 | tf_op jit(solution)/shard_map/all_to_all | solution.py:24
  247.1 2.8 copy-start.38
  247.1 4.7 %copy-start.23 = (bf16[128,16]{0,1:T(8,128)(2,1)S(1)}, bf16[128,16]{0,1:T(8,128)(2,1)}, u32[]{:S(2)}) copy-start(bf16[128,16]{0,1:T(8,128)(2,1)} %copy-done.22) | copy-start | bytes 12292
  (2 other events, 1.2 us)
Sparse Core Ops, SparseCore 0:
  17.9 41.7 all-gather.3
  172.0 71.7 all-gather.5

commit v2 on v1

--- a/solution.py
+++ b/solution.py
@@ -12,8 +12,10 @@
 TASKS = 8
 RANK = 16
 ROW = ("row_0", "row_1")
-SEQ = ("seq_0", "seq_1", "seq_2")
-Z, FAR, CORE = SEQ
+SEQ = ("seq_0", "near", "seq_1", "seq_2")
+Z, NEAR, FAR, CORE = SEQ
+QUAD = (NEAR, FAR)
+LINE, SIDE = ROW
 SEQ_ROW = SEQ + ROW
 SWAP = [(0, 1), (1, 0)]
 BF = jnp.bfloat16
@@ -55,6 +57,20 @@
     first = jnp.where(place == 0, mine, other)
     second = jnp.where(place == 0, other, mine)
     return jnp.concatenate([first, second], axis=axis)
+
+
+def total(array):
+    return lax.optimization_barrier(array.astype(F32).sum(axis=0))
+
+
+def fold(array):
+    array = jnp.concatenate([array[:, :128], array[:, 128:]], axis=0)
+    return jnp.concatenate([array[8 * k : 8 * k + 8] for k in range(4)], axis=1)
+
+
+def unfold(array):
+    array = jnp.concatenate([array[:, :, 128 * k : 128 * k + 128] for k in range(4)], axis=1)
+    return jnp.concatenate([array[:, :RANK], array[:, RANK:]], axis=2)
 
 
 def attend(state, queries, query_places, keys, values, key_places):
@@ -96,13 +112,26 @@
     ring = lax.axis_size(Z)
     row_count = lax.axis_size(ROW)
     z = lax.axis_index(Z)
+    near = lax.axis_index(NEAR)
     far = lax.axis_index(FAR)
+    side = lax.axis_index(SIDE)
     core = lax.axis_index(CORE)
     row_index = lax.axis_index(ROW)
     columns = local_weight.shape[1]
     units = hidden_in.shape[0]
     share = hidden_in.shape[1]
 
+    weights = jnp.concatenate([local_weight, fold(global_up), fold(local_up)], axis=0)
+    weights = lax.all_gather(weights, ROW, axis=0, tiled=False)
+    local_whole = weights[:, :width].reshape(-1, columns)
+    up_whole = unfold(weights[:, width : width + 8])
+    up_whole = jnp.transpose(up_whole, (1, 0, 2)).reshape(RANK, -1)
+    line = lax.axis_size(LINE)
+    local_ups = unfold(weights[:, width + 8 :]).reshape(line, 2, RANK, units)
+    local_ups = lax.dynamic_index_in_dim(local_ups, side, 1, keepdims=False)
+    local_ups = jnp.concatenate([local_ups[k] for k in range(line)], axis=1)
+    cotangents = jnp.concatenate([cotangent, lax.ppermute(cotangent, SIDE, SWAP)], axis=0)
+
     def head(array, which):
         return lax.dynamic_slice_in_dim(array, which * HEAD, HEAD, 1)
 
@@ -110,33 +139,33 @@
     mine = jnp.concatenate([head(a, core) for a in trio], axis=1)
     other = jnp.concatenate([head(a, 1 - core) for a in trio], axis=1)
     both = jnp.concatenate([mine, lax.ppermute(other, CORE, SWAP)], axis=0)
-    queries = both[:, :HEAD]
     hidden = jnp.concatenate([hidden_in.T, hidden_out.T], axis=0)
     halves = [hidden[:, k * HEAD : (k + 1) * HEAD] for k in range(units // HEAD)]
-    arrived = lax.ppermute(jnp.concatenate([queries, *halves], axis=0), FAR, SWAP)
     chip_rows = 2 * rows
     tall = 2 * share
-    far_hidden = jnp.concatenate(
+    quad = to_everyone(jnp.concatenate([both[:, :HEAD], *halves], axis=0), QUAD)
+    sides = lax.axis_size(QUAD)
+    queries = quad[:, :chip_rows].reshape(sides * chip_rows, HEAD)
+    quad_hidden = jnp.concatenate(
         [
-            arrived[chip_rows + k * tall : chip_rows + (k + 1) * tall]
+            quad[:, chip_rows + k * tall : chip_rows + (k + 1) * tall].reshape(sides * tall, HEAD)
             for k in range(units // HEAD)
         ],
         axis=1,
     )
-    queries = jnp.concatenate([queries, arrived[:chip_rows]], axis=0)
-    packet = jnp.concatenate([both[:, HEAD:], hidden, far_hidden], axis=0)
-
-    def places(z_index, far_index):
-        start = (z_index * 4 + far_index * 2) * rows
+    packet = jnp.concatenate([both[:, HEAD:], quad_hidden], axis=0)
+
+    def places(z_index, near_index, far_index):
+        start = (z_index * 8 + near_index * 4 + far_index * 2) * rows
         count = jnp.arange(rows, dtype=jnp.int32)
         return jnp.concatenate([start + core * rows + count, start + (1 - core) * rows + count])
 
-    query_places = jnp.concatenate([places(z, far), places(z, 1 - far)])
-    total = 2 * chip_rows
+    query_places = jnp.concatenate([places(z, k // 2, k % 2) for k in range(sides)])
+    count = sides * chip_rows
     state = (
-        jnp.full((total, 1), -1e30, F32),
-        jnp.zeros((total, 1), F32),
-        jnp.zeros((total, HEAD), F32),
+        jnp.full((count, 1), -1e30, F32),
+        jnp.zeros((count, 1), F32),
+        jnp.zeros((count, HEAD), F32),
     )
     up = [(i, (i + 1) % ring) for i in range(ring)]
     down = [(i, (i - 1) % ring) for i in range(ring)]
@@ -144,7 +173,7 @@
     def visit(state, packets, indices):
         keys = jnp.concatenate([p[:chip_rows, :HEAD] for p in packets])
         values = jnp.concatenate([p[:chip_rows, HEAD:] for p in packets])
-        key_places = jnp.concatenate([places(i, far) for i in indices])
+        key_places = jnp.concatenate([places(i, near, far) for i in indices])
         return attend(state, queries, query_places, keys, values, key_places)
 
     riders = [None] * ring
@@ -163,58 +192,49 @@
         state = visit(state, now, at)
         now, at = later, then
     state = visit(state, now, at)
+    state, local_whole, up_whole, local_ups, cotangents = lax.optimization_barrier(
+        (state, local_whole, up_whole, local_ups, cotangents)
+    )
+
+    riders = jnp.roll(jnp.stack(riders), z, axis=0).reshape(ring * sides * tall, units)
+    riders = lax.all_gather(riders, LINE, axis=0, tiled=False)
 
     top, mass, out = state
     level = jnp.where(mass > 0, top + jnp.log(jnp.where(mass > 0, mass, 1.0)), -1e30)
     out = out / jnp.where(mass > 0, mass, 1.0)
-    sent = level[chip_rows:]
-    high = sent.astype(BF)
-    middle = (sent - high.astype(F32)).astype(BF)
-    low = (sent - high.astype(F32) - middle.astype(F32)).astype(BF)
-    wide = [jnp.broadcast_to(a, (chip_rows, n)) for a, n in ((high, 32), (middle, 32), (low, 64))]
-    met = lax.ppermute(jnp.concatenate([out[chip_rows:].astype(BF), *wide], axis=1), FAR, SWAP)
-    met = met.astype(F32)
-    far_level = met[:, 128:129] + met[:, 160:161] + met[:, 192:193]
-    own_level = level[:chip_rows]
-    peak = jnp.maximum(own_level, far_level)
-    own_part = jnp.exp(own_level - peak)
-    far_part = jnp.exp(far_level - peak)
-    merged = (own_part * out[:chip_rows] + far_part * met[:, :HEAD]) / (own_part + far_part)
+    high = level.astype(BF)
+    middle = (level - high.astype(F32)).astype(BF)
+    low = (level - high.astype(F32) - middle.astype(F32)).astype(BF)
+    wide = [jnp.broadcast_to(a, (count, n)) for a, n in ((high, 32), (middle, 32), (low, 64))]
+    met = jnp.concatenate([out.astype(BF), *wide], axis=1)
+    met = exchange(met.reshape(sides, chip_rows, 2 * HEAD), QUAD).astype(F32)
+    levels = met[:, :, 128:129] + met[:, :, 160:161] + met[:, :, 192:193]
+    parts = jnp.exp(levels - jnp.max(levels, axis=0, keepdims=True))
+    merged = (parts * met[:, :, :HEAD]).sum(axis=0) / parts.sum(axis=0)
     merged = merged.astype(BF)
     partner = lax.ppermute(merged[rows:], CORE, SWAP)
     attended = in_pair_order(merged[:rows], partner, core, 1)
-
-    riders = jnp.stack(riders)
-    riders = jnp.roll(riders, z, axis=0)
-    riders = riders.reshape(ring, 2, tall, units)
-    riders = in_pair_order(riders[:, 0:1], riders[:, 1:2], far, 1)
-    rest = lax.ppermute(riders, CORE, SWAP)
-    riders = in_pair_order(riders[:, :, None], rest[:, :, None], core, 2)
-    riders = riders.reshape(ring, 2, 2, 2, share, units)
-    rows_in = riders[:, :, :, 0].reshape(columns, units)
-    rows_out = riders[:, :, :, 1].reshape(columns, units)
-    lanes = 128
-    stacked = jnp.concatenate(
-        [rows_in, local_up, jnp.zeros((lanes - RANK, units), BF)], axis=0
-    )
-
-    up_rows = jnp.concatenate([global_up[:, :128], global_up[:, 128:]], axis=0)
-    up_rows = jnp.concatenate([up_rows[8 * k : 8 * k + 8] for k in range(4)], axis=1)
-    weights = jnp.concatenate([local_weight, up_rows], axis=0)
-    weights = lax.all_gather(weights, ROW, axis=0, tiled=False)
-    local_whole = weights[:, :width].reshape(-1, columns)
-    up_rows = weights[:, width:]
-    up_rows = jnp.concatenate([up_rows[:, :, 128 * k : 128 * k + 128] for k in range(4)], axis=1)
-    up_whole = jnp.concatenate([up_rows[:, :RANK], up_rows[:, RANK:]], axis=2)
-    cotangent_all = lax.all_gather(cotangent, ROW, axis=0, tiled=True)
-    through = contract(cotangent_all, rows_out, 1, 0)
 
     task_scales = select_rows(global_scales, patch_tasks)
     part = contract(output_weight, attended, 0, 1).astype(BF).reshape(row_count, width, rows)
     low_part = contract(global_down, attended, 0, 1).astype(BF)
     low_part = jnp.broadcast_to(low_part[None], (row_count, RANK, rows))
     arrived = exchange(jnp.concatenate([part, low_part], axis=1), ROW)
+    arrived, riders = lax.optimization_barrier((arrived, riders))
     arrived = arrived.astype(F32).sum(axis=0)
+
+    rest = lax.ppermute(riders, CORE, SWAP)
+    split = (line, ring * sides, 2, 1, share, units)
+    riders = in_pair_order(riders.reshape(split), rest.reshape(split), core, 3)
+    riders = jnp.moveaxis(riders, 2, 0).reshape(2, line, columns, units)
+    rows_in, rows_out = (
+        jnp.concatenate([riders[way, k] for k in range(line)], axis=1) for way in range(2)
+    )
+    lanes = 128
+    stacked = jnp.concatenate(
+        [rows_in, local_ups, jnp.zeros((lanes - RANK, line * units), BF)], axis=0
+    )
+
     reduced = jnp.transpose(arrived[width:])
     scaled = (reduced * task_scales).astype(BF)
     mixed = arrived[:width] + jnp.transpose(residual.astype(F32)) + contract(global_up, scaled, 0, 1)
@@ -225,7 +245,7 @@
     own_ids = lax.dynamic_slice_in_dim(byte_ids, row_index * own_bytes, own_bytes)
     projected = contract(mixed_b, local_weight, 0, 0).astype(BF)
     projected = exchange(projected.reshape(row_count, own_patches, columns), ROW)
-    projected = projected.astype(F32).sum(axis=0).astype(BF)
+    projected = total(projected).astype(BF)
 
     picks = (own_ids[:, None] == jnp.arange(VOCAB, dtype=jnp.int32)[None, :]).astype(BF)
     embedded = jnp.dot(picks, byte_table, preferred_element_type=F32)
@@ -240,13 +260,13 @@
     joined = jnp.concatenate(
         [normed, shrunk, jnp.zeros((own_bytes, lanes - RANK), BF)], axis=1
     )
-    joined = to_everyone(joined, ROW).reshape(row_count * own_bytes, columns + lanes)
+    joined = jnp.concatenate([joined, lax.ppermute(joined, SIDE, SWAP)], axis=0)
+    through = contract(cotangents, rows_out, 1, 0)
     upper = contract(joined, stacked, 1, 0)
     grown = (through * gelu_slope(upper)).astype(BF)
-    grad_local_up = contract(joined[:, columns:], grown, 0, 0)[:RANK]
-    back = contract(grown, stacked, 1, 1).astype(BF)
-    back = exchange(back.reshape(row_count, own_bytes, columns + lanes), ROW)
-    back = back.astype(F32).sum(axis=0)
+    back = contract(grown, stacked, 1, 1)
+    back = back[:own_bytes] + lax.ppermute(back[own_bytes:].astype(BF), SIDE, SWAP).astype(F32)
+    ups = contract(joined[:, columns:], grown, 0, 0)[:RANK].astype(BF)
     back_norm = back[:, :columns]
     back_rank = back[:, columns : columns + RANK]
     grad_local_scales = task_totals(byte_tasks, back_rank * lowered)
@@ -258,19 +278,23 @@
     back_inputs = cotangent.astype(F32) + inverse * (
         gained - inputs * inverse * inverse * average
     )
-    patch_grad = back_inputs.reshape(own_patches, PATCH, -1).sum(axis=1).astype(BF)
+    patch_grad = back_inputs.reshape(own_patches, PATCH, -1).sum(axis=1)
+    patch_grad = lax.optimization_barrier(patch_grad).astype(BF)
 
     spare = jnp.zeros((TASKS, columns - RANK), F32)
     local_rows = jnp.concatenate([grad_local_scales, spare], axis=1)
     local_rows = jnp.concatenate([grad_local_down, local_rows, jnp.zeros_like(local_rows)])
     row_pack = jnp.concatenate([patch_grad, local_rows.astype(BF)], axis=0)
-    row_pack = to_everyone(row_pack, ROW)
+    row_pack = jnp.broadcast_to(row_pack[None], (row_count, *row_pack.shape))
+    ups = jnp.stack([ups[:, units * k : units * (k + 1)] for k in range(line)])
+    ups = jnp.stack([jnp.where(side == k, ups, jnp.zeros_like(ups)) for k in range(2)], axis=1)
+    ups = jnp.pad(ups.reshape(row_count, RANK, units), [(0, 0), (0, 0), (0, columns - units)])
+    row_pack = exchange(jnp.concatenate([row_pack, ups], axis=1), ROW)
     patch_grads = row_pack[:, :own_patches].reshape(rows, columns)
-    local_sums = row_pack[:, own_patches:].astype(F32).sum(axis=0)
+    local_sums = total(row_pack[:, own_patches:])
     back_mixed = contract(patch_grads, local_weight, 1, 1).astype(BF)
     back_whole = contract(patch_grads, local_whole, 1, 1).astype(BF)
-    up_flat = jnp.transpose(up_whole, (1, 0, 2)).reshape(RANK, -1)
-    back_scaled = contract(back_whole, up_flat, 1, 1)
+    back_scaled = contract(back_whole, up_whole, 1, 1)
     grad_global_up = contract(scaled, back_mixed, 0, 0)
     grad_global_scales = task_totals(patch_tasks, back_scaled * reduced)
     back_reduced = (back_scaled * task_scales).astype(BF)
@@ -282,7 +306,7 @@
         [
             grad_global_down,
             grad_global_up,
-            grad_local_up,
+            local_sums[2 * RANK :, :units],
             local_sums[:RANK, :width],
             local_sums[:RANK, width:],
             small,
@@ -291,8 +315,8 @@
     ).astype(BF)
     shape = packed.shape
     pieces = packed.reshape(lax.axis_size(SEQ), -1)
-    pieces = exchange(pieces, SEQ).astype(F32).sum(axis=0).astype(BF)
-    packed = to_everyone(pieces, SEQ).reshape(shape).astype(F32)
+    pieces = exchange(pieces, SEQ).astype(F32).sum(axis=0)
+    packed = to_everyone(pieces, SEQ).reshape(shape)
     return (
         jnp.transpose(packed[:16]),
         packed[16:32],
@@ -304,7 +328,7 @@
 
 
 def solution(mesh):
-    torus = Mesh(mesh.devices.reshape(16, 2, 2, 4, 2), SEQ_ROW)
+    torus = Mesh(mesh.devices.reshape(8, 2, 2, 2, 4, 2), SEQ_ROW)
     placed = (
         P(SEQ, ROW),
         P(SEQ, ROW),

time: 321 us -> 292 us (0.910)
  waiting for transfers between devices: 94.5 us -> 50.3 us
  starting transfers between devices: 107 us -> 82.4 us
  local copies, waits for them, and re-layouts: 15.5 us -> 31.7 us
  blocking collectives: 53.1 us -> 65.6 us
  other arithmetic: 11.1 us -> 19.1 us
    all_to_all x5 -> x4, waiting for transfers between devices: 54 us -> 6.1 us  [exchange(): return lax.all_to_all(pieces, axis, split_axis=0, concat_axis=0, tiled=True)]
    all_gather x1, waiting for transfers between devices: 0.01 us -> 16.7 us  [body(): riders = lax.all_gather(riders, LINE, axis=0, tiled=False)]
    ppermute x8 -> x4, starting transfers between devices: 22.1 us -> 7.68 us  [body(): rising = lax.ppermute(rising, Z, up)]
    all_to_all x2 -> x3, blocking collectives: 53.1 us -> 65.6 us  [exchange(): return lax.all_to_all(pieces, axis, split_axis=0, concat_axis=0, tiled=True)]
    ppermute x7 -> x3, starting transfers between devices: 30.8 us -> 18.7 us  [body(): falling = lax.ppermute(falling, Z, down)]
    all_gather x1, waiting for transfers between devices: 10.8 us -> 0.01 us  [body(): weights = lax.all_gather(weights, ROW, axis=0, tiled=False)]
    ppermute x8 -> x4, waiting for transfers between devices: 9.48 us -> 18.3 us  [body(): rising = lax.ppermute(rising, Z, up)]
    unnamed x121 -> x98, local copies, waits for them, and re-layouts: 2.78 us -> 11.3 us
  transfers between devices with their start and end apart: 27 -> 19, of which waited for: 24 -> 10; matrix products, arithmetic and copies ran while one was open for 11% -> 15% of each run, Pallas kernels for 0% -> 0%
where the time goes in v2:
time: 292 us; the launch traced here: 290 us
  starting transfers between devices  82.4 us (28%)
  blocking collectives  65.6 us (22%)
  waiting for transfers between devices  50.3 us (17%)
  local copies, waits for them, and re-layouts  31.7 us (11%)
  matrix products  23.9 us (8%)
  other arithmetic  19.1 us (7%)
  between operations  17 us (6%)
    all_to_all x3, blocking collectives, exchange(): return lax.all_to_all(pieces, axis, split_axis=0, concat_axis=0, tiled=True)  65.6 us
    all_to_all x4, starting transfers between devices, exchange(): return lax.all_to_all(pieces, axis, split_axis=0, concat_axis=0, tiled=True)  22.3 us
    ppermute x3, starting transfers between devices, body(): falling = lax.ppermute(falling, Z, down)  18.7 us
    ppermute x4, waiting for transfers between devices, body(): rising = lax.ppermute(rising, Z, up)  18.3 us
    all_gather x1, waiting for transfers between devices, body(): riders = lax.all_gather(riders, LINE, axis=0, tiled=False)  16.7 us
    dot_general x17, matrix products, contract(): lax.dot_general(left, right, (((left_dim,), (right_dim,)), ((), ())), pre...  13.8 us
    ppermute x1, starting transfers between devices, body(): partner = lax.ppermute(merged[rows:], CORE, SWAP)  11.6 us
    unnamed x98, local copies, waits for them, and re-layouts  11.3 us
  transfers between devices with their start and end apart: 19, of which 10 were waited for; matrix products, arithmetic and copies ran while one was open for 15% of the time, Pallas kernels for 0%

profile of v2, /device:TPU:1, one launch (start us, length us, event | category | flops | bytes accessed | tf_op | source)
XLA Modules:
  0.0 289.9 jit_solution(1459353194951950247)
XLA Ops:
  8.1 0.9 constant_dynamic-slice_fusion.6
  9.8 8.8 %collective-permute-start = (bf16[128,384]{1,0:T(8,128)(2,1)S(1)}, bf16[128,384]{1,0:T(8,128)(2,1)S(1)}, u32[]{:S(2)}, u32[]{:S(2)}) collective-permute-start(bf16[128,384]{1,0:T(8,128)(2,1)S(1)} %pad_maximum_fusion.5), channel_id=1, source_target_pairs={{0,8},{8,0},{1,9},{9,1},{2,10},{10,2},{3,11},{11,3},{4,12},{12,4},... | collective-permute-start | bytes 294920 | tf_op jit(solution)/shard_map/ppermute | solution.py:141
  19.4 1.7 maximum_maximum_fusion.1
  21.1 1.9 collective-permute-start.8
  25.0 3.5 %all-to-all-start = ((bf16[4,288,128]{2,1,0:T(8,128)(2,1)}), bf16[4,288,128]{2,1,0:T(8,128)(2,1)S(1)}, u32[]{:S(2)}, u32[]{:S(2)}) async-start(bf16[4,288,128]{2,1,0:T(8,128)(2,1)} %broadcast_in_dim.60), calls=%async_computation | async-start | bytes 589824 | tf_op jit(solution)/shard_map/all_to_all | solution.py:26
  29.3 6.1 %all-to-all-done = bf16[4,288,128]{2,1,0:T(8,128)(2,1)S(1)} async-done(((bf16[4,288,128]{2,1,0:T(8,128)(2,1)}), bf16[4,288,128]{2,1,0:T(8,128)(2,1)S(1)}, u32[]{:S(2)}, u32[]{:S(2)}) %all-to-all-start) | async-done | bytes 294944 | tf_op jit(solution)/shard_map/all_to_all | solution.py:26
  35.4 7.0 %collective-permute-start.2 = (bf16[320,256]{1,0:T(8,128)(2,1)S(1)}, bf16[320,256]{1,0:T(8,128)(2,1)S(1)}, u32[]{:S(2)}, u32[]{:S(2)}) collective-permute-start(bf16[320,256]{1,0:T(8,128)(2,1)S(1)} %maximum_maximum_fusion.2), channel_id=1, source_target_pairs={{0,448},{64,0},{128,64},{192,128},{256,192},{320,256},{384,320},{4... | collective-permute-start | bytes 491528 | tf_op jit(solution)/shard_map/ppermute | solution.py:188
  42.4 1.9 collective-permute-start.1
  44.8 7.3 %collective-permute-done.1 = bf16[320,256]{1,0:T(8,128)(2,1)S(1)} collective-permute-done((bf16[320,256]{1,0:T(8,128)(2,1)S(1)}, bf16[320,256]{1,0:T(8,128)(2,1)S(1)}, u32[]{:S(2)}, u32[]{:S(2)}) %collective-permute-start.1) | collective-permute-done | bytes 163872 | tf_op jit(solution)/shard_map/ppermute | solution.py:184
  53.1 1.9 collective-permute-start.3
  55.1 5.5 %collective-permute-start.4 = (bf16[320,256]{1,0:T(8,128)(2,1)S(1)}, bf16[320,256]{1,0:T(8,128)(2,1)S(1)}, u32[]{:S(2)}, u32[]{:S(2)}) collective-permute-start(bf16[320,256]{1,0:T(8,128)(2,1)S(1)} %collective-permute-done.2), channel_id=1, source_target_pairs={{0,448},{64,0},{128,64},{192,128},{256,192},{320,256},{384,320},{4... | collective-permute-start | bytes 491528 | tf_op jit(solution)/shard_map/ppermute | solution.py:188
  60.6 2.2 collective-permute-done.4
  62.8 6.2 %collective-permute-start.6 = (bf16[320,256]{1,0:T(8,128)(2,1)S(1)}, bf16[320,256]{1,0:T(8,128)(2,1)S(1)}, u32[]{:S(2)}, u32[]{:S(2)}) collective-permute-start(bf16[320,256]{1,0:T(8,128)(2,1)S(1)} %collective-permute-done.4), channel_id=1, source_target_pairs={{0,448},{64,0},{128,64},{192,128},{256,192},{320,256},{384,320},{4... | collective-permute-start | bytes 491528 | tf_op jit(solution)/shard_map/ppermute | solution.py:188
  69.0 1.9 collective-permute-start.5
  71.0 1.7 collective-permute-done.6
  72.8 4.7 %collective-permute-done.5 = bf16[320,256]{1,0:T(8,128)(2,1)S(1)} collective-permute-done((bf16[320,256]{1,0:T(8,128)(2,1)S(1)}, bf16[320,256]{1,0:T(8,128)(2,1)S(1)}, u32[]{:S(2)}, u32[]{:S(2)}) %collective-permute-start.5) | collective-permute-done | bytes 163872 | tf_op jit(solution)/shard_map/ppermute | solution.py:184
  77.9 1.4 fusion.12
  79.3 1.9 collective-permute-start.7
  81.2 6.3 %collective-permute-done.7 = bf16[320,256]{1,0:T(8,128)(2,1)S(1)} collective-permute-done((bf16[320,256]{1,0:T(8,128)(2,1)S(1)}, bf16[320,256]{1,0:T(8,128)(2,1)S(1)}, u32[]{:S(2)}, u32[]{:S(2)}) %collective-permute-start.7) | collective-permute-done | bytes 163872 | tf_op jit(solution)/shard_map/ppermute | solution.py:184
  88.4 1.4 fusion.14
  92.4 1.3 convolution_add_fusion.3
  93.7 1.9 slice.426
  95.6 0.9 fusion.168
  98.7 1.0 pad_maximum_fusion.1
  99.7 2.0 copy.90
  101.8 7.7 %all-to-all-start.1 = ((bf16[4,256,256]{1,2,0:T(8,128)(2,1)}), bf16[4,256,256]{1,2,0:T(8,128)(2,1)}, u32[]{:S(2)}, u32[]{:S(2)}) async-start(bf16[4,256,256]{1,2,0:T(8,128)(2,1)} %copy.90), calls=%async_computation.1 | async-start | bytes 1048576 | tf_op jit(solution)/shard_map/all_to_all | solution.py:26
  110.1 1.4 constant_dynamic-update-slice_fusion.6
  111.4 1.4 constant_dynamic-update-slice_fusion.5
  112.8 1.4 constant_dynamic-update-slice_fusion.4
  114.2 1.4 constant_dynamic-update-slice_fusion.3
  115.6 1.4 constant_dynamic-update-slice_fusion.2
  117.5 1.7 constant_dynamic-slice_fusion
  119.2 1.1 convert_element_type.149
  120.5 11.6 %collective-permute-start.9 = (bf16[128,128]{0,1:T(8,128)(2,1)S(1)}, bf16[128,128]{0,1:T(8,128)(2,1)S(1)}, u32[]{:S(2)}, u32[]{:S(2)}) collective-permute-start(bf16[128,128]{0,1:T(8,128)(2,1)S(1)} %slice.440), channel_id=1, source_target_pairs={{0,8},{8,0},{1,9},{9,1},{2,10},{10,2},{3,11},{11,3},{4,12},{12,4},... | collective-permute-start | bytes 98312 | tf_op jit(solution)/shard_map/ppermute | solution.py:215
  132.1 0.8 collective-permute-done.9
  133.0 1.1 fusion
  134.1 2.1 copy.100
  136.3 1.9 pad_maximum_fusion
  138.2 6.9 %all-to-all-start.2 = ((bf16[8,272,128]{2,1,0:T(8,128)(2,1)}), bf16[8,272,128]{2,1,0:T(8,128)(2,1)}, u32[]{:S(2)}, u32[]{:S(2)}) async-start(bf16[8,272,128]{2,1,0:T(8,128)(2,1)} %pad_maximum_fusion), calls=%async_computation.2 | async-start | bytes 1114112 | tf_op jit(solution)/shard_map/all_to_all | solution.py:26
  145.9 16.7 %all-gather.4.cloned.1.call-done = bf16[4,512,256]{2,1,0:T(8,128)(2,1)} async-done(((bf16[1,512,256]{2,1,0:T(8,128)(2,1)}), bf16[4,512,256]{2,1,0:T(8,128)(2,1)}) %all-gather.4.cloned.1.call-update) | async-done | bytes 1048592 | tf_op jit(solution)/shard_map/all_gather | solution.py:200
  162.6 1.1 convert_reduce_fusion
  164.4 1.6 multiply_convert_fusion.4
  166.7 1.9 convolution_convert_fusion.3
  168.6 4.3 %all-to-all-start.3 = ((bf16[8,16,512]{2,1,0:T(8,128)(2,1)}), bf16[8,16,512]{2,1,0:T(8,128)(2,1)S(1)}, u32[]{:S(2)}, u32[]{:S(2)}) async-start(bf16[8,16,512]{2,1,0:T(8,128)(2,1)} %bitcast.41), calls=%async_computation.3 | async-start | bytes 262144 | tf_op jit(solution)/shard_map/all_to_all | solution.py:26
  172.9 0.9 fusion.125
  176.7 3.7 %collective-permute-start.10 = (bf16[4,512,256]{2,1,0:T(8,128)(2,1)}, bf16[4,512,256]{2,1,0:T(8,128)(2,1)}, u32[]{:S(2)}, u32[]{:S(2)}) collective-permute-start(bf16[4,512,256]{2,1,0:T(8,128)(2,1)} %all-gather.4.cloned.1.call-done), channel_id=1, source_target_pairs={{0,8},{8,0},{1,9},{9,1},{2,10},{10,2},{3,11},{11,3},{4,12},{12,4},... | collective-permute-start | bytes 3145736 | tf_op jit(solution)/shard_map/ppermute | solution.py:226
  180.4 1.3 multiply_reduce_fusion.1
  182.5 0.9 multiply_convert_fusion.3
  184.7 1.5 pad_maximum_fusion.4
  186.2 3.6 %collective-permute-start.11 = (bf16[128,640]{1,0:T(8,128)(2,1)}, bf16[128,640]{1,0:T(8,128)(2,1)}, u32[]{:S(2)}, u32[]{:S(2)}) collective-permute-start(bf16[128,640]{1,0:T(8,128)(2,1)} %pad_maximum_fusion.4), channel_id=1, source_target_pairs={{0,1},{1,0},{2,3},{3,2},{4,5},{5,4},{6,7},{7,6},{8,9},{9,8},{10,11... | collective-permute-start | bytes 491528 | tf_op jit(solution)/shard_map/ppermute | solution.py:263
  190.6 1.7 broadcast_select_fusion.1
  192.8 0.9 collective-permute-done.11
  193.8 1.6 fusion.79
  196.9 1.2 convolution_convert_fusion.2
  198.1 4.1 %collective-permute-start.12 = (bf16[128,640]{1,0:T(8,128)(2,1)S(1)}, bf16[128,640]{1,0:T(8,128)(2,1)S(1)}, u32[]{:S(2)}, u32[]{:S(2)}) collective-permute-start(bf16[128,640]{1,0:T(8,128)(2,1)S(1)} %slice.576), channel_id=1, source_target_pairs={{0,1},{1,0},{2,3},{3,2},{4,5},{5,4},{6,7},{7,6},{8,9},{9,8},{10,11... | collective-permute-start | bytes 491528 | tf_op jit(solution)/shard_map/ppermute | solution.py:268
  202.2 3.4 %collective-permute-done.12 = bf16[128,640]{1,0:T(8,128)(2,1)S(1)} collective-permute-done((bf16[128,640]{1,0:T(8,128)(2,1)S(1)}, bf16[128,640]{1,0:T(8,128)(2,1)S(1)}, u32[]{:S(2)}, u32[]{:S(2)}) %collective-permute-start.12) | collective-permute-done | bytes 163872 | tf_op jit(solution)/shard_map/ppermute | solution.py:268
  206.9 13.1 %all_to_all.37 = bf16[8,64,512]{2,1,0:T(8,128)(2,1)S(1)} all-to-all(bf16[8,64,512]{2,1,0:T(8,128)(2,1)S(1)} %fusion.69), channel_id=1, replica_groups=mesh['seq_0'=8,'near'=2,'seq_1'=2,'seq_2'=2,'row_0'=4,'row_1'=2] {'row_0..., dimensions={0} | all-to-all | bytes 1048576 | tf_op jit(solution)/shard_map/all_to_all | solution.py:26
  220.8 1.9 fusion.6
  222.7 0.9 convolution_convert_fusion.8
  223.6 0.9 fusion.21
  224.9 1.1 convert_reduce_fusion.1
  226.6 0.9 reduce.10
  227.6 31.4 %all_to_all.38 = bf16[64,2,192]{2,1,0:T(2,128)(2,1)S(1)} all-to-all(bf16[64,2,192]{2,1,0:T(2,128)(2,1)S(1)} %reshape.518), channel_id=1, replica_groups=mesh['seq_0'=8,'near'=2,'seq_1'=2,'seq_2'=2,'row_0'=4,'row_1'=2] {'seq_0..., dimensions={0} | all-to-all | bytes 98304 | tf_op jit(solution)/shard_map/all_to_all | solution.py:26
  259.4 21.0 %all_to_all.39 = f32[64,1,384]{2,1,0:T(1,128)S(1)} all-to-all(f32[64,1,384]{2,1,0:T(1,128)S(1)} %broadcast_in_dim.149), channel_id=1, replica_groups=mesh['seq_0'=8,'near'=2,'seq_1'=2,'seq_2'=2,'row_0'=4,'row_1'=2] {'seq_0..., dimensions={0} | all-to-all | bytes 196608 | tf_op jit(solution)/shard_map/all_to_all | solution.py:26
  (231 shorter events, 28.4 us)
Async XLA Ops:
  8.0 125.0 %copy-start = (bf16[256,2048]{1,0:T(8,128)(2,1)S(1)}, bf16[256,2048]{1,0:T(8,128)(2,1)}, u32[]{:S(2)}) copy-start(bf16[256,2048]{1,0:T(8,128)(2,1)} %param.25) | copy-start | bytes 3145732
  8.0 20.6 %copy-start.6 = (bf16[128,512]{1,0:T(8,128)(2,1)S(1)}, bf16[128,512]{1,0:T(8,128)(2,1)}, u32[]{:S(2)}) copy-start(bf16[128,512]{1,0:T(8,128)(2,1)} %param.39) | copy-start | bytes 393220
  8.0 16.1 %copy-start.27 = (bf16[256,8]{0,1:T(8,128)(2,1)S(1)}, bf16[256,8]{0,1:T(8,128)(2,1)}, u32[]{:S(2)}) copy-start(bf16[256,8]{0,1:T(8,128)(2,1)} %param.35) | copy-start | bytes 12292
  8.0 16.1 %copy-start.28 = (bf16[256,8]{0,1:T(8,128)(2,1)S(1)}, bf16[256,8]{0,1:T(8,128)(2,1)}, u32[]{:S(2)}) copy-start(bf16[256,8]{0,1:T(8,128)(2,1)} %param.34) | copy-start | bytes 12292
  8.1 85.6 %all-gather.6.cloned.1.call-start = ((), (), s32[]{:S(2)}) async-start(), calls=%async_computation.8 | async-start | bytes 2506752 | tf_op jit(solution)/shard_map/all_gather | solution.py:125
  9.8 14.3 %collective-permute-start = (bf16[128,384]{1,0:T(8,128)(2,1)S(1)}, bf16[128,384]{1,0:T(8,128)(2,1)S(1)}, u32[]{:S(2)}, u32[]{:S(2)}) collective-permute-start(bf16[128,384]{1,0:T(8,128)(2,1)S(1)} %pad_maximum_fusion.5), channel_id=1, source_target_pairs={{0,8},{8,0},{1,9},{9,1},{2,10},{10,2},{3,11},{11,3},{4,12},{12,4},... | collective-permute-start | bytes 294920 | tf_op jit(solution)/shard_map/ppermute | solution.py:141
  21.1 7.4 %collective-permute-start.8 = (bf16[128,512]{1,0:T(8,128)(2,1)}, bf16[128,512]{1,0:T(8,128)(2,1)S(1)}, u32[]{:S(2)}, u32[]{:S(2)}) collective-permute-start(bf16[128,512]{1,0:T(8,128)(2,1)} %param.39), channel_id=1, source_target_pairs={{0,1},{1,0},{2,3},{3,2},{4,5},{5,4},{6,7},{7,6},{8,9},{9,8},{10,11... | collective-permute-start | bytes 393224 | tf_op jit(solution)/shard_map/ppermute | solution.py:133
  25.0 10.4 %all-to-all-start = ((bf16[4,288,128]{2,1,0:T(8,128)(2,1)}), bf16[4,288,128]{2,1,0:T(8,128)(2,1)S(1)}, u32[]{:S(2)}, u32[]{:S(2)}) async-start(bf16[4,288,128]{2,1,0:T(8,128)(2,1)} %broadcast_in_dim.60), calls=%async_computation | async-start | bytes 589824 | tf_op jit(solution)/shard_map/all_to_all | solution.py:26
  35.4 9.3 %collective-permute-start.2 = (bf16[320,256]{1,0:T(8,128)(2,1)S(1)}, bf16[320,256]{1,0:T(8,128)(2,1)S(1)}, u32[]{:S(2)}, u32[]{:S(2)}) collective-permute-start(bf16[320,256]{1,0:T(8,128)(2,1)S(1)} %maximum_maximum_fusion.2), channel_id=1, source_target_pairs={{0,448},{64,0},{128,64},{192,128},{256,192},{320,256},{384,320},{4... | collective-permute-start | bytes 491528 | tf_op jit(solution)/shard_map/ppermute | solution.py:188
  42.4 9.6 %collective-permute-start.1 = (bf16[320,256]{1,0:T(8,128)(2,1)S(1)}, bf16[320,256]{1,0:T(8,128)(2,1)S(1)}, u32[]{:S(2)}, u32[]{:S(2)}) collective-permute-start(bf16[320,256]{1,0:T(8,128)(2,1)S(1)} %maximum_maximum_fusion.2), channel_id=1, source_target_pairs={{0,64},{64,128},{128,192},{192,256},{256,320},{320,384},{384,448},... | collective-permute-start | bytes 491528 | tf_op jit(solution)/shard_map/ppermute | solution.py:184
  53.1 15.9 %collective-permute-start.3 = (bf16[320,256]{1,0:T(8,128)(2,1)S(1)}, bf16[320,256]{1,0:T(8,128)(2,1)S(1)}, u32[]{:S(2)}, u32[]{:S(2)}) collective-permute-start(bf16[320,256]{1,0:T(8,128)(2,1)S(1)} %collective-permute-done.1), channel_id=1, source_target_pairs={{0,64},{64,128},{128,192},{192,256},{256,320},{320,384},{384,448},... | collective-permute-start | bytes 491528 | tf_op jit(solution)/shard_map/ppermute | solution.py:184
  55.1 7.7 %collective-permute-start.4 = (bf16[320,256]{1,0:T(8,128)(2,1)S(1)}, bf16[320,256]{1,0:T(8,128)(2,1)S(1)}, u32[]{:S(2)}, u32[]{:S(2)}) collective-permute-start(bf16[320,256]{1,0:T(8,128)(2,1)S(1)} %collective-permute-done.2), channel_id=1, source_target_pairs={{0,448},{64,0},{128,64},{192,128},{256,192},{320,256},{384,320},{4... | collective-permute-start | bytes 491528 | tf_op jit(solution)/shard_map/ppermute | solution.py:188
  62.8 14.7 %copy-start.15 = (bf16[320,256]{1,0:T(8,128)(2,1)}, bf16[320,256]{1,0:T(8,128)(2,1)S(1)}, u32[]{:S(2)}) copy-start(bf16[320,256]{1,0:T(8,128)(2,1)S(1)} %collective-permute-done.4) | copy-start | bytes 491524
  62.8 9.9 %collective-permute-start.6 = (bf16[320,256]{1,0:T(8,128)(2,1)S(1)}, bf16[320,256]{1,0:T(8,128)(2,1)S(1)}, u32[]{:S(2)}, u32[]{:S(2)}) collective-permute-start(bf16[320,256]{1,0:T(8,128)(2,1)S(1)} %collective-permute-done.4), channel_id=1, source_target_pairs={{0,448},{64,0},{128,64},{192,128},{256,192},{320,256},{384,320},{4... | collective-permute-start | bytes 491528 | tf_op jit(solution)/shard_map/ppermute | solution.py:188
  69.0 18.5 %copy-start.14 = (bf16[320,256]{1,0:T(8,128)(2,1)}, bf16[320,256]{1,0:T(8,128)(2,1)S(1)}, u32[]{:S(2)}) copy-start(bf16[320,256]{1,0:T(8,128)(2,1)S(1)} %collective-permute-done.3) | copy-start | bytes 491524
  69.0 8.4 %collective-permute-start.5 = (bf16[320,256]{1,0:T(8,128)(2,1)S(1)}, bf16[320,256]{1,0:T(8,128)(2,1)S(1)}, u32[]{:S(2)}, u32[]{:S(2)}) collective-permute-start(bf16[320,256]{1,0:T(8,128)(2,1)S(1)} %collective-permute-done.3), channel_id=1, source_target_pairs={{0,64},{64,128},{128,192},{192,256},{256,320},{320,384},{384,448},... | collective-permute-start | bytes 491528 | tf_op jit(solution)/shard_map/ppermute | solution.py:184
  72.7 8.4 %copy-start.16 = (bf16[320,256]{1,0:T(8,128)(2,1)}, bf16[320,256]{1,0:T(8,128)(2,1)S(1)}, u32[]{:S(2)}) copy-start(bf16[320,256]{1,0:T(8,128)(2,1)S(1)} %collective-permute-done.6) | copy-start | bytes 491524
  77.4 10.1 %copy-start.17 = (bf16[320,256]{1,0:T(8,128)(2,1)}, bf16[320,256]{1,0:T(8,128)(2,1)S(1)}, u32[]{:S(2)}) copy-start(bf16[320,256]{1,0:T(8,128)(2,1)S(1)} %collective-permute-done.5) | copy-start | bytes 491524
  79.3 8.3 %collective-permute-start.7 = (bf16[320,256]{1,0:T(8,128)(2,1)S(1)}, bf16[320,256]{1,0:T(8,128)(2,1)S(1)}, u32[]{:S(2)}, u32[]{:S(2)}) collective-permute-start(bf16[320,256]{1,0:T(8,128)(2,1)S(1)} %collective-permute-done.5), channel_id=1, source_target_pairs={{0,64},{64,128},{128,192},{192,256},{256,320},{320,384},{384,448},... | collective-permute-start | bytes 491528 | tf_op jit(solution)/shard_map/ppermute | solution.py:184
  87.5 4.9 %copy-start.21 = (bf16[320,256]{1,0:T(8,128)(2,1)}, bf16[320,256]{1,0:T(8,128)(2,1)S(1)}, u32[]{:S(2)}) copy-start(bf16[320,256]{1,0:T(8,128)(2,1)S(1)} %collective-permute-done.7) | copy-start | bytes 491524
  87.6 2.2 copy-start.18
  93.7 4.2 %copy-start.4 = (f32[1024,128]{1,0:T(8,128)S(1)}, f32[1024,128]{1,0:T(8,128)}, u32[]{:S(2)}) copy-start(f32[1024,128]{1,0:T(8,128)} %convolution_add_fusion.3) | copy-start | bytes 1572868
  101.8 17.5 %all-to-all-start.1 = ((bf16[4,256,256]{1,2,0:T(8,128)(2,1)}), bf16[4,256,256]{1,2,0:T(8,128)(2,1)}, u32[]{:S(2)}, u32[]{:S(2)}) async-start(bf16[4,256,256]{1,2,0:T(8,128)(2,1)} %copy.90), calls=%async_computation.1 | async-start | bytes 1048576 | tf_op jit(solution)/shard_map/all_to_all | solution.py:26
  109.5 53.1 %all-gather.4.cloned.1.call-start = ((), (), s32[]{:S(2)}) async-start(), calls=%async_computation.7 | async-start | bytes 1310720 | tf_op jit(solution)/shard_map/all_gather | solution.py:200
  120.4 15.8 %copy-start.33 = (bf16[256,16]{0,1:T(8,128)(2,1)S(1)}, bf16[256,16]{0,1:T(8,128)(2,1)}, u32[]{:S(2)}) copy-start(bf16[256,16]{0,1:T(8,128)(2,1)} %param.26) | copy-start | bytes 24580
  120.5 12.4 %collective-permute-start.9 = (bf16[128,128]{0,1:T(8,128)(2,1)S(1)}, bf16[128,128]{0,1:T(8,128)(2,1)S(1)}, u32[]{:S(2)}, u32[]{:S(2)}) collective-permute-start(bf16[128,128]{0,1:T(8,128)(2,1)S(1)} %slice.440), channel_id=1, source_target_pairs={{0,8},{8,0},{1,9},{9,1},{2,10},{10,2},{3,11},{11,3},{4,12},{12,4},... | collective-permute-start | bytes 98312 | tf_op jit(solution)/shard_map/ppermute | solution.py:215
  133.0 5.3 %copy-start.19 = (bf16[128,128]{0,1:T(8,128)(2,1)}, bf16[128,128]{0,1:T(8,128)(2,1)S(1)}, u32[]{:S(2)}) copy-start(bf16[128,128]{0,1:T(8,128)(2,1)S(1)} %get-tuple-element.92) | copy-start | bytes 98308
  133.0 5.3 %copy-start.20 = (bf16[128,128]{0,1:T(8,128)(2,1)}, bf16[128,128]{0,1:T(8,128)(2,1)S(1)}, u32[]{:S(2)}) copy-start(bf16[128,128]{0,1:T(8,128)(2,1)S(1)} %get-tuple-element.93) | copy-start | bytes 98308
  134.1 11.0 %copy-start.34 = (s32[128]{0:T(128)S(1)}, s32[128]{0:T(128)}, u32[]{:S(2)}) copy-start(s32[128]{0:T(128)} %param.23) | copy-start | bytes 1540
  134.1 11.7 %copy-start.29 = (bf16[8,512]{1,0:T(8,128)(2,1)S(1)}, bf16[8,512]{1,0:T(8,128)(2,1)}, u32[]{:S(2)}) copy-start(bf16[8,512]{1,0:T(8,128)(2,1)} %param.32) | copy-start | bytes 24580
  136.2 30.5 %copy-start.1 = (bf16[256,512]{1,0:T(8,128)(2,1)S(1)}, bf16[256,512]{1,0:T(8,128)(2,1)}, u32[]{:S(2)}) copy-start(bf16[256,512]{1,0:T(8,128)(2,1)} %param.29) | copy-start | bytes 786436
  138.2 24.3 %all-to-all-start.2 = ((bf16[8,272,128]{2,1,0:T(8,128)(2,1)}), bf16[8,272,128]{2,1,0:T(8,128)(2,1)}, u32[]{:S(2)}, u32[]{:S(2)}) async-start(bf16[8,272,128]{2,1,0:T(8,128)(2,1)} %pad_maximum_fusion), calls=%async_computation.2 | async-start | bytes 1114112 | tf_op jit(solution)/shard_map/all_to_all | solution.py:26
  163.7 0.7 copy-start.5
  168.6 11.8 %all-to-all-start.3 = ((bf16[8,16,512]{2,1,0:T(8,128)(2,1)}), bf16[8,16,512]{2,1,0:T(8,128)(2,1)S(1)}, u32[]{:S(2)}, u32[]{:S(2)}) async-start(bf16[8,16,512]{2,1,0:T(8,128)(2,1)} %bitcast.41), calls=%async_computation.3 | async-start | bytes 262144 | tf_op jit(solution)/shard_map/all_to_all | solution.py:26
  173.8 6.6 %copy-start.24 = (f32[128,16]{0,1:T(8,128)}, f32[128,16]{0,1:T(8,128)S(1)}, u32[]{:S(2)}) copy-start(f32[128,16]{0,1:T(8,128)S(1)} %fusion.125) | copy-start | bytes 24580
  176.7 13.9 %collective-permute-start.10 = (bf16[4,512,256]{2,1,0:T(8,128)(2,1)}, bf16[4,512,256]{2,1,0:T(8,128)(2,1)}, u32[]{:S(2)}, u32[]{:S(2)}) collective-permute-start(bf16[4,512,256]{2,1,0:T(8,128)(2,1)} %all-gather.4.cloned.1.call-done), channel_id=1, source_target_pairs={{0,8},{8,0},{1,9},{9,1},{2,10},{10,2},{3,11},{11,3},{4,12},{12,4},... | collective-permute-start | bytes 3145736 | tf_op jit(solution)/shard_map/ppermute | solution.py:226
  184.1 0.6 copy-start.9
  186.2 7.6 %collective-permute-start.11 = (bf16[128,640]{1,0:T(8,128)(2,1)}, bf16[128,640]{1,0:T(8,128)(2,1)}, u32[]{:S(2)}, u32[]{:S(2)}) collective-permute-start(bf16[128,640]{1,0:T(8,128)(2,1)} %pad_maximum_fusion.4), channel_id=1, source_target_pairs={{0,1},{1,0},{2,3},{3,2},{4,5},{5,4},{6,7},{7,6},{8,9},{9,8},{10,11... | collective-permute-start | bytes 491528 | tf_op jit(solution)/shard_map/ppermute | solution.py:263
  192.6 1.1 copy-start.8
  192.7 1.1 copy-start.10
  192.7 1.1 copy-start.23
  192.7 1.1 copy-start.31
  193.8 1.6 copy-start.11
  196.8 8.9 %copy-start.12 = (f32[128,16]{1,0:T(8,128)S(1)}, f32[128,16]{1,0:T(8,128)}, u32[]{:S(2)}) copy-start(f32[128,16]{1,0:T(8,128)} %copy.97) | copy-start | bytes 24580
  196.8 9.1 %copy-start.22 = (bf16[512,16]{0,1:T(8,128)(2,1)S(1)}, bf16[512,16]{0,1:T(8,128)(2,1)}, u32[]{:S(2)}) copy-start(bf16[512,16]{0,1:T(8,128)(2,1)} %param.36) | copy-start | bytes 49156
  196.8 9.1 %copy-start.25 = (f32[512]{0:T(512)S(1)}, f32[512]{0:T(512)}, u32[]{:S(2)}) copy-start(f32[512]{0:T(512)} %param.33) | copy-start | bytes 6148
  196.8 9.3 %copy-start.13 = (f32[128,16]{1,0:T(8,128)S(1)}, f32[128,16]{1,0:T(8,128)}, u32[]{:S(2)}) copy-start(f32[128,16]{1,0:T(8,128)} %copy.98) | copy-start | bytes 24580
  196.8 9.3 %copy-start.30 = (s32[128]{0:T(128)S(1)}, s32[128]{0:T(128)}, u32[]{:S(2)}) copy-start(s32[128]{0:T(128)} %eq.44) | copy-start | bytes 1540
  196.8 9.6 %copy-start.7 = (bf16[128,512]{1,0:T(8,128)(2,1)S(1)}, bf16[128,512]{1,0:T(8,128)(2,1)}, u32[]{:S(2)}) copy-start(bf16[128,512]{1,0:T(8,128)(2,1)} %param.39) | copy-start | bytes 393220
  198.0 8.6 %copy-start.32 = (bf16[48]{0:T(256)(128)(2,1)S(1)}, bf16[48]{0:T(256)(128)(2,1)}, u32[]{:S(2)}) copy-start(bf16[48]{0:T(256)(128)(2,1)} %pad.22.clone) | copy-start | bytes 292
  198.1 7.6 %collective-permute-start.12 = (bf16[128,640]{1,0:T(8,128)(2,1)S(1)}, bf16[128,640]{1,0:T(8,128)(2,1)S(1)}, u32[]{:S(2)}, u32[]{:S(2)}) collective-permute-start(bf16[128,640]{1,0:T(8,128)(2,1)S(1)} %slice.576), channel_id=1, source_target_pairs={{0,1},{1,0},{2,3},{3,2},{4,5},{5,4},{6,7},{7,6},{8,9},{9,8},{10,11... | collective-permute-start | bytes 491528 | tf_op jit(solution)/shard_map/ppermute | solution.py:268
  206.8 15.9 %copy-start.35 = (s32[128]{0:T(128)S(1)}, s32[128]{0:T(128)}, u32[]{:S(2)}) copy-start(s32[128]{0:T(128)} %param.23) | copy-start | bytes 1540
  206.8 17.8 %copy-start.2 = (bf16[256,512]{1,0:T(8,128)(2,1)S(1)}, bf16[256,512]{1,0:T(8,128)(2,1)}, u32[]{:S(2)}) copy-start(bf16[256,512]{1,0:T(8,128)(2,1)} %param.29) | copy-start | bytes 786436
  206.8 17.7 %copy-start.26 = (bf16[128,16]{0,1:T(8,128)(2,1)S(1)}, bf16[128,16]{0,1:T(8,128)(2,1)}, u32[]{:S(2)}) copy-start(bf16[128,16]{0,1:T(8,128)(2,1)} %get-tuple-element.127) | copy-start | bytes 12292
  220.0 0.8 copy-start.3
Sparse Core Ops, SparseCore 0:
  21.2 60.5 all-gather.5
Sparse Core Ops, SparseCore 1:
  119.3 43.2 all-gather.3

commit v3 on v2

--- a/solution.py
+++ b/solution.py
@@ -15,6 +15,7 @@
 SEQ = ("seq_0", "near", "seq_1", "seq_2")
 Z, NEAR, FAR, CORE = SEQ
 QUAD = (NEAR, FAR)
+EIGHT = (NEAR, FAR, CORE)
 LINE, SIDE = ROW
 SEQ_ROW = SEQ + ROW
 SWAP = [(0, 1), (1, 0)]
@@ -121,8 +122,70 @@
     units = hidden_in.shape[0]
     share = hidden_in.shape[1]
 
+    hidden = jnp.concatenate([hidden_in.T, hidden_out.T], axis=0)
+    hidden = in_pair_order(hidden, lax.ppermute(hidden, FAR, SWAP), far, 0)
     weights = jnp.concatenate([local_weight, fold(global_up), fold(local_up)], axis=0)
     weights = lax.all_gather(weights, ROW, axis=0, tiled=False)
+    cotangents = jnp.concatenate([cotangent, lax.ppermute(cotangent, SIDE, SWAP)], axis=0)
+
+    def head(array, which):
+        return lax.dynamic_slice_in_dim(array, which * HEAD, HEAD, 1)
+
+    trio = (patch_queries, patch_keys, patch_values)
+    mine = jnp.concatenate([head(a, core) for a in trio], axis=1)
+    other = jnp.concatenate([head(a, 1 - core) for a in trio], axis=1)
+    both = jnp.concatenate([mine, lax.ppermute(other, CORE, SWAP)], axis=0)
+    chip_rows = 2 * rows
+    packet = both[:, HEAD:]
+    quad = to_everyone(both[:, :HEAD], QUAD)
+    sides = lax.axis_size(QUAD)
+    queries = quad.reshape(sides * chip_rows, HEAD)
+
+    def places(z_index, near_index, far_index):
+        start = (z_index * 8 + near_index * 4 + far_index * 2) * rows
+        count = jnp.arange(rows, dtype=jnp.int32)
+        return jnp.concatenate([start + core * rows + count, start + (1 - core) * rows + count])
+
+    query_places = jnp.concatenate([places(z, k // 2, k % 2) for k in range(sides)])
+    count = sides * chip_rows
+    state = (
+        jnp.full((count, 1), -1e30, F32),
+        jnp.zeros((count, 1), F32),
+        jnp.zeros((count, HEAD), F32),
+    )
+    up = [(i, (i + 1) % ring) for i in range(ring)]
+    down = [(i, (i - 1) % ring) for i in range(ring)]
+
+    def visit(state, packets, indices):
+        keys = jnp.concatenate([p[:, :HEAD] for p in packets])
+        values = jnp.concatenate([p[:, HEAD:] for p in packets])
+        key_places = jnp.concatenate([places(i, near, far) for i in indices])
+        return attend(state, queries, query_places, keys, values, key_places)
+
+    rising = falling = packet
+    held, at = [[packet]], [[z]]
+    for step in range(1, ring // 2 + 1):
+        rising = lax.ppermute(rising, Z, up)
+        held.append([rising])
+        at.append([(z - step) % ring])
+        if step < ring // 2:
+            falling = lax.ppermute(falling, Z, down)
+            held[-1].append(falling)
+            at[-1].append((z + step) % ring)
+        if step == 1:
+            rising, falling, hidden, queries = lax.optimization_barrier(
+                (rising, falling, hidden, queries)
+            )
+            hidden = to_everyone(hidden, (Z, NEAR)).reshape(-1, units)
+        elif step == 2:
+            rising, falling, hidden = lax.optimization_barrier((rising, falling, hidden))
+        if step >= 2:
+            state = visit(state, held[step - 2], at[step - 2])
+    state = visit(state, held[-2], at[-2])
+    state = visit(state, held[-1], at[-1])
+    state, weights, hidden = lax.optimization_barrier((state, weights, hidden))
+    riders = lax.all_gather(hidden, LINE, axis=0, tiled=False)
+
     local_whole = weights[:, :width].reshape(-1, columns)
     up_whole = unfold(weights[:, width : width + 8])
     up_whole = jnp.transpose(up_whole, (1, 0, 2)).reshape(RANK, -1)
@@ -130,82 +193,17 @@
     local_ups = unfold(weights[:, width + 8 :]).reshape(line, 2, RANK, units)
     local_ups = lax.dynamic_index_in_dim(local_ups, side, 1, keepdims=False)
     local_ups = jnp.concatenate([local_ups[k] for k in range(line)], axis=1)
-    cotangents = jnp.concatenate([cotangent, lax.ppermute(cotangent, SIDE, SWAP)], axis=0)
-
-    def head(array, which):
-        return lax.dynamic_slice_in_dim(array, which * HEAD, HEAD, 1)
-
-    trio = (patch_queries, patch_keys, patch_values)
-    mine = jnp.concatenate([head(a, core) for a in trio], axis=1)
-    other = jnp.concatenate([head(a, 1 - core) for a in trio], axis=1)
-    both = jnp.concatenate([mine, lax.ppermute(other, CORE, SWAP)], axis=0)
-    hidden = jnp.concatenate([hidden_in.T, hidden_out.T], axis=0)
-    halves = [hidden[:, k * HEAD : (k + 1) * HEAD] for k in range(units // HEAD)]
-    chip_rows = 2 * rows
-    tall = 2 * share
-    quad = to_everyone(jnp.concatenate([both[:, :HEAD], *halves], axis=0), QUAD)
-    sides = lax.axis_size(QUAD)
-    queries = quad[:, :chip_rows].reshape(sides * chip_rows, HEAD)
-    quad_hidden = jnp.concatenate(
-        [
-            quad[:, chip_rows + k * tall : chip_rows + (k + 1) * tall].reshape(sides * tall, HEAD)
-            for k in range(units // HEAD)
-        ],
-        axis=1,
-    )
-    packet = jnp.concatenate([both[:, HEAD:], quad_hidden], axis=0)
-
-    def places(z_index, near_index, far_index):
-        start = (z_index * 8 + near_index * 4 + far_index * 2) * rows
-        count = jnp.arange(rows, dtype=jnp.int32)
-        return jnp.concatenate([start + core * rows + count, start + (1 - core) * rows + count])
-
-    query_places = jnp.concatenate([places(z, k // 2, k % 2) for k in range(sides)])
-    count = sides * chip_rows
-    state = (
-        jnp.full((count, 1), -1e30, F32),
-        jnp.zeros((count, 1), F32),
-        jnp.zeros((count, HEAD), F32),
-    )
-    up = [(i, (i + 1) % ring) for i in range(ring)]
-    down = [(i, (i - 1) % ring) for i in range(ring)]
-
-    def visit(state, packets, indices):
-        keys = jnp.concatenate([p[:chip_rows, :HEAD] for p in packets])
-        values = jnp.concatenate([p[:chip_rows, HEAD:] for p in packets])
-        key_places = jnp.concatenate([places(i, near, far) for i in indices])
-        return attend(state, queries, query_places, keys, values, key_places)
-
-    riders = [None] * ring
-    riders[0] = packet[chip_rows:]
-    rising = falling = packet
-    now, at = [packet], [z]
-    for step in range(1, ring // 2 + 1):
-        rising = lax.ppermute(rising, Z, up)
-        riders[-step % ring] = rising[chip_rows:]
-        later, then = [rising], [(z - step) % ring]
-        if step < ring // 2:
-            falling = lax.ppermute(falling, Z, down)
-            riders[step] = falling[chip_rows:]
-            later.append(falling)
-            then.append((z + step) % ring)
-        state = visit(state, now, at)
-        now, at = later, then
-    state = visit(state, now, at)
-    state, local_whole, up_whole, local_ups, cotangents = lax.optimization_barrier(
-        (state, local_whole, up_whole, local_ups, cotangents)
-    )
-
-    riders = jnp.roll(jnp.stack(riders), z, axis=0).reshape(ring * sides * tall, units)
-    riders = lax.all_gather(riders, LINE, axis=0, tiled=False)
 
     top, mass, out = state
     level = jnp.where(mass > 0, top + jnp.log(jnp.where(mass > 0, mass, 1.0)), -1e30)
     out = out / jnp.where(mass > 0, mass, 1.0)
-    high = level.astype(BF)
-    middle = (level - high.astype(F32)).astype(BF)
-    low = (level - high.astype(F32) - middle.astype(F32)).astype(BF)
-    wide = [jnp.broadcast_to(a, (count, n)) for a, n in ((high, 32), (middle, 32), (low, 64))]
+    high = lax.reduce_precision(level, 8, 7)
+    middle = lax.reduce_precision(level - high, 8, 7)
+    low = level - high - middle
+    wide = [
+        jnp.broadcast_to(a.astype(BF), (count, n))
+        for a, n in ((high, 32), (middle, 32), (low, 64))
+    ]
     met = jnp.concatenate([out.astype(BF), *wide], axis=1)
     met = exchange(met.reshape(sides, chip_rows, 2 * HEAD), QUAD).astype(F32)
     levels = met[:, :, 128:129] + met[:, :, 160:161] + met[:, :, 192:193]
@@ -222,18 +220,6 @@
     arrived = exchange(jnp.concatenate([part, low_part], axis=1), ROW)
     arrived, riders = lax.optimization_barrier((arrived, riders))
     arrived = arrived.astype(F32).sum(axis=0)
-
-    rest = lax.ppermute(riders, CORE, SWAP)
-    split = (line, ring * sides, 2, 1, share, units)
-    riders = in_pair_order(riders.reshape(split), rest.reshape(split), core, 3)
-    riders = jnp.moveaxis(riders, 2, 0).reshape(2, line, columns, units)
-    rows_in, rows_out = (
-        jnp.concatenate([riders[way, k] for k in range(line)], axis=1) for way in range(2)
-    )
-    lanes = 128
-    stacked = jnp.concatenate(
-        [rows_in, local_ups, jnp.zeros((lanes - RANK, line * units), BF)], axis=0
-    )
 
     reduced = jnp.transpose(arrived[width:])
     scaled = (reduced * task_scales).astype(BF)
@@ -246,6 +232,18 @@
     projected = contract(mixed_b, local_weight, 0, 0).astype(BF)
     projected = exchange(projected.reshape(row_count, own_patches, columns), ROW)
     projected = total(projected).astype(BF)
+
+    rest = lax.ppermute(riders, CORE, SWAP)
+    split = (line, columns // (2 * share), 2, 1, share, units)
+    riders = in_pair_order(riders.reshape(split), rest.reshape(split), core, 3)
+    riders = jnp.moveaxis(riders, 2, 0).reshape(2, line, columns, units)
+    rows_in, rows_out = (
+        jnp.concatenate([riders[way, k] for k in range(line)], axis=1) for way in range(2)
+    )
+    lanes = 128
+    stacked = jnp.concatenate(
+        [rows_in, local_ups, jnp.zeros((lanes - RANK, line * units), BF)], axis=0
+    )
 
     picks = (own_ids[:, None] == jnp.arange(VOCAB, dtype=jnp.int32)[None, :]).astype(BF)
     embedded = jnp.dot(picks, byte_table, preferred_element_type=F32)
@@ -314,9 +312,10 @@
         ]
     ).astype(BF)
     shape = packed.shape
-    pieces = packed.reshape(lax.axis_size(SEQ), -1)
-    pieces = exchange(pieces, SEQ).astype(F32).sum(axis=0)
-    packed = to_everyone(pieces, SEQ).reshape(shape)
+    pieces = packed.reshape(lax.axis_size(EIGHT), -1, shape[1])
+    pieces = exchange(pieces, EIGHT).astype(F32).sum(axis=0)
+    pieces = to_everyone(pieces, Z).sum(axis=0)
+    packed = to_everyone(pieces, EIGHT).reshape(shape)
     return (
         jnp.transpose(packed[:16]),
         packed[16:32],

time: 292 us -> 276 us (0.945)
  blocking collectives: 65.6 us -> 48.2 us
  starting transfers between devices: 82.4 us -> 94.4 us
  waiting for transfers between devices: 50.3 us -> 39 us
  local copies, waits for them, and re-layouts: 31.7 us -> 25.6 us
  matrix products: 23.9 us -> 28 us
  other arithmetic: 19.1 us -> 22.9 us
    all_to_all x3, blocking collectives: 65.6 us -> 48.2 us  [exchange(): return lax.all_to_all(pieces, axis, split_axis=0, concat_axis=0, tiled=True)]
    all_gather x1, waiting for transfers between devices: 16.7 us -> 0.01 us  [body(): riders = lax.all_gather(hidden, LINE, axis=0, tiled=False)]
    all_to_all x4 -> x6, waiting for transfers between devices: 6.1 us -> 21.1 us  [exchange(): return lax.all_to_all(pieces, axis, split_axis=0, concat_axis=0, tiled=True)]
    unnamed x98 -> x93, local copies, waits for them, and re-layouts: 11.3 us -> 4.27 us
    all_to_all x4 -> x6, starting transfers between devices: 22.3 us -> 28 us  [exchange(): return lax.all_to_all(pieces, axis, split_axis=0, concat_axis=0, tiled=True)]
    ppermute x4, waiting for transfers between devices: 18.3 us -> 12.7 us  [body(): rising = lax.ppermute(rising, Z, up)]
    ppermute x4, starting transfers between devices: 7.68 us -> 12.7 us  [body(): rising = lax.ppermute(rising, Z, up)]
    ppermute x3, waiting for transfers between devices: 3.98 us -> 0.01 us  [body(): falling = lax.ppermute(falling, Z, down)]
  transfers between devices with their start and end apart: 19 -> 22, of which waited for: 10 -> 9; matrix products, arithmetic and copies ran while one was open for 15% -> 21% of each run, Pallas kernels for 0% -> 0%
where the time goes in v3:
time: 276 us; the launch traced here: 274 us
  starting transfers between devices  94.4 us (34%)
  blocking collectives  48.2 us (17%)
  waiting for transfers between devices  39 us (14%)
  matrix products  28 us (10%)
  local copies, waits for them, and re-layouts  25.6 us (9%)
  other arithmetic  22.9 us (8%)
  between operations  15.5 us (6%)
    all_to_all x3, blocking collectives, exchange(): return lax.all_to_all(pieces, axis, split_axis=0, concat_axis=0, tiled=True)  48.2 us
    all_to_all x6, starting transfers between devices, exchange(): return lax.all_to_all(pieces, axis, split_axis=0, concat_axis=0, tiled=True)  28 us
    all_to_all x6, waiting for transfers between devices, exchange(): return lax.all_to_all(pieces, axis, split_axis=0, concat_axis=0, tiled=True)  21.1 us
    ppermute x3, starting transfers between devices, body(): falling = lax.ppermute(falling, Z, down)  18.5 us
    dot_general x17, matrix products, contract(): lax.dot_general(left, right, (((left_dim,), (right_dim,)), ((), ())), pre...  17.2 us
    ppermute x4, waiting for transfers between devices, body(): rising = lax.ppermute(rising, Z, up)  12.7 us
    ppermute x4, starting transfers between devices, body(): rising = lax.ppermute(rising, Z, up)  12.7 us
    ppermute x1, starting transfers between devices, body(): partner = lax.ppermute(merged[rows:], CORE, SWAP)  12.3 us
  transfers between devices with their start and end apart: 22, of which 9 were waited for; matrix products, arithmetic and copies ran while one was open for 21% of the time, Pallas kernels for 0%

profile of v3, /device:TPU:1, one launch (start us, length us, event | category | flops | bytes accessed | tf_op | source)
XLA Modules:
  0.0 273.6 jit_solution(2417509873470097470)
XLA Ops:
  7.3 0.9 constant_dynamic-slice_fusion.5
  9.0 8.8 %collective-permute-start = (bf16[128,384]{1,0:T(8,128)(2,1)S(1)}, bf16[128,384]{1,0:T(8,128)(2,1)S(1)}, u32[]{:S(2)}, u32[]{:S(2)}) collective-permute-start(bf16[128,384]{1,0:T(8,128)(2,1)S(1)} %pad_maximum_fusion.4), channel_id=1, source_target_pairs={{0,8},{8,0},{1,9},{9,1},{2,10},{10,2},{3,11},{11,3},{4,12},{12,4},... | collective-permute-start | bytes 294920 | tf_op jit(solution)/shard_map/ppermute | solution.py:137
  18.5 1.9 collective-permute-start.3
  21.2 1.7 maximum_maximum_fusion.1
  25.1 8.9 %collective-permute-start.2 = (bf16[256,256]{1,0:T(8,128)(2,1)S(1)}, bf16[256,256]{1,0:T(8,128)(2,1)S(1)}, u32[]{:S(2)}, u32[]{:S(2)}) collective-permute-start(bf16[256,256]{1,0:T(8,128)(2,1)S(1)} %slice.355), channel_id=1, source_target_pairs={{0,448},{64,0},{128,64},{192,128},{256,192},{320,256},{384,320},{4... | collective-permute-start | bytes 393224 | tf_op jit(solution)/shard_map/ppermute | solution.py:172
  34.8 3.4 %all-to-all-start = ((bf16[4,256,128]{2,1,0:T(8,128)(2,1)}), bf16[4,256,128]{2,1,0:T(8,128)(2,1)S(1)}, u32[]{:S(2)}, u32[]{:S(2)}) async-start(bf16[4,256,128]{2,1,0:T(8,128)(2,1)} %broadcast_in_dim.64), calls=%async_computation | async-start | bytes 524288 | tf_op jit(solution)/shard_map/all_to_all | solution.py:27
  38.2 1.9 collective-permute-start.1
  40.2 7.9 %collective-permute-done.1 = bf16[256,256]{1,0:T(8,128)(2,1)S(1)} collective-permute-done((bf16[256,256]{1,0:T(8,128)(2,1)S(1)}, bf16[256,256]{1,0:T(8,128)(2,1)S(1)}, u32[]{:S(2)}, u32[]{:S(2)}) %collective-permute-start.1) | collective-permute-done | bytes 131104 | tf_op jit(solution)/shard_map/ppermute | solution.py:168
  48.1 1.9 collective-permute-start.4
  50.1 5.5 %collective-permute-start.5 = (bf16[256,256]{1,0:T(8,128)(2,1)S(1)}, bf16[256,256]{1,0:T(8,128)(2,1)S(1)}, u32[]{:S(2)}, u32[]{:S(2)}) collective-permute-start(bf16[256,256]{1,0:T(8,128)(2,1)S(1)} %collective-permute-done.2), channel_id=1, source_target_pairs={{0,448},{64,0},{128,64},{192,128},{256,192},{320,256},{384,320},{4... | collective-permute-start | bytes 393224 | tf_op jit(solution)/shard_map/ppermute | solution.py:172
  56.3 7.0 %all-to-all-start.1 = ((bf16[16,32,256]{2,1,0:T(8,128)(2,1)}), bf16[16,32,256]{2,1,0:T(8,128)(2,1)S(1)}, u32[]{:S(2)}, u32[]{:S(2)}) async-start(bf16[16,32,256]{2,1,0:T(8,128)(2,1)} %broadcast_in_dim.68), calls=%async_computation.1 | async-start | bytes 524288 | tf_op jit(solution)/shard_map/all_to_all | solution.py:27
  63.2 1.8 fusion.1
  65.4 1.4 fusion.11
  66.8 9.2 %all-to-all-done.1 = bf16[16,32,256]{2,1,0:T(8,128)(2,1)S(1)} async-done(((bf16[16,32,256]{2,1,0:T(8,128)(2,1)}), bf16[16,32,256]{2,1,0:T(8,128)(2,1)S(1)}, u32[]{:S(2)}, u32[]{:S(2)}) %all-to-all-start.1) | async-done | bytes 262176 | tf_op jit(solution)/shard_map/all_to_all | solution.py:27
  76.0 6.3 %collective-permute-start.6 = (bf16[256,256]{1,0:T(8,128)(2,1)S(1)}, bf16[256,256]{1,0:T(8,128)(2,1)S(1)}, u32[]{:S(2)}, u32[]{:S(2)}) collective-permute-start(bf16[256,256]{1,0:T(8,128)(2,1)S(1)} %collective-permute-done.4), channel_id=1, source_target_pairs={{0,64},{64,128},{128,192},{192,256},{256,320},{320,384},{384,448},... | collective-permute-start | bytes 393224 | tf_op jit(solution)/shard_map/ppermute | solution.py:168
  82.3 4.1 %collective-permute-start.7 = (bf16[256,256]{1,0:T(8,128)(2,1)S(1)}, bf16[256,256]{1,0:T(8,128)(2,1)S(1)}, u32[]{:S(2)}, u32[]{:S(2)}) collective-permute-start(bf16[256,256]{1,0:T(8,128)(2,1)S(1)} %collective-permute-done.5), channel_id=1, source_target_pairs={{0,448},{64,0},{128,64},{192,128},{256,192},{320,256},{384,320},{4... | collective-permute-start | bytes 393224 | tf_op jit(solution)/shard_map/ppermute | solution.py:172
  86.5 1.3 collective-permute-done.6
  87.8 2.5 collective-permute-start.8
  90.8 2.1 fusion.13
  93.0 3.5 %collective-permute-done.8 = bf16[256,256]{1,0:T(8,128)(2,1)S(1)} collective-permute-done((bf16[256,256]{1,0:T(8,128)(2,1)S(1)}, bf16[256,256]{1,0:T(8,128)(2,1)S(1)}, u32[]{:S(2)}, u32[]{:S(2)}) %collective-permute-start.8) | collective-permute-done | bytes 131104 | tf_op jit(solution)/shard_map/ppermute | solution.py:168
  97.3 1.4 fusion.15
  103.0 1.0 copy.99
  104.0 3.8 %all-to-all-start.2 = ((bf16[4,256,256]{1,2,0:T(8,128)(2,1)}), bf16[4,256,256]{1,2,0:T(8,128)(2,1)S(1)}, u32[]{:S(2)}, u32[]{:S(2)}) async-start(bf16[4,256,256]{1,2,0:T(8,128)(2,1)} %copy.99), calls=%async_computation.2 | async-start | bytes 1048576 | tf_op jit(solution)/shard_map/all_to_all | solution.py:27
  108.5 6.2 %all-to-all-done.2 = bf16[4,256,256]{1,2,0:T(8,128)(2,1)S(1)} async-done(((bf16[4,256,256]{1,2,0:T(8,128)(2,1)}), bf16[4,256,256]{1,2,0:T(8,128)(2,1)S(1)}, u32[]{:S(2)}, u32[]{:S(2)}) %all-to-all-start.2) | async-done | bytes 524320 | tf_op jit(solution)/shard_map/all_to_all | solution.py:27
  114.9 12.3 %collective-permute-start.9 = (bf16[128,128]{0,1:T(8,128)(2,1)S(1)}, bf16[128,128]{0,1:T(8,128)(2,1)S(1)}, u32[]{:S(2)}, u32[]{:S(2)}) collective-permute-start(bf16[128,128]{0,1:T(8,128)(2,1)S(1)} %slice.378), channel_id=1, source_target_pairs={{0,8},{8,0},{1,9},{9,1},{2,10},{10,2},{3,11},{11,3},{4,12},{12,4},... | collective-permute-start | bytes 98312 | tf_op jit(solution)/shard_map/ppermute | solution.py:213
  127.3 0.8 collective-permute-done.9
  128.7 1.1 fusion
  129.8 2.2 copy.113
  132.1 0.9 fusion.25
  133.0 1.9 pad_maximum_fusion
  134.9 4.6 %all-to-all-start.3 = ((bf16[8,272,128]{2,1,0:T(8,128)(2,1)}), bf16[8,272,128]{2,1,0:T(8,128)(2,1)}, u32[]{:S(2)}, u32[]{:S(2)}) async-start(bf16[8,272,128]{2,1,0:T(8,128)(2,1)} %pad_maximum_fusion), calls=%async_computation.3 | async-start | bytes 1114112 | tf_op jit(solution)/shard_map/all_to_all | solution.py:27
  139.5 3.5 %collective-permute-start.10 = (bf16[128,512]{1,0:T(8,128)(2,1)}, bf16[128,512]{1,0:T(8,128)(2,1)}, u32[]{:S(2)}, u32[]{:S(2)}) collective-permute-start(bf16[128,512]{1,0:T(8,128)(2,1)} %param.39), channel_id=1, source_target_pairs={{0,1},{1,0},{2,3},{3,2},{4,5},{5,4},{6,7},{7,6},{8,9},{9,8},{10,11... | collective-permute-start | bytes 393224 | tf_op jit(solution)/shard_map/ppermute | solution.py:129
  144.6 1.5 fusion.123
  146.1 1.4 copy.106
  148.7 1.3 dynamic_slice.28
  150.7 1.1 convert_reduce_fusion
  152.6 1.6 multiply_convert_fusion.4
  154.1 1.7 copy.119
  155.8 1.9 convolution_convert_fusion.3
  157.7 4.0 %all-to-all-start.4 = ((bf16[8,16,512]{2,1,0:T(8,128)(2,1)}), bf16[8,16,512]{2,1,0:T(8,128)(2,1)S(1)}, u32[]{:S(2)}, u32[]{:S(2)}) async-start(bf16[8,16,512]{2,1,0:T(8,128)(2,1)} %bitcast.149), calls=%async_computation.4 | async-start | bytes 262144 | tf_op jit(solution)/shard_map/all_to_all | solution.py:27
  163.1 3.4 %collective-permute-start.11 = (bf16[4,512,256]{2,1,0:T(8,128)(2,1)}, bf16[4,512,256]{2,1,0:T(8,128)(2,1)}, u32[]{:S(2)}, u32[]{:S(2)}) collective-permute-start(bf16[4,512,256]{2,1,0:T(8,128)(2,1)} %bitcast.141), channel_id=1, source_target_pairs={{0,8},{8,0},{1,9},{9,1},{2,10},{10,2},{3,11},{11,3},{4,12},{12,4},... | collective-permute-start | bytes 3145736 | tf_op jit(solution)/shard_map/ppermute | solution.py:236
  167.2 1.3 multiply_reduce_fusion.1
  170.0 0.9 multiply_convert_fusion.3
  172.2 1.7 pad_maximum_fusion.3
  173.9 2.9 %collective-permute-start.12 = (bf16[128,640]{1,0:T(8,128)(2,1)}, bf16[128,640]{1,0:T(8,128)(2,1)}, u32[]{:S(2)}, u32[]{:S(2)}) collective-permute-start(bf16[128,640]{1,0:T(8,128)(2,1)} %pad_maximum_fusion.3), channel_id=1, source_target_pairs={{0,1},{1,0},{2,3},{3,2},{4,5},{5,4},{6,7},{7,6},{8,9},{9,8},{10,11... | collective-permute-start | bytes 491528 | tf_op jit(solution)/shard_map/ppermute | solution.py:261
  177.5 1.7 broadcast_select_fusion.1
  180.3 4.1 %maximum_maximum_fusion = bf16[640,1024]{1,0:T(8,128)(2,1)S(1)} fusion(bf16[16,256]{1,0:T(8,128)(2,1)S(1)} %copy-done.22, bf16[16,256]{1,0:T(8,128)(2,1)S(1)} %copy-done.20, bf16[16,256]{1,0:T(8,128)(2,1)S(1)} %copy-done.21, bf16[16,256]{1,0:T(8,128)(2,1)S(1)} %copy-done.19, bf16[512,256]{1,0:T(8,128)(2,1)S(1)} %get-tuple-element.68, ...), kind=kLoop, calls=%fused_computation.21 | loop fusion | flops 11796480 | bytes 2393344 | tf_op jit(solution)/shard_map/concatenate | solution.py:244
  184.4 1.5 fusion.75
  186.0 1.5 fusion.6
  188.2 1.1 convolution_convert_fusion.2
  189.4 2.4 collective-permute-start.13
  191.8 3.6 %collective-permute-done.13 = bf16[128,640]{1,0:T(8,128)(2,1)S(1)} collective-permute-done((bf16[128,640]{1,0:T(8,128)(2,1)S(1)}, bf16[128,640]{1,0:T(8,128)(2,1)S(1)}, u32[]{:S(2)}, u32[]{:S(2)}) %collective-permute-start.13) | collective-permute-done | bytes 163872 | tf_op jit(solution)/shard_map/ppermute | solution.py:266
  196.6 0.8 fusion.65
  197.4 5.3 %all-to-all-start.5 = ((bf16[8,64,512]{2,1,0:T(8,128)(2,1)}), bf16[8,64,512]{2,1,0:T(8,128)(2,1)}, u32[]{:S(2)}, u32[]{:S(2)}) async-start(bf16[8,64,512]{2,1,0:T(8,128)(2,1)} %fusion.65), calls=%async_computation.5 | async-start | bytes 1048576 | tf_op jit(solution)/shard_map/all_to_all | solution.py:27
  202.7 1.2 copy.108
  203.9 1.5 slice.338
  205.6 4.9 %all-to-all-done.5 = bf16[8,64,512]{2,1,0:T(8,128)(2,1)} async-done(((bf16[8,64,512]{2,1,0:T(8,128)(2,1)}), bf16[8,64,512]{2,1,0:T(8,128)(2,1)}, u32[]{:S(2)}, u32[]{:S(2)}) %all-to-all-start.5) | async-done | bytes 524320 | tf_op jit(solution)/shard_map/all_to_all | solution.py:27
  210.5 0.9 slice.397
  211.4 2.6 fusion.7
  214.0 0.9 convolution_convert_fusion.8
  215.5 1.1 convert_reduce_fusion.1
  216.6 12.4 %all_to_all.45 = bf16[8,12,256]{2,1,0:T(8,128)(2,1)S(1)} all-to-all(bf16[8,12,256]{2,1,0:T(8,128)(2,1)S(1)} %convert_element_type.155), channel_id=1, replica_groups=mesh['seq_0'=8,'near'=2,'seq_1'=2,'seq_2'=2,'row_0'=4,'row_1'=2] {'near'..., dimensions={0} | all-to-all | bytes 98304 | tf_op jit(solution)/shard_map/all_to_all | solution.py:27
  229.0 24.0 %all_to_all.46 = f32[8,12,256]{2,1,0:T(8,128)S(1)} all-to-all(f32[8,12,256]{2,1,0:T(8,128)S(1)} %broadcast_in_dim.162), channel_id=1, replica_groups=mesh['seq_0'=8,'near'=2,'seq_1'=2,'seq_2'=2,'row_0'=4,'row_1'=2] {'seq_0'}, dimensions={0} | all-to-all | bytes 196608 | tf_op jit(solution)/shard_map/all_to_all | solution.py:27
  253.1 11.8 %all_to_all.47 = f32[8,12,256]{2,1,0:T(8,128)S(1)} all-to-all(f32[8,12,256]{2,1,0:T(8,128)S(1)} %broadcast_in_dim.163), channel_id=1, replica_groups=mesh['seq_0'=8,'near'=2,'seq_1'=2,'seq_2'=2,'row_0'=4,'row_1'=2] {'near'..., dimensions={0} | all-to-all | bytes 196608 | tf_op jit(solution)/shard_map/all_to_all | solution.py:27
  (227 shorter events, 28.3 us)
Async XLA Ops:
  7.2 121.6 %copy-start = (bf16[256,2048]{1,0:T(8,128)(2,1)S(1)}, bf16[256,2048]{1,0:T(8,128)(2,1)}, u32[]{:S(2)}) copy-start(bf16[256,2048]{1,0:T(8,128)(2,1)} %param.25) | copy-start | bytes 3145732
  7.2 31.0 %copy-start.25 = (bf16[256,8]{0,1:T(8,128)(2,1)S(1)}, bf16[256,8]{0,1:T(8,128)(2,1)}, u32[]{:S(2)}) copy-start(bf16[256,8]{0,1:T(8,128)(2,1)} %param.35) | copy-start | bytes 12292
  7.2 31.0 %copy-start.26 = (bf16[256,8]{0,1:T(8,128)(2,1)S(1)}, bf16[256,8]{0,1:T(8,128)(2,1)}, u32[]{:S(2)}) copy-start(bf16[256,8]{0,1:T(8,128)(2,1)} %param.34) | copy-start | bytes 12292
  7.2 94.6 %all-gather.5.cloned.1.call-start = ((), (), s32[]{:S(2)}) async-start(), calls=%async_computation.9 | async-start | bytes 2506752 | tf_op jit(solution)/shard_map/all_gather | solution.py:128
  9.0 16.1 %collective-permute-start = (bf16[128,384]{1,0:T(8,128)(2,1)S(1)}, bf16[128,384]{1,0:T(8,128)(2,1)S(1)}, u32[]{:S(2)}, u32[]{:S(2)}) collective-permute-start(bf16[128,384]{1,0:T(8,128)(2,1)S(1)} %pad_maximum_fusion.4), channel_id=1, source_target_pairs={{0,8},{8,0},{1,9},{9,1},{2,10},{10,2},{3,11},{11,3},{4,12},{12,4},... | collective-permute-start | bytes 294920 | tf_op jit(solution)/shard_map/ppermute | solution.py:137
  18.5 19.7 %collective-permute-start.3 = (bf16[16,256]{1,0:T(8,128)(2,1)S(1)}, bf16[16,256]{1,0:T(8,128)(2,1)S(1)}, u32[]{:S(2)}, u32[]{:S(2)}) collective-permute-start(bf16[16,256]{1,0:T(8,128)(2,1)S(1)} %pad_maximum_fusion.12), channel_id=1, source_target_pairs={{0,16},{16,0},{1,17},{17,1},{2,18},{18,2},{3,19},{19,3},{4,20},{20... | collective-permute-start | bytes 24584 | tf_op jit(solution)/shard_map/ppermute | solution.py:126
  23.2 42.2 %copy-start.31 = (s32[256]{0:T(256)}, s32[256]{0:T(256)S(1)}, u32[]{:S(2)}) copy-start(s32[256]{0:T(256)S(1)} %pad_add_fusion.3) | copy-start | bytes 3076
  23.8 41.2 %copy-start.34 = (s32[512]{0:T(512)}, s32[512]{0:T(512)S(1)}, u32[]{:S(2)}) copy-start(s32[512]{0:T(512)S(1)} %pad_add_fusion) | copy-start | bytes 6148
  25.1 15.1 %collective-permute-start.2 = (bf16[256,256]{1,0:T(8,128)(2,1)S(1)}, bf16[256,256]{1,0:T(8,128)(2,1)S(1)}, u32[]{:S(2)}, u32[]{:S(2)}) collective-permute-start(bf16[256,256]{1,0:T(8,128)(2,1)S(1)} %slice.355), channel_id=1, source_target_pairs={{0,448},{64,0},{128,64},{192,128},{256,192},{320,256},{384,320},{4... | collective-permute-start | bytes 393224 | tf_op jit(solution)/shard_map/ppermute | solution.py:172
  34.8 13.4 %all-to-all-start = ((bf16[4,256,128]{2,1,0:T(8,128)(2,1)}), bf16[4,256,128]{2,1,0:T(8,128)(2,1)S(1)}, u32[]{:S(2)}, u32[]{:S(2)}) async-start(bf16[4,256,128]{2,1,0:T(8,128)(2,1)} %broadcast_in_dim.64), calls=%async_computation | async-start | bytes 524288 | tf_op jit(solution)/shard_map/all_to_all | solution.py:27
  38.2 9.9 %collective-permute-start.1 = (bf16[256,256]{1,0:T(8,128)(2,1)S(1)}, bf16[256,256]{1,0:T(8,128)(2,1)S(1)}, u32[]{:S(2)}, u32[]{:S(2)}) collective-permute-start(bf16[256,256]{1,0:T(8,128)(2,1)S(1)} %slice.355), channel_id=1, source_target_pairs={{0,64},{64,128},{128,192},{192,256},{256,320},{320,384},{384,448},... | collective-permute-start | bytes 393224 | tf_op jit(solution)/shard_map/ppermute | solution.py:168
  48.1 18.7 %collective-permute-start.4 = (bf16[256,256]{1,0:T(8,128)(2,1)S(1)}, bf16[256,256]{1,0:T(8,128)(2,1)S(1)}, u32[]{:S(2)}, u32[]{:S(2)}) collective-permute-start(bf16[256,256]{1,0:T(8,128)(2,1)S(1)} %collective-permute-done.1), channel_id=1, source_target_pairs={{0,64},{64,128},{128,192},{192,256},{256,320},{320,384},{384,448},... | collective-permute-start | bytes 393224 | tf_op jit(solution)/shard_map/ppermute | solution.py:168
  50.1 16.7 %collective-permute-start.5 = (bf16[256,256]{1,0:T(8,128)(2,1)S(1)}, bf16[256,256]{1,0:T(8,128)(2,1)S(1)}, u32[]{:S(2)}, u32[]{:S(2)}) collective-permute-start(bf16[256,256]{1,0:T(8,128)(2,1)S(1)} %collective-permute-done.2), channel_id=1, source_target_pairs={{0,448},{64,0},{128,64},{192,128},{256,192},{320,256},{384,320},{4... | collective-permute-start | bytes 393224 | tf_op jit(solution)/shard_map/ppermute | solution.py:172
  56.3 19.7 %all-to-all-start.1 = ((bf16[16,32,256]{2,1,0:T(8,128)(2,1)}), bf16[16,32,256]{2,1,0:T(8,128)(2,1)S(1)}, u32[]{:S(2)}, u32[]{:S(2)}) async-start(bf16[16,32,256]{2,1,0:T(8,128)(2,1)} %broadcast_in_dim.68), calls=%async_computation.1 | async-start | bytes 524288 | tf_op jit(solution)/shard_map/all_to_all | solution.py:27
  76.0 16.9 %copy-start.6 = (bf16[16,32,256]{2,1,0:T(8,128)(2,1)}, bf16[16,32,256]{2,1,0:T(8,128)(2,1)S(1)}, u32[]{:S(2)}) copy-start(bf16[16,32,256]{2,1,0:T(8,128)(2,1)S(1)} %all-to-all-done.1) | copy-start | bytes 786436
  76.0 14.8 %copy-start.41 = (f32[1024,512]{0,1:T(8,128)S(1)}, f32[1024,512]{0,1:T(8,128)}, u32[]{:S(2)}) copy-start(f32[1024,512]{0,1:T(8,128)} %get-tuple-element.133) | copy-start | bytes 6291460
  76.0 11.7 %collective-permute-start.6 = (bf16[256,256]{1,0:T(8,128)(2,1)S(1)}, bf16[256,256]{1,0:T(8,128)(2,1)S(1)}, u32[]{:S(2)}, u32[]{:S(2)}) collective-permute-start(bf16[256,256]{1,0:T(8,128)(2,1)S(1)} %collective-permute-done.4), channel_id=1, source_target_pairs={{0,64},{64,128},{128,192},{192,256},{256,320},{320,384},{384,448},... | collective-permute-start | bytes 393224 | tf_op jit(solution)/shard_map/ppermute | solution.py:168
  82.3 8.0 %collective-permute-start.7 = (bf16[256,256]{1,0:T(8,128)(2,1)S(1)}, bf16[256,256]{1,0:T(8,128)(2,1)S(1)}, u32[]{:S(2)}, u32[]{:S(2)}) collective-permute-start(bf16[256,256]{1,0:T(8,128)(2,1)S(1)} %collective-permute-done.5), channel_id=1, source_target_pairs={{0,448},{64,0},{128,64},{192,128},{256,192},{320,256},{384,320},{4... | collective-permute-start | bytes 393224 | tf_op jit(solution)/shard_map/ppermute | solution.py:172
  87.8 8.7 %collective-permute-start.8 = (bf16[256,256]{1,0:T(8,128)(2,1)S(1)}, bf16[256,256]{1,0:T(8,128)(2,1)S(1)}, u32[]{:S(2)}, u32[]{:S(2)}) collective-permute-start(bf16[256,256]{1,0:T(8,128)(2,1)S(1)} %collective-permute-done.6), channel_id=1, source_target_pairs={{0,64},{64,128},{128,192},{192,256},{256,320},{320,384},{384,448},... | collective-permute-start | bytes 393224 | tf_op jit(solution)/shard_map/ppermute | solution.py:168
  90.8 5.7 %copy-start.27 = (s32[256]{0:T(256)S(1)}, s32[256]{0:T(256)}, u32[]{:S(2)}) copy-start(s32[256]{0:T(256)} %pad_add_fusion.4) | copy-start | bytes 3076
  90.8 6.0 %copy-start.32 = (s32[256]{0:T(256)S(1)}, s32[256]{0:T(256)}, u32[]{:S(2)}) copy-start(s32[256]{0:T(256)} %copy-done.31) | copy-start | bytes 3076
  92.9 4.4 %copy-start.28 = (s32[512]{0:T(512)S(1)}, s32[512]{0:T(512)}, u32[]{:S(2)}) copy-start(s32[512]{0:T(512)} %pad_add_fusion.2) | copy-start | bytes 6148
  93.0 4.4 %copy-start.29 = (s32[512]{0:T(512)S(1)}, s32[512]{0:T(512)}, u32[]{:S(2)}) copy-start(s32[512]{0:T(512)} %pad_add_fusion.1) | copy-start | bytes 6148
  97.3 1.5 copy-start.35
  97.3 1.5 copy-start.42
  104.0 10.7 %all-to-all-start.2 = ((bf16[4,256,256]{1,2,0:T(8,128)(2,1)}), bf16[4,256,256]{1,2,0:T(8,128)(2,1)S(1)}, u32[]{:S(2)}, u32[]{:S(2)}) async-start(bf16[4,256,256]{1,2,0:T(8,128)(2,1)} %copy.99), calls=%async_computation.2 | async-start | bytes 1048576 | tf_op jit(solution)/shard_map/all_to_all | solution.py:27
  107.7 43.0 %all-gather.7.cloned.1.call-start = ((), (), s32[]{:S(2)}) async-start(), calls=%async_computation.10 | async-start | bytes 1310720 | tf_op jit(solution)/shard_map/all_gather | solution.py:187
  114.7 17.3 %copy-start.37 = (bf16[256,16]{0,1:T(8,128)(2,1)S(1)}, bf16[256,16]{0,1:T(8,128)(2,1)}, u32[]{:S(2)}) copy-start(bf16[256,16]{0,1:T(8,128)(2,1)} %param.26) | copy-start | bytes 24580
  114.9 13.2 %collective-permute-start.9 = (bf16[128,128]{0,1:T(8,128)(2,1)S(1)}, bf16[128,128]{0,1:T(8,128)(2,1)S(1)}, u32[]{:S(2)}, u32[]{:S(2)}) collective-permute-start(bf16[128,128]{0,1:T(8,128)(2,1)S(1)} %slice.378), channel_id=1, source_target_pairs={{0,8},{8,0},{1,9},{9,1},{2,10},{10,2},{3,11},{11,3},{4,12},{12,4},... | collective-permute-start | bytes 98312 | tf_op jit(solution)/shard_map/ppermute | solution.py:213
  128.1 0.6 copy-start.15
  129.8 13.2 %copy-start.38 = (s32[128]{0:T(128)S(1)}, s32[128]{0:T(128)}, u32[]{:S(2)}) copy-start(s32[128]{0:T(128)} %param.23) | copy-start | bytes 1540
  129.8 20.2 %copy-start.1 = (bf16[2176,512]{1,0:T(8,128)(2,1)S(1)}, bf16[2176,512]{1,0:T(8,128)(2,1)}, u32[]{:S(2)}) copy-start(bf16[2176,512]{1,0:T(8,128)(2,1)} %all-gather.5.cloned.1.call-done) | copy-start | bytes 6684676
  132.1 23.7 %copy-start.4 = (bf16[256,512]{1,0:T(8,128)(2,1)S(1)}, bf16[256,512]{1,0:T(8,128)(2,1)}, u32[]{:S(2)}) copy-start(bf16[256,512]{1,0:T(8,128)(2,1)} %param.29) | copy-start | bytes 786436
  134.9 15.8 %all-to-all-start.3 = ((bf16[8,272,128]{2,1,0:T(8,128)(2,1)}), bf16[8,272,128]{2,1,0:T(8,128)(2,1)}, u32[]{:S(2)}, u32[]{:S(2)}) async-start(bf16[8,272,128]{2,1,0:T(8,128)(2,1)} %pad_maximum_fusion), calls=%async_computation.3 | async-start | bytes 1114112 | tf_op jit(solution)/shard_map/all_to_all | solution.py:27
  139.5 46.4 %collective-permute-start.10 = (bf16[128,512]{1,0:T(8,128)(2,1)}, bf16[128,512]{1,0:T(8,128)(2,1)}, u32[]{:S(2)}, u32[]{:S(2)}) collective-permute-start(bf16[128,512]{1,0:T(8,128)(2,1)} %param.39), channel_id=1, source_target_pairs={{0,1},{1,0},{2,3},{3,2},{4,5},{5,4},{6,7},{7,6},{8,9},{9,8},{10,11... | collective-permute-start | bytes 393224 | tf_op jit(solution)/shard_map/ppermute | solution.py:129
  151.9 0.7 copy-start.7
  157.7 9.5 %all-to-all-start.4 = ((bf16[8,16,512]{2,1,0:T(8,128)(2,1)}), bf16[8,16,512]{2,1,0:T(8,128)(2,1)S(1)}, u32[]{:S(2)}, u32[]{:S(2)}) async-start(bf16[8,16,512]{2,1,0:T(8,128)(2,1)} %bitcast.149), calls=%async_computation.4 | async-start | bytes 262144 | tf_op jit(solution)/shard_map/all_to_all | solution.py:27
  163.1 14.4 %collective-permute-start.11 = (bf16[4,512,256]{2,1,0:T(8,128)(2,1)}, bf16[4,512,256]{2,1,0:T(8,128)(2,1)}, u32[]{:S(2)}, u32[]{:S(2)}) collective-permute-start(bf16[4,512,256]{2,1,0:T(8,128)(2,1)} %bitcast.141), channel_id=1, source_target_pairs={{0,8},{8,0},{1,9},{9,1},{2,10},{10,2},{3,11},{11,3},{4,12},{12,4},... | collective-permute-start | bytes 3145736 | tf_op jit(solution)/shard_map/ppermute | solution.py:236
  169.3 0.7 copy-start.2
  171.6 0.6 copy-start.9
  173.9 10.6 %collective-permute-start.12 = (bf16[128,640]{1,0:T(8,128)(2,1)}, bf16[128,640]{1,0:T(8,128)(2,1)}, u32[]{:S(2)}, u32[]{:S(2)}) collective-permute-start(bf16[128,640]{1,0:T(8,128)(2,1)} %pad_maximum_fusion.3), channel_id=1, source_target_pairs={{0,1},{1,0},{2,3},{3,2},{4,5},{5,4},{6,7},{7,6},{8,9},{9,8},{10,11... | collective-permute-start | bytes 491528 | tf_op jit(solution)/shard_map/ppermute | solution.py:261
  179.5 0.7 copy-start.19
  179.6 0.7 copy-start.20
  179.6 0.7 copy-start.21
  179.6 0.7 copy-start.22
  179.6 0.7 copy-start.30
  179.8 4.7 %copy-start.3 = (bf16[128,512]{1,0:T(8,128)(2,1)S(1)}, bf16[128,512]{1,0:T(8,128)(2,1)}, u32[]{:S(2)}) copy-start(bf16[128,512]{1,0:T(8,128)(2,1)} %copy-done.2) | copy-start | bytes 393220
  179.8 4.7 %copy-start.8 = (bf16[128,16]{1,0:T(8,128)(2,1)S(1)}, bf16[128,16]{1,0:T(8,128)(2,1)}, u32[]{:S(2)}) copy-start(bf16[128,16]{1,0:T(8,128)(2,1)} %copy.105) | copy-start | bytes 12292
  179.8 4.7 %copy-start.10 = (bf16[128,112]{1,0:T(8,128)(2,1)S(1)}, bf16[128,112]{1,0:T(8,128)(2,1)}, u32[]{:S(2)}) copy-start(bf16[128,112]{1,0:T(8,128)(2,1)} %copy-done.9) | copy-start | bytes 86020
  180.3 5.7 %copy-start.17 = (bf16[128,512]{1,0:T(8,128)(2,1)S(1)}, bf16[128,512]{1,0:T(8,128)(2,1)}, u32[]{:S(2)}) copy-start(bf16[128,512]{1,0:T(8,128)(2,1)} %param.39) | copy-start | bytes 393220
  187.5 8.0 %copy-start.11 = (f32[128,16]{1,0:T(8,128)S(1)}, f32[128,16]{1,0:T(8,128)}, u32[]{:S(2)}) copy-start(f32[128,16]{1,0:T(8,128)} %copy.106) | copy-start | bytes 24580
  187.5 8.1 %copy-start.18 = (bf16[512,16]{0,1:T(8,128)(2,1)S(1)}, bf16[512,16]{0,1:T(8,128)(2,1)}, u32[]{:S(2)}) copy-start(bf16[512,16]{0,1:T(8,128)(2,1)} %param.36) | copy-start | bytes 49156
  187.5 8.1 %copy-start.23 = (f32[512]{0:T(512)S(1)}, f32[512]{0:T(512)}, u32[]{:S(2)}) copy-start(f32[512]{0:T(512)} %param.33) | copy-start | bytes 6148
  188.2 7.8 %copy-start.12 = (f32[128,16]{1,0:T(8,128)S(1)}, f32[128,16]{1,0:T(8,128)}, u32[]{:S(2)}) copy-start(f32[128,16]{1,0:T(8,128)} %copy.107) | copy-start | bytes 24580
  188.2 7.8 %copy-start.33 = (s32[128]{0:T(128)S(1)}, s32[128]{0:T(128)}, u32[]{:S(2)}) copy-start(s32[128]{0:T(128)} %eq.44) | copy-start | bytes 1540
  189.3 7.1 %copy-start.36 = (bf16[48]{0:T(256)(128)(2,1)S(1)}, bf16[48]{0:T(256)(128)(2,1)}, u32[]{:S(2)}) copy-start(bf16[48]{0:T(256)(128)(2,1)} %pad.26.clone) | copy-start | bytes 292
  189.4 6.1 %collective-permute-start.13 = (bf16[128,640]{1,0:T(8,128)(2,1)S(1)}, bf16[128,640]{1,0:T(8,128)(2,1)S(1)}, u32[]{:S(2)}, u32[]{:S(2)}) collective-permute-start(bf16[128,640]{1,0:T(8,128)(2,1)S(1)} %slice.470), channel_id=1, source_target_pairs={{0,1},{1,0},{2,3},{3,2},{4,5},{5,4},{6,7},{7,6},{8,9},{9,8},{10,11... | collective-permute-start | bytes 491528 | tf_op jit(solution)/shard_map/ppermute | solution.py:266
  197.4 13.1 %all-to-all-start.5 = ((bf16[8,64,512]{2,1,0:T(8,128)(2,1)}), bf16[8,64,512]{2,1,0:T(8,128)(2,1)}, u32[]{:S(2)}, u32[]{:S(2)}) async-start(bf16[8,64,512]{2,1,0:T(8,128)(2,1)} %fusion.65), calls=%async_computation.5 | async-start | bytes 1048576 | tf_op jit(solution)/shard_map/all_to_all | solution.py:27
  205.5 8.5 %copy-start.39 = (s32[128]{0:T(128)S(1)}, s32[128]{0:T(128)}, u32[]{:S(2)}) copy-start(s32[128]{0:T(128)} %param.23) | copy-start | bytes 1540
  205.5 9.5 %copy-start.14 = (bf16[128,128]{0,1:T(8,128)(2,1)S(1)}, bf16[128,128]{0,1:T(8,128)(2,1)}, u32[]{:S(2)}) copy-start(bf16[128,128]{0,1:T(8,128)(2,1)} %copy-done.13) | copy-start | bytes 98308
  205.5 9.5 %copy-start.16 = (bf16[128,128]{0,1:T(8,128)(2,1)S(1)}, bf16[128,128]{0,1:T(8,128)(2,1)}, u32[]{:S(2)}) copy-start(bf16[128,128]{0,1:T(8,128)(2,1)} %copy-done.15) | copy-start | bytes 98308
  205.5 9.5 %copy-start.40 = (f32[128,16]{0,1:T(8,128)S(1)}, f32[128,16]{0,1:T(8,128)}, u32[]{:S(2)}) copy-start(f32[128,16]{0,1:T(8,128)} %get-tuple-element.138) | copy-start | bytes 24580
  205.5 9.6 %copy-start.5 = (bf16[256,512]{1,0:T(8,128)(2,1)S(1)}, bf16[256,512]{1,0:T(8,128)(2,1)}, u32[]{:S(2)}) copy-start(bf16[256,512]{1,0:T(8,128)(2,1)} %param.29) | copy-start | bytes 786436
  205.5 9.6 %copy-start.24 = (bf16[128,16]{0,1:T(8,128)(2,1)S(1)}, bf16[128,16]{0,1:T(8,128)(2,1)}, u32[]{:S(2)}) copy-start(bf16[128,16]{0,1:T(8,128)(2,1)} %get-tuple-element.137) | copy-start | bytes 12292
  (1 other events, 0.6 us)
Sparse Core Ops, SparseCore 0:
  23.0 63.7 all-gather.4
  110.6 33.8 all-gather.6

commit v4 on v3

--- a/solution.py
+++ b/solution.py
@@ -123,7 +123,6 @@
     share = hidden_in.shape[1]
 
     hidden = jnp.concatenate([hidden_in.T, hidden_out.T], axis=0)
-    hidden = in_pair_order(hidden, lax.ppermute(hidden, FAR, SWAP), far, 0)
     weights = jnp.concatenate([local_weight, fold(global_up), fold(local_up)], axis=0)
     weights = lax.all_gather(weights, ROW, axis=0, tiled=False)
     cotangents = jnp.concatenate([cotangent, lax.ppermute(cotangent, SIDE, SWAP)], axis=0)
@@ -176,15 +175,15 @@
             rising, falling, hidden, queries = lax.optimization_barrier(
                 (rising, falling, hidden, queries)
             )
-            hidden = to_everyone(hidden, (Z, NEAR)).reshape(-1, units)
+            hidden = to_everyone(hidden, (FAR, LINE, CORE)).reshape(-1, units)
         elif step == 2:
             rising, falling, hidden = lax.optimization_barrier((rising, falling, hidden))
         if step >= 2:
             state = visit(state, held[step - 2], at[step - 2])
     state = visit(state, held[-2], at[-2])
-    state = visit(state, held[-1], at[-1])
-    state, weights, hidden = lax.optimization_barrier((state, weights, hidden))
-    riders = lax.all_gather(hidden, LINE, axis=0, tiled=False)
+    now, weights, hidden = lax.optimization_barrier((held[-1], weights, hidden))
+    state = visit(state, now, at[-1])
+    riders = lax.all_gather(hidden, (Z, NEAR), axis=0, tiled=True)
 
     local_whole = weights[:, :width].reshape(-1, columns)
     up_whole = unfold(weights[:, width : width + 8])
@@ -218,7 +217,6 @@
     low_part = contract(global_down, attended, 0, 1).astype(BF)
     low_part = jnp.broadcast_to(low_part[None], (row_count, RANK, rows))
     arrived = exchange(jnp.concatenate([part, low_part], axis=1), ROW)
-    arrived, riders = lax.optimization_barrier((arrived, riders))
     arrived = arrived.astype(F32).sum(axis=0)
 
     reduced = jnp.transpose(arrived[width:])
@@ -233,10 +231,8 @@
     projected = exchange(projected.reshape(row_count, own_patches, columns), ROW)
     projected = total(projected).astype(BF)
 
-    rest = lax.ppermute(riders, CORE, SWAP)
-    split = (line, columns // (2 * share), 2, 1, share, units)
-    riders = in_pair_order(riders.reshape(split), rest.reshape(split), core, 3)
-    riders = jnp.moveaxis(riders, 2, 0).reshape(2, line, columns, units)
+    riders = riders.reshape(columns // (2 * share), line, 2, 2, share, units)
+    riders = jnp.transpose(riders, (3, 1, 0, 2, 4, 5)).reshape(2, line, columns, units)
     rows_in, rows_out = (
         jnp.concatenate([riders[way, k] for k in range(line)], axis=1) for way in range(2)
     )
@@ -313,9 +309,9 @@
     ).astype(BF)
     shape = packed.shape
     pieces = packed.reshape(lax.axis_size(EIGHT), -1, shape[1])
-    pieces = exchange(pieces, EIGHT).astype(F32).sum(axis=0)
-    pieces = to_everyone(pieces, Z).sum(axis=0)
-    packed = to_everyone(pieces, EIGHT).reshape(shape)
+    pieces = total(exchange(pieces, EIGHT)).astype(BF)
+    pieces = total(to_everyone(pieces, Z)).astype(BF)
+    packed = to_everyone(pieces, EIGHT).reshape(shape).astype(F32)
     return (
         jnp.transpose(packed[:16]),
         packed[16:32],

time: 276 us -> 273 us (0.989)
  starting transfers between devices: 94.4 us -> 80.4 us
  local copies, waits for them, and re-layouts: 25.6 us -> 34 us
  waiting for transfers between devices: 39 us -> 33.2 us
  matrix products: 28 us -> 32.4 us
  blocking collectives: 48.2 us -> 52.5 us
    ppermute x1, starting transfers between devices: 12.3 us -> 4.09 us  [body(): partner = lax.ppermute(merged[rows:], CORE, SWAP)]
    ppermute x2 -> x0, starting transfers between devices: 5.28 us -> none  [the longest x1 3.37 us: body(): rest = lax.ppermute(riders, CORE, SWAP)]
    ppermute x4, waiting for transfers between devices: 12.7 us -> 8.04 us  [body(): rising = lax.ppermute(rising, Z, up)]
    all_to_all x3, blocking collectives: 48.2 us -> 52.5 us  [exchange(): return lax.all_to_all(pieces, axis, split_axis=0, concat_axis=0, tiled=True)]
    ppermute x3, starting transfers between devices: 18.5 us -> 14.3 us  [body(): falling = lax.ppermute(falling, Z, down)]
    dot_general x17, matrix products: 17.2 us -> 21.3 us  [contract(): lax.dot_general(left, right, (((left_dim,), (right_dim,)), ((), ())), pre...]
    all_to_all x6, waiting for transfers between devices: 21.1 us -> 17.1 us  [exchange(): return lax.all_to_all(pieces, axis, split_axis=0, concat_axis=0, tiled=True)]
    ppermute x3, waiting for transfers between devices: 0.01 us -> 3.81 us  [body(): falling = lax.ppermute(falling, Z, down)]
  transfers between devices with their start and end apart: 22 -> 20, of which waited for: 9 -> 11; matrix products, arithmetic and copies ran while one was open for 21% -> 22% of each run, Pallas kernels for 0% -> 0%
where the time goes in v4:
time: 273 us; the launch traced here: 270 us
  starting transfers between devices  80.4 us (29%)
  blocking collectives  52.5 us (19%)
  local copies, waits for them, and re-layouts  34 us (12%)
  waiting for transfers between devices  33.2 us (12%)
  matrix products  32.4 us (12%)
  other arithmetic  22.4 us (8%)
  between operations  15.4 us (6%)
    all_to_all x3, blocking collectives, exchange(): return lax.all_to_all(pieces, axis, split_axis=0, concat_axis=0, tiled=True)  52.5 us
    all_to_all x6, starting transfers between devices, exchange(): return lax.all_to_all(pieces, axis, split_axis=0, concat_axis=0, tiled=True)  30.6 us
    dot_general x17, matrix products, contract(): lax.dot_general(left, right, (((left_dim,), (right_dim,)), ((), ())), pre...  21.3 us
    all_to_all x6, waiting for transfers between devices, exchange(): return lax.all_to_all(pieces, axis, split_axis=0, concat_axis=0, tiled=True)  17.1 us
    ppermute x3, starting transfers between devices, body(): falling = lax.ppermute(falling, Z, down)  14.3 us
    ppermute x4, starting transfers between devices, body(): rising = lax.ppermute(rising, Z, up)  13.4 us
    ppermute x1, starting transfers between devices, body(): both = jnp.concatenate([mine, lax.ppermute(other, CORE, SWAP)], axis=0)  8.79 us
    ppermute x4, waiting for transfers between devices, body(): rising = lax.ppermute(rising, Z, up)  8.04 us
  transfers between devices with their start and end apart: 20, of which 11 were waited for; matrix products, arithmetic and copies ran while one was open for 22% of the time, Pallas kernels for 0%

profile of v4, /device:TPU:1, one launch (start us, length us, event | category | flops | bytes accessed | tf_op | source)
XLA Modules:
  0.0 270.3 jit_solution(3023507984047065412)
XLA Ops:
  7.3 0.9 constant_dynamic-slice_fusion.5
  9.0 8.8 %collective-permute-start = (bf16[128,384]{1,0:T(8,128)(2,1)S(1)}, bf16[128,384]{1,0:T(8,128)(2,1)S(1)}, u32[]{:S(2)}, u32[]{:S(2)}) collective-permute-start(bf16[128,384]{1,0:T(8,128)(2,1)S(1)} %pad_maximum_fusion.4), channel_id=1, source_target_pairs={{0,8},{8,0},{1,9},{9,1},{2,10},{10,2},{3,11},{11,3},{4,12},{12,4},... | collective-permute-start | bytes 294920 | tf_op jit(solution)/shard_map/ppermute | solution.py:136
  18.6 1.7 maximum_maximum_fusion.1
  23.3 3.4 %all-to-all-start = ((bf16[4,256,128]{2,1,0:T(8,128)(2,1)}), bf16[4,256,128]{2,1,0:T(8,128)(2,1)S(1)}, u32[]{:S(2)}, u32[]{:S(2)}) async-start(bf16[4,256,128]{2,1,0:T(8,128)(2,1)} %broadcast_in_dim.57), calls=%async_computation | async-start | bytes 524288 | tf_op jit(solution)/shard_map/all_to_all | solution.py:27
  26.7 1.9 collective-permute-start.1
  28.7 7.2 %collective-permute-start.2 = (bf16[256,256]{1,0:T(8,128)(2,1)S(1)}, bf16[256,256]{1,0:T(8,128)(2,1)S(1)}, u32[]{:S(2)}, u32[]{:S(2)}) collective-permute-start(bf16[256,256]{1,0:T(8,128)(2,1)S(1)} %slice.355), channel_id=1, source_target_pairs={{0,448},{64,0},{128,64},{192,128},{256,192},{320,256},{384,320},{4... | collective-permute-start | bytes 393224 | tf_op jit(solution)/shard_map/ppermute | solution.py:171
  35.9 2.9 %collective-permute-done.1 = bf16[256,256]{1,0:T(8,128)(2,1)S(1)} collective-permute-done((bf16[256,256]{1,0:T(8,128)(2,1)S(1)}, bf16[256,256]{1,0:T(8,128)(2,1)S(1)}, u32[]{:S(2)}, u32[]{:S(2)}) %collective-permute-start.1) | collective-permute-done | bytes 131104 | tf_op jit(solution)/shard_map/ppermute | solution.py:167
  41.1 8.9 %all-to-all-start.1 = ((bf16[16,16,256]{2,1,0:T(8,128)(2,1)}), bf16[16,16,256]{2,1,0:T(8,128)(2,1)S(1)}, u32[]{:S(2)}, u32[]{:S(2)}) async-start(bf16[16,16,256]{2,1,0:T(8,128)(2,1)} %broadcast_in_dim.63), calls=%async_computation.1 | async-start | bytes 262144 | tf_op jit(solution)/shard_map/all_to_all | solution.py:27
  50.1 5.5 %collective-permute-start.3 = (bf16[256,256]{1,0:T(8,128)(2,1)S(1)}, bf16[256,256]{1,0:T(8,128)(2,1)S(1)}, u32[]{:S(2)}, u32[]{:S(2)}) collective-permute-start(bf16[256,256]{1,0:T(8,128)(2,1)S(1)} %collective-permute-done.1), channel_id=1, source_target_pairs={{0,64},{64,128},{128,192},{192,256},{256,320},{320,384},{384,448},... | collective-permute-start | bytes 393224 | tf_op jit(solution)/shard_map/ppermute | solution.py:167
  55.6 3.5 %collective-permute-start.4 = (bf16[256,256]{1,0:T(8,128)(2,1)S(1)}, bf16[256,256]{1,0:T(8,128)(2,1)S(1)}, u32[]{:S(2)}, u32[]{:S(2)}) collective-permute-start(bf16[256,256]{1,0:T(8,128)(2,1)S(1)} %collective-permute-done.2), channel_id=1, source_target_pairs={{0,448},{64,0},{128,64},{192,128},{256,192},{320,256},{384,320},{4... | collective-permute-start | bytes 393224 | tf_op jit(solution)/shard_map/ppermute | solution.py:171
  59.1 1.3 fusion.179
  60.4 1.8 fusion.1
  62.8 3.5 %collective-permute-done.4 = bf16[256,256]{1,0:T(8,128)(2,1)S(1)} collective-permute-done((bf16[256,256]{1,0:T(8,128)(2,1)S(1)}, bf16[256,256]{1,0:T(8,128)(2,1)S(1)}, u32[]{:S(2)}, u32[]{:S(2)}) %collective-permute-start.4) | collective-permute-done | bytes 131104 | tf_op jit(solution)/shard_map/ppermute | solution.py:171
  66.3 3.9 %collective-permute-start.5 = (bf16[256,256]{1,0:T(8,128)(2,1)S(1)}, bf16[256,256]{1,0:T(8,128)(2,1)S(1)}, u32[]{:S(2)}, u32[]{:S(2)}) collective-permute-start(bf16[256,256]{1,0:T(8,128)(2,1)S(1)} %collective-permute-done.3), channel_id=1, source_target_pairs={{0,64},{64,128},{128,192},{192,256},{256,320},{320,384},{384,448},... | collective-permute-start | bytes 393224 | tf_op jit(solution)/shard_map/ppermute | solution.py:167
  70.2 3.6 %collective-permute-start.6 = (bf16[256,256]{1,0:T(8,128)(2,1)S(1)}, bf16[256,256]{1,0:T(8,128)(2,1)S(1)}, u32[]{:S(2)}, u32[]{:S(2)}) collective-permute-start(bf16[256,256]{1,0:T(8,128)(2,1)S(1)} %collective-permute-done.4), channel_id=1, source_target_pairs={{0,448},{64,0},{128,64},{192,128},{256,192},{320,256},{384,320},{4... | collective-permute-start | bytes 393224 | tf_op jit(solution)/shard_map/ppermute | solution.py:171
  75.0 2.0 collective-permute-done.5
  77.0 2.0 collective-permute-start.7
  80.8 4.4 %fusion.13 = (f32[1024]{0:T(1024)}, f32[1024]{0:T(1024)}, f32[1024]{0:T(1024)}, f32[1024,512]{0,1:T(8,128)}) fusion(f32[1024,512]{0,1:T(8,128)S(1)} %copy-done.52, f32[1024]{0:T(1024)S(1)} %get-tuple-element.111, s32[1024]{0:T(1024)S(1)} %constant_dynamic-update-slice_fusion.6, s32[512]{0:T(512)S(1)} %copy-done.46, s32[512]{0:T(512)} %pad_add_fusion.1, ...), kind=kOutput, calls=%fused_computation.33 | convolution fusion | flops 141816832 | bytes 6711296 | tf_op jit(solution)/shard_map/dot_general | solution.py:36
  85.1 3.2 %collective-permute-done.7 = bf16[256,256]{1,0:T(8,128)(2,1)} collective-permute-done((bf16[256,256]{1,0:T(8,128)(2,1)S(1)}, bf16[256,256]{1,0:T(8,128)(2,1)}, u32[]{:S(2)}, u32[]{:S(2)}) %collective-permute-start.7) | collective-permute-done | bytes 131104 | tf_op jit(solution)/shard_map/ppermute | solution.py:167
  88.3 1.2 fusion.178
  90.2 2.6 fusion.15
  93.6 1.2 fusion.12
  98.1 1.2 fusion.19
  100.2 5.6 %all-to-all-start.2 = ((bf16[4,256,256]{1,2,0:T(8,128)(2,1)}), bf16[4,256,256]{1,2,0:T(8,128)(2,1)S(1)}, u32[]{:S(2)}, u32[]{:S(2)}) async-start(bf16[4,256,256]{1,2,0:T(8,128)(2,1)} %bitcast.118), calls=%async_computation.2 | async-start | bytes 1048576 | tf_op jit(solution)/shard_map/all_to_all | solution.py:27
  106.5 7.5 %all-to-all-done.2 = bf16[4,256,256]{1,2,0:T(8,128)(2,1)S(1)} async-done(((bf16[4,256,256]{1,2,0:T(8,128)(2,1)}), bf16[4,256,256]{1,2,0:T(8,128)(2,1)S(1)}, u32[]{:S(2)}, u32[]{:S(2)}) %all-to-all-start.2) | async-done | bytes 524320 | tf_op jit(solution)/shard_map/all_to_all | solution.py:27
  114.3 4.1 %collective-permute-start.8 = (bf16[128,128]{0,1:T(8,128)(2,1)S(1)}, bf16[128,128]{0,1:T(8,128)(2,1)S(1)}, u32[]{:S(2)}, u32[]{:S(2)}) collective-permute-start(bf16[128,128]{0,1:T(8,128)(2,1)S(1)} %slice.376), channel_id=1, source_target_pairs={{0,8},{8,0},{1,9},{9,1},{2,10},{10,2},{3,11},{11,3},{4,12},{12,4},... | collective-permute-start | bytes 98312 | tf_op jit(solution)/shard_map/ppermute | solution.py:212
  119.9 1.1 fusion
  121.0 2.2 copy.111
  123.2 0.9 fusion.27
  124.2 1.9 pad_maximum_fusion
  126.1 4.2 %all-to-all-start.3 = ((bf16[8,272,128]{2,1,0:T(8,128)(2,1)}), bf16[8,272,128]{2,1,0:T(8,128)(2,1)}, u32[]{:S(2)}, u32[]{:S(2)}) async-start(bf16[8,272,128]{2,1,0:T(8,128)(2,1)} %pad_maximum_fusion), calls=%async_computation.3 | async-start | bytes 1114112 | tf_op jit(solution)/shard_map/all_to_all | solution.py:27
  130.3 3.2 %collective-permute-start.9 = (bf16[128,512]{1,0:T(8,128)(2,1)}, bf16[128,512]{1,0:T(8,128)(2,1)}, u32[]{:S(2)}, u32[]{:S(2)}) collective-permute-start(bf16[128,512]{1,0:T(8,128)(2,1)} %param.39), channel_id=1, source_target_pairs={{0,1},{1,0},{2,3},{3,2},{4,5},{5,4},{6,7},{7,6},{8,9},{9,8},{10,11... | collective-permute-start | bytes 393224 | tf_op jit(solution)/shard_map/ppermute | solution.py:128
  135.6 1.4 eq.80
  137.0 1.6 fusion.123
  138.6 1.4 copy.104
  141.2 1.3 dynamic_slice.28
  143.2 1.1 convert_reduce_fusion
  145.7 1.7 copy.116
  147.4 1.6 multiply_convert_fusion.4
  149.0 1.9 convolution_convert_fusion.3
  150.9 4.0 %all-to-all-start.4 = ((bf16[8,16,512]{2,1,0:T(8,128)(2,1)}), bf16[8,16,512]{2,1,0:T(8,128)(2,1)S(1)}, u32[]{:S(2)}, u32[]{:S(2)}) async-start(bf16[8,16,512]{2,1,0:T(8,128)(2,1)} %bitcast.136), calls=%async_computation.4 | async-start | bytes 262144 | tf_op jit(solution)/shard_map/all_to_all | solution.py:27
  156.3 4.1 %all-to-all-done.4 = bf16[8,16,512]{2,1,0:T(8,128)(2,1)S(1)} async-done(((bf16[8,16,512]{2,1,0:T(8,128)(2,1)}), bf16[8,16,512]{2,1,0:T(8,128)(2,1)S(1)}, u32[]{:S(2)}, u32[]{:S(2)}) %all-to-all-start.4) | async-done | bytes 131104 | tf_op jit(solution)/shard_map/all_to_all | solution.py:27
  160.5 1.3 multiply_reduce_fusion.1
  165.4 1.7 pad_maximum_fusion.3
  167.1 2.6 collective-permute-start.10
  170.4 1.1 all-gather.4.cloned.1.call-done
  171.5 1.8 copy.102
  174.1 4.1 %maximum_maximum_fusion = bf16[640,1024]{1,0:T(8,128)(2,1)S(1)} fusion(bf16[16,256]{1,0:T(8,128)(2,1)S(1)} %copy-done.31, bf16[16,256]{1,0:T(8,128)(2,1)S(1)} %copy-done.29, bf16[16,256]{1,0:T(8,128)(2,1)S(1)} %copy-done.30, bf16[16,256]{1,0:T(8,128)(2,1)S(1)} %copy-done.28, bf16[512,256]{1,0:T(8,128)(2,1)S(1)} %get-tuple-element.55, ...), kind=kLoop, calls=%fused_computation.20 | loop fusion | flops 11796480 | bytes 2393344 | tf_op jit(solution)/shard_map/concatenate | solution.py:240
  178.2 1.5 fusion.77
  179.7 1.5 fusion.6
  182.0 3.3 %collective-permute-start.11 = (bf16[128,640]{1,0:T(8,128)(2,1)S(1)}, bf16[128,640]{1,0:T(8,128)(2,1)S(1)}, u32[]{:S(2)}, u32[]{:S(2)}) collective-permute-start(bf16[128,640]{1,0:T(8,128)(2,1)S(1)} %slice.468), channel_id=1, source_target_pairs={{0,1},{1,0},{2,3},{3,2},{4,5},{5,4},{6,7},{7,6},{8,9},{9,8},{10,11... | collective-permute-start | bytes 491528 | tf_op jit(solution)/shard_map/ppermute | solution.py:262
  185.3 1.1 convolution_convert_fusion.2
  186.4 1.6 collective-permute-done.11
  190.1 4.5 %all-to-all-start.5 = ((bf16[8,64,512]{2,1,0:T(8,128)(2,1)}), bf16[8,64,512]{2,1,0:T(8,128)(2,1)}, u32[]{:S(2)}, u32[]{:S(2)}) async-start(bf16[8,64,512]{2,1,0:T(8,128)(2,1)} %fusion.67), calls=%async_computation.5 | async-start | bytes 1048576 | tf_op jit(solution)/shard_map/all_to_all | solution.py:27
  194.6 1.2 copy.106
  195.8 1.5 slice.338
  197.5 5.4 %all-to-all-done.5 = bf16[8,64,512]{2,1,0:T(8,128)(2,1)} async-done(((bf16[8,64,512]{2,1,0:T(8,128)(2,1)}), bf16[8,64,512]{2,1,0:T(8,128)(2,1)}, u32[]{:S(2)}, u32[]{:S(2)}) %all-to-all-start.5) | async-done | bytes 524320 | tf_op jit(solution)/shard_map/all_to_all | solution.py:27
  202.9 0.9 slice.395
  203.8 2.6 fusion.7
  206.4 0.9 convolution_convert_fusion.8
  207.9 1.1 convert_reduce_fusion.1
  209.1 23.6 %all_to_all.45 = bf16[8,12,256]{2,1,0:T(8,128)(2,1)S(1)} all-to-all(bf16[8,12,256]{2,1,0:T(8,128)(2,1)S(1)} %convert_element_type.185), channel_id=1, replica_groups=mesh['seq_0'=8,'near'=2,'seq_1'=2,'seq_2'=2,'row_0'=4,'row_1'=2] {'near'..., dimensions={0} | all-to-all | bytes 98304 | tf_op jit(solution)/shard_map/all_to_all | solution.py:27
  232.6 18.5 %all_to_all.46 = bf16[8,12,256]{2,1,0:T(8,128)(2,1)S(1)} all-to-all(bf16[8,12,256]{2,1,0:T(8,128)(2,1)S(1)} %broadcast_in_dim.74), channel_id=1, replica_groups=mesh['seq_0'=8,'near'=2,'seq_1'=2,'seq_2'=2,'row_0'=4,'row_1'=2] {'seq_0'}, dimensions={0} | all-to-all | bytes 98304 | tf_op jit(solution)/shard_map/all_to_all | solution.py:27
  251.2 10.5 %all_to_all.47 = bf16[8,12,256]{2,1,0:T(8,128)(2,1)S(1)} all-to-all(bf16[8,12,256]{2,1,0:T(8,128)(2,1)S(1)} %broadcast_in_dim.75), channel_id=1, replica_groups=mesh['seq_0'=8,'near'=2,'seq_1'=2,'seq_2'=2,'row_0'=4,'row_1'=2] {'near'..., dimensions={0} | all-to-all | bytes 98304 | tf_op jit(solution)/shard_map/all_to_all | solution.py:27
  (237 shorter events, 35.1 us)
Async XLA Ops:
  7.2 112.7 %copy-start = (bf16[256,2048]{1,0:T(8,128)(2,1)S(1)}, bf16[256,2048]{1,0:T(8,128)(2,1)}, u32[]{:S(2)}) copy-start(bf16[256,2048]{1,0:T(8,128)(2,1)} %param.25) | copy-start | bytes 3145732
  7.2 21.5 %copy-start.43 = (bf16[256,8]{0,1:T(8,128)(2,1)S(1)}, bf16[256,8]{0,1:T(8,128)(2,1)}, u32[]{:S(2)}) copy-start(bf16[256,8]{0,1:T(8,128)(2,1)} %param.34) | copy-start | bytes 12292
  7.2 21.5 %copy-start.42 = (bf16[256,8]{0,1:T(8,128)(2,1)S(1)}, bf16[256,8]{0,1:T(8,128)(2,1)}, u32[]{:S(2)}) copy-start(bf16[256,8]{0,1:T(8,128)(2,1)} %param.35) | copy-start | bytes 12292
  7.2 81.1 %all-gather.6.cloned.1.call-start = ((), (), s32[]{:S(2)}) async-start(), calls=%async_computation.10 | async-start | bytes 2506752 | tf_op jit(solution)/shard_map/all_gather | solution.py:127
  9.0 13.4 %collective-permute-start = (bf16[128,384]{1,0:T(8,128)(2,1)S(1)}, bf16[128,384]{1,0:T(8,128)(2,1)S(1)}, u32[]{:S(2)}, u32[]{:S(2)}) collective-permute-start(bf16[128,384]{1,0:T(8,128)(2,1)S(1)} %pad_maximum_fusion.4), channel_id=1, source_target_pairs={{0,8},{8,0},{1,9},{9,1},{2,10},{10,2},{3,11},{11,3},{4,12},{12,4},... | collective-permute-start | bytes 294920 | tf_op jit(solution)/shard_map/ppermute | solution.py:136
  20.6 41.6 %copy-start.38 = (s32[256]{0:T(256)}, s32[256]{0:T(256)S(1)}, u32[]{:S(2)}) copy-start(s32[256]{0:T(256)S(1)} %pad_add_fusion.3) | copy-start | bytes 3076
  21.2 41.0 %copy-start.45 = (s32[512]{0:T(512)}, s32[512]{0:T(512)S(1)}, u32[]{:S(2)}) copy-start(s32[512]{0:T(512)S(1)} %pad_add_fusion) | copy-start | bytes 6148
  22.4 39.7 %copy-start.8 = (bf16[256,384]{1,0:T(8,128)(2,1)}, bf16[256,384]{1,0:T(8,128)(2,1)S(1)}, u32[]{:S(2)}) copy-start(bf16[256,384]{1,0:T(8,128)(2,1)S(1)} %pad_maximum_fusion.2) | copy-start | bytes 589828
  23.3 17.2 %all-to-all-start = ((bf16[4,256,128]{2,1,0:T(8,128)(2,1)}), bf16[4,256,128]{2,1,0:T(8,128)(2,1)S(1)}, u32[]{:S(2)}, u32[]{:S(2)}) async-start(bf16[4,256,128]{2,1,0:T(8,128)(2,1)} %broadcast_in_dim.57), calls=%async_computation | async-start | bytes 524288 | tf_op jit(solution)/shard_map/all_to_all | solution.py:27
  26.7 12.1 %collective-permute-start.1 = (bf16[256,256]{1,0:T(8,128)(2,1)S(1)}, bf16[256,256]{1,0:T(8,128)(2,1)S(1)}, u32[]{:S(2)}, u32[]{:S(2)}) collective-permute-start(bf16[256,256]{1,0:T(8,128)(2,1)S(1)} %slice.355), channel_id=1, source_target_pairs={{0,64},{64,128},{128,192},{192,256},{256,320},{320,384},{384,448},... | collective-permute-start | bytes 393224 | tf_op jit(solution)/shard_map/ppermute | solution.py:167
  28.7 11.1 %collective-permute-start.2 = (bf16[256,256]{1,0:T(8,128)(2,1)S(1)}, bf16[256,256]{1,0:T(8,128)(2,1)S(1)}, u32[]{:S(2)}, u32[]{:S(2)}) collective-permute-start(bf16[256,256]{1,0:T(8,128)(2,1)S(1)} %slice.355), channel_id=1, source_target_pairs={{0,448},{64,0},{128,64},{192,128},{256,192},{320,256},{384,320},{4... | collective-permute-start | bytes 393224 | tf_op jit(solution)/shard_map/ppermute | solution.py:171
  41.1 21.7 %all-to-all-start.1 = ((bf16[16,16,256]{2,1,0:T(8,128)(2,1)}), bf16[16,16,256]{2,1,0:T(8,128)(2,1)S(1)}, u32[]{:S(2)}, u32[]{:S(2)}) async-start(bf16[16,16,256]{2,1,0:T(8,128)(2,1)} %broadcast_in_dim.63), calls=%async_computation.1 | async-start | bytes 262144 | tf_op jit(solution)/shard_map/all_to_all | solution.py:27
  50.1 12.7 %collective-permute-start.3 = (bf16[256,256]{1,0:T(8,128)(2,1)S(1)}, bf16[256,256]{1,0:T(8,128)(2,1)S(1)}, u32[]{:S(2)}, u32[]{:S(2)}) collective-permute-start(bf16[256,256]{1,0:T(8,128)(2,1)S(1)} %collective-permute-done.1), channel_id=1, source_target_pairs={{0,64},{64,128},{128,192},{192,256},{256,320},{320,384},{384,448},... | collective-permute-start | bytes 393224 | tf_op jit(solution)/shard_map/ppermute | solution.py:167
  55.6 10.7 %collective-permute-start.4 = (bf16[256,256]{1,0:T(8,128)(2,1)S(1)}, bf16[256,256]{1,0:T(8,128)(2,1)S(1)}, u32[]{:S(2)}, u32[]{:S(2)}) collective-permute-start(bf16[256,256]{1,0:T(8,128)(2,1)S(1)} %collective-permute-done.2), channel_id=1, source_target_pairs={{0,448},{64,0},{128,64},{192,128},{256,192},{320,256},{384,320},{4... | collective-permute-start | bytes 393224 | tf_op jit(solution)/shard_map/ppermute | solution.py:171
  62.8 22.3 %copy-start.10 = (bf16[16,16,256]{2,1,0:T(8,128)(2,1)}, bf16[16,16,256]{2,1,0:T(8,128)(2,1)S(1)}, u32[]{:S(2)}) copy-start(bf16[16,16,256]{2,1,0:T(8,128)(2,1)S(1)} %all-to-all-done.1) | copy-start | bytes 393220
  66.2 14.5 %copy-start.46 = (s32[512]{0:T(512)S(1)}, s32[512]{0:T(512)}, u32[]{:S(2)}) copy-start(s32[512]{0:T(512)} %copy-done.45) | copy-start | bytes 6148
  66.3 14.5 %copy-start.52 = (f32[1024,512]{0,1:T(8,128)S(1)}, f32[1024,512]{0,1:T(8,128)}, u32[]{:S(2)}) copy-start(f32[1024,512]{0,1:T(8,128)} %get-tuple-element.118) | copy-start | bytes 6291460
  66.3 10.7 %collective-permute-start.5 = (bf16[256,256]{1,0:T(8,128)(2,1)S(1)}, bf16[256,256]{1,0:T(8,128)(2,1)S(1)}, u32[]{:S(2)}, u32[]{:S(2)}) collective-permute-start(bf16[256,256]{1,0:T(8,128)(2,1)S(1)} %collective-permute-done.3), channel_id=1, source_target_pairs={{0,64},{64,128},{128,192},{192,256},{256,320},{320,384},{384,448},... | collective-permute-start | bytes 393224 | tf_op jit(solution)/shard_map/ppermute | solution.py:167
  70.2 9.5 %collective-permute-start.6 = (bf16[256,256]{1,0:T(8,128)(2,1)S(1)}, bf16[256,256]{1,0:T(8,128)(2,1)S(1)}, u32[]{:S(2)}, u32[]{:S(2)}) collective-permute-start(bf16[256,256]{1,0:T(8,128)(2,1)S(1)} %collective-permute-done.4), channel_id=1, source_target_pairs={{0,448},{64,0},{128,64},{192,128},{256,192},{320,256},{384,320},{4... | collective-permute-start | bytes 393224 | tf_op jit(solution)/shard_map/ppermute | solution.py:171
  77.0 11.3 %collective-permute-start.7 = (bf16[256,256]{1,0:T(8,128)(2,1)S(1)}, bf16[256,256]{1,0:T(8,128)(2,1)}, u32[]{:S(2)}, u32[]{:S(2)}) collective-permute-start(bf16[256,256]{1,0:T(8,128)(2,1)S(1)} %collective-permute-done.5), channel_id=1, source_target_pairs={{0,64},{64,128},{128,192},{192,256},{256,320},{320,384},{384,448},... | collective-permute-start | bytes 393224 | tf_op jit(solution)/shard_map/ppermute | solution.py:167
  90.2 2.7 %copy-start.7 = (f32[1024,256]{0,1:T(8,128)S(1)}, f32[1024,256]{0,1:T(8,128)}, u32[]{:S(2)}) copy-start(f32[1024,256]{0,1:T(8,128)} %get-tuple-element.116) | copy-start | bytes 3145732
  90.2 2.7 %copy-start.37 = (s32[256]{0:T(256)S(1)}, s32[256]{0:T(256)}, u32[]{:S(2)}) copy-start(s32[256]{0:T(256)} %pad_add_fusion.4) | copy-start | bytes 3076
  90.2 2.7 %copy-start.39 = (s32[256]{0:T(256)S(1)}, s32[256]{0:T(256)}, u32[]{:S(2)}) copy-start(s32[256]{0:T(256)} %copy-done.38) | copy-start | bytes 3076
  92.8 0.7 copy-start.40
  92.8 2.0 copy-start.21
  92.9 2.0 copy-start.22
  92.9 2.0 copy-start.47
  92.9 2.0 copy-start.53
  94.9 1.6 copy-start.6
  94.9 1.6 copy-start.23
  94.9 1.6 copy-start.24
  94.9 1.6 copy-start.35
  96.5 0.8 copy-start.25
  96.5 0.9 copy-start.26
  96.5 0.9 copy-start.34
  100.2 13.8 %all-to-all-start.2 = ((bf16[4,256,256]{1,2,0:T(8,128)(2,1)}), bf16[4,256,256]{1,2,0:T(8,128)(2,1)S(1)}, u32[]{:S(2)}, u32[]{:S(2)}) async-start(bf16[4,256,256]{1,2,0:T(8,128)(2,1)} %bitcast.118), calls=%async_computation.2 | async-start | bytes 1048576 | tf_op jit(solution)/shard_map/all_to_all | solution.py:27
  105.8 65.7 %all-gather.4.cloned.1.call-start = ((), (), s32[]{:S(2)}) async-start(), calls=%async_computation.9 | async-start | bytes 2228224 | tf_op jit(solution)/shard_map/all_gather | solution.py:186
  114.1 9.1 %copy-start.49 = (bf16[256,16]{0,1:T(8,128)(2,1)S(1)}, bf16[256,16]{0,1:T(8,128)(2,1)}, u32[]{:S(2)}) copy-start(bf16[256,16]{0,1:T(8,128)(2,1)} %param.26) | copy-start | bytes 24580
  114.3 4.9 %collective-permute-start.8 = (bf16[128,128]{0,1:T(8,128)(2,1)S(1)}, bf16[128,128]{0,1:T(8,128)(2,1)S(1)}, u32[]{:S(2)}, u32[]{:S(2)}) collective-permute-start(bf16[128,128]{0,1:T(8,128)(2,1)S(1)} %slice.376), channel_id=1, source_target_pairs={{0,8},{8,0},{1,9},{9,1},{2,10},{10,2},{3,11},{11,3},{4,12},{12,4},... | collective-permute-start | bytes 98312 | tf_op jit(solution)/shard_map/ppermute | solution.py:212
  121.0 21.6 %copy-start.1 = (bf16[2176,512]{1,0:T(8,128)(2,1)S(1)}, bf16[2176,512]{1,0:T(8,128)(2,1)}, u32[]{:S(2)}) copy-start(bf16[2176,512]{1,0:T(8,128)(2,1)} %all-gather.6.cloned.1.call-done) | copy-start | bytes 6684676
  123.2 25.8 %copy-start.4 = (bf16[256,512]{1,0:T(8,128)(2,1)S(1)}, bf16[256,512]{1,0:T(8,128)(2,1)}, u32[]{:S(2)}) copy-start(bf16[256,512]{1,0:T(8,128)(2,1)} %param.29) | copy-start | bytes 786436
  126.1 17.1 %all-to-all-start.3 = ((bf16[8,272,128]{2,1,0:T(8,128)(2,1)}), bf16[8,272,128]{2,1,0:T(8,128)(2,1)}, u32[]{:S(2)}, u32[]{:S(2)}) async-start(bf16[8,272,128]{2,1,0:T(8,128)(2,1)} %pad_maximum_fusion), calls=%async_computation.3 | async-start | bytes 1114112 | tf_op jit(solution)/shard_map/all_to_all | solution.py:27
  130.3 49.4 %collective-permute-start.9 = (bf16[128,512]{1,0:T(8,128)(2,1)}, bf16[128,512]{1,0:T(8,128)(2,1)}, u32[]{:S(2)}, u32[]{:S(2)}) collective-permute-start(bf16[128,512]{1,0:T(8,128)(2,1)} %param.39), channel_id=1, source_target_pairs={{0,1},{1,0},{2,3},{3,2},{4,5},{5,4},{6,7},{7,6},{8,9},{9,8},{10,11... | collective-permute-start | bytes 393224 | tf_op jit(solution)/shard_map/ppermute | solution.py:128
  150.9 9.5 %all-to-all-start.4 = ((bf16[8,16,512]{2,1,0:T(8,128)(2,1)}), bf16[8,16,512]{2,1,0:T(8,128)(2,1)S(1)}, u32[]{:S(2)}, u32[]{:S(2)}) async-start(bf16[8,16,512]{2,1,0:T(8,128)(2,1)} %bitcast.136), calls=%async_computation.4 | async-start | bytes 262144 | tf_op jit(solution)/shard_map/all_to_all | solution.py:27
  167.1 11.1 %collective-permute-start.10 = (bf16[128,640]{1,0:T(8,128)(2,1)}, bf16[128,640]{1,0:T(8,128)(2,1)}, u32[]{:S(2)}, u32[]{:S(2)}) collective-permute-start(bf16[128,640]{1,0:T(8,128)(2,1)} %pad_maximum_fusion.3), channel_id=1, source_target_pairs={{0,1},{1,0},{2,3},{3,2},{4,5},{5,4},{6,7},{7,6},{8,9},{9,8},{10,11... | collective-permute-start | bytes 491528 | tf_op jit(solution)/shard_map/ppermute | solution.py:257
  173.3 0.7 copy-start.31
  173.5 4.7 %copy-start.3 = (bf16[128,512]{1,0:T(8,128)(2,1)S(1)}, bf16[128,512]{1,0:T(8,128)(2,1)}, u32[]{:S(2)}) copy-start(bf16[128,512]{1,0:T(8,128)(2,1)} %copy-done.2) | copy-start | bytes 393220
  173.5 4.7 %copy-start.11 = (bf16[128,16]{1,0:T(8,128)(2,1)S(1)}, bf16[128,16]{1,0:T(8,128)(2,1)}, u32[]{:S(2)}) copy-start(bf16[128,16]{1,0:T(8,128)(2,1)} %copy.103) | copy-start | bytes 12292
  173.5 4.7 %copy-start.13 = (bf16[128,112]{1,0:T(8,128)(2,1)S(1)}, bf16[128,112]{1,0:T(8,128)(2,1)}, u32[]{:S(2)}) copy-start(bf16[128,112]{1,0:T(8,128)(2,1)} %copy-done.12) | copy-start | bytes 86020
  174.1 5.7 %copy-start.20 = (bf16[128,512]{1,0:T(8,128)(2,1)S(1)}, bf16[128,512]{1,0:T(8,128)(2,1)}, u32[]{:S(2)}) copy-start(bf16[128,512]{1,0:T(8,128)(2,1)} %param.39) | copy-start | bytes 393220
  181.3 6.8 %copy-start.14 = (f32[128,16]{1,0:T(8,128)S(1)}, f32[128,16]{1,0:T(8,128)}, u32[]{:S(2)}) copy-start(f32[128,16]{1,0:T(8,128)} %copy.104) | copy-start | bytes 24580
  181.3 6.8 %copy-start.27 = (bf16[512,16]{0,1:T(8,128)(2,1)S(1)}, bf16[512,16]{0,1:T(8,128)(2,1)}, u32[]{:S(2)}) copy-start(bf16[512,16]{0,1:T(8,128)(2,1)} %param.36) | copy-start | bytes 49156
  181.3 6.8 %copy-start.32 = (f32[512]{0:T(512)S(1)}, f32[512]{0:T(512)}, u32[]{:S(2)}) copy-start(f32[512]{0:T(512)} %param.33) | copy-start | bytes 6148
  181.9 6.8 %copy-start.15 = (f32[128,16]{1,0:T(8,128)S(1)}, f32[128,16]{1,0:T(8,128)}, u32[]{:S(2)}) copy-start(f32[128,16]{1,0:T(8,128)} %copy.105) | copy-start | bytes 24580
  182.0 6.8 %copy-start.44 = (s32[128]{0:T(128)S(1)}, s32[128]{0:T(128)}, u32[]{:S(2)}) copy-start(s32[128]{0:T(128)} %eq.80) | copy-start | bytes 1540
  182.0 7.1 %copy-start.48 = (bf16[48]{0:T(256)(128)(2,1)S(1)}, bf16[48]{0:T(256)(128)(2,1)}, u32[]{:S(2)}) copy-start(bf16[48]{0:T(256)(128)(2,1)} %pad.26.clone) | copy-start | bytes 292
  182.0 6.1 %collective-permute-start.11 = (bf16[128,640]{1,0:T(8,128)(2,1)S(1)}, bf16[128,640]{1,0:T(8,128)(2,1)S(1)}, u32[]{:S(2)}, u32[]{:S(2)}) collective-permute-start(bf16[128,640]{1,0:T(8,128)(2,1)S(1)} %slice.468), channel_id=1, source_target_pairs={{0,1},{1,0},{2,3},{3,2},{4,5},{5,4},{6,7},{7,6},{8,9},{9,8},{10,11... | collective-permute-start | bytes 491528 | tf_op jit(solution)/shard_map/ppermute | solution.py:262
  190.1 12.8 %all-to-all-start.5 = ((bf16[8,64,512]{2,1,0:T(8,128)(2,1)}), bf16[8,64,512]{2,1,0:T(8,128)(2,1)}, u32[]{:S(2)}, u32[]{:S(2)}) async-start(bf16[8,64,512]{2,1,0:T(8,128)(2,1)} %fusion.67), calls=%async_computation.5 | async-start | bytes 1048576 | tf_op jit(solution)/shard_map/all_to_all | solution.py:27
  197.4 9.1 %copy-start.50 = (s32[128]{0:T(128)S(1)}, s32[128]{0:T(128)}, u32[]{:S(2)}) copy-start(s32[128]{0:T(128)} %param.23) | copy-start | bytes 1540
  197.4 10.0 %copy-start.17 = (bf16[128,128]{0,1:T(8,128)(2,1)S(1)}, bf16[128,128]{0,1:T(8,128)(2,1)}, u32[]{:S(2)}) copy-start(bf16[128,128]{0,1:T(8,128)(2,1)} %copy-done.16) | copy-start | bytes 98308
  197.4 10.0 %copy-start.19 = (bf16[128,128]{0,1:T(8,128)(2,1)S(1)}, bf16[128,128]{0,1:T(8,128)(2,1)}, u32[]{:S(2)}) copy-start(bf16[128,128]{0,1:T(8,128)(2,1)} %copy-done.18) | copy-start | bytes 98308
  197.4 10.0 %copy-start.51 = (f32[128,16]{0,1:T(8,128)S(1)}, f32[128,16]{0,1:T(8,128)}, u32[]{:S(2)}) copy-start(f32[128,16]{0,1:T(8,128)} %get-tuple-element.121) | copy-start | bytes 24580
  197.4 10.2 %copy-start.5 = (bf16[256,512]{1,0:T(8,128)(2,1)S(1)}, bf16[256,512]{1,0:T(8,128)(2,1)}, u32[]{:S(2)}) copy-start(bf16[256,512]{1,0:T(8,128)(2,1)} %param.29) | copy-start | bytes 786436
  197.4 10.2 %copy-start.33 = (bf16[128,16]{0,1:T(8,128)(2,1)S(1)}, bf16[128,16]{0,1:T(8,128)(2,1)}, u32[]{:S(2)}) copy-start(bf16[128,16]{0,1:T(8,128)(2,1)} %get-tuple-element.120) | copy-start | bytes 12292
  (10 other events, 6.7 us)
Sparse Core Ops, SparseCore 0:
  20.4 61.9 all-gather.5
  108.7 62.7 all-gather.3

commit v5 on v4

--- a/solution.py
+++ b/solution.py
@@ -1,8 +1,11 @@
+import functools
 import math
 
 import jax
 import jax.numpy as jnp
 from jax import lax
+from jax.experimental import pallas as pl
+from jax.experimental.pallas import tpu as pltpu
 from jax.sharding import Mesh
 from jax.sharding import PartitionSpec as P
 
@@ -74,17 +77,78 @@
     return jnp.concatenate([array[:, :RANK], array[:, RANK:]], axis=2)
 
 
-def attend(state, queries, query_places, keys, values, key_places):
-    top, mass, out = state
-    scores = contract(queries, keys, 1, 1) * (1.0 / math.sqrt(HEAD))
-    allowed = key_places[None, :] <= query_places[:, None]
-    scores = jnp.where(allowed, scores, -1e30)
-    new_top = jnp.maximum(top, jnp.max(scores, axis=1, keepdims=True))
-    weights = jnp.where(allowed, jnp.exp(scores - new_top), 0.0)
-    shrink = jnp.exp(top - new_top)
-    mass = mass * shrink + jnp.sum(weights, axis=1, keepdims=True)
-    out = out * shrink + jnp.dot(weights.astype(BF), values, preferred_element_type=F32)
-    return (new_top, mass, out)
+def attend_kernel(spots, queries, *refs, count, start, finish):
+    packets, refs = refs[:count], refs[count:]
+    rows = queries.shape[0]
+    half = rows // 2
+    if start:
+        top = jnp.full((rows, 1), -1e20, F32)
+        mass = jnp.zeros((rows, HEAD), F32)
+        out = jnp.zeros((rows, HEAD), F32)
+    else:
+        top, mass, out = refs[0][:, :1], refs[1][...], refs[2][...]
+        refs = refs[3:]
+    core = spots[0]
+
+    def inside(shape, dim):
+        at = lax.broadcasted_iota(jnp.int32, shape, dim)
+        return jnp.where(at < half, at + core * half, at - core * half)
+
+    query_places = (spots[1] + pl.program_id(0)) * rows + inside((rows, 1), 0)
+    own = queries[...]
+    for index in range(count):
+        keys = packets[index][:, :HEAD]
+        values = packets[index][:, HEAD:]
+        key_places = spots[2 + index] * rows + inside((1, rows), 1)
+        scores = contract(own, keys, 1, 1) * (1.0 / math.sqrt(HEAD))
+        scores = jnp.where(key_places <= query_places, scores, -1e30)
+        new_top = jnp.maximum(top, jnp.max(scores, axis=1, keepdims=True))
+        weights = jnp.exp(scores - new_top)
+        shrink = jnp.exp(top - new_top)
+        mass = mass * shrink + (weights[:, :HEAD] + weights[:, HEAD:])
+        out = out * shrink + jnp.dot(weights.astype(BF), values, preferred_element_type=F32)
+        top = new_top
+    if not finish:
+        refs[0][...] = jnp.broadcast_to(top, (rows, HEAD))
+        refs[1][...] = mass
+        refs[2][...] = out
+        return
+    mass = jnp.sum(mass, axis=1, keepdims=True)
+    safe = jnp.where(mass > 0, mass, 1.0)
+    level = jnp.where(mass > 0, top + jnp.log(safe), -1e30)
+    level = jnp.broadcast_to(level, (rows, HEAD))
+    high = level.astype(BF).astype(F32)
+    middle = (level - high).astype(BF).astype(F32)
+    low = level - high - middle
+    lane = lax.broadcasted_iota(jnp.int32, (rows, HEAD), 1)
+    level = jnp.where(lane < 32, high, jnp.where(lane < 64, middle, low))
+    refs[0][:, :HEAD] = (out / safe).astype(BF)
+    refs[0][:, HEAD:] = level.astype(BF)
+
+
+def attend(spots, queries, packets, state, finish):
+    total_rows = queries.shape[0]
+    rows = packets[0].shape[0]
+    block = pl.BlockSpec((rows, HEAD), lambda k: (k, 0))
+    whole = pl.BlockSpec(packets[0].shape, lambda k: (0, 0))
+    start = state is None
+    state = () if start else state
+    if finish:
+        shapes = jax.ShapeDtypeStruct((total_rows, 2 * HEAD), BF)
+        outs = pl.BlockSpec((rows, 2 * HEAD), lambda k: (k, 0))
+    else:
+        shapes = (jax.ShapeDtypeStruct((total_rows, HEAD), F32),) * 3
+        outs = (block,) * 3
+    return pl.pallas_call(
+        functools.partial(attend_kernel, count=len(packets), start=start, finish=finish),
+        grid=(total_rows // rows,),
+        in_specs=[pl.BlockSpec(memory_space=pltpu.SMEM), block]
+        + [whole] * len(packets)
+        + [block] * len(state),
+        out_specs=outs,
+        out_shape=shapes,
+        name="attend",
+    )(spots, queries, *packets, *state)
 
 
 def body(
@@ -116,6 +180,7 @@
     near = lax.axis_index(NEAR)
     far = lax.axis_index(FAR)
     side = lax.axis_index(SIDE)
+    line = lax.axis_size(LINE)
     core = lax.axis_index(CORE)
     row_index = lax.axis_index(ROW)
     columns = local_weight.shape[1]
@@ -140,70 +205,42 @@
     sides = lax.axis_size(QUAD)
     queries = quad.reshape(sides * chip_rows, HEAD)
 
-    def places(z_index, near_index, far_index):
-        start = (z_index * 8 + near_index * 4 + far_index * 2) * rows
-        count = jnp.arange(rows, dtype=jnp.int32)
-        return jnp.concatenate([start + core * rows + count, start + (1 - core) * rows + count])
-
-    query_places = jnp.concatenate([places(z, k // 2, k % 2) for k in range(sides)])
-    count = sides * chip_rows
-    state = (
-        jnp.full((count, 1), -1e30, F32),
-        jnp.zeros((count, 1), F32),
-        jnp.zeros((count, HEAD), F32),
-    )
     up = [(i, (i + 1) % ring) for i in range(ring)]
     down = [(i, (i - 1) % ring) for i in range(ring)]
 
-    def visit(state, packets, indices):
-        keys = jnp.concatenate([p[:, :HEAD] for p in packets])
-        values = jnp.concatenate([p[:, HEAD:] for p in packets])
-        key_places = jnp.concatenate([places(i, near, far) for i in indices])
-        return attend(state, queries, query_places, keys, values, key_places)
-
     rising = falling = packet
-    held, at = [[packet]], [[z]]
+    held, at = [packet], [z]
     for step in range(1, ring // 2 + 1):
         rising = lax.ppermute(rising, Z, up)
-        held.append([rising])
-        at.append([(z - step) % ring])
+        held.append(rising)
+        at.append((z - step) % ring)
         if step < ring // 2:
             falling = lax.ppermute(falling, Z, down)
-            held[-1].append(falling)
-            at[-1].append((z + step) % ring)
+            held.append(falling)
+            at.append((z + step) % ring)
         if step == 1:
             rising, falling, hidden, queries = lax.optimization_barrier(
                 (rising, falling, hidden, queries)
             )
-            hidden = to_everyone(hidden, (FAR, LINE, CORE)).reshape(-1, units)
+            hidden = to_everyone(hidden, (FAR, LINE, CORE))
+            hidden = hidden.reshape(2, line, 2, 2, share, units)
+            hidden = jnp.transpose(hidden, (1, 3, 0, 2, 4, 5)).reshape(-1, units)
         elif step == 2:
             rising, falling, hidden = lax.optimization_barrier((rising, falling, hidden))
-        if step >= 2:
-            state = visit(state, held[step - 2], at[step - 2])
-    state = visit(state, held[-2], at[-2])
-    now, weights, hidden = lax.optimization_barrier((held[-1], weights, hidden))
-    state = visit(state, now, at[-1])
+    spots = jnp.stack([z * sides] + [k * sides + near * 2 + far for k in at]).astype(jnp.int32)
+    spots = jnp.concatenate([core.astype(jnp.int32)[None], spots])
+    state = attend(spots, queries, held[:-1], None, False)
+    last, weights, hidden = lax.optimization_barrier((held[-1], weights, hidden))
+    met = attend(jnp.concatenate([spots[:2], spots[-1:]]), queries, [last], state, True)
     riders = lax.all_gather(hidden, (Z, NEAR), axis=0, tiled=True)
 
     local_whole = weights[:, :width].reshape(-1, columns)
     up_whole = unfold(weights[:, width : width + 8])
     up_whole = jnp.transpose(up_whole, (1, 0, 2)).reshape(RANK, -1)
-    line = lax.axis_size(LINE)
     local_ups = unfold(weights[:, width + 8 :]).reshape(line, 2, RANK, units)
     local_ups = lax.dynamic_index_in_dim(local_ups, side, 1, keepdims=False)
     local_ups = jnp.concatenate([local_ups[k] for k in range(line)], axis=1)
 
-    top, mass, out = state
-    level = jnp.where(mass > 0, top + jnp.log(jnp.where(mass > 0, mass, 1.0)), -1e30)
-    out = out / jnp.where(mass > 0, mass, 1.0)
-    high = lax.reduce_precision(level, 8, 7)
-    middle = lax.reduce_precision(level - high, 8, 7)
-    low = level - high - middle
-    wide = [
-        jnp.broadcast_to(a.astype(BF), (count, n))
-        for a, n in ((high, 32), (middle, 32), (low, 64))
-    ]
-    met = jnp.concatenate([out.astype(BF), *wide], axis=1)
     met = exchange(met.reshape(sides, chip_rows, 2 * HEAD), QUAD).astype(F32)
     levels = met[:, :, 128:129] + met[:, :, 160:161] + met[:, :, 192:193]
     parts = jnp.exp(levels - jnp.max(levels, axis=0, keepdims=True))
@@ -231,8 +268,8 @@
     projected = exchange(projected.reshape(row_count, own_patches, columns), ROW)
     projected = total(projected).astype(BF)
 
-    riders = riders.reshape(columns // (2 * share), line, 2, 2, share, units)
-    riders = jnp.transpose(riders, (3, 1, 0, 2, 4, 5)).reshape(2, line, columns, units)
+    riders = riders.reshape(-1, line, 2, 4 * share, units)
+    riders = jnp.transpose(riders, (2, 1, 0, 3, 4)).reshape(2, line, columns, units)
     rows_in, rows_out = (
         jnp.concatenate([riders[way, k] for k in range(line)], axis=1) for way in range(2)
     )

time: 273 us -> 268 us (0.982)
  blocking collectives: 52.5 us -> 71.9 us
  matrix products: 32.4 us -> 18.8 us
  starting transfers between devices: 80.4 us -> 68.5 us
  Pallas kernels: 0 us -> 11.8 us
  other arithmetic: 22.4 us -> 16.6 us
  local copies, waits for them, and re-layouts: 34 us -> 30.1 us
    all_to_all x3 -> x4, blocking collectives: 52.5 us -> 71.9 us  [exchange(): return lax.all_to_all(pieces, axis, split_axis=0, concat_axis=0, tiled=True)]
    pallas_call x0 -> x2, Pallas kernels: none -> 11.8 us  [attend(): pl.pallas_call(functools.partial(attend_kernel, count=len(packets), start...]
    all_to_all x6 -> x5, starting transfers between devices: 30.6 us -> 20.1 us  [exchange(): return lax.all_to_all(pieces, axis, split_axis=0, concat_axis=0, tiled=True)]
    dot_general x17 -> x12, matrix products: 21.3 us -> 12.3 us  [contract(): lax.dot_general(left, right, (((left_dim,), (right_dim,)), ((), ())), pre...]
    dot_general x5 -> x0, matrix products: 4.63 us -> none  [attend(): jnp.dot(weights.astype(BF), values, preferred_element_type=F32)]
    ppermute x4, waiting for transfers between devices: 8.04 us -> 3.56 us  [body(): rising = lax.ppermute(rising, Z, up)]
    slice x7 -> x0, local copies, waits for them, and re-layouts: 3.81 us -> none  [the longest x6 3.8 us: visit(): values = jnp.concatenate([p[:, HEAD:] for p in packets])]
    reduce_sum x2 -> x0, other arithmetic: 3.08 us -> none  [attend(): mass = mass * shrink + jnp.sum(weights, axis=1, keepdims=True)]
  transfers between devices with their start and end apart: 20 -> 19, of which waited for: 11 -> 11; matrix products, arithmetic and copies ran while one was open for 22% -> 16% of each run, Pallas kernels for 0% -> 3%
where the time goes in v5:
time: 268 us; the launch traced here: 266 us
  blocking collectives  71.9 us (27%)
  starting transfers between devices  68.5 us (26%)
  waiting for transfers between devices  33.5 us (12%)
  local copies, waits for them, and re-layouts  30.1 us (11%)
  matrix products  18.8 us (7%)
  other arithmetic  16.6 us (6%)
  between operations  15 us (6%)
  Pallas kernels  11.8 us (4%)
    all_to_all x4, blocking collectives, exchange(): return lax.all_to_all(pieces, axis, split_axis=0, concat_axis=0, tiled=True)  71.9 us
    all_to_all x5, starting transfers between devices, exchange(): return lax.all_to_all(pieces, axis, split_axis=0, concat_axis=0, tiled=True)  20.1 us
    all_to_all x5, waiting for transfers between devices, exchange(): return lax.all_to_all(pieces, axis, split_axis=0, concat_axis=0, tiled=True)  17.4 us
    ppermute x3, starting transfers between devices, body(): falling = lax.ppermute(falling, Z, down)  14.5 us
    ppermute x4, starting transfers between devices, body(): rising = lax.ppermute(rising, Z, up)  12.7 us
    dot_general x12, matrix products, contract(): lax.dot_general(left, right, (((left_dim,), (right_dim,)), ((), ())), pre...  12.3 us
    pallas_call x2, Pallas kernels, attend(): pl.pallas_call(functools.partial(attend_kernel, count=len(packets), start...  11.8 us
    ppermute x1, starting transfers between devices, body(): both = jnp.concatenate([mine, lax.ppermute(other, CORE, SWAP)], axis=0)  8.79 us
  transfers between devices with their start and end apart: 19, of which 11 were waited for; matrix products, arithmetic and copies ran while one was open for 16% of the time, Pallas kernels for 3%

profile of v5, /device:TPU:1, one launch (start us, length us, event | category | flops | bytes accessed | tf_op | source)
XLA Modules:
  0.0 266.2 jit_solution(8844640382318396667)
XLA Ops:
  7.2 0.8 fusion.73
  8.1 1.7 maximum_maximum_fusion.1
  10.6 0.8 constant_dynamic-slice_fusion.3
  11.4 8.8 %collective-permute-start = (bf16[128,384]{1,0:T(8,128)(2,1)S(1)}, bf16[128,384]{1,0:T(8,128)(2,1)S(1)}, u32[]{:S(2)}, u32[]{:S(2)}) collective-permute-start(bf16[128,384]{1,0:T(8,128)(2,1)S(1)} %pad_maximum_fusion.3), channel_id=1, source_target_pairs={{0,8},{8,0},{1,9},{9,1},{2,10},{10,2},{3,11},{11,3},{4,12},{12,4},... | collective-permute-start | bytes 294920 | tf_op jit(solution)/shard_map/ppermute | solution.py:201
  20.2 0.9 collective-permute-done
  21.9 3.4 %all-to-all-start = ((bf16[4,256,128]{2,1,0:T(8,128)(2,1)}), bf16[4,256,128]{2,1,0:T(8,128)(2,1)S(1)}, u32[]{:S(2)}, u32[]{:S(2)}) async-start(bf16[4,256,128]{2,1,0:T(8,128)(2,1)} %broadcast_in_dim.23), calls=%async_computation | async-start | bytes 524288 | tf_op jit(solution)/shard_map/all_to_all | solution.py:30
  25.4 1.9 collective-permute-start.1
  27.3 7.2 %collective-permute-start.2 = (bf16[256,256]{1,0:T(8,128)(2,1)S(1)}, bf16[256,256]{1,0:T(8,128)(2,1)S(1)}, u32[]{:S(2)}, u32[]{:S(2)}) collective-permute-start(bf16[256,256]{1,0:T(8,128)(2,1)S(1)} %slice.291.refs_0_), channel_id=1, source_target_pairs={{0,448},{64,0},{128,64},{192,128},{256,192},{320,256},{384,320},{4... | collective-permute-start | bytes 393224 | tf_op jit(solution)/shard_map/ppermute | solution.py:218
  34.6 2.5 collective-permute-done.1.refs_1_
  37.1 1.0 collective-permute-done.2.refs_2_
  38.2 4.4 %collective-permute-start.3 = (bf16[256,256]{1,0:T(8,128)(2,1)S(1)}, bf16[256,256]{1,0:T(8,128)(2,1)S(1)}, u32[]{:S(2)}, u32[]{:S(2)}) collective-permute-start(bf16[256,256]{1,0:T(8,128)(2,1)S(1)} %collective-permute-done.1.refs_1_), channel_id=1, source_target_pairs={{0,64},{64,128},{128,192},{192,256},{256,320},{320,384},{384,448},... | collective-permute-start | bytes 393224 | tf_op jit(solution)/shard_map/ppermute | solution.py:214
  42.6 3.0 %collective-permute-start.4 = (bf16[256,256]{1,0:T(8,128)(2,1)S(1)}, bf16[256,256]{1,0:T(8,128)(2,1)S(1)}, u32[]{:S(2)}, u32[]{:S(2)}) collective-permute-start(bf16[256,256]{1,0:T(8,128)(2,1)S(1)} %collective-permute-done.2.refs_2_), channel_id=1, source_target_pairs={{0,448},{64,0},{128,64},{192,128},{256,192},{320,256},{384,320},{4... | collective-permute-start | bytes 393224 | tf_op jit(solution)/shard_map/ppermute | solution.py:218
  45.6 19.6 %all_to_all.45 = bf16[16,16,256]{2,1,0:T(8,128)(2,1)S(1)} all-to-all(bf16[16,16,256]{2,1,0:T(8,128)(2,1)S(1)} %broadcast_in_dim.24), channel_id=1, replica_groups=mesh['seq_0'=8,'near'=2,'seq_1'=2,'seq_2'=2,'row_0'=4,'row_1'=2] {'seq_1..., dimensions={0} | all-to-all | bytes 262144 | tf_op jit(solution)/shard_map/all_to_all | solution.py:30
  65.9 3.1 %collective-permute-start.5 = (bf16[256,256]{1,0:T(8,128)(2,1)S(1)}, bf16[256,256]{1,0:T(8,128)(2,1)S(1)}, u32[]{:S(2)}, u32[]{:S(2)}) collective-permute-start(bf16[256,256]{1,0:T(8,128)(2,1)S(1)} %collective-permute-done.3.refs_3_), channel_id=1, source_target_pairs={{0,64},{64,128},{128,192},{192,256},{256,320},{320,384},{384,448},... | collective-permute-start | bytes 393224 | tf_op jit(solution)/shard_map/ppermute | solution.py:214
  69.0 4.3 %collective-permute-start.7 = (bf16[256,256]{1,0:T(8,128)(2,1)S(1)}, bf16[256,256]{1,0:T(8,128)(2,1)S(1)}, u32[]{:S(2)}, u32[]{:S(2)}) collective-permute-start(bf16[256,256]{1,0:T(8,128)(2,1)S(1)} %collective-permute-done.4.refs_4_), channel_id=1, source_target_pairs={{0,448},{64,0},{128,64},{192,128},{256,192},{320,256},{384,320},{4... | collective-permute-start | bytes 393224 | tf_op jit(solution)/shard_map/ppermute | solution.py:218
  73.3 1.0 collective-permute-done.5.refs_5_
  74.3 3.3 %collective-permute-start.6 = (bf16[256,256]{1,0:T(8,128)(2,1)S(1)}, bf16[256,256]{1,0:T(8,128)(2,1)S(1)}, u32[]{:S(2)}, u32[]{:S(2)}) collective-permute-start(bf16[256,256]{1,0:T(8,128)(2,1)S(1)} %collective-permute-done.5.refs_5_), channel_id=1, source_target_pairs={{0,64},{64,128},{128,192},{192,256},{256,320},{320,384},{384,448},... | collective-permute-start | bytes 393224 | tf_op jit(solution)/shard_map/ppermute | solution.py:214
  79.0 2.2 collective-permute-done.7.refs_6_
  81.9 7.1 %attend.2 = (f32[1024,128]{1,0:T(8,128)}, f32[1024,128]{1,0:T(8,128)}, f32[1024,128]{1,0:T(8,128)}) custom-call(s32[10]{0:T(128)} %concatenate.120.spots, bf16[1024,128]{1,0:T(8,128)(2,1)} %bitcast.130, bf16[256,256]{1,0:T(8,128)(2,1)} %copy-done.8, bf16[256,256]{1,0:T(8,128)(2,1)} %copy-done.14, bf16[256,256]{1,0:T(8,128)(2,1)} %copy-done.15, ...), custom_call_target="tpu_custom_call" | custom-call | tf_op jit(solution)/shard_map/attend/pallas_call | solution.py:142
  89.7 4.7 %attend.3 = bf16[1024,256]{1,0:T(8,128)(2,1)} custom-call(s32[3]{0:T(128)} %pad_add_fusion.spots, bf16[1024,128]{1,0:T(8,128)(2,1)} %bitcast.131, bf16[256,256]{1,0:T(8,128)(2,1)} %copy-done.25, f32[1024,128]{1,0:T(8,128)} %get-tuple-element.27.refs_1_, f32[1024,128]{1,0:T(8,128)} %get-tuple-element.28.refs_2_, f32[1024,128]{1,0:T(8,128)} %get-tuple-element.29.refs_3_), custom_call_target="tpu_custom_call" | custom-call | tf_op jit(solution)/shard_map/attend/pallas_call | solution.py:142
  94.4 2.0 copy.105
  96.5 3.5 %all-to-all-start.2 = ((bf16[4,256,256]{1,2,0:T(8,128)(2,1)}), bf16[4,256,256]{1,2,0:T(8,128)(2,1)S(1)}, u32[]{:S(2)}, u32[]{:S(2)}) async-start(bf16[4,256,256]{1,2,0:T(8,128)(2,1)} %copy.105), calls=%async_computation.2 | async-start | bytes 1048576 | tf_op jit(solution)/shard_map/all_to_all | solution.py:30
  100.7 8.1 %all-to-all-done.2 = bf16[4,256,256]{1,2,0:T(8,128)(2,1)S(1)} async-done(((bf16[4,256,256]{1,2,0:T(8,128)(2,1)}), bf16[4,256,256]{1,2,0:T(8,128)(2,1)S(1)}, u32[]{:S(2)}, u32[]{:S(2)}) %all-to-all-start.2) | async-done | bytes 524320 | tf_op jit(solution)/shard_map/all_to_all | solution.py:30
  109.1 3.4 %collective-permute-start.8 = (bf16[128,128]{0,1:T(8,128)(2,1)S(1)}, bf16[128,128]{0,1:T(8,128)(2,1)S(1)}, u32[]{:S(2)}, u32[]{:S(2)}) collective-permute-start(bf16[128,128]{0,1:T(8,128)(2,1)S(1)} %slice.297), channel_id=1, source_target_pairs={{0,8},{8,0},{1,9},{9,1},{2,10},{10,2},{3,11},{11,3},{4,12},{12,4},... | collective-permute-start | bytes 98312 | tf_op jit(solution)/shard_map/ppermute | solution.py:249
  112.5 0.8 collective-permute-done.8
  114.0 1.1 fusion
  115.1 2.2 copy.119
  117.3 0.9 fusion.10
  118.3 1.9 pad_maximum_fusion
  120.2 4.2 %all-to-all-start.3 = ((bf16[8,272,128]{2,1,0:T(8,128)(2,1)}), bf16[8,272,128]{2,1,0:T(8,128)(2,1)}, u32[]{:S(2)}, u32[]{:S(2)}) async-start(bf16[8,272,128]{2,1,0:T(8,128)(2,1)} %pad_maximum_fusion), calls=%async_computation.3 | async-start | bytes 1114112 | tf_op jit(solution)/shard_map/all_to_all | solution.py:30
  124.4 3.2 %collective-permute-start.9 = (bf16[128,512]{1,0:T(8,128)(2,1)}, bf16[128,512]{1,0:T(8,128)(2,1)}, u32[]{:S(2)}, u32[]{:S(2)}) collective-permute-start(bf16[128,512]{1,0:T(8,128)(2,1)} %param.39), channel_id=1, source_target_pairs={{0,1},{1,0},{2,3},{3,2},{4,5},{5,4},{6,7},{7,6},{8,9},{9,8},{10,11... | collective-permute-start | bytes 393224 | tf_op jit(solution)/shard_map/ppermute | solution.py:193
  129.1 1.5 fusion.48
  130.7 1.4 copy.112
  133.4 1.3 dynamic_slice.28
  135.4 1.1 convert_reduce_fusion
  137.8 1.7 copy.124
  139.5 1.6 multiply_convert_fusion.4
  141.1 1.9 convolution_convert_fusion.3
  143.0 4.0 %all-to-all-start.4 = ((bf16[8,16,512]{2,1,0:T(8,128)(2,1)}), bf16[8,16,512]{2,1,0:T(8,128)(2,1)S(1)}, u32[]{:S(2)}, u32[]{:S(2)}) async-start(bf16[8,16,512]{2,1,0:T(8,128)(2,1)} %bitcast.139), calls=%async_computation.4 | async-start | bytes 262144 | tf_op jit(solution)/shard_map/all_to_all | solution.py:30
  148.4 4.1 %all-to-all-done.4 = bf16[8,16,512]{2,1,0:T(8,128)(2,1)S(1)} async-done(((bf16[8,16,512]{2,1,0:T(8,128)(2,1)}), bf16[8,16,512]{2,1,0:T(8,128)(2,1)S(1)}, u32[]{:S(2)}, u32[]{:S(2)}) %all-to-all-start.4) | async-done | bytes 131104 | tf_op jit(solution)/shard_map/all_to_all | solution.py:30
  152.6 1.3 multiply_reduce_fusion.1
  155.3 0.9 multiply_convert_fusion.3
  157.5 1.7 pad_maximum_fusion.2
  159.2 2.3 collective-permute-start.10
  162.3 4.1 %all-gather.4.cloned.1.call-done = bf16[4096,256]{1,0:T(8,128)(2,1)} async-done(((bf16[256,256]{1,0:T(8,128)(2,1)}), bf16[4096,256]{1,0:T(8,128)(2,1)}) %all-gather.4.cloned.1.call-update) | async-done | bytes 2097168 | tf_op jit(solution)/shard_map/all_gather | solution.py:235
  166.4 1.8 copy.110
  168.9 4.1 %maximum_maximum_fusion = bf16[640,1024]{1,0:T(8,128)(2,1)S(1)} fusion(bf16[16,256]{1,0:T(8,128)(2,1)S(1)} %copy-done.30, bf16[16,256]{1,0:T(8,128)(2,1)S(1)} %copy-done.28, bf16[16,256]{1,0:T(8,128)(2,1)S(1)} %copy-done.29, bf16[16,256]{1,0:T(8,128)(2,1)S(1)} %copy-done.27, bf16[512,256]{1,0:T(8,128)(2,1)S(1)} %get-tuple-element.45, ...), kind=kLoop, calls=%fused_computation.5 | loop fusion | flops 11796480 | bytes 2393344 | tf_op jit(solution)/shard_map/concatenate | solution.py:277
  173.0 1.5 fusion.25
  174.6 1.5 fusion.1
  176.8 1.1 convolution_convert_fusion.2
  178.0 3.3 %collective-permute-start.11 = (bf16[128,640]{1,0:T(8,128)(2,1)S(1)}, bf16[128,640]{1,0:T(8,128)(2,1)S(1)}, u32[]{:S(2)}, u32[]{:S(2)}) collective-permute-start(bf16[128,640]{1,0:T(8,128)(2,1)S(1)} %slice.381), channel_id=1, source_target_pairs={{0,1},{1,0},{2,3},{3,2},{4,5},{5,4},{6,7},{7,6},{8,9},{9,8},{10,11... | collective-permute-start | bytes 491528 | tf_op jit(solution)/shard_map/ppermute | solution.py:299
  181.3 2.7 %collective-permute-done.11 = bf16[128,640]{1,0:T(8,128)(2,1)S(1)} collective-permute-done((bf16[128,640]{1,0:T(8,128)(2,1)S(1)}, bf16[128,640]{1,0:T(8,128)(2,1)S(1)}, u32[]{:S(2)}, u32[]{:S(2)}) %collective-permute-start.11) | collective-permute-done | bytes 163872 | tf_op jit(solution)/shard_map/ppermute | solution.py:299
  185.2 0.8 fusion.23
  186.0 5.0 %all-to-all-start.5 = ((bf16[8,64,512]{2,1,0:T(8,128)(2,1)}), bf16[8,64,512]{2,1,0:T(8,128)(2,1)}, u32[]{:S(2)}, u32[]{:S(2)}) async-start(bf16[8,64,512]{2,1,0:T(8,128)(2,1)} %fusion.23), calls=%async_computation.5 | async-start | bytes 1048576 | tf_op jit(solution)/shard_map/all_to_all | solution.py:30
  191.0 1.2 copy.114
  192.3 1.5 slice.274
  193.9 5.1 %all-to-all-done.5 = bf16[8,64,512]{2,1,0:T(8,128)(2,1)} async-done(((bf16[8,64,512]{2,1,0:T(8,128)(2,1)}), bf16[8,64,512]{2,1,0:T(8,128)(2,1)}, u32[]{:S(2)}, u32[]{:S(2)}) %all-to-all-start.5) | async-done | bytes 524320 | tf_op jit(solution)/shard_map/all_to_all | solution.py:30
  199.0 0.9 slice.316
  199.9 2.6 fusion.2
  202.6 0.9 convolution_convert_fusion.8
  204.1 1.1 convert_reduce_fusion.1
  205.2 23.6 %all_to_all.46 = bf16[8,12,256]{2,1,0:T(8,128)(2,1)S(1)} all-to-all(bf16[8,12,256]{2,1,0:T(8,128)(2,1)S(1)} %convert_element_type.134), channel_id=1, replica_groups=mesh['seq_0'=8,'near'=2,'seq_1'=2,'seq_2'=2,'row_0'=4,'row_1'=2] {'near'..., dimensions={0} | all-to-all | bytes 98304 | tf_op jit(solution)/shard_map/all_to_all | solution.py:30
  228.8 18.2 %all_to_all.47 = bf16[8,12,256]{2,1,0:T(8,128)(2,1)S(1)} all-to-all(bf16[8,12,256]{2,1,0:T(8,128)(2,1)S(1)} %broadcast_in_dim.31), channel_id=1, replica_groups=mesh['seq_0'=8,'near'=2,'seq_1'=2,'seq_2'=2,'row_0'=4,'row_1'=2] {'seq_0'}, dimensions={0} | all-to-all | bytes 98304 | tf_op jit(solution)/shard_map/all_to_all | solution.py:30
  247.1 10.5 %all_to_all.48 = bf16[8,12,256]{2,1,0:T(8,128)(2,1)S(1)} all-to-all(bf16[8,12,256]{2,1,0:T(8,128)(2,1)S(1)} %broadcast_in_dim.32), channel_id=1, replica_groups=mesh['seq_0'=8,'near'=2,'seq_1'=2,'seq_2'=2,'row_0'=4,'row_1'=2] {'near'..., dimensions={0} | all-to-all | bytes 98304 | tf_op jit(solution)/shard_map/all_to_all | solution.py:30
  (169 shorter events, 21.2 us)
Async XLA Ops:
  7.2 106.8 %copy-start = (bf16[256,2048]{1,0:T(8,128)(2,1)S(1)}, bf16[256,2048]{1,0:T(8,128)(2,1)}, u32[]{:S(2)}) copy-start(bf16[256,2048]{1,0:T(8,128)(2,1)} %param.25) | copy-start | bytes 3145732
  7.2 27.4 %copy-start.34 = (bf16[256,8]{0,1:T(8,128)(2,1)S(1)}, bf16[256,8]{0,1:T(8,128)(2,1)}, u32[]{:S(2)}) copy-start(bf16[256,8]{0,1:T(8,128)(2,1)} %param.35) | copy-start | bytes 12292
  7.2 27.4 %copy-start.35 = (bf16[256,8]{0,1:T(8,128)(2,1)S(1)}, bf16[256,8]{0,1:T(8,128)(2,1)}, u32[]{:S(2)}) copy-start(bf16[256,8]{0,1:T(8,128)(2,1)} %param.34) | copy-start | bytes 12292
  7.2 81.8 %all-gather.6.cloned.1.call-start = ((), (), s32[]{:S(2)}) async-start(), calls=%async_computation.10 | async-start | bytes 2506752 | tf_op jit(solution)/shard_map/all_gather | solution.py:192
  11.4 9.7 %collective-permute-start = (bf16[128,384]{1,0:T(8,128)(2,1)S(1)}, bf16[128,384]{1,0:T(8,128)(2,1)S(1)}, u32[]{:S(2)}, u32[]{:S(2)}) collective-permute-start(bf16[128,384]{1,0:T(8,128)(2,1)S(1)} %pad_maximum_fusion.3), channel_id=1, source_target_pairs={{0,8},{8,0},{1,9},{9,1},{2,10},{10,2},{3,11},{11,3},{4,12},{12,4},... | collective-permute-start | bytes 294920 | tf_op jit(solution)/shard_map/ppermute | solution.py:201
  21.9 16.3 %all-to-all-start = ((bf16[4,256,128]{2,1,0:T(8,128)(2,1)}), bf16[4,256,128]{2,1,0:T(8,128)(2,1)S(1)}, u32[]{:S(2)}, u32[]{:S(2)}) async-start(bf16[4,256,128]{2,1,0:T(8,128)(2,1)} %broadcast_in_dim.23), calls=%async_computation | async-start | bytes 524288 | tf_op jit(solution)/shard_map/all_to_all | solution.py:30
  25.4 55.8 %copy-start.8 = (bf16[256,256]{1,0:T(8,128)(2,1)}, bf16[256,256]{1,0:T(8,128)(2,1)S(1)}, u32[]{:S(2)}) copy-start(bf16[256,256]{1,0:T(8,128)(2,1)S(1)} %slice.291.refs_0_) | copy-start | bytes 393220
  25.4 11.7 %collective-permute-start.1 = (bf16[256,256]{1,0:T(8,128)(2,1)S(1)}, bf16[256,256]{1,0:T(8,128)(2,1)S(1)}, u32[]{:S(2)}, u32[]{:S(2)}) collective-permute-start(bf16[256,256]{1,0:T(8,128)(2,1)S(1)} %slice.291.refs_0_), channel_id=1, source_target_pairs={{0,64},{64,128},{128,192},{192,256},{256,320},{320,384},{384,448},... | collective-permute-start | bytes 393224 | tf_op jit(solution)/shard_map/ppermute | solution.py:214
  27.3 10.9 %collective-permute-start.2 = (bf16[256,256]{1,0:T(8,128)(2,1)S(1)}, bf16[256,256]{1,0:T(8,128)(2,1)S(1)}, u32[]{:S(2)}, u32[]{:S(2)}) collective-permute-start(bf16[256,256]{1,0:T(8,128)(2,1)S(1)} %slice.291.refs_0_), channel_id=1, source_target_pairs={{0,448},{64,0},{128,64},{192,128},{256,192},{320,256},{384,320},{4... | collective-permute-start | bytes 393224 | tf_op jit(solution)/shard_map/ppermute | solution.py:218
  37.1 44.1 %copy-start.14 = (bf16[256,256]{1,0:T(8,128)(2,1)}, bf16[256,256]{1,0:T(8,128)(2,1)S(1)}, u32[]{:S(2)}) copy-start(bf16[256,256]{1,0:T(8,128)(2,1)S(1)} %collective-permute-done.1.refs_1_) | copy-start | bytes 393220
  38.2 43.1 %copy-start.15 = (bf16[256,256]{1,0:T(8,128)(2,1)}, bf16[256,256]{1,0:T(8,128)(2,1)S(1)}, u32[]{:S(2)}) copy-start(bf16[256,256]{1,0:T(8,128)(2,1)S(1)} %collective-permute-done.2.refs_2_) | copy-start | bytes 393220
  38.2 43.1 %copy-start.6 = (bf16[4,256,128]{2,1,0:T(8,128)(2,1)}, bf16[4,256,128]{2,1,0:T(8,128)(2,1)S(1)}, u32[]{:S(2)}) copy-start(bf16[4,256,128]{2,1,0:T(8,128)(2,1)S(1)} %all-to-all-done) | copy-start | bytes 786436
  38.2 27.7 %collective-permute-start.3 = (bf16[256,256]{1,0:T(8,128)(2,1)S(1)}, bf16[256,256]{1,0:T(8,128)(2,1)S(1)}, u32[]{:S(2)}, u32[]{:S(2)}) collective-permute-start(bf16[256,256]{1,0:T(8,128)(2,1)S(1)} %collective-permute-done.1.refs_1_), channel_id=1, source_target_pairs={{0,64},{64,128},{128,192},{192,256},{256,320},{320,384},{384,448},... | collective-permute-start | bytes 393224 | tf_op jit(solution)/shard_map/ppermute | solution.py:214
  42.6 23.3 %collective-permute-start.4 = (bf16[256,256]{1,0:T(8,128)(2,1)S(1)}, bf16[256,256]{1,0:T(8,128)(2,1)S(1)}, u32[]{:S(2)}, u32[]{:S(2)}) collective-permute-start(bf16[256,256]{1,0:T(8,128)(2,1)S(1)} %collective-permute-done.2.refs_2_), channel_id=1, source_target_pairs={{0,448},{64,0},{128,64},{192,128},{256,192},{320,256},{384,320},{4... | collective-permute-start | bytes 393224 | tf_op jit(solution)/shard_map/ppermute | solution.py:218
  65.9 15.3 %copy-start.16 = (bf16[256,256]{1,0:T(8,128)(2,1)}, bf16[256,256]{1,0:T(8,128)(2,1)S(1)}, u32[]{:S(2)}) copy-start(bf16[256,256]{1,0:T(8,128)(2,1)S(1)} %collective-permute-done.3.refs_3_) | copy-start | bytes 393220
  65.9 15.3 %copy-start.17 = (bf16[256,256]{1,0:T(8,128)(2,1)}, bf16[256,256]{1,0:T(8,128)(2,1)S(1)}, u32[]{:S(2)}) copy-start(bf16[256,256]{1,0:T(8,128)(2,1)S(1)} %collective-permute-done.4.refs_4_) | copy-start | bytes 393220
  65.9 8.4 %collective-permute-start.5 = (bf16[256,256]{1,0:T(8,128)(2,1)S(1)}, bf16[256,256]{1,0:T(8,128)(2,1)S(1)}, u32[]{:S(2)}, u32[]{:S(2)}) collective-permute-start(bf16[256,256]{1,0:T(8,128)(2,1)S(1)} %collective-permute-done.3.refs_3_), channel_id=1, source_target_pairs={{0,64},{64,128},{128,192},{192,256},{256,320},{320,384},{384,448},... | collective-permute-start | bytes 393224 | tf_op jit(solution)/shard_map/ppermute | solution.py:214
  69.0 12.2 %collective-permute-start.7 = (bf16[256,256]{1,0:T(8,128)(2,1)S(1)}, bf16[256,256]{1,0:T(8,128)(2,1)S(1)}, u32[]{:S(2)}, u32[]{:S(2)}) collective-permute-start(bf16[256,256]{1,0:T(8,128)(2,1)S(1)} %collective-permute-done.4.refs_4_), channel_id=1, source_target_pairs={{0,448},{64,0},{128,64},{192,128},{256,192},{320,256},{384,320},{4... | collective-permute-start | bytes 393224 | tf_op jit(solution)/shard_map/ppermute | solution.py:218
  74.3 6.9 %copy-start.18 = (bf16[256,256]{1,0:T(8,128)(2,1)}, bf16[256,256]{1,0:T(8,128)(2,1)S(1)}, u32[]{:S(2)}) copy-start(bf16[256,256]{1,0:T(8,128)(2,1)S(1)} %collective-permute-done.5.refs_5_) | copy-start | bytes 393220
  74.3 14.6 %collective-permute-start.6 = (bf16[256,256]{1,0:T(8,128)(2,1)S(1)}, bf16[256,256]{1,0:T(8,128)(2,1)S(1)}, u32[]{:S(2)}, u32[]{:S(2)}) collective-permute-start(bf16[256,256]{1,0:T(8,128)(2,1)S(1)} %collective-permute-done.5.refs_5_), channel_id=1, source_target_pairs={{0,64},{64,128},{128,192},{192,256},{256,320},{320,384},{384,448},... | collective-permute-start | bytes 393224 | tf_op jit(solution)/shard_map/ppermute | solution.py:214
  81.3 0.7 copy-start.19
  89.0 0.7 copy-start.25
  96.5 12.4 %all-to-all-start.2 = ((bf16[4,256,256]{1,2,0:T(8,128)(2,1)}), bf16[4,256,256]{1,2,0:T(8,128)(2,1)S(1)}, u32[]{:S(2)}, u32[]{:S(2)}) async-start(bf16[4,256,256]{1,2,0:T(8,128)(2,1)} %copy.105), calls=%async_computation.2 | async-start | bytes 1048576 | tf_op jit(solution)/shard_map/all_to_all | solution.py:30
  99.9 66.4 %all-gather.4.cloned.1.call-start = ((), (), s32[]{:S(2)}) async-start(), calls=%async_computation.9 | async-start | bytes 2228224 | tf_op jit(solution)/shard_map/all_gather | solution.py:235
  108.9 8.4 %copy-start.38 = (bf16[256,16]{0,1:T(8,128)(2,1)S(1)}, bf16[256,16]{0,1:T(8,128)(2,1)}, u32[]{:S(2)}) copy-start(bf16[256,16]{0,1:T(8,128)(2,1)} %param.26) | copy-start | bytes 24580
  109.1 4.3 %collective-permute-start.8 = (bf16[128,128]{0,1:T(8,128)(2,1)S(1)}, bf16[128,128]{0,1:T(8,128)(2,1)S(1)}, u32[]{:S(2)}, u32[]{:S(2)}) collective-permute-start(bf16[128,128]{0,1:T(8,128)(2,1)S(1)} %slice.297), channel_id=1, source_target_pairs={{0,8},{8,0},{1,9},{9,1},{2,10},{10,2},{3,11},{11,3},{4,12},{12,4},... | collective-permute-start | bytes 98312 | tf_op jit(solution)/shard_map/ppermute | solution.py:249
  113.4 0.6 copy-start.20
  113.4 0.6 copy-start.22
  115.1 12.5 %copy-start.39 = (s32[128]{0:T(128)S(1)}, s32[128]{0:T(128)}, u32[]{:S(2)}) copy-start(s32[128]{0:T(128)} %param.23) | copy-start | bytes 1540
  115.1 19.6 %copy-start.1 = (bf16[2176,512]{1,0:T(8,128)(2,1)S(1)}, bf16[2176,512]{1,0:T(8,128)(2,1)}, u32[]{:S(2)}) copy-start(bf16[2176,512]{1,0:T(8,128)(2,1)} %all-gather.6.cloned.1.call-done) | copy-start | bytes 6684676
  117.3 23.7 %copy-start.4 = (bf16[256,512]{1,0:T(8,128)(2,1)S(1)}, bf16[256,512]{1,0:T(8,128)(2,1)}, u32[]{:S(2)}) copy-start(bf16[256,512]{1,0:T(8,128)(2,1)} %param.29) | copy-start | bytes 786436
  120.2 15.1 %all-to-all-start.3 = ((bf16[8,272,128]{2,1,0:T(8,128)(2,1)}), bf16[8,272,128]{2,1,0:T(8,128)(2,1)}, u32[]{:S(2)}, u32[]{:S(2)}) async-start(bf16[8,272,128]{2,1,0:T(8,128)(2,1)} %pad_maximum_fusion), calls=%async_computation.3 | async-start | bytes 1114112 | tf_op jit(solution)/shard_map/all_to_all | solution.py:30
  124.4 50.1 %collective-permute-start.9 = (bf16[128,512]{1,0:T(8,128)(2,1)}, bf16[128,512]{1,0:T(8,128)(2,1)}, u32[]{:S(2)}, u32[]{:S(2)}) collective-permute-start(bf16[128,512]{1,0:T(8,128)(2,1)} %param.39), channel_id=1, source_target_pairs={{0,1},{1,0},{2,3},{3,2},{4,5},{5,4},{6,7},{7,6},{8,9},{9,8},{10,11... | collective-permute-start | bytes 393224 | tf_op jit(solution)/shard_map/ppermute | solution.py:193
  136.5 0.7 copy-start.7
  143.0 9.5 %all-to-all-start.4 = ((bf16[8,16,512]{2,1,0:T(8,128)(2,1)}), bf16[8,16,512]{2,1,0:T(8,128)(2,1)S(1)}, u32[]{:S(2)}, u32[]{:S(2)}) async-start(bf16[8,16,512]{2,1,0:T(8,128)(2,1)} %bitcast.139), calls=%async_computation.4 | async-start | bytes 262144 | tf_op jit(solution)/shard_map/all_to_all | solution.py:30
  154.7 0.7 copy-start.2
  156.9 0.6 copy-start.10
  159.2 13.8 %collective-permute-start.10 = (bf16[128,640]{1,0:T(8,128)(2,1)}, bf16[128,640]{1,0:T(8,128)(2,1)}, u32[]{:S(2)}, u32[]{:S(2)}) collective-permute-start(bf16[128,640]{1,0:T(8,128)(2,1)} %pad_maximum_fusion.2), channel_id=1, source_target_pairs={{0,1},{1,0},{2,3},{3,2},{4,5},{5,4},{6,7},{7,6},{8,9},{9,8},{10,11... | collective-permute-start | bytes 491528 | tf_op jit(solution)/shard_map/ppermute | solution.py:294
  168.2 0.7 copy-start.27
  168.2 0.7 copy-start.28
  168.2 0.7 copy-start.29
  168.2 0.7 copy-start.30
  168.2 0.7 copy-start.33
  168.4 4.7 %copy-start.3 = (bf16[128,512]{1,0:T(8,128)(2,1)S(1)}, bf16[128,512]{1,0:T(8,128)(2,1)}, u32[]{:S(2)}) copy-start(bf16[128,512]{1,0:T(8,128)(2,1)} %copy-done.2) | copy-start | bytes 393220
  168.4 4.7 %copy-start.9 = (bf16[128,16]{1,0:T(8,128)(2,1)S(1)}, bf16[128,16]{1,0:T(8,128)(2,1)}, u32[]{:S(2)}) copy-start(bf16[128,16]{1,0:T(8,128)(2,1)} %copy.111) | copy-start | bytes 12292
  168.4 4.7 %copy-start.11 = (bf16[128,112]{1,0:T(8,128)(2,1)S(1)}, bf16[128,112]{1,0:T(8,128)(2,1)}, u32[]{:S(2)}) copy-start(bf16[128,112]{1,0:T(8,128)(2,1)} %copy-done.10) | copy-start | bytes 86020
  168.9 5.7 %copy-start.24 = (bf16[128,512]{1,0:T(8,128)(2,1)S(1)}, bf16[128,512]{1,0:T(8,128)(2,1)}, u32[]{:S(2)}) copy-start(bf16[128,512]{1,0:T(8,128)(2,1)} %param.39) | copy-start | bytes 393220
  176.1 8.0 %copy-start.12 = (f32[128,16]{1,0:T(8,128)S(1)}, f32[128,16]{1,0:T(8,128)}, u32[]{:S(2)}) copy-start(f32[128,16]{1,0:T(8,128)} %copy.112) | copy-start | bytes 24580
  176.1 8.1 %copy-start.26 = (bf16[512,16]{0,1:T(8,128)(2,1)S(1)}, bf16[512,16]{0,1:T(8,128)(2,1)}, u32[]{:S(2)}) copy-start(bf16[512,16]{0,1:T(8,128)(2,1)} %param.36) | copy-start | bytes 49156
  176.1 8.1 %copy-start.31 = (f32[512]{0:T(512)S(1)}, f32[512]{0:T(512)}, u32[]{:S(2)}) copy-start(f32[512]{0:T(512)} %param.33) | copy-start | bytes 6148
  176.8 7.7 %copy-start.13 = (f32[128,16]{1,0:T(8,128)S(1)}, f32[128,16]{1,0:T(8,128)}, u32[]{:S(2)}) copy-start(f32[128,16]{1,0:T(8,128)} %copy.113) | copy-start | bytes 24580
  176.8 7.7 %copy-start.36 = (s32[128]{0:T(128)S(1)}, s32[128]{0:T(128)}, u32[]{:S(2)}) copy-start(s32[128]{0:T(128)} %eq.80) | copy-start | bytes 1540
  177.9 7.1 %copy-start.37 = (bf16[48]{0:T(256)(128)(2,1)S(1)}, bf16[48]{0:T(256)(128)(2,1)}, u32[]{:S(2)}) copy-start(bf16[48]{0:T(256)(128)(2,1)} %pad.26.clone) | copy-start | bytes 292
  178.0 6.1 %collective-permute-start.11 = (bf16[128,640]{1,0:T(8,128)(2,1)S(1)}, bf16[128,640]{1,0:T(8,128)(2,1)S(1)}, u32[]{:S(2)}, u32[]{:S(2)}) collective-permute-start(bf16[128,640]{1,0:T(8,128)(2,1)S(1)} %slice.381), channel_id=1, source_target_pairs={{0,1},{1,0},{2,3},{3,2},{4,5},{5,4},{6,7},{7,6},{8,9},{9,8},{10,11... | collective-permute-start | bytes 491528 | tf_op jit(solution)/shard_map/ppermute | solution.py:299
  186.0 13.0 %all-to-all-start.5 = ((bf16[8,64,512]{2,1,0:T(8,128)(2,1)}), bf16[8,64,512]{2,1,0:T(8,128)(2,1)}, u32[]{:S(2)}, u32[]{:S(2)}) async-start(bf16[8,64,512]{2,1,0:T(8,128)(2,1)} %fusion.23), calls=%async_computation.5 | async-start | bytes 1048576 | tf_op jit(solution)/shard_map/all_to_all | solution.py:30
  193.8 8.8 %copy-start.40 = (s32[128]{0:T(128)S(1)}, s32[128]{0:T(128)}, u32[]{:S(2)}) copy-start(s32[128]{0:T(128)} %param.23) | copy-start | bytes 1540
  193.8 9.7 %copy-start.21 = (bf16[128,128]{0,1:T(8,128)(2,1)S(1)}, bf16[128,128]{0,1:T(8,128)(2,1)}, u32[]{:S(2)}) copy-start(bf16[128,128]{0,1:T(8,128)(2,1)} %copy-done.20) | copy-start | bytes 98308
  193.8 9.7 %copy-start.23 = (bf16[128,128]{0,1:T(8,128)(2,1)S(1)}, bf16[128,128]{0,1:T(8,128)(2,1)}, u32[]{:S(2)}) copy-start(bf16[128,128]{0,1:T(8,128)(2,1)} %copy-done.22) | copy-start | bytes 98308
  193.8 9.7 %copy-start.41 = (f32[128,16]{0,1:T(8,128)S(1)}, f32[128,16]{0,1:T(8,128)}, u32[]{:S(2)}) copy-start(f32[128,16]{0,1:T(8,128)} %get-tuple-element.86) | copy-start | bytes 24580
  193.8 9.9 %copy-start.5 = (bf16[256,512]{1,0:T(8,128)(2,1)S(1)}, bf16[256,512]{1,0:T(8,128)(2,1)}, u32[]{:S(2)}) copy-start(bf16[256,512]{1,0:T(8,128)(2,1)} %param.29) | copy-start | bytes 786436
  193.8 9.9 %copy-start.32 = (bf16[128,16]{0,1:T(8,128)(2,1)S(1)}, bf16[128,16]{0,1:T(8,128)(2,1)}, u32[]{:S(2)}) copy-start(bf16[128,16]{0,1:T(8,128)(2,1)} %get-tuple-element.85) | copy-start | bytes 12292
Sparse Core Ops, SparseCore 0:
  10.1 68.6 all-gather.5
  102.9 63.4 all-gather.3

commit v6 on v5

--- a/solution.py
+++ b/solution.py
@@ -134,8 +134,8 @@
     start = state is None
     state = () if start else state
     if finish:
-        shapes = jax.ShapeDtypeStruct((total_rows, 2 * HEAD), BF)
-        outs = pl.BlockSpec((rows, 2 * HEAD), lambda k: (k, 0))
+        shapes = jax.ShapeDtypeStruct((total_rows // rows, rows, 2 * HEAD), BF)
+        outs = pl.BlockSpec((None, rows, 2 * HEAD), lambda k: (k, 0, 0))
     else:
         shapes = (jax.ShapeDtypeStruct((total_rows, HEAD), F32),) * 3
         outs = (block,) * 3
@@ -222,9 +222,9 @@
             rising, falling, hidden, queries = lax.optimization_barrier(
                 (rising, falling, hidden, queries)
             )
-            hidden = to_everyone(hidden, (FAR, LINE, CORE))
-            hidden = hidden.reshape(2, line, 2, 2, share, units)
-            hidden = jnp.transpose(hidden, (1, 3, 0, 2, 4, 5)).reshape(-1, units)
+            hidden = to_everyone(hidden, (NEAR, FAR, LINE))
+            hidden = hidden.reshape(sides, line, 2, share, units)
+            hidden = jnp.transpose(hidden, (1, 2, 0, 3, 4)).reshape(-1, units)
         elif step == 2:
             rising, falling, hidden = lax.optimization_barrier((rising, falling, hidden))
     spots = jnp.stack([z * sides] + [k * sides + near * 2 + far for k in at]).astype(jnp.int32)
@@ -232,16 +232,15 @@
     state = attend(spots, queries, held[:-1], None, False)
     last, weights, hidden = lax.optimization_barrier((held[-1], weights, hidden))
     met = attend(jnp.concatenate([spots[:2], spots[-1:]]), queries, [last], state, True)
-    riders = lax.all_gather(hidden, (Z, NEAR), axis=0, tiled=True)
+    riders = lax.all_gather(hidden, Z, axis=0, tiled=True)
 
     local_whole = weights[:, :width].reshape(-1, columns)
     up_whole = unfold(weights[:, width : width + 8])
     up_whole = jnp.transpose(up_whole, (1, 0, 2)).reshape(RANK, -1)
     local_ups = unfold(weights[:, width + 8 :]).reshape(line, 2, RANK, units)
     local_ups = lax.dynamic_index_in_dim(local_ups, side, 1, keepdims=False)
-    local_ups = jnp.concatenate([local_ups[k] for k in range(line)], axis=1)
-
-    met = exchange(met.reshape(sides, chip_rows, 2 * HEAD), QUAD).astype(F32)
+
+    met = exchange(met, QUAD).astype(F32)
     levels = met[:, :, 128:129] + met[:, :, 160:161] + met[:, :, 192:193]
     parts = jnp.exp(levels - jnp.max(levels, axis=0, keepdims=True))
     merged = (parts * met[:, :, :HEAD]).sum(axis=0) / parts.sum(axis=0)
@@ -266,17 +265,17 @@
     own_ids = lax.dynamic_slice_in_dim(byte_ids, row_index * own_bytes, own_bytes)
     projected = contract(mixed_b, local_weight, 0, 0).astype(BF)
     projected = exchange(projected.reshape(row_count, own_patches, columns), ROW)
+    projected, riders = lax.optimization_barrier((projected, riders))
     projected = total(projected).astype(BF)
 
-    riders = riders.reshape(-1, line, 2, 4 * share, units)
-    riders = jnp.transpose(riders, (2, 1, 0, 3, 4)).reshape(2, line, columns, units)
-    rows_in, rows_out = (
-        jnp.concatenate([riders[way, k] for k in range(line)], axis=1) for way in range(2)
-    )
+    rest = lax.ppermute(riders, CORE, SWAP)
+    split = (ring, line, 2, sides, 1, share, units)
+    riders = in_pair_order(riders.reshape(split), rest.reshape(split), core, 4)
+    riders = jnp.transpose(riders, (2, 1, 0, 3, 4, 5, 6)).reshape(2, line, columns, units)
+    rows_in, rows_out = riders[0], riders[1]
     lanes = 128
-    stacked = jnp.concatenate(
-        [rows_in, local_ups, jnp.zeros((lanes - RANK, line * units), BF)], axis=0
-    )
+    spare_rows = jnp.zeros((line, lanes - RANK, units), BF)
+    stacked = jnp.concatenate([rows_in, local_ups, spare_rows], axis=1)
 
     picks = (own_ids[:, None] == jnp.arange(VOCAB, dtype=jnp.int32)[None, :]).astype(BF)
     embedded = jnp.dot(picks, byte_table, preferred_element_type=F32)
@@ -292,10 +291,12 @@
         [normed, shrunk, jnp.zeros((own_bytes, lanes - RANK), BF)], axis=1
     )
     joined = jnp.concatenate([joined, lax.ppermute(joined, SIDE, SWAP)], axis=0)
-    through = contract(cotangents, rows_out, 1, 0)
-    upper = contract(joined, stacked, 1, 0)
+    through = contract(cotangents, rows_out, 1, 1)
+    upper = contract(joined, stacked, 1, 1)
     grown = (through * gelu_slope(upper)).astype(BF)
-    back = contract(grown, stacked, 1, 1)
+    back = lax.dot_general(
+        grown, stacked, (((1, 2), (0, 2)), ((), ())), preferred_element_type=F32
+    )
     back = back[:own_bytes] + lax.ppermute(back[own_bytes:].astype(BF), SIDE, SWAP).astype(F32)
     ups = contract(joined[:, columns:], grown, 0, 0)[:RANK].astype(BF)
     back_norm = back[:, :columns]
@@ -317,7 +318,7 @@
     local_rows = jnp.concatenate([grad_local_down, local_rows, jnp.zeros_like(local_rows)])
     row_pack = jnp.concatenate([patch_grad, local_rows.astype(BF)], axis=0)
     row_pack = jnp.broadcast_to(row_pack[None], (row_count, *row_pack.shape))
-    ups = jnp.stack([ups[:, units * k : units * (k + 1)] for k in range(line)])
+    ups = jnp.transpose(ups, (1, 0, 2))
     ups = jnp.stack([jnp.where(side == k, ups, jnp.zeros_like(ups)) for k in range(2)], axis=1)
     ups = jnp.pad(ups.reshape(row_count, RANK, units), [(0, 0), (0, 0), (0, columns - units)])
     row_pack = exchange(jnp.concatenate([row_pack, ups], axis=1), ROW)

time: 268 us -> 254 us (0.948)
  blocking collectives: 71.9 us -> 54.6 us
  starting transfers between devices: 68.5 us -> 85.2 us
  waiting for transfers between devices: 33.5 us -> 48.1 us
  local copies, waits for them, and re-layouts: 30.1 us -> 16.8 us
  matrix products: 18.8 us -> 11.5 us
  other arithmetic: 16.6 us -> 9.32 us
    all_to_all x4, blocking collectives: 71.9 us -> 54.6 us  [exchange(): return lax.all_to_all(pieces, axis, split_axis=0, concat_axis=0, tiled=True)]
    all_gather x1, waiting for transfers between devices: 4.08 us -> 20.8 us  [body(): riders = lax.all_gather(hidden, Z, axis=0, tiled=True)]
    all_to_all x5, waiting for transfers between devices: 17.4 us -> 9.62 us  [exchange(): return lax.all_to_all(pieces, axis, split_axis=0, concat_axis=0, tiled=True)]
    all_to_all x5, starting transfers between devices: 20.1 us -> 25.6 us  [exchange(): return lax.all_to_all(pieces, axis, split_axis=0, concat_axis=0, tiled=True)]
    dot_general x12 -> x11, matrix products: 12.3 us -> 7.45 us  [contract(): lax.dot_general(left, right, (((left_dim,), (right_dim,)), ((), ())), pre...]
    ppermute x0 -> x1, starting transfers between devices: none -> 4.66 us  [body(): rest = lax.ppermute(riders, CORE, SWAP)]
    unnamed x91 -> x81, local copies, waits for them, and re-layouts: 6.17 us -> 2.07 us
    concatenate x1, other arithmetic: 4.09 us -> 0.08 us  [body(): joined = jnp.concatenate([joined, lax.ppermute(joined, SIDE, SWAP)], axis=0)]
  transfers between devices with their start and end apart: 19 -> 20, of which waited for: 11 -> 13; matrix products, arithmetic and copies ran while one was open for 16% -> 8% of each run, Pallas kernels for 3% -> 3%
where the time goes in v6:
time: 254 us; the launch traced here: 252 us
  starting transfers between devices  85.2 us (34%)
  blocking collectives  54.6 us (21%)
  waiting for transfers between devices  48.1 us (19%)
  local copies, waits for them, and re-layouts  16.8 us (7%)
  between operations  15.1 us (6%)
  Pallas kernels  11.8 us (5%)
  matrix products  11.5 us (5%)
  other arithmetic  9.32 us (4%)
    all_to_all x4, blocking collectives, exchange(): return lax.all_to_all(pieces, axis, split_axis=0, concat_axis=0, tiled=True)  54.6 us
    all_to_all x5, starting transfers between devices, exchange(): return lax.all_to_all(pieces, axis, split_axis=0, concat_axis=0, tiled=True)  25.6 us
    all_gather x1, waiting for transfers between devices, body(): riders = lax.all_gather(hidden, Z, axis=0, tiled=True)  20.8 us
    ppermute x3, starting transfers between devices, body(): falling = lax.ppermute(falling, Z, down)  15 us
    ppermute x4, starting transfers between devices, body(): rising = lax.ppermute(rising, Z, up)  13.6 us
    pallas_call x2, Pallas kernels, attend(): pl.pallas_call(functools.partial(attend_kernel, count=len(packets), start...  11.8 us
    all_to_all x5, waiting for transfers between devices, exchange(): return lax.all_to_all(pieces, axis, split_axis=0, concat_axis=0, tiled=True)  9.62 us
    ppermute x1, starting transfers between devices, body(): both = jnp.concatenate([mine, lax.ppermute(other, CORE, SWAP)], axis=0)  8.79 us
  transfers between devices with their start and end apart: 20, of which 13 were waited for; matrix products, arithmetic and copies ran while one was open for 8% of the time, Pallas kernels for 3%

profile of v6, /device:TPU:1, one launch (start us, length us, event | category | flops | bytes accessed | tf_op | source)
XLA Modules:
  0.0 252.4 jit_solution(6611966570932074344)
XLA Ops:
  7.2 0.8 fusion.56
  8.1 1.7 maximum_maximum_fusion.3
  9.8 0.8 constant_dynamic-slice_fusion.5
  10.6 0.8 constant_dynamic-slice_fusion.3
  11.4 8.8 %collective-permute-start = (bf16[128,384]{1,0:T(8,128)(2,1)S(1)}, bf16[128,384]{1,0:T(8,128)(2,1)S(1)}, u32[]{:S(2)}, u32[]{:S(2)}) collective-permute-start(bf16[128,384]{1,0:T(8,128)(2,1)S(1)} %pad_maximum_fusion.4), channel_id=1, source_target_pairs={{0,8},{8,0},{1,9},{9,1},{2,10},{10,2},{3,11},{11,3},{4,12},{12,4},... | collective-permute-start | bytes 294920 | tf_op jit(solution)/shard_map/ppermute | solution.py:201
  20.2 0.9 collective-permute-done
  21.2 0.7 broadcast_in_dim.23
  21.9 3.4 %all-to-all-start = ((bf16[4,256,128]{2,1,0:T(8,128)(2,1)}), bf16[4,256,128]{2,1,0:T(8,128)(2,1)S(1)}, u32[]{:S(2)}, u32[]{:S(2)}) async-start(bf16[4,256,128]{2,1,0:T(8,128)(2,1)} %broadcast_in_dim.23), calls=%async_computation | async-start | bytes 524288 | tf_op jit(solution)/shard_map/all_to_all | solution.py:30
  25.4 1.9 collective-permute-start.1
  27.3 7.2 %collective-permute-start.2 = (bf16[256,256]{1,0:T(8,128)(2,1)S(1)}, bf16[256,256]{1,0:T(8,128)(2,1)S(1)}, u32[]{:S(2)}, u32[]{:S(2)}) collective-permute-start(bf16[256,256]{1,0:T(8,128)(2,1)S(1)} %slice.232.refs_0_), channel_id=1, source_target_pairs={{0,448},{64,0},{128,64},{192,128},{256,192},{320,256},{384,320},{4... | collective-permute-start | bytes 393224 | tf_op jit(solution)/shard_map/ppermute | solution.py:218
  34.6 2.5 %collective-permute-done.1.refs_1_ = bf16[256,256]{1,0:T(8,128)(2,1)S(1)} collective-permute-done((bf16[256,256]{1,0:T(8,128)(2,1)S(1)}, bf16[256,256]{1,0:T(8,128)(2,1)S(1)}, u32[]{:S(2)}, u32[]{:S(2)}) %collective-permute-start.1) | collective-permute-done | bytes 131104 | tf_op jit(solution)/shard_map/ppermute | solution.py:214
  37.1 1.0 collective-permute-done.2.refs_2_
  38.2 0.7 broadcast_in_dim.24
  38.9 8.7 %all-to-all-start.1 = ((bf16[16,16,256]{2,1,0:T(8,128)(2,1)}), bf16[16,16,256]{2,1,0:T(8,128)(2,1)S(1)}, u32[]{:S(2)}, u32[]{:S(2)}) async-start(bf16[16,16,256]{2,1,0:T(8,128)(2,1)} %broadcast_in_dim.24), calls=%async_computation.1 | async-start | bytes 262144 | tf_op jit(solution)/shard_map/all_to_all | solution.py:30
  47.6 3.0 %collective-permute-start.3 = (bf16[256,256]{1,0:T(8,128)(2,1)S(1)}, bf16[256,256]{1,0:T(8,128)(2,1)S(1)}, u32[]{:S(2)}, u32[]{:S(2)}) collective-permute-start(bf16[256,256]{1,0:T(8,128)(2,1)S(1)} %collective-permute-done.1.refs_1_), channel_id=1, source_target_pairs={{0,64},{64,128},{128,192},{192,256},{256,320},{320,384},{384,448},... | collective-permute-start | bytes 393224 | tf_op jit(solution)/shard_map/ppermute | solution.py:214
  50.7 5.0 %collective-permute-start.4 = (bf16[256,256]{1,0:T(8,128)(2,1)S(1)}, bf16[256,256]{1,0:T(8,128)(2,1)S(1)}, u32[]{:S(2)}, u32[]{:S(2)}) collective-permute-start(bf16[256,256]{1,0:T(8,128)(2,1)S(1)} %collective-permute-done.2.refs_2_), channel_id=1, source_target_pairs={{0,448},{64,0},{128,64},{192,128},{256,192},{320,256},{384,320},{4... | collective-permute-start | bytes 393224 | tf_op jit(solution)/shard_map/ppermute | solution.py:218
  55.7 0.7 copy.97
  56.4 0.9 collective-permute-done.3.refs_3_
  57.3 3.3 %collective-permute-done.4.refs_4_ = bf16[256,256]{1,0:T(8,128)(2,1)S(1)} collective-permute-done((bf16[256,256]{1,0:T(8,128)(2,1)S(1)}, bf16[256,256]{1,0:T(8,128)(2,1)S(1)}, u32[]{:S(2)}, u32[]{:S(2)}) %collective-permute-start.4) | collective-permute-done | bytes 131104 | tf_op jit(solution)/shard_map/ppermute | solution.py:218
  60.6 4.6 %collective-permute-start.5 = (bf16[256,256]{1,0:T(8,128)(2,1)S(1)}, bf16[256,256]{1,0:T(8,128)(2,1)S(1)}, u32[]{:S(2)}, u32[]{:S(2)}) collective-permute-start(bf16[256,256]{1,0:T(8,128)(2,1)S(1)} %collective-permute-done.3.refs_3_), channel_id=1, source_target_pairs={{0,64},{64,128},{128,192},{192,256},{256,320},{320,384},{384,448},... | collective-permute-start | bytes 393224 | tf_op jit(solution)/shard_map/ppermute | solution.py:214
  65.2 2.8 %collective-permute-start.7 = (bf16[256,256]{1,0:T(8,128)(2,1)S(1)}, bf16[256,256]{1,0:T(8,128)(2,1)S(1)}, u32[]{:S(2)}, u32[]{:S(2)}) collective-permute-start(bf16[256,256]{1,0:T(8,128)(2,1)S(1)} %collective-permute-done.4.refs_4_), channel_id=1, source_target_pairs={{0,448},{64,0},{128,64},{192,128},{256,192},{320,256},{384,320},{4... | collective-permute-start | bytes 393224 | tf_op jit(solution)/shard_map/ppermute | solution.py:218
  68.5 4.1 %collective-permute-start.6 = (bf16[256,256]{1,0:T(8,128)(2,1)S(1)}, bf16[256,256]{1,0:T(8,128)(2,1)S(1)}, u32[]{:S(2)}, u32[]{:S(2)}) collective-permute-start(bf16[256,256]{1,0:T(8,128)(2,1)S(1)} %collective-permute-done.5.refs_5_), channel_id=1, source_target_pairs={{0,64},{64,128},{128,192},{192,256},{256,320},{320,384},{384,448},... | collective-permute-start | bytes 393224 | tf_op jit(solution)/shard_map/ppermute | solution.py:214
  74.0 0.7 copy-done.12
  74.7 7.1 %attend.2 = (f32[1024,128]{1,0:T(8,128)}, f32[1024,128]{1,0:T(8,128)}, f32[1024,128]{1,0:T(8,128)}) custom-call(s32[10]{0:T(128)} %concatenate.100.spots, bf16[1024,128]{1,0:T(8,128)(2,1)} %bitcast.115, bf16[256,256]{1,0:T(8,128)(2,1)} %copy-done.5, bf16[256,256]{1,0:T(8,128)(2,1)} %copy-done.7, bf16[256,256]{1,0:T(8,128)(2,1)} %copy-done.8, ...), custom_call_target="tpu_custom_call" | custom-call | tf_op jit(solution)/shard_map/attend/pallas_call | solution.py:142
  82.4 4.7 %attend.3 = bf16[4,256,256]{2,1,0:T(8,128)(2,1)} custom-call(s32[3]{0:T(128)} %pad_add_fusion.spots, bf16[1024,128]{1,0:T(8,128)(2,1)} %bitcast.116, bf16[256,256]{1,0:T(8,128)(2,1)} %copy-done.16, f32[1024,128]{1,0:T(8,128)} %get-tuple-element.29.refs_1_, f32[1024,128]{1,0:T(8,128)} %get-tuple-element.30.refs_2_, f32[1024,128]{1,0:T(8,128)} %get-tuple-element.31.refs_3_), custom_call_target="tpu_custom_call" | custom-call | tf_op jit(solution)/shard_map/attend/pallas_call | solution.py:142
  87.1 14.0 %all_to_all.45 = bf16[4,256,256]{2,1,0:T(8,128)(2,1)S(1)} all-to-all(bf16[4,256,256]{2,1,0:T(8,128)(2,1)} %attend.3), channel_id=1, replica_groups=mesh['seq_0'=8,'near'=2,'seq_1'=2,'seq_2'=2,'row_0'=4,'row_1'=2] {'near'..., dimensions={0} | all-to-all | bytes 1048576 | tf_op jit(solution)/shard_map/all_to_all | solution.py:30
  102.3 7.1 %collective-permute-start.8 = (bf16[128,128]{1,0:T(8,128)(2,1)S(1)}, bf16[128,128]{1,0:T(8,128)(2,1)S(1)}, u32[]{:S(2)}, u32[]{:S(2)}) collective-permute-start(bf16[128,128]{1,0:T(8,128)(2,1)S(1)} %slice.238), channel_id=1, source_target_pairs={{0,8},{8,0},{1,9},{9,1},{2,10},{10,2},{3,11},{11,3},{4,12},{12,4},... | collective-permute-start | bytes 98312 | tf_op jit(solution)/shard_map/ppermute | solution.py:248
  109.5 0.8 collective-permute-done.8
  111.1 0.9 pad_maximum_fusion
  112.0 5.3 %all-to-all-start.3 = ((bf16[8,272,128]{2,1,0:T(8,128)(2,1)}), bf16[8,272,128]{2,1,0:T(8,128)(2,1)S(1)}, u32[]{:S(2)}, u32[]{:S(2)}) async-start(bf16[8,272,128]{2,1,0:T(8,128)(2,1)} %pad_maximum_fusion), calls=%async_computation.3 | async-start | bytes 1114112 | tf_op jit(solution)/shard_map/all_to_all | solution.py:30
  117.4 3.5 %collective-permute-start.9 = (bf16[128,512]{1,0:T(8,128)(2,1)S(1)}, bf16[128,512]{1,0:T(8,128)(2,1)}, u32[]{:S(2)}, u32[]{:S(2)}) collective-permute-start(bf16[128,512]{1,0:T(8,128)(2,1)S(1)} %copy-done.15), channel_id=1, source_target_pairs={{0,1},{1,0},{2,3},{3,2},{4,5},{5,4},{6,7},{7,6},{8,9},{9,8},{10,11... | collective-permute-start | bytes 393224 | tf_op jit(solution)/shard_map/ppermute | solution.py:193
  121.6 0.7 pad.25.clone
  122.8 0.8 dynamic_slice.28
  123.6 3.8 %all-to-all-done.3 = bf16[8,272,128]{2,1,0:T(8,128)(2,1)S(1)} async-done(((bf16[8,272,128]{2,1,0:T(8,128)(2,1)}), bf16[8,272,128]{2,1,0:T(8,128)(2,1)S(1)}, u32[]{:S(2)}, u32[]{:S(2)}) %all-to-all-start.3) | async-done | bytes 557088 | tf_op jit(solution)/shard_map/all_to_all | solution.py:30
  127.6 0.9 multiply_convert_fusion.4
  128.5 1.0 convolution_convert_fusion.2
  129.5 3.4 %all-to-all-start.4 = ((bf16[8,16,512]{2,1,0:T(8,128)(2,1)}), bf16[8,16,512]{2,1,0:T(8,128)(2,1)S(1)}, u32[]{:S(2)}, u32[]{:S(2)}) async-start(bf16[8,16,512]{2,1,0:T(8,128)(2,1)} %bitcast.24), calls=%async_computation.4 | async-start | bytes 262144 | tf_op jit(solution)/shard_map/all_to_all | solution.py:30
  132.8 0.9 fusion.52
  133.7 20.8 %all-gather.4.cloned.1.call-done = bf16[2048,256]{1,0:T(8,128)(2,1)} async-done(((bf16[256,256]{1,0:T(8,128)(2,1)}), bf16[2048,256]{1,0:T(8,128)(2,1)}) %all-gather.4.cloned.1.call-update) | async-done | bytes 1048592 | tf_op jit(solution)/shard_map/all_gather | solution.py:235
  154.5 4.7 %collective-permute-start.10 = (bf16[2048,256]{1,0:T(8,128)(2,1)}, bf16[2048,256]{1,0:T(8,128)(2,1)}, u32[]{:S(2)}, u32[]{:S(2)}) collective-permute-start(bf16[2048,256]{1,0:T(8,128)(2,1)} %all-gather.4.cloned.1.call-done), channel_id=1, source_target_pairs={{0,8},{8,0},{1,9},{9,1},{2,10},{10,2},{3,11},{11,3},{4,12},{12,4},... | collective-permute-start | bytes 3145736 | tf_op jit(solution)/shard_map/ppermute | solution.py:271
  159.7 0.8 multiply_convert_fusion.3
  160.7 3.7 %collective-permute-start.11 = (bf16[128,640]{1,0:T(8,128)(2,1)S(1)}, bf16[128,640]{1,0:T(8,128)(2,1)S(1)}, u32[]{:S(2)}, u32[]{:S(2)}) collective-permute-start(bf16[128,640]{1,0:T(8,128)(2,1)S(1)} %pad_maximum_fusion.3), channel_id=1, source_target_pairs={{0,1},{1,0},{2,3},{3,2},{4,5},{5,4},{6,7},{7,6},{8,9},{9,8},{10,11... | collective-permute-start | bytes 491528 | tf_op jit(solution)/shard_map/ppermute | solution.py:293
  164.4 0.8 copy.105
  165.2 3.7 %collective-permute-done.11 = bf16[128,640]{1,0:T(8,128)(2,1)S(1)} collective-permute-done((bf16[128,640]{1,0:T(8,128)(2,1)S(1)}, bf16[128,640]{1,0:T(8,128)(2,1)S(1)}, u32[]{:S(2)}, u32[]{:S(2)}) %collective-permute-start.11) | collective-permute-done | bytes 163872 | tf_op jit(solution)/shard_map/ppermute | solution.py:293
  169.0 1.4 broadcast_select_fusion.1
  171.5 0.7 fusion.16
  172.2 1.5 fusion.1
  173.7 0.7 convolution_bitcast_fusion
  174.7 3.2 %collective-permute-start.12 = (bf16[128,640]{1,0:T(8,128)(2,1)S(1)}, bf16[128,640]{1,0:T(8,128)(2,1)S(1)}, u32[]{:S(2)}, u32[]{:S(2)}) collective-permute-start(bf16[128,640]{1,0:T(8,128)(2,1)S(1)} %slice.305), channel_id=1, source_target_pairs={{0,1},{1,0},{2,3},{3,2},{4,5},{5,4},{6,7},{7,6},{8,9},{9,8},{10,11... | collective-permute-start | bytes 491528 | tf_op jit(solution)/shard_map/ppermute | solution.py:300
  177.9 3.8 %collective-permute-done.12 = bf16[128,640]{1,0:T(8,128)(2,1)S(1)} collective-permute-done((bf16[128,640]{1,0:T(8,128)(2,1)S(1)}, bf16[128,640]{1,0:T(8,128)(2,1)S(1)}, u32[]{:S(2)}, u32[]{:S(2)}) %collective-permute-start.12) | collective-permute-done | bytes 163872 | tf_op jit(solution)/shard_map/ppermute | solution.py:300
  182.9 0.8 fusion.19
  183.8 4.8 %all-to-all-start.5 = ((bf16[8,64,512]{2,1,0:T(8,128)(2,1)}), bf16[8,64,512]{2,1,0:T(8,128)(2,1)}, u32[]{:S(2)}, u32[]{:S(2)}) async-start(bf16[8,64,512]{2,1,0:T(8,128)(2,1)} %fusion.19), calls=%async_computation.5 | async-start | bytes 1048576 | tf_op jit(solution)/shard_map/all_to_all | solution.py:30
  188.6 1.8 slice.215
  190.4 0.6 copy.117
  191.1 5.8 %all-to-all-done.5 = bf16[8,64,512]{2,1,0:T(8,128)(2,1)} async-done(((bf16[8,64,512]{2,1,0:T(8,128)(2,1)}), bf16[8,64,512]{2,1,0:T(8,128)(2,1)}, u32[]{:S(2)}, u32[]{:S(2)}) %all-to-all-start.5) | async-done | bytes 524320 | tf_op jit(solution)/shard_map/all_to_all | solution.py:30
  196.8 0.9 slice.249
  197.7 1.9 fusion.2
  199.6 0.9 convolution_convert_fusion.7
  200.6 0.9 fusion.7
  201.9 1.1 convert_reduce_fusion.1
  203.0 12.0 %all_to_all.46 = bf16[8,12,256]{2,1,0:T(8,128)(2,1)S(1)} all-to-all(bf16[8,12,256]{2,1,0:T(8,128)(2,1)S(1)} %convert_element_type.134), channel_id=1, replica_groups=mesh['seq_0'=8,'near'=2,'seq_1'=2,'seq_2'=2,'row_0'=4,'row_1'=2] {'near'..., dimensions={0} | all-to-all | bytes 98304 | tf_op jit(solution)/shard_map/all_to_all | solution.py:30
  215.0 18.1 %all_to_all.47 = bf16[8,12,256]{2,1,0:T(8,128)(2,1)S(1)} all-to-all(bf16[8,12,256]{2,1,0:T(8,128)(2,1)S(1)} %broadcast_in_dim.31), channel_id=1, replica_groups=mesh['seq_0'=8,'near'=2,'seq_1'=2,'seq_2'=2,'row_0'=4,'row_1'=2] {'seq_0'}, dimensions={0} | all-to-all | bytes 98304 | tf_op jit(solution)/shard_map/all_to_all | solution.py:30
  233.2 10.5 %all_to_all.48 = bf16[8,12,256]{2,1,0:T(8,128)(2,1)S(1)} all-to-all(bf16[8,12,256]{2,1,0:T(8,128)(2,1)S(1)} %broadcast_in_dim.32), channel_id=1, replica_groups=mesh['seq_0'=8,'near'=2,'seq_1'=2,'seq_2'=2,'row_0'=4,'row_1'=2] {'near'..., dimensions={0} | all-to-all | bytes 98304 | tf_op jit(solution)/shard_map/all_to_all | solution.py:30
  243.7 0.6 fusion.55
  (162 shorter events, 10.9 us)
Async XLA Ops:
  7.2 103.1 %copy-start = (bf16[256,2048]{1,0:T(8,128)(2,1)S(1)}, bf16[256,2048]{1,0:T(8,128)(2,1)}, u32[]{:S(2)}) copy-start(bf16[256,2048]{1,0:T(8,128)(2,1)} %param.25) | copy-start | bytes 3145732
  7.2 27.4 %copy-start.25 = (bf16[256,8]{0,1:T(8,128)(2,1)S(1)}, bf16[256,8]{0,1:T(8,128)(2,1)}, u32[]{:S(2)}) copy-start(bf16[256,8]{0,1:T(8,128)(2,1)} %param.35) | copy-start | bytes 12292
  7.2 27.4 %copy-start.26 = (bf16[256,8]{0,1:T(8,128)(2,1)S(1)}, bf16[256,8]{0,1:T(8,128)(2,1)}, u32[]{:S(2)}) copy-start(bf16[256,8]{0,1:T(8,128)(2,1)} %param.34) | copy-start | bytes 12292
  7.2 74.6 %all-gather.6.cloned.1.call-start = ((), (), s32[]{:S(2)}) async-start(), calls=%async_computation.10 | async-start | bytes 2506752 | tf_op jit(solution)/shard_map/all_gather | solution.py:192
  11.4 9.7 %collective-permute-start = (bf16[128,384]{1,0:T(8,128)(2,1)S(1)}, bf16[128,384]{1,0:T(8,128)(2,1)S(1)}, u32[]{:S(2)}, u32[]{:S(2)}) collective-permute-start(bf16[128,384]{1,0:T(8,128)(2,1)S(1)} %pad_maximum_fusion.4), channel_id=1, source_target_pairs={{0,8},{8,0},{1,9},{9,1},{2,10},{10,2},{3,11},{11,3},{4,12},{12,4},... | collective-permute-start | bytes 294920 | tf_op jit(solution)/shard_map/ppermute | solution.py:201
  21.9 16.3 %all-to-all-start = ((bf16[4,256,128]{2,1,0:T(8,128)(2,1)}), bf16[4,256,128]{2,1,0:T(8,128)(2,1)S(1)}, u32[]{:S(2)}, u32[]{:S(2)}) async-start(bf16[4,256,128]{2,1,0:T(8,128)(2,1)} %broadcast_in_dim.23), calls=%async_computation | async-start | bytes 524288 | tf_op jit(solution)/shard_map/all_to_all | solution.py:30
  25.4 48.6 %copy-start.5 = (bf16[256,256]{1,0:T(8,128)(2,1)}, bf16[256,256]{1,0:T(8,128)(2,1)S(1)}, u32[]{:S(2)}) copy-start(bf16[256,256]{1,0:T(8,128)(2,1)S(1)} %slice.232.refs_0_) | copy-start | bytes 393220
  25.4 11.7 %collective-permute-start.1 = (bf16[256,256]{1,0:T(8,128)(2,1)S(1)}, bf16[256,256]{1,0:T(8,128)(2,1)S(1)}, u32[]{:S(2)}, u32[]{:S(2)}) collective-permute-start(bf16[256,256]{1,0:T(8,128)(2,1)S(1)} %slice.232.refs_0_), channel_id=1, source_target_pairs={{0,64},{64,128},{128,192},{192,256},{256,320},{320,384},{384,448},... | collective-permute-start | bytes 393224 | tf_op jit(solution)/shard_map/ppermute | solution.py:214
  27.3 10.9 %collective-permute-start.2 = (bf16[256,256]{1,0:T(8,128)(2,1)S(1)}, bf16[256,256]{1,0:T(8,128)(2,1)S(1)}, u32[]{:S(2)}, u32[]{:S(2)}) collective-permute-start(bf16[256,256]{1,0:T(8,128)(2,1)S(1)} %slice.232.refs_0_), channel_id=1, source_target_pairs={{0,448},{64,0},{128,64},{192,128},{256,192},{320,256},{384,320},{4... | collective-permute-start | bytes 393224 | tf_op jit(solution)/shard_map/ppermute | solution.py:218
  37.1 36.8 %copy-start.7 = (bf16[256,256]{1,0:T(8,128)(2,1)}, bf16[256,256]{1,0:T(8,128)(2,1)S(1)}, u32[]{:S(2)}) copy-start(bf16[256,256]{1,0:T(8,128)(2,1)S(1)} %collective-permute-done.1.refs_1_) | copy-start | bytes 393220
  38.2 35.8 %copy-start.8 = (bf16[256,256]{1,0:T(8,128)(2,1)}, bf16[256,256]{1,0:T(8,128)(2,1)S(1)}, u32[]{:S(2)}) copy-start(bf16[256,256]{1,0:T(8,128)(2,1)S(1)} %collective-permute-done.2.refs_2_) | copy-start | bytes 393220
  38.2 35.8 %copy-start.2 = (bf16[4,256,128]{2,1,0:T(8,128)(2,1)}, bf16[4,256,128]{2,1,0:T(8,128)(2,1)S(1)}, u32[]{:S(2)}) copy-start(bf16[4,256,128]{2,1,0:T(8,128)(2,1)S(1)} %all-to-all-done) | copy-start | bytes 786436
  38.9 16.8 %all-to-all-start.1 = ((bf16[16,16,256]{2,1,0:T(8,128)(2,1)}), bf16[16,16,256]{2,1,0:T(8,128)(2,1)S(1)}, u32[]{:S(2)}, u32[]{:S(2)}) async-start(bf16[16,16,256]{2,1,0:T(8,128)(2,1)} %broadcast_in_dim.24), calls=%async_computation.1 | async-start | bytes 262144 | tf_op jit(solution)/shard_map/all_to_all | solution.py:30
  47.6 106.9 %all-gather.4.cloned.1.call-start = ((), (), s32[]{:S(2)}) async-start(), calls=%async_computation.9 | async-start | bytes 1179648 | tf_op jit(solution)/shard_map/all_gather | solution.py:235
  47.6 9.7 %collective-permute-start.3 = (bf16[256,256]{1,0:T(8,128)(2,1)S(1)}, bf16[256,256]{1,0:T(8,128)(2,1)S(1)}, u32[]{:S(2)}, u32[]{:S(2)}) collective-permute-start(bf16[256,256]{1,0:T(8,128)(2,1)S(1)} %collective-permute-done.1.refs_1_), channel_id=1, source_target_pairs={{0,64},{64,128},{128,192},{192,256},{256,320},{320,384},{384,448},... | collective-permute-start | bytes 393224 | tf_op jit(solution)/shard_map/ppermute | solution.py:214
  50.7 9.9 %collective-permute-start.4 = (bf16[256,256]{1,0:T(8,128)(2,1)S(1)}, bf16[256,256]{1,0:T(8,128)(2,1)S(1)}, u32[]{:S(2)}, u32[]{:S(2)}) collective-permute-start(bf16[256,256]{1,0:T(8,128)(2,1)S(1)} %collective-permute-done.2.refs_2_), channel_id=1, source_target_pairs={{0,448},{64,0},{128,64},{192,128},{256,192},{320,256},{384,320},{4... | collective-permute-start | bytes 393224 | tf_op jit(solution)/shard_map/ppermute | solution.py:218
  57.3 16.7 %copy-start.9 = (bf16[256,256]{1,0:T(8,128)(2,1)}, bf16[256,256]{1,0:T(8,128)(2,1)S(1)}, u32[]{:S(2)}) copy-start(bf16[256,256]{1,0:T(8,128)(2,1)S(1)} %collective-permute-done.3.refs_3_) | copy-start | bytes 393220
  60.6 13.4 %copy-start.10 = (bf16[256,256]{1,0:T(8,128)(2,1)}, bf16[256,256]{1,0:T(8,128)(2,1)S(1)}, u32[]{:S(2)}) copy-start(bf16[256,256]{1,0:T(8,128)(2,1)S(1)} %collective-permute-done.4.refs_4_) | copy-start | bytes 393220
  60.6 7.9 %collective-permute-start.5 = (bf16[256,256]{1,0:T(8,128)(2,1)S(1)}, bf16[256,256]{1,0:T(8,128)(2,1)S(1)}, u32[]{:S(2)}, u32[]{:S(2)}) collective-permute-start(bf16[256,256]{1,0:T(8,128)(2,1)S(1)} %collective-permute-done.3.refs_3_), channel_id=1, source_target_pairs={{0,64},{64,128},{128,192},{192,256},{256,320},{320,384},{384,448},... | collective-permute-start | bytes 393224 | tf_op jit(solution)/shard_map/ppermute | solution.py:214
  65.2 8.8 %collective-permute-start.7 = (bf16[256,256]{1,0:T(8,128)(2,1)S(1)}, bf16[256,256]{1,0:T(8,128)(2,1)S(1)}, u32[]{:S(2)}, u32[]{:S(2)}) collective-permute-start(bf16[256,256]{1,0:T(8,128)(2,1)S(1)} %collective-permute-done.4.refs_4_), channel_id=1, source_target_pairs={{0,448},{64,0},{128,64},{192,128},{256,192},{320,256},{384,320},{4... | collective-permute-start | bytes 393224 | tf_op jit(solution)/shard_map/ppermute | solution.py:218
  68.5 5.5 %copy-start.11 = (bf16[256,256]{1,0:T(8,128)(2,1)}, bf16[256,256]{1,0:T(8,128)(2,1)S(1)}, u32[]{:S(2)}) copy-start(bf16[256,256]{1,0:T(8,128)(2,1)S(1)} %collective-permute-done.5.refs_5_) | copy-start | bytes 393220
  68.5 13.2 %collective-permute-start.6 = (bf16[256,256]{1,0:T(8,128)(2,1)S(1)}, bf16[256,256]{1,0:T(8,128)(2,1)S(1)}, u32[]{:S(2)}, u32[]{:S(2)}) collective-permute-start(bf16[256,256]{1,0:T(8,128)(2,1)S(1)} %collective-permute-done.5.refs_5_), channel_id=1, source_target_pairs={{0,64},{64,128},{128,192},{192,256},{256,320},{320,384},{384,448},... | collective-permute-start | bytes 393224 | tf_op jit(solution)/shard_map/ppermute | solution.py:214
  74.0 0.7 copy-start.12
  81.7 0.6 copy-start.16
  101.6 9.4 %copy-start.33 = (bf16[256,16]{0,1:T(8,128)(2,1)S(1)}, bf16[256,16]{0,1:T(8,128)(2,1)}, u32[]{:S(2)}) copy-start(bf16[256,16]{0,1:T(8,128)(2,1)} %param.26) | copy-start | bytes 24580
  102.3 7.9 %collective-permute-start.8 = (bf16[128,128]{1,0:T(8,128)(2,1)S(1)}, bf16[128,128]{1,0:T(8,128)(2,1)S(1)}, u32[]{:S(2)}, u32[]{:S(2)}) collective-permute-start(bf16[128,128]{1,0:T(8,128)(2,1)S(1)} %slice.238), channel_id=1, source_target_pairs={{0,8},{8,0},{1,9},{9,1},{2,10},{10,2},{3,11},{11,3},{4,12},{12,4},... | collective-permute-start | bytes 98312 | tf_op jit(solution)/shard_map/ppermute | solution.py:248
  110.3 1.8 copy-start.13
  110.3 1.7 copy-start.14
  110.6 6.8 %copy-start.15 = (bf16[128,512]{1,0:T(8,128)(2,1)S(1)}, bf16[128,512]{1,0:T(8,128)(2,1)}, u32[]{:S(2)}) copy-start(bf16[128,512]{1,0:T(8,128)(2,1)} %param.39) | copy-start | bytes 393220
  110.6 10.3 %copy-start.36 = (s32[128]{0:T(128)S(1)}, s32[128]{0:T(128)}, u32[]{:S(2)}) copy-start(s32[128]{0:T(128)} %param.23) | copy-start | bytes 1540
  110.6 10.5 %copy-start.24 = (bf16[8,512]{1,0:T(8,128)(2,1)S(1)}, bf16[8,512]{1,0:T(8,128)(2,1)}, u32[]{:S(2)}) copy-start(bf16[8,512]{1,0:T(8,128)(2,1)} %param.32) | copy-start | bytes 24580
  110.7 10.5 %copy-start.34 = (f32[8,16]{1,0:T(8,128)S(1)}, f32[8,16]{1,0:T(8,128)}, u32[]{:S(2)}) copy-start(f32[8,16]{1,0:T(8,128)} %param.38) | copy-start | bytes 1540
  111.0 16.6 %copy-start.35 = (f32[8,16]{1,0:T(8,128)S(1)}, f32[8,16]{1,0:T(8,128)}, u32[]{:S(2)}) copy-start(f32[8,16]{1,0:T(8,128)} %param.28) | copy-start | bytes 1540
  111.0 17.5 %copy-start.1 = (bf16[256,512]{1,0:T(8,128)(2,1)S(1)}, bf16[256,512]{1,0:T(8,128)(2,1)}, u32[]{:S(2)}) copy-start(bf16[256,512]{1,0:T(8,128)(2,1)} %param.29) | copy-start | bytes 786436
  111.0 17.5 %copy-start.17 = (bf16[128,256]{1,0:T(8,128)(2,1)S(1)}, bf16[128,256]{1,0:T(8,128)(2,1)}, u32[]{:S(2)}) copy-start(bf16[128,256]{1,0:T(8,128)(2,1)} %param.24) | copy-start | bytes 196612
  111.0 17.5 %copy-start.19 = (bf16[16,256]{1,0:T(8,128)(2,1)S(1)}, bf16[16,256]{1,0:T(8,128)(2,1)}, u32[]{:S(2)}) copy-start(bf16[16,256]{1,0:T(8,128)(2,1)} %param.27) | copy-start | bytes 24580
  112.0 47.2 %copy-start.6 = (bf16[256,512]{1,0:T(8,128)(2,1)S(1)}, bf16[256,512]{1,0:T(8,128)(2,1)}, u32[]{:S(2)}) copy-start(bf16[256,512]{1,0:T(8,128)(2,1)} %param.31) | copy-start | bytes 786436
  112.0 47.5 %copy-start.20 = (f32[512]{0:T(512)S(1)}, f32[512]{0:T(512)}, u32[]{:S(2)}) copy-start(f32[512]{0:T(512)} %param.33) | copy-start | bytes 6148
  112.0 15.3 %all-to-all-start.3 = ((bf16[8,272,128]{2,1,0:T(8,128)(2,1)}), bf16[8,272,128]{2,1,0:T(8,128)(2,1)S(1)}, u32[]{:S(2)}, u32[]{:S(2)}) async-start(bf16[8,272,128]{2,1,0:T(8,128)(2,1)} %pad_maximum_fusion), calls=%async_computation.3 | async-start | bytes 1114112 | tf_op jit(solution)/shard_map/all_to_all | solution.py:30
  117.4 42.3 %copy-start.18 = (bf16[512,16]{0,1:T(8,128)(2,1)S(1)}, bf16[512,16]{0,1:T(8,128)(2,1)}, u32[]{:S(2)}) copy-start(bf16[512,16]{0,1:T(8,128)(2,1)} %param.36) | copy-start | bytes 49156
  117.4 54.8 %collective-permute-start.9 = (bf16[128,512]{1,0:T(8,128)(2,1)S(1)}, bf16[128,512]{1,0:T(8,128)(2,1)}, u32[]{:S(2)}, u32[]{:S(2)}) collective-permute-start(bf16[128,512]{1,0:T(8,128)(2,1)S(1)} %copy-done.15), channel_id=1, source_target_pairs={{0,1},{1,0},{2,3},{3,2},{4,5},{5,4},{6,7},{7,6},{8,9},{9,8},{10,11... | collective-permute-start | bytes 393224 | tf_op jit(solution)/shard_map/ppermute | solution.py:193
  121.2 6.3 %copy-start.29 = (s32[128]{0:T(128)}, s32[128]{0:T(128)S(1)}, u32[]{:S(2)}) copy-start(s32[128]{0:T(128)S(1)} %eq.41) | copy-start | bytes 1540
  127.4 6.2 %copy-start.4 = (f32[272,128]{1,0:T(8,128)}, f32[272,128]{1,0:T(8,128)S(1)}, u32[]{:S(2)}) copy-start(f32[272,128]{1,0:T(8,128)S(1)} %convert_reduce_fusion) | copy-start | bytes 417796
  128.5 32.1 %copy-start.22 = (bf16[128,16]{0,1:T(8,128)(2,1)}, bf16[128,16]{0,1:T(8,128)(2,1)S(1)}, u32[]{:S(2)}) copy-start(bf16[128,16]{0,1:T(8,128)(2,1)S(1)} %get-tuple-element.77) | copy-start | bytes 12292
  129.5 25.1 %all-to-all-start.4 = ((bf16[8,16,512]{2,1,0:T(8,128)(2,1)}), bf16[8,16,512]{2,1,0:T(8,128)(2,1)S(1)}, u32[]{:S(2)}, u32[]{:S(2)}) async-start(bf16[8,16,512]{2,1,0:T(8,128)(2,1)} %bitcast.24), calls=%async_computation.4 | async-start | bytes 262144 | tf_op jit(solution)/shard_map/all_to_all | solution.py:30
  154.5 14.5 %copy-start.3 = (bf16[2048,256]{1,0:T(8,128)(2,1)S(1)}, bf16[2048,256]{1,0:T(8,128)(2,1)}, u32[]{:S(2)}) copy-start(bf16[2048,256]{1,0:T(8,128)(2,1)} %all-gather.4.cloned.1.call-done) | copy-start | bytes 3145732
  154.5 14.5 %collective-permute-start.10 = (bf16[2048,256]{1,0:T(8,128)(2,1)}, bf16[2048,256]{1,0:T(8,128)(2,1)}, u32[]{:S(2)}, u32[]{:S(2)}) collective-permute-start(bf16[2048,256]{1,0:T(8,128)(2,1)} %all-gather.4.cloned.1.call-done), channel_id=1, source_target_pairs={{0,8},{8,0},{1,9},{9,1},{2,10},{10,2},{3,11},{11,3},{4,12},{12,4},... | collective-permute-start | bytes 3145736 | tf_op jit(solution)/shard_map/ppermute | solution.py:271
  159.6 0.9 copy-start.27
  160.7 8.2 %collective-permute-start.11 = (bf16[128,640]{1,0:T(8,128)(2,1)S(1)}, bf16[128,640]{1,0:T(8,128)(2,1)S(1)}, u32[]{:S(2)}, u32[]{:S(2)}) collective-permute-start(bf16[128,640]{1,0:T(8,128)(2,1)S(1)} %pad_maximum_fusion.3), channel_id=1, source_target_pairs={{0,1},{1,0},{2,3},{3,2},{4,5},{5,4},{6,7},{7,6},{8,9},{9,8},{10,11... | collective-permute-start | bytes 491528 | tf_op jit(solution)/shard_map/ppermute | solution.py:293
  170.8 0.7 copy-start.31
  174.4 7.6 %copy-start.21 = (f32[512]{0:T(512)S(1)}, f32[512]{0:T(512)}, u32[]{:S(2)}) copy-start(f32[512]{0:T(512)} %param.33) | copy-start | bytes 6148
  174.4 7.9 %copy-start.30 = (s32[128]{0:T(128)S(1)}, s32[128]{0:T(128)}, u32[]{:S(2)}) copy-start(s32[128]{0:T(128)} %copy-done.29) | copy-start | bytes 1540
  174.4 8.1 %copy-start.28 = (f32[128]{0:T(128)S(1)}, f32[128]{0:T(128)}, u32[]{:S(2)}) copy-start(f32[128]{0:T(128)} %copy-done.27) | copy-start | bytes 1540
  174.7 8.1 %copy-start.32 = (bf16[48]{0:T(256)(128)(2,1)S(1)}, bf16[48]{0:T(256)(128)(2,1)}, u32[]{:S(2)}) copy-start(bf16[48]{0:T(256)(128)(2,1)} %pad.22.clone) | copy-start | bytes 292
  174.7 7.1 %collective-permute-start.12 = (bf16[128,640]{1,0:T(8,128)(2,1)S(1)}, bf16[128,640]{1,0:T(8,128)(2,1)S(1)}, u32[]{:S(2)}, u32[]{:S(2)}) collective-permute-start(bf16[128,640]{1,0:T(8,128)(2,1)S(1)} %slice.305), channel_id=1, source_target_pairs={{0,1},{1,0},{2,3},{3,2},{4,5},{5,4},{6,7},{7,6},{8,9},{9,8},{10,11... | collective-permute-start | bytes 491528 | tf_op jit(solution)/shard_map/ppermute | solution.py:300
  183.8 13.1 %all-to-all-start.5 = ((bf16[8,64,512]{2,1,0:T(8,128)(2,1)}), bf16[8,64,512]{2,1,0:T(8,128)(2,1)}, u32[]{:S(2)}, u32[]{:S(2)}) async-start(bf16[8,64,512]{2,1,0:T(8,128)(2,1)} %fusion.19), calls=%async_computation.5 | async-start | bytes 1048576 | tf_op jit(solution)/shard_map/all_to_all | solution.py:30
  190.4 9.2 %copy-start.37 = (s32[128]{0:T(128)S(1)}, s32[128]{0:T(128)}, u32[]{:S(2)}) copy-start(s32[128]{0:T(128)} %param.23) | copy-start | bytes 1540
  190.4 11.1 %copy-start.23 = (bf16[128,16]{0,1:T(8,128)(2,1)S(1)}, bf16[128,16]{0,1:T(8,128)(2,1)}, u32[]{:S(2)}) copy-start(bf16[128,16]{0,1:T(8,128)(2,1)} %copy-done.22) | copy-start | bytes 12292
Sparse Core Ops, SparseCore 0:
  10.1 68.6 all-gather.5
  109.6 44.8 all-gather.3

commit v7 on v6

--- a/solution.py
+++ b/solution.py
@@ -126,15 +126,39 @@
     refs[0][:, HEAD:] = level.astype(BF)
 
 
-def attend(spots, queries, packets, state, finish):
-    total_rows = queries.shape[0]
-    rows = packets[0].shape[0]
+def in_place_kernel(spots, *refs):
+    out = refs[-1]
+    for index, piece in enumerate(refs[:-1]):
+        tall = piece.shape[0]
+        out[pl.ds(pl.multiple_of(spots[index] * tall, tall), tall), :] = piece[...]
+
+
+def in_place(spots, pieces, tall):
+    wide = pieces[0].shape[1]
+    count = len(pieces)
+    specs = [
+        pl.BlockSpec((tall, wide), functools.partial(lambda at, k: (at, 0), p.shape[0] // tall - 1))
+        for p in pieces
+    ]
+    return pl.pallas_call(
+        in_place_kernel,
+        grid=(1,),
+        in_specs=[pl.BlockSpec(memory_space=pltpu.SMEM)] + specs,
+        out_specs=pl.BlockSpec((count * tall, wide), lambda k: (0, 0)),
+        out_shape=jax.ShapeDtypeStruct((count * tall, wide), pieces[0].dtype),
+        name="in_place",
+    )(spots, *pieces)
+
+
+def attend(spots, queries, packets, state, finish, rows):
+    total_rows = queries.shape[0] * rows
     block = pl.BlockSpec((rows, HEAD), lambda k: (k, 0))
-    whole = pl.BlockSpec(packets[0].shape, lambda k: (0, 0))
+    asked = pl.BlockSpec((None, rows, HEAD), lambda k: (k, 0, 0))
+    whole = pl.BlockSpec((rows, 2 * HEAD), lambda k: (0, 0))
     start = state is None
     state = () if start else state
     if finish:
-        shapes = jax.ShapeDtypeStruct((total_rows // rows, rows, 2 * HEAD), BF)
+        shapes = jax.ShapeDtypeStruct((queries.shape[0], rows, 2 * HEAD), BF)
         outs = pl.BlockSpec((None, rows, 2 * HEAD), lambda k: (k, 0, 0))
     else:
         shapes = (jax.ShapeDtypeStruct((total_rows, HEAD), F32),) * 3
@@ -142,7 +166,7 @@
     return pl.pallas_call(
         functools.partial(attend_kernel, count=len(packets), start=start, finish=finish),
         grid=(total_rows // rows,),
-        in_specs=[pl.BlockSpec(memory_space=pltpu.SMEM), block]
+        in_specs=[pl.BlockSpec(memory_space=pltpu.SMEM), asked]
         + [whole] * len(packets)
         + [block] * len(state),
         out_specs=outs,
@@ -201,38 +225,50 @@
     both = jnp.concatenate([mine, lax.ppermute(other, CORE, SWAP)], axis=0)
     chip_rows = 2 * rows
     packet = both[:, HEAD:]
-    quad = to_everyone(both[:, :HEAD], QUAD)
+    halves = [hidden[:, k * HEAD : (k + 1) * HEAD] for k in range(units // HEAD)]
+    queries = to_everyone(jnp.concatenate([both[:, :HEAD], *halves], axis=0), QUAD)
     sides = lax.axis_size(QUAD)
-    queries = quad.reshape(sides * chip_rows, HEAD)
+    tall = sides * 2 * share
 
     up = [(i, (i + 1) % ring) for i in range(ring)]
     down = [(i, (i - 1) % ring) for i in range(ring)]
 
-    rising = falling = packet
-    held, at = [packet], [z]
-    for step in range(1, ring // 2 + 1):
+    rising = lax.ppermute(packet, Z, up)
+    falling = lax.ppermute(packet, Z, down)
+    held, at = [packet, rising, falling], [z, z - 1, z + 1]
+    rising, falling, queries = lax.optimization_barrier((rising, falling, queries))
+    riders = jnp.concatenate(
+        [
+            queries[:, chip_rows + k * 2 * share :][:, : 2 * share].reshape(tall, HEAD)
+            for k in range(units // HEAD)
+        ],
+        axis=1,
+    )
+    pieces, whose = [riders], [z]
+    rising = jnp.concatenate([rising, riders], axis=0)
+    falling = jnp.concatenate([falling, riders], axis=0)
+    for step in range(2, ring // 2):
         rising = lax.ppermute(rising, Z, up)
-        held.append(rising)
-        at.append((z - step) % ring)
-        if step < ring // 2:
-            falling = lax.ppermute(falling, Z, down)
-            held.append(falling)
-            at.append((z + step) % ring)
-        if step == 1:
-            rising, falling, hidden, queries = lax.optimization_barrier(
-                (rising, falling, hidden, queries)
-            )
-            hidden = to_everyone(hidden, (NEAR, FAR, LINE))
-            hidden = hidden.reshape(sides, line, 2, share, units)
-            hidden = jnp.transpose(hidden, (1, 2, 0, 3, 4)).reshape(-1, units)
-        elif step == 2:
-            rising, falling, hidden = lax.optimization_barrier((rising, falling, hidden))
+        falling = lax.ppermute(falling, Z, down)
+        held += [rising, falling]
+        at += [z - step, z + step]
+        pieces += [rising, falling]
+        whose += [z - step + 1, z + step - 1]
+    rising = lax.ppermute(rising, Z, up)
+    falling = lax.ppermute(falling[chip_rows:], Z, down)
+    held.append(rising)
+    at.append(z - ring // 2)
+    pieces += [rising, falling, lax.ppermute(rising[chip_rows:], Z, up)]
+    whose += [z - ring // 2 + 1, z + ring // 2 - 1, z - ring // 2]
+    at = [k % ring for k in at]
+    whose = jnp.stack([k % ring for k in whose]).astype(jnp.int32)
     spots = jnp.stack([z * sides] + [k * sides + near * 2 + far for k in at]).astype(jnp.int32)
     spots = jnp.concatenate([core.astype(jnp.int32)[None], spots])
-    state = attend(spots, queries, held[:-1], None, False)
-    last, weights, hidden = lax.optimization_barrier((held[-1], weights, hidden))
-    met = attend(jnp.concatenate([spots[:2], spots[-1:]]), queries, [last], state, True)
-    riders = lax.all_gather(hidden, Z, axis=0, tiled=True)
+    state = attend(spots, queries, held[:-1], None, False, chip_rows)
+    last, weights = lax.optimization_barrier((held[-1], weights))
+    spots = jnp.concatenate([spots[:2], spots[-1:]])
+    met = attend(spots, queries, [last], state, True, chip_rows)
+    riders = lax.all_gather(in_place(whose, pieces, tall), LINE, axis=0, tiled=False)
 
     local_whole = weights[:, :width].reshape(-1, columns)
     up_whole = unfold(weights[:, width : width + 8])
@@ -269,9 +305,9 @@
     projected = total(projected).astype(BF)
 
     rest = lax.ppermute(riders, CORE, SWAP)
-    split = (ring, line, 2, sides, 1, share, units)
-    riders = in_pair_order(riders.reshape(split), rest.reshape(split), core, 4)
-    riders = jnp.transpose(riders, (2, 1, 0, 3, 4, 5, 6)).reshape(2, line, columns, units)
+    split = (line, columns // (2 * share), 2, 1, share, units)
+    riders = in_pair_order(riders.reshape(split), rest.reshape(split), core, 3)
+    riders = jnp.moveaxis(riders, 2, 0).reshape(2, line, columns, units)
     rows_in, rows_out = riders[0], riders[1]
     lanes = 128
     spare_rows = jnp.zeros((line, lanes - RANK, units), BF)

time: 254 us -> 241 us (0.949)
  waiting for transfers between devices: 48.1 us -> 32.6 us
  blocking collectives: 54.6 us -> 46.7 us
  local copies, waits for them, and re-layouts: 16.8 us -> 19.8 us
  other arithmetic: 9.32 us -> 12.1 us
    ppermute x0 -> x4, starting transfers between devices: none -> 16.8 us  [the longest x1 7.2 us: body(): falling = lax.ppermute(packet, Z, down)]
    all_gather x1, waiting for transfers between devices: 20.8 us -> 6.74 us  [body(): lax.all_gather(in_place(whose, pieces, tall), LINE, axis=0, tiled=False)]
    ppermute x3 -> x2, starting transfers between devices: 15 us -> 4.89 us  [body(): falling = lax.ppermute(falling, Z, down)]
    all_to_all x4 -> x3, blocking collectives: 54.6 us -> 46.7 us  [exchange(): return lax.all_to_all(pieces, axis, split_axis=0, concat_axis=0, tiled=True)]
    all_to_all x5, starting transfers between devices: 25.6 us -> 19.1 us  [exchange(): return lax.all_to_all(pieces, axis, split_axis=0, concat_axis=0, tiled=True)]
    ppermute x4 -> x3, starting transfers between devices: 13.6 us -> 18.4 us  [body(): rising = lax.ppermute(rising, Z, up)]
    ppermute x0 -> x4, waiting for transfers between devices: none -> 3.5 us  [the longest x1 2.99 us: body(): rising = lax.ppermute(packet, Z, up)]
    ppermute x1, starting transfers between devices: 7.09 us -> 4.3 us  [body(): partner = lax.ppermute(merged[rows:], CORE, SWAP)]
  transfers between devices with their start and end apart: 20 -> 22, of which waited for: 13 -> 11; matrix products, arithmetic and copies ran while one was open for 8% -> 10% of each run, Pallas kernels for 3% -> 4%
where the time goes in v7:
time: 241 us; the launch traced here: 238 us
  starting transfers between devices  86.3 us (36%)
  blocking collectives  46.7 us (19%)
  waiting for transfers between devices  32.6 us (14%)
  local copies, waits for them, and re-layouts  19.8 us (8%)
  between operations  16.6 us (7%)
  Pallas kernels  13.4 us (6%)
  other arithmetic  12.1 us (5%)
  matrix products  10.9 us (5%)
    all_to_all x3, blocking collectives, exchange(): return lax.all_to_all(pieces, axis, split_axis=0, concat_axis=0, tiled=True)  46.7 us
    all_to_all x5, starting transfers between devices, exchange(): return lax.all_to_all(pieces, axis, split_axis=0, concat_axis=0, tiled=True)  19.1 us
    ppermute x3, starting transfers between devices, body(): rising = lax.ppermute(rising, Z, up)  18.4 us
    pallas_call x2, Pallas kernels, attend(): pl.pallas_call(functools.partial(attend_kernel, count=len(packets), start...  11.8 us
    ppermute x1, starting transfers between devices, body(): both = jnp.concatenate([mine, lax.ppermute(other, CORE, SWAP)], axis=0)  8.79 us
    all_to_all x5, waiting for transfers between devices, exchange(): return lax.all_to_all(pieces, axis, split_axis=0, concat_axis=0, tiled=True)  8.39 us
    dot_general x11, matrix products, contract(): lax.dot_general(left, right, (((left_dim,), (right_dim,)), ((), ())), pre...  7.46 us
    ppermute x1, starting transfers between devices, body(): falling = lax.ppermute(packet, Z, down)  7.2 us
  transfers between devices with their start and end apart: 22, of which 11 were waited for; matrix products, arithmetic and copies ran while one was open for 10% of the time, Pallas kernels for 4%

profile of v7, /device:TPU:1, one launch (start us, length us, event | category | flops | bytes accessed | tf_op | source)
XLA Modules:
  0.0 238.4 jit_solution(2421904861837009389)
XLA Ops:
  8.1 0.9 fusion.62
  8.9 1.7 maximum_maximum_fusion.3
  10.6 0.8 constant_dynamic-slice_fusion.5
  11.4 0.8 constant_dynamic-slice_fusion.3
  12.3 8.8 %collective-permute-start = (bf16[128,384]{1,0:T(8,128)(2,1)S(1)}, bf16[128,384]{1,0:T(8,128)(2,1)S(1)}, u32[]{:S(2)}, u32[]{:S(2)}) collective-permute-start(bf16[128,384]{1,0:T(8,128)(2,1)S(1)} %pad_maximum_fusion.6), channel_id=1, source_target_pairs={{0,8},{8,0},{1,9},{9,1},{2,10},{10,2},{3,11},{11,3},{4,12},{12,4},... | collective-permute-start | bytes 294920 | tf_op jit(solution)/shard_map/ppermute | solution.py:225
  21.1 0.7 fusion.49
  22.0 0.7 fusion.32
  22.7 0.8 broadcast_in_dim.21
  23.5 3.5 %all-to-all-start = ((bf16[4,288,128]{2,1,0:T(8,128)(2,1)}), bf16[4,288,128]{2,1,0:T(8,128)(2,1)S(1)}, u32[]{:S(2)}, u32[]{:S(2)}) async-start(bf16[4,288,128]{2,1,0:T(8,128)(2,1)} %broadcast_in_dim.21), calls=%async_computation | async-start | bytes 589824 | tf_op jit(solution)/shard_map/all_to_all | solution.py:30
  27.0 1.9 collective-permute-start.1
  28.9 7.2 %collective-permute-start.2 = (bf16[256,256]{1,0:T(8,128)(2,1)S(1)}, bf16[256,256]{1,0:T(8,128)(2,1)S(1)}, u32[]{:S(2)}, u32[]{:S(2)}) collective-permute-start(bf16[256,256]{1,0:T(8,128)(2,1)S(1)} %slice.258.refs_0_), channel_id=1, source_target_pairs={{0,448},{64,0},{128,64},{192,128},{256,192},{320,256},{384,320},{4... | collective-permute-start | bytes 393224 | tf_op jit(solution)/shard_map/ppermute | solution.py:237
  36.1 3.0 %collective-permute-done.1.refs_1_ = bf16[256,256]{1,0:T(8,128)(2,1)S(1)} collective-permute-done((bf16[256,256]{1,0:T(8,128)(2,1)S(1)}, bf16[256,256]{1,0:T(8,128)(2,1)S(1)}, u32[]{:S(2)}, u32[]{:S(2)}) %collective-permute-start.1) | collective-permute-done | bytes 131104 | tf_op jit(solution)/shard_map/ppermute | solution.py:236
  39.7 4.4 %collective-permute-start.3 = (bf16[320,256]{1,0:T(8,128)(2,1)S(1)}, bf16[320,256]{1,0:T(8,128)(2,1)S(1)}, u32[]{:S(2)}, u32[]{:S(2)}) collective-permute-start(bf16[320,256]{1,0:T(8,128)(2,1)S(1)} %get-tuple-element.62), channel_id=1, source_target_pairs={{0,64},{64,128},{128,192},{192,256},{256,320},{320,384},{384,448},... | collective-permute-start | bytes 491528 | tf_op jit(solution)/shard_map/ppermute | solution.py:251
  44.1 3.0 %collective-permute-start.6 = (bf16[320,256]{1,0:T(8,128)(2,1)S(1)}, bf16[320,256]{1,0:T(8,128)(2,1)S(1)}, u32[]{:S(2)}, u32[]{:S(2)}) collective-permute-start(bf16[320,256]{1,0:T(8,128)(2,1)S(1)} %get-tuple-element.61), channel_id=1, source_target_pairs={{0,448},{64,0},{128,64},{192,128},{256,192},{320,256},{384,320},{4... | collective-permute-start | bytes 491528 | tf_op jit(solution)/shard_map/ppermute | solution.py:252
  47.1 1.2 collective-permute-done.3.refs_3_.refs_1_
  48.2 9.0 %collective-permute-start.4 = (bf16[320,256]{1,0:T(8,128)(2,1)S(1)}, bf16[320,256]{1,0:T(8,128)(2,1)S(1)}, u32[]{:S(2)}, u32[]{:S(2)}) collective-permute-start(bf16[320,256]{1,0:T(8,128)(2,1)S(1)} %collective-permute-done.3.refs_3_.refs_1_), channel_id=1, source_target_pairs={{0,64},{64,128},{128,192},{192,256},{256,320},{320,384},{384,448},... | collective-permute-start | bytes 491528 | tf_op jit(solution)/shard_map/ppermute | solution.py:251
  57.3 1.9 collective-permute-start.7
  59.2 3.7 %collective-permute-done.4.refs_5_.refs_3_ = bf16[320,256]{1,0:T(8,128)(2,1)S(1)} collective-permute-done((bf16[320,256]{1,0:T(8,128)(2,1)S(1)}, bf16[320,256]{1,0:T(8,128)(2,1)S(1)}, u32[]{:S(2)}, u32[]{:S(2)}) %collective-permute-start.4) | collective-permute-done | bytes 163872 | tf_op jit(solution)/shard_map/ppermute | solution.py:251
  62.9 5.0 %collective-permute-start.5 = (bf16[320,256]{1,0:T(8,128)(2,1)S(1)}, bf16[320,256]{1,0:T(8,128)(2,1)S(1)}, u32[]{:S(2)}, u32[]{:S(2)}) collective-permute-start(bf16[320,256]{1,0:T(8,128)(2,1)S(1)} %collective-permute-done.4.refs_5_.refs_3_), channel_id=1, source_target_pairs={{0,64},{64,128},{128,192},{192,256},{256,320},{320,384},{384,448},... | collective-permute-start | bytes 491528 | tf_op jit(solution)/shard_map/ppermute | solution.py:257
  68.1 0.7 concatenate.115.spots
  69.3 1.6 collective-permute-done.7.refs_6_.refs_4_
  71.0 0.7 copy-done.5
  71.6 7.1 %attend.2 = (f32[1024,128]{1,0:T(8,128)}, f32[1024,128]{1,0:T(8,128)}, f32[1024,128]{1,0:T(8,128)}) custom-call(s32[10]{0:T(128)} %concatenate.115.spots, bf16[4,288,128]{2,1,0:T(8,128)(2,1)} %copy-done.1, bf16[256,256]{1,0:T(8,128)(2,1)} %copy-done.12, bf16[256,256]{1,0:T(8,128)(2,1)} %copy-done.10, bf16[256,256]{1,0:T(8,128)(2,1)} %copy-done.11, ...), custom_call_target="tpu_custom_call" | custom-call | tf_op jit(solution)/shard_map/attend/pallas_call | solution.py:166
  79.4 4.7 %attend.3 = bf16[4,256,256]{2,1,0:T(8,128)(2,1)} custom-call(s32[3]{0:T(128)} %pad_add_fusion.spots, bf16[4,288,128]{2,1,0:T(8,128)(2,1)} %copy-done.1, bf16[320,256]{1,0:T(8,128)(2,1)} %copy-done.4, f32[1024,128]{1,0:T(8,128)} %get-tuple-element.20.refs_1_, f32[1024,128]{1,0:T(8,128)} %get-tuple-element.21.refs_2_, f32[1024,128]{1,0:T(8,128)} %get-tuple-element.22.refs_3_), custom_call_target="tpu_custom_call" | custom-call | tf_op jit(solution)/shard_map/attend/pallas_call | solution.py:166
  84.1 3.6 %all-to-all-start.1 = ((bf16[4,256,256]{2,1,0:T(8,128)(2,1)}), bf16[4,256,256]{2,1,0:T(8,128)(2,1)S(1)}, u32[]{:S(2)}, u32[]{:S(2)}) async-start(bf16[4,256,256]{2,1,0:T(8,128)(2,1)} %attend.3), calls=%async_computation.1 | async-start | bytes 1048576 | tf_op jit(solution)/shard_map/all_to_all | solution.py:30
  88.3 0.8 slice.269
  89.0 5.8 %collective-permute-start.9 = (bf16[64,256]{1,0:T(8,128)(2,1)S(1)}, bf16[64,256]{1,0:T(8,128)(2,1)S(1)}, u32[]{:S(2)}, u32[]{:S(2)}) collective-permute-start(bf16[64,256]{1,0:T(8,128)(2,1)S(1)} %slice.269), channel_id=1, source_target_pairs={{0,448},{64,0},{128,64},{192,128},{256,192},{320,256},{384,320},{4... | collective-permute-start | bytes 98312 | tf_op jit(solution)/shard_map/ppermute | solution.py:258
  94.9 0.8 slice.270
  95.6 1.9 collective-permute-start.10
  98.8 4.3 %collective-permute-start.8 = (bf16[128,128]{1,0:T(8,128)(2,1)S(1)}, bf16[128,128]{1,0:T(8,128)(2,1)S(1)}, u32[]{:S(2)}, u32[]{:S(2)}) collective-permute-start(bf16[128,128]{1,0:T(8,128)(2,1)S(1)} %slice.266), channel_id=1, source_target_pairs={{0,8},{8,0},{1,9},{9,1},{2,10},{10,2},{3,11},{11,3},{4,12},{12,4},... | collective-permute-start | bytes 98312 | tf_op jit(solution)/shard_map/ppermute | solution.py:284
  105.0 1.6 in_place.1
  107.5 0.9 pad_maximum_fusion.1
  108.3 4.4 %all-to-all-start.2 = ((bf16[8,272,128]{2,1,0:T(8,128)(2,1)}), bf16[8,272,128]{2,1,0:T(8,128)(2,1)S(1)}, u32[]{:S(2)}, u32[]{:S(2)}) async-start(bf16[8,272,128]{2,1,0:T(8,128)(2,1)} %pad_maximum_fusion.1), calls=%async_computation.2 | async-start | bytes 1114112 | tf_op jit(solution)/shard_map/all_to_all | solution.py:30
  112.8 3.5 %collective-permute-start.11 = (bf16[128,512]{1,0:T(8,128)(2,1)S(1)}, bf16[128,512]{1,0:T(8,128)(2,1)}, u32[]{:S(2)}, u32[]{:S(2)}) collective-permute-start(bf16[128,512]{1,0:T(8,128)(2,1)S(1)} %copy-done.16), channel_id=1, source_target_pairs={{0,1},{1,0},{2,3},{3,2},{4,5},{5,4},{6,7},{7,6},{8,9},{9,8},{10,11... | collective-permute-start | bytes 393224 | tf_op jit(solution)/shard_map/ppermute | solution.py:217
  118.1 0.7 pad.22.clone
  118.8 0.8 dynamic_slice.28
  119.5 2.8 %all-to-all-done.2 = bf16[8,272,128]{2,1,0:T(8,128)(2,1)S(1)} async-done(((bf16[8,272,128]{2,1,0:T(8,128)(2,1)}), bf16[8,272,128]{2,1,0:T(8,128)(2,1)S(1)}, u32[]{:S(2)}, u32[]{:S(2)}) %all-to-all-start.2) | async-done | bytes 557088 | tf_op jit(solution)/shard_map/all_to_all | solution.py:30
  122.5 0.9 multiply_convert_fusion.4
  123.4 1.0 convolution_convert_fusion.2
  124.4 3.5 %all-to-all-start.3 = ((bf16[8,16,512]{2,1,0:T(8,128)(2,1)}), bf16[8,16,512]{2,1,0:T(8,128)(2,1)S(1)}, u32[]{:S(2)}, u32[]{:S(2)}) async-start(bf16[8,16,512]{2,1,0:T(8,128)(2,1)} %bitcast.22), calls=%async_computation.3 | async-start | bytes 262144 | tf_op jit(solution)/shard_map/all_to_all | solution.py:30
  127.9 1.5 fusion.57
  129.4 6.7 %all-gather.7.cloned.1.call-done = bf16[2048,256]{1,0:T(8,128)(2,1)} async-done(((bf16[512,256]{1,0:T(8,128)(2,1)}), bf16[2048,256]{1,0:T(8,128)(2,1)}) %all-gather.7.cloned.1.call-update) | async-done | bytes 1048592 | tf_op jit(solution)/shard_map/all_gather | solution.py:271
  136.1 4.1 %collective-permute-start.12 = (bf16[4,512,256]{2,1,0:T(8,128)(2,1)}, bf16[4,512,256]{2,1,0:T(8,128)(2,1)}, u32[]{:S(2)}, u32[]{:S(2)}) collective-permute-start(bf16[4,512,256]{2,1,0:T(8,128)(2,1)} %bitcast.126), channel_id=1, source_target_pairs={{0,8},{8,0},{1,9},{9,1},{2,10},{10,2},{3,11},{11,3},{4,12},{12,4},... | collective-permute-start | bytes 3145736 | tf_op jit(solution)/shard_map/ppermute | solution.py:307
  141.7 3.2 %collective-permute-start.13 = (bf16[128,640]{1,0:T(8,128)(2,1)S(1)}, bf16[128,640]{1,0:T(8,128)(2,1)S(1)}, u32[]{:S(2)}, u32[]{:S(2)}) collective-permute-start(bf16[128,640]{1,0:T(8,128)(2,1)S(1)} %pad_maximum_fusion.5), channel_id=1, source_target_pairs={{0,1},{1,0},{2,3},{3,2},{4,5},{5,4},{6,7},{7,6},{8,9},{9,8},{10,11... | collective-permute-start | bytes 491528 | tf_op jit(solution)/shard_map/ppermute | solution.py:329
  144.9 0.8 maximum_maximum_fusion.4
  145.8 3.6 %collective-permute-done.13 = bf16[128,640]{1,0:T(8,128)(2,1)S(1)} collective-permute-done((bf16[128,640]{1,0:T(8,128)(2,1)S(1)}, bf16[128,640]{1,0:T(8,128)(2,1)S(1)}, u32[]{:S(2)}, u32[]{:S(2)}) %collective-permute-start.13) | collective-permute-done | bytes 163872 | tf_op jit(solution)/shard_map/ppermute | solution.py:329
  149.5 1.4 broadcast_select_fusion.1
  151.8 0.7 fusion.16
  152.4 1.5 fusion.1
  154.0 0.7 convolution_bitcast_fusion
  155.0 3.2 %collective-permute-start.14 = (bf16[128,640]{1,0:T(8,128)(2,1)S(1)}, bf16[128,640]{1,0:T(8,128)(2,1)S(1)}, u32[]{:S(2)}, u32[]{:S(2)}) collective-permute-start(bf16[128,640]{1,0:T(8,128)(2,1)S(1)} %slice.341), channel_id=1, source_target_pairs={{0,1},{1,0},{2,3},{3,2},{4,5},{5,4},{6,7},{7,6},{8,9},{9,8},{10,11... | collective-permute-start | bytes 491528 | tf_op jit(solution)/shard_map/ppermute | solution.py:336
  158.3 3.6 %collective-permute-done.14 = bf16[128,640]{1,0:T(8,128)(2,1)S(1)} collective-permute-done((bf16[128,640]{1,0:T(8,128)(2,1)S(1)}, bf16[128,640]{1,0:T(8,128)(2,1)S(1)}, u32[]{:S(2)}, u32[]{:S(2)}) %collective-permute-start.14) | collective-permute-done | bytes 163872 | tf_op jit(solution)/shard_map/ppermute | solution.py:336
  163.0 0.9 fusion.19
  163.8 4.1 %all-to-all-start.4 = ((bf16[8,64,512]{2,1,0:T(8,128)(2,1)}), bf16[8,64,512]{2,1,0:T(8,128)(2,1)}, u32[]{:S(2)}, u32[]{:S(2)}) async-start(bf16[8,64,512]{2,1,0:T(8,128)(2,1)} %fusion.19), calls=%async_computation.4 | async-start | bytes 1048576 | tf_op jit(solution)/shard_map/all_to_all | solution.py:30
  168.0 1.8 slice.241
  170.6 5.6 %all-to-all-done.4 = bf16[8,64,512]{2,1,0:T(8,128)(2,1)} async-done(((bf16[8,64,512]{2,1,0:T(8,128)(2,1)}), bf16[8,64,512]{2,1,0:T(8,128)(2,1)}, u32[]{:S(2)}, u32[]{:S(2)}) %all-to-all-start.4) | async-done | bytes 524320 | tf_op jit(solution)/shard_map/all_to_all | solution.py:30
  176.2 0.9 slice.279
  177.1 1.9 fusion.2
  179.0 0.9 convolution_convert_fusion.7
  179.9 0.9 fusion.7
  181.2 1.1 convert_reduce_fusion.1
  182.3 13.8 %all_to_all.40 = bf16[8,12,256]{2,1,0:T(8,128)(2,1)S(1)} all-to-all(bf16[8,12,256]{2,1,0:T(8,128)(2,1)S(1)} %convert_element_type.134), channel_id=1, replica_groups=mesh['seq_0'=8,'near'=2,'seq_1'=2,'seq_2'=2,'row_0'=4,'row_1'=2] {'near'..., dimensions={0} | all-to-all | bytes 98304 | tf_op jit(solution)/shard_map/all_to_all | solution.py:30
  196.2 22.4 %all_to_all.41 = bf16[8,12,256]{2,1,0:T(8,128)(2,1)S(1)} all-to-all(bf16[8,12,256]{2,1,0:T(8,128)(2,1)S(1)} %broadcast_in_dim.28), channel_id=1, replica_groups=mesh['seq_0'=8,'near'=2,'seq_1'=2,'seq_2'=2,'row_0'=4,'row_1'=2] {'seq_0'}, dimensions={0} | all-to-all | bytes 98304 | tf_op jit(solution)/shard_map/all_to_all | solution.py:30
  218.7 10.5 %all_to_all.42 = bf16[8,12,256]{2,1,0:T(8,128)(2,1)S(1)} all-to-all(bf16[8,12,256]{2,1,0:T(8,128)(2,1)S(1)} %broadcast_in_dim.29), channel_id=1, replica_groups=mesh['seq_0'=8,'near'=2,'seq_1'=2,'seq_2'=2,'row_0'=4,'row_1'=2] {'near'..., dimensions={0} | all-to-all | bytes 98304 | tf_op jit(solution)/shard_map/all_to_all | solution.py:30
  (176 shorter events, 15.3 us)
Async XLA Ops:
  8.0 98.6 %copy-start = (bf16[256,2048]{1,0:T(8,128)(2,1)S(1)}, bf16[256,2048]{1,0:T(8,128)(2,1)}, u32[]{:S(2)}) copy-start(bf16[256,2048]{1,0:T(8,128)(2,1)} %param.25) | copy-start | bytes 3145732
  8.0 70.7 %all-gather.5.cloned.1.call-start = ((), (), s32[]{:S(2)}) async-start(), calls=%async_computation.8 | async-start | bytes 2506752 | tf_op jit(solution)/shard_map/all_gather | solution.py:216
  12.3 9.7 %collective-permute-start = (bf16[128,384]{1,0:T(8,128)(2,1)S(1)}, bf16[128,384]{1,0:T(8,128)(2,1)S(1)}, u32[]{:S(2)}, u32[]{:S(2)}) collective-permute-start(bf16[128,384]{1,0:T(8,128)(2,1)S(1)} %pad_maximum_fusion.6), channel_id=1, source_target_pairs={{0,8},{8,0},{1,9},{9,1},{2,10},{10,2},{3,11},{11,3},{4,12},{12,4},... | collective-permute-start | bytes 294920 | tf_op jit(solution)/shard_map/ppermute | solution.py:225
  23.5 16.2 %all-to-all-start = ((bf16[4,288,128]{2,1,0:T(8,128)(2,1)}), bf16[4,288,128]{2,1,0:T(8,128)(2,1)S(1)}, u32[]{:S(2)}, u32[]{:S(2)}) async-start(bf16[4,288,128]{2,1,0:T(8,128)(2,1)} %broadcast_in_dim.21), calls=%async_computation | async-start | bytes 589824 | tf_op jit(solution)/shard_map/all_to_all | solution.py:30
  27.0 43.9 %copy-start.12 = (bf16[256,256]{1,0:T(8,128)(2,1)}, bf16[256,256]{1,0:T(8,128)(2,1)S(1)}, u32[]{:S(2)}) copy-start(bf16[256,256]{1,0:T(8,128)(2,1)S(1)} %slice.258.refs_0_) | copy-start | bytes 393220
  27.0 12.1 %collective-permute-start.1 = (bf16[256,256]{1,0:T(8,128)(2,1)S(1)}, bf16[256,256]{1,0:T(8,128)(2,1)S(1)}, u32[]{:S(2)}, u32[]{:S(2)}) collective-permute-start(bf16[256,256]{1,0:T(8,128)(2,1)S(1)} %slice.258.refs_0_), channel_id=1, source_target_pairs={{0,64},{64,128},{128,192},{192,256},{256,320},{320,384},{384,448},... | collective-permute-start | bytes 393224 | tf_op jit(solution)/shard_map/ppermute | solution.py:236
  28.9 10.7 %collective-permute-start.2 = (bf16[256,256]{1,0:T(8,128)(2,1)S(1)}, bf16[256,256]{1,0:T(8,128)(2,1)S(1)}, u32[]{:S(2)}, u32[]{:S(2)}) collective-permute-start(bf16[256,256]{1,0:T(8,128)(2,1)S(1)} %slice.258.refs_0_), channel_id=1, source_target_pairs={{0,448},{64,0},{128,64},{192,128},{256,192},{320,256},{384,320},{4... | collective-permute-start | bytes 393224 | tf_op jit(solution)/shard_map/ppermute | solution.py:237
  39.1 31.8 %copy-start.10 = (bf16[256,256]{1,0:T(8,128)(2,1)}, bf16[256,256]{1,0:T(8,128)(2,1)S(1)}, u32[]{:S(2)}) copy-start(bf16[256,256]{1,0:T(8,128)(2,1)S(1)} %collective-permute-done.1.refs_1_) | copy-start | bytes 393220
  39.6 31.3 %copy-start.11 = (bf16[256,256]{1,0:T(8,128)(2,1)}, bf16[256,256]{1,0:T(8,128)(2,1)S(1)}, u32[]{:S(2)}) copy-start(bf16[256,256]{1,0:T(8,128)(2,1)S(1)} %collective-permute-done.2.refs_2_) | copy-start | bytes 393220
  39.6 31.3 %copy-start.1 = (bf16[4,288,128]{2,1,0:T(8,128)(2,1)}, bf16[4,288,128]{2,1,0:T(8,128)(2,1)S(1)}, u32[]{:S(2)}) copy-start(bf16[4,288,128]{2,1,0:T(8,128)(2,1)S(1)} %all-to-all-done.queries) | copy-start | bytes 884740
  39.7 8.6 %collective-permute-start.3 = (bf16[320,256]{1,0:T(8,128)(2,1)S(1)}, bf16[320,256]{1,0:T(8,128)(2,1)S(1)}, u32[]{:S(2)}, u32[]{:S(2)}) collective-permute-start(bf16[320,256]{1,0:T(8,128)(2,1)S(1)} %get-tuple-element.62), channel_id=1, source_target_pairs={{0,64},{64,128},{128,192},{192,256},{256,320},{320,384},{384,448},... | collective-permute-start | bytes 491528 | tf_op jit(solution)/shard_map/ppermute | solution.py:251
  44.1 13.2 %collective-permute-start.6 = (bf16[320,256]{1,0:T(8,128)(2,1)S(1)}, bf16[320,256]{1,0:T(8,128)(2,1)S(1)}, u32[]{:S(2)}, u32[]{:S(2)}) collective-permute-start(bf16[320,256]{1,0:T(8,128)(2,1)S(1)} %get-tuple-element.61), channel_id=1, source_target_pairs={{0,448},{64,0},{128,64},{192,128},{256,192},{320,256},{384,320},{4... | collective-permute-start | bytes 491528 | tf_op jit(solution)/shard_map/ppermute | solution.py:252
  48.2 22.7 %copy-start.6 = (bf16[320,256]{1,0:T(8,128)(2,1)}, bf16[320,256]{1,0:T(8,128)(2,1)S(1)}, u32[]{:S(2)}) copy-start(bf16[320,256]{1,0:T(8,128)(2,1)S(1)} %collective-permute-done.3.refs_3_.refs_1_) | copy-start | bytes 491524
  48.2 14.7 %collective-permute-start.4 = (bf16[320,256]{1,0:T(8,128)(2,1)S(1)}, bf16[320,256]{1,0:T(8,128)(2,1)S(1)}, u32[]{:S(2)}, u32[]{:S(2)}) collective-permute-start(bf16[320,256]{1,0:T(8,128)(2,1)S(1)} %collective-permute-done.3.refs_3_.refs_1_), channel_id=1, source_target_pairs={{0,64},{64,128},{128,192},{192,256},{256,320},{320,384},{384,448},... | collective-permute-start | bytes 491528 | tf_op jit(solution)/shard_map/ppermute | solution.py:251
  57.3 13.7 %copy-start.7 = (bf16[320,256]{1,0:T(8,128)(2,1)}, bf16[320,256]{1,0:T(8,128)(2,1)S(1)}, u32[]{:S(2)}) copy-start(bf16[320,256]{1,0:T(8,128)(2,1)S(1)} %collective-permute-done.6.refs_4_.refs_2_) | copy-start | bytes 491524
  57.3 13.6 %collective-permute-start.7 = (bf16[320,256]{1,0:T(8,128)(2,1)S(1)}, bf16[320,256]{1,0:T(8,128)(2,1)S(1)}, u32[]{:S(2)}, u32[]{:S(2)}) collective-permute-start(bf16[320,256]{1,0:T(8,128)(2,1)S(1)} %collective-permute-done.6.refs_4_.refs_2_), channel_id=1, source_target_pairs={{0,448},{64,0},{128,64},{192,128},{256,192},{320,256},{384,320},{4... | collective-permute-start | bytes 491528 | tf_op jit(solution)/shard_map/ppermute | solution.py:252
  62.9 8.0 %copy-start.8 = (bf16[320,256]{1,0:T(8,128)(2,1)}, bf16[320,256]{1,0:T(8,128)(2,1)S(1)}, u32[]{:S(2)}) copy-start(bf16[320,256]{1,0:T(8,128)(2,1)S(1)} %collective-permute-done.4.refs_5_.refs_3_) | copy-start | bytes 491524
  62.9 15.8 %collective-permute-start.5 = (bf16[320,256]{1,0:T(8,128)(2,1)S(1)}, bf16[320,256]{1,0:T(8,128)(2,1)S(1)}, u32[]{:S(2)}, u32[]{:S(2)}) collective-permute-start(bf16[320,256]{1,0:T(8,128)(2,1)S(1)} %collective-permute-done.4.refs_5_.refs_3_), channel_id=1, source_target_pairs={{0,64},{64,128},{128,192},{192,256},{256,320},{320,384},{384,448},... | collective-permute-start | bytes 491528 | tf_op jit(solution)/shard_map/ppermute | solution.py:257
  71.0 0.7 copy-start.5
  78.7 0.7 copy-start.4
  84.1 13.5 %all-to-all-start.1 = ((bf16[4,256,256]{2,1,0:T(8,128)(2,1)}), bf16[4,256,256]{2,1,0:T(8,128)(2,1)S(1)}, u32[]{:S(2)}, u32[]{:S(2)}) async-start(bf16[4,256,256]{2,1,0:T(8,128)(2,1)} %attend.3), calls=%async_computation.1 | async-start | bytes 1048576 | tf_op jit(solution)/shard_map/all_to_all | solution.py:30
  87.7 48.5 %all-gather.7.cloned.1.call-start = ((), (), s32[]{:S(2)}) async-start(), calls=%async_computation.9 | async-start | bytes 1310720 | tf_op jit(solution)/shard_map/all_gather | solution.py:271
  89.0 14.7 %collective-permute-start.9 = (bf16[64,256]{1,0:T(8,128)(2,1)S(1)}, bf16[64,256]{1,0:T(8,128)(2,1)S(1)}, u32[]{:S(2)}, u32[]{:S(2)}) collective-permute-start(bf16[64,256]{1,0:T(8,128)(2,1)S(1)} %slice.269), channel_id=1, source_target_pairs={{0,448},{64,0},{128,64},{192,128},{256,192},{320,256},{384,320},{4... | collective-permute-start | bytes 98312 | tf_op jit(solution)/shard_map/ppermute | solution.py:258
  95.6 8.1 %collective-permute-start.10 = (bf16[64,256]{1,0:T(8,128)(2,1)S(1)}, bf16[64,256]{1,0:T(8,128)(2,1)S(1)}, u32[]{:S(2)}, u32[]{:S(2)}) collective-permute-start(bf16[64,256]{1,0:T(8,128)(2,1)S(1)} %slice.270), channel_id=1, source_target_pairs={{0,64},{64,128},{128,192},{192,256},{256,320},{320,384},{384,448},... | collective-permute-start | bytes 98312 | tf_op jit(solution)/shard_map/ppermute | solution.py:261
  98.8 7.8 %collective-permute-start.8 = (bf16[128,128]{1,0:T(8,128)(2,1)S(1)}, bf16[128,128]{1,0:T(8,128)(2,1)S(1)}, u32[]{:S(2)}, u32[]{:S(2)}) collective-permute-start(bf16[128,128]{1,0:T(8,128)(2,1)S(1)} %slice.266), channel_id=1, source_target_pairs={{0,8},{8,0},{1,9},{9,1},{2,10},{10,2},{3,11},{11,3},{4,12},{12,4},... | collective-permute-start | bytes 98312 | tf_op jit(solution)/shard_map/ppermute | solution.py:284
  103.7 3.6 %copy-start.37 = (bf16[256,16]{0,1:T(8,128)(2,1)S(1)}, bf16[256,16]{0,1:T(8,128)(2,1)}, u32[]{:S(2)}) copy-start(bf16[256,16]{0,1:T(8,128)(2,1)} %param.26) | copy-start | bytes 24580
  103.7 0.6 copy-start.24
  104.3 0.6 copy-start.25
  106.6 1.7 copy-start.14
  106.6 1.7 copy-start.15
  107.0 5.8 %copy-start.16 = (bf16[128,512]{1,0:T(8,128)(2,1)S(1)}, bf16[128,512]{1,0:T(8,128)(2,1)}, u32[]{:S(2)}) copy-start(bf16[128,512]{1,0:T(8,128)(2,1)} %param.39) | copy-start | bytes 393220
  107.0 9.3 %copy-start.40 = (s32[128]{0:T(128)S(1)}, s32[128]{0:T(128)}, u32[]{:S(2)}) copy-start(s32[128]{0:T(128)} %param.23) | copy-start | bytes 1540
  107.0 9.6 %copy-start.30 = (bf16[8,512]{1,0:T(8,128)(2,1)S(1)}, bf16[8,512]{1,0:T(8,128)(2,1)}, u32[]{:S(2)}) copy-start(bf16[8,512]{1,0:T(8,128)(2,1)} %param.32) | copy-start | bytes 24580
  107.0 10.1 %copy-start.38 = (f32[8,16]{1,0:T(8,128)S(1)}, f32[8,16]{1,0:T(8,128)}, u32[]{:S(2)}) copy-start(f32[8,16]{1,0:T(8,128)} %param.38) | copy-start | bytes 1540
  107.3 15.3 %copy-start.39 = (f32[8,16]{1,0:T(8,128)S(1)}, f32[8,16]{1,0:T(8,128)}, u32[]{:S(2)}) copy-start(f32[8,16]{1,0:T(8,128)} %param.28) | copy-start | bytes 1540
  107.3 16.1 %copy-start.2 = (bf16[256,512]{1,0:T(8,128)(2,1)S(1)}, bf16[256,512]{1,0:T(8,128)(2,1)}, u32[]{:S(2)}) copy-start(bf16[256,512]{1,0:T(8,128)(2,1)} %param.29) | copy-start | bytes 786436
  107.3 16.1 %copy-start.17 = (bf16[128,256]{1,0:T(8,128)(2,1)S(1)}, bf16[128,256]{1,0:T(8,128)(2,1)}, u32[]{:S(2)}) copy-start(bf16[128,256]{1,0:T(8,128)(2,1)} %param.24) | copy-start | bytes 196612
  107.3 16.1 %copy-start.23 = (bf16[16,256]{1,0:T(8,128)(2,1)S(1)}, bf16[16,256]{1,0:T(8,128)(2,1)}, u32[]{:S(2)}) copy-start(bf16[16,256]{1,0:T(8,128)(2,1)} %param.27) | copy-start | bytes 24580
  108.3 32.0 %copy-start.13 = (bf16[256,512]{1,0:T(8,128)(2,1)S(1)}, bf16[256,512]{1,0:T(8,128)(2,1)}, u32[]{:S(2)}) copy-start(bf16[256,512]{1,0:T(8,128)(2,1)} %param.31) | copy-start | bytes 786436
  108.3 32.9 %copy-start.26 = (f32[512]{0:T(512)S(1)}, f32[512]{0:T(512)}, u32[]{:S(2)}) copy-start(f32[512]{0:T(512)} %param.33) | copy-start | bytes 6148
  108.3 14.0 %all-to-all-start.2 = ((bf16[8,272,128]{2,1,0:T(8,128)(2,1)}), bf16[8,272,128]{2,1,0:T(8,128)(2,1)S(1)}, u32[]{:S(2)}, u32[]{:S(2)}) async-start(bf16[8,272,128]{2,1,0:T(8,128)(2,1)} %pad_maximum_fusion.1), calls=%async_computation.2 | async-start | bytes 1114112 | tf_op jit(solution)/shard_map/all_to_all | solution.py:30
  112.8 28.5 %copy-start.18 = (bf16[512,16]{0,1:T(8,128)(2,1)S(1)}, bf16[512,16]{0,1:T(8,128)(2,1)}, u32[]{:S(2)}) copy-start(bf16[512,16]{0,1:T(8,128)(2,1)} %param.36) | copy-start | bytes 49156
  112.8 39.7 %collective-permute-start.11 = (bf16[128,512]{1,0:T(8,128)(2,1)S(1)}, bf16[128,512]{1,0:T(8,128)(2,1)}, u32[]{:S(2)}, u32[]{:S(2)}) collective-permute-start(bf16[128,512]{1,0:T(8,128)(2,1)S(1)} %copy-done.16), channel_id=1, source_target_pairs={{0,1},{1,0},{2,3},{3,2},{4,5},{5,4},{6,7},{7,6},{8,9},{9,8},{10,11... | collective-permute-start | bytes 393224 | tf_op jit(solution)/shard_map/ppermute | solution.py:217
  116.5 0.5 copy-start.33
  122.4 7.0 %copy-start.9 = (f32[272,128]{1,0:T(8,128)}, f32[272,128]{1,0:T(8,128)S(1)}, u32[]{:S(2)}) copy-start(f32[272,128]{1,0:T(8,128)S(1)} %convert_reduce_fusion) | copy-start | bytes 417796
  123.4 6.0 %copy-start.28 = (bf16[128,16]{0,1:T(8,128)(2,1)}, bf16[128,16]{0,1:T(8,128)(2,1)S(1)}, u32[]{:S(2)}) copy-start(bf16[128,16]{0,1:T(8,128)(2,1)S(1)} %get-tuple-element.71) | copy-start | bytes 12292
  124.4 11.7 %all-to-all-start.3 = ((bf16[8,16,512]{2,1,0:T(8,128)(2,1)}), bf16[8,16,512]{2,1,0:T(8,128)(2,1)S(1)}, u32[]{:S(2)}, u32[]{:S(2)}) async-start(bf16[8,16,512]{2,1,0:T(8,128)(2,1)} %bitcast.22), calls=%async_computation.3 | async-start | bytes 262144 | tf_op jit(solution)/shard_map/all_to_all | solution.py:30
  136.1 13.4 %copy-start.3 = (bf16[2048,256]{1,0:T(8,128)(2,1)S(1)}, bf16[2048,256]{1,0:T(8,128)(2,1)}, u32[]{:S(2)}) copy-start(bf16[2048,256]{1,0:T(8,128)(2,1)} %all-gather.7.cloned.1.call-done) | copy-start | bytes 3145732
  136.1 13.4 %collective-permute-start.12 = (bf16[4,512,256]{2,1,0:T(8,128)(2,1)}, bf16[4,512,256]{2,1,0:T(8,128)(2,1)}, u32[]{:S(2)}, u32[]{:S(2)}) collective-permute-start(bf16[4,512,256]{2,1,0:T(8,128)(2,1)} %bitcast.126), channel_id=1, source_target_pairs={{0,8},{8,0},{1,9},{9,1},{2,10},{10,2},{3,11},{11,3},{4,12},{12,4},... | collective-permute-start | bytes 3145736 | tf_op jit(solution)/shard_map/ppermute | solution.py:307
  140.7 0.5 copy-start.31
  141.7 7.7 %collective-permute-start.13 = (bf16[128,640]{1,0:T(8,128)(2,1)S(1)}, bf16[128,640]{1,0:T(8,128)(2,1)S(1)}, u32[]{:S(2)}, u32[]{:S(2)}) collective-permute-start(bf16[128,640]{1,0:T(8,128)(2,1)S(1)} %pad_maximum_fusion.5), channel_id=1, source_target_pairs={{0,1},{1,0},{2,3},{3,2},{4,5},{5,4},{6,7},{7,6},{8,9},{9,8},{10,11... | collective-permute-start | bytes 491528 | tf_op jit(solution)/shard_map/ppermute | solution.py:329
  151.1 0.7 copy-start.35
  154.7 7.4 %copy-start.27 = (f32[512]{0:T(512)S(1)}, f32[512]{0:T(512)}, u32[]{:S(2)}) copy-start(f32[512]{0:T(512)} %param.33) | copy-start | bytes 6148
  154.7 7.6 %copy-start.34 = (s32[128]{0:T(128)S(1)}, s32[128]{0:T(128)}, u32[]{:S(2)}) copy-start(s32[128]{0:T(128)} %copy-done.33) | copy-start | bytes 1540
  154.7 7.9 %copy-start.32 = (f32[128]{0:T(128)S(1)}, f32[128]{0:T(128)}, u32[]{:S(2)}) copy-start(f32[128]{0:T(128)} %copy-done.31) | copy-start | bytes 1540
  155.0 7.9 %copy-start.36 = (bf16[48]{0:T(256)(128)(2,1)S(1)}, bf16[48]{0:T(256)(128)(2,1)}, u32[]{:S(2)}) copy-start(bf16[48]{0:T(256)(128)(2,1)} %pad.22.clone) | copy-start | bytes 292
  155.0 6.8 %collective-permute-start.14 = (bf16[128,640]{1,0:T(8,128)(2,1)S(1)}, bf16[128,640]{1,0:T(8,128)(2,1)S(1)}, u32[]{:S(2)}, u32[]{:S(2)}) collective-permute-start(bf16[128,640]{1,0:T(8,128)(2,1)S(1)} %slice.341), channel_id=1, source_target_pairs={{0,1},{1,0},{2,3},{3,2},{4,5},{5,4},{6,7},{7,6},{8,9},{9,8},{10,11... | collective-permute-start | bytes 491528 | tf_op jit(solution)/shard_map/ppermute | solution.py:336
  163.8 12.3 %all-to-all-start.4 = ((bf16[8,64,512]{2,1,0:T(8,128)(2,1)}), bf16[8,64,512]{2,1,0:T(8,128)(2,1)}, u32[]{:S(2)}, u32[]{:S(2)}) async-start(bf16[8,64,512]{2,1,0:T(8,128)(2,1)} %fusion.19), calls=%async_computation.4 | async-start | bytes 1048576 | tf_op jit(solution)/shard_map/all_to_all | solution.py:30
  168.0 1.9 copy-start.19
  168.0 1.9 copy-start.20
  168.0 1.9 copy-start.21
  168.0 1.9 copy-start.22
  169.9 9.1 %copy-start.41 = (s32[128]{0:T(128)S(1)}, s32[128]{0:T(128)}, u32[]{:S(2)}) copy-start(s32[128]{0:T(128)} %param.23) | copy-start | bytes 1540
  169.9 11.0 %copy-start.29 = (bf16[128,16]{0,1:T(8,128)(2,1)S(1)}, bf16[128,16]{0,1:T(8,128)(2,1)}, u32[]{:S(2)}) copy-start(bf16[128,16]{0,1:T(8,128)(2,1)} %copy-done.28) | copy-start | bytes 12292
Sparse Core Ops, SparseCore 0:
  10.9 67.2 all-gather.4
Sparse Core Ops, SparseCore 1:
  106.7 29.4 all-gather.6

commit v8 on v7

--- a/solution.py
+++ b/solution.py
@@ -79,51 +79,56 @@
 
 def attend_kernel(spots, queries, *refs, count, start, finish):
     packets, refs = refs[:count], refs[count:]
-    rows = queries.shape[0]
+    blocks, rows = queries.shape[:2]
     half = rows // 2
-    if start:
-        top = jnp.full((rows, 1), -1e20, F32)
-        mass = jnp.zeros((rows, HEAD), F32)
-        out = jnp.zeros((rows, HEAD), F32)
-    else:
-        top, mass, out = refs[0][:, :1], refs[1][...], refs[2][...]
-        refs = refs[3:]
     core = spots[0]
+    state_in = () if start else refs[:3]
+    refs = refs[len(state_in) :]
 
     def inside(shape, dim):
         at = lax.broadcasted_iota(jnp.int32, shape, dim)
         return jnp.where(at < half, at + core * half, at - core * half)
 
-    query_places = (spots[1] + pl.program_id(0)) * rows + inside((rows, 1), 0)
-    own = queries[...]
-    for index in range(count):
-        keys = packets[index][:, :HEAD]
-        values = packets[index][:, HEAD:]
-        key_places = spots[2 + index] * rows + inside((1, rows), 1)
-        scores = contract(own, keys, 1, 1) * (1.0 / math.sqrt(HEAD))
-        scores = jnp.where(key_places <= query_places, scores, -1e30)
-        new_top = jnp.maximum(top, jnp.max(scores, axis=1, keepdims=True))
-        weights = jnp.exp(scores - new_top)
-        shrink = jnp.exp(top - new_top)
-        mass = mass * shrink + (weights[:, :HEAD] + weights[:, HEAD:])
-        out = out * shrink + jnp.dot(weights.astype(BF), values, preferred_element_type=F32)
-        top = new_top
-    if not finish:
-        refs[0][...] = jnp.broadcast_to(top, (rows, HEAD))
-        refs[1][...] = mass
-        refs[2][...] = out
-        return
-    mass = jnp.sum(mass, axis=1, keepdims=True)
-    safe = jnp.where(mass > 0, mass, 1.0)
-    level = jnp.where(mass > 0, top + jnp.log(safe), -1e30)
-    level = jnp.broadcast_to(level, (rows, HEAD))
-    high = level.astype(BF).astype(F32)
-    middle = (level - high).astype(BF).astype(F32)
-    low = level - high - middle
-    lane = lax.broadcasted_iota(jnp.int32, (rows, HEAD), 1)
-    level = jnp.where(lane < 32, high, jnp.where(lane < 64, middle, low))
-    refs[0][:, :HEAD] = (out / safe).astype(BF)
-    refs[0][:, HEAD:] = level.astype(BF)
+    for block in range(blocks):
+        here = pl.ds(block * rows, rows)
+        if start:
+            top = jnp.full((rows, 1), -1e20, F32)
+            mass = jnp.zeros((rows, HEAD), F32)
+            out = jnp.zeros((rows, HEAD), F32)
+        else:
+            top = state_in[0][here, :1]
+            mass, out = state_in[1][here, :], state_in[2][here, :]
+        place = spots[1] + pl.program_id(0) * blocks + block
+        query_places = place * rows + inside((rows, 1), 0)
+        own = queries[block]
+        for index in range(count):
+            keys = packets[index][:, :HEAD]
+            values = packets[index][:, HEAD:]
+            key_places = spots[2 + index] * rows + inside((1, rows), 1)
+            scores = contract(own, keys, 1, 1) * (1.0 / math.sqrt(HEAD))
+            scores = jnp.where(key_places <= query_places, scores, -1e30)
+            new_top = jnp.maximum(top, jnp.max(scores, axis=1, keepdims=True))
+            weights = jnp.exp(scores - new_top)
+            shrink = jnp.exp(top - new_top)
+            mass = mass * shrink + (weights[:, :HEAD] + weights[:, HEAD:])
+            out = out * shrink + jnp.dot(weights.astype(BF), values, preferred_element_type=F32)
+            top = new_top
+        if not finish:
+            refs[0][here, :] = jnp.broadcast_to(top, (rows, HEAD))
+            refs[1][here, :] = mass
+            refs[2][here, :] = out
+            continue
+        mass = jnp.sum(mass, axis=1, keepdims=True)
+        safe = jnp.where(mass > 0, mass, 1.0)
+        level = jnp.where(mass > 0, top + jnp.log(safe), -1e30)
+        level = jnp.broadcast_to(level, (rows, HEAD))
+        high = level.astype(BF).astype(F32)
+        middle = (level - high).astype(BF).astype(F32)
+        low = level - high - middle
+        lane = lax.broadcasted_iota(jnp.int32, (rows, HEAD), 1)
+        level = jnp.where(lane < 32, high, jnp.where(lane < 64, middle, low))
+        refs[0][block, :, :HEAD] = (out / safe).astype(BF)
+        refs[0][block, :, HEAD:] = level.astype(BF)
 
 
 def in_place_kernel(spots, *refs):
@@ -151,21 +156,22 @@
 
 
 def attend(spots, queries, packets, state, finish, rows):
-    total_rows = queries.shape[0] * rows
-    block = pl.BlockSpec((rows, HEAD), lambda k: (k, 0))
-    asked = pl.BlockSpec((None, rows, HEAD), lambda k: (k, 0, 0))
+    sides = queries.shape[0]
+    blocks = sides if finish else 2
+    block = pl.BlockSpec((blocks * rows, HEAD), lambda k: (k, 0))
+    asked = pl.BlockSpec((blocks, rows, HEAD), lambda k: (k, 0, 0))
     whole = pl.BlockSpec((rows, 2 * HEAD), lambda k: (0, 0))
     start = state is None
     state = () if start else state
     if finish:
-        shapes = jax.ShapeDtypeStruct((queries.shape[0], rows, 2 * HEAD), BF)
-        outs = pl.BlockSpec((None, rows, 2 * HEAD), lambda k: (k, 0, 0))
+        shapes = jax.ShapeDtypeStruct((sides, rows, 2 * HEAD), BF)
+        outs = pl.BlockSpec((blocks, rows, 2 * HEAD), lambda k: (k, 0, 0))
     else:
-        shapes = (jax.ShapeDtypeStruct((total_rows, HEAD), F32),) * 3
+        shapes = (jax.ShapeDtypeStruct((sides * rows, HEAD), F32),) * 3
         outs = (block,) * 3
     return pl.pallas_call(
         functools.partial(attend_kernel, count=len(packets), start=start, finish=finish),
-        grid=(total_rows // rows,),
+        grid=(sides // blocks,),
         in_specs=[pl.BlockSpec(memory_space=pltpu.SMEM), asked]
         + [whole] * len(packets)
         + [block] * len(state),
@@ -211,17 +217,18 @@
     units = hidden_in.shape[0]
     share = hidden_in.shape[1]
 
-    hidden = jnp.concatenate([hidden_in.T, hidden_out.T], axis=0)
-    weights = jnp.concatenate([local_weight, fold(global_up), fold(local_up)], axis=0)
-    weights = lax.all_gather(weights, ROW, axis=0, tiled=False)
-    cotangents = jnp.concatenate([cotangent, lax.ppermute(cotangent, SIDE, SWAP)], axis=0)
-
     def head(array, which):
         return lax.dynamic_slice_in_dim(array, which * HEAD, HEAD, 1)
 
     trio = (patch_queries, patch_keys, patch_values)
     mine = jnp.concatenate([head(a, core) for a in trio], axis=1)
     other = jnp.concatenate([head(a, 1 - core) for a in trio], axis=1)
+    hidden = jnp.concatenate([hidden_in.T, hidden_out.T], axis=0)
+    other, *early = lax.optimization_barrier((other, local_weight, global_up, local_up))
+    weights = jnp.concatenate([early[0], fold(early[1]), fold(early[2])], axis=0)
+    weights = lax.all_gather(weights, ROW, axis=0, tiled=False)
+    cotangents = jnp.concatenate([cotangent, lax.ppermute(cotangent, SIDE, SWAP)], axis=0)
+
     both = jnp.concatenate([mine, lax.ppermute(other, CORE, SWAP)], axis=0)
     chip_rows = 2 * rows
     packet = both[:, HEAD:]
@@ -258,16 +265,19 @@
     falling = lax.ppermute(falling[chip_rows:], Z, down)
     held.append(rising)
     at.append(z - ring // 2)
-    pieces += [rising, falling, lax.ppermute(rising[chip_rows:], Z, up)]
+    pieces.append(rising)
     whose += [z - ring // 2 + 1, z + ring // 2 - 1, z - ring // 2]
     at = [k % ring for k in at]
     whose = jnp.stack([k % ring for k in whose]).astype(jnp.int32)
     spots = jnp.stack([z * sides] + [k * sides + near * 2 + far for k in at]).astype(jnp.int32)
     spots = jnp.concatenate([core.astype(jnp.int32)[None], spots])
     state = attend(spots, queries, held[:-1], None, False, chip_rows)
-    last, weights = lax.optimization_barrier((held[-1], weights))
+    state, last, weights, falling = lax.optimization_barrier((state, rising, weights, falling))
+    final = lax.ppermute(last[chip_rows:], Z, up)
     spots = jnp.concatenate([spots[:2], spots[-1:]])
     met = attend(spots, queries, [last], state, True, chip_rows)
+    met, final = lax.optimization_barrier((met, final))
+    pieces += [falling, final]
     riders = lax.all_gather(in_place(whose, pieces, tall), LINE, axis=0, tiled=False)
 
     local_whole = weights[:, :width].reshape(-1, columns)

time: 241 us -> 241 us (level)
  waiting for transfers between devices: 32.6 us -> 40.6 us
  local copies, waits for them, and re-layouts: 19.8 us -> 16.4 us
    all_to_all x5, waiting for transfers between devices: 8.39 us -> 16.5 us  [exchange(): return lax.all_to_all(pieces, axis, split_axis=0, concat_axis=0, tiled=True)]
    ppermute x1, starting transfers between devices: 1.91 us -> 5.84 us  [body(): final = lax.ppermute(last[chip_rows:], Z, up)]
    ppermute x1, starting transfers between devices: 5.81 us -> 1.91 us  [body(): falling = lax.ppermute(falling[chip_rows:], Z, down)]
    all_gather x1, waiting for transfers between devices: 6.74 us -> 3.86 us  [body(): lax.all_gather(in_place(whose, pieces, tall), LINE, axis=0, tiled=False)]
    unnamed x89, local copies, waits for them, and re-layouts: 4.28 us -> 1.84 us
  transfers between devices with their start and end apart: 22 -> 22, of which waited for: 11 -> 13; matrix products, arithmetic and copies ran while one was open for 10% -> 8% of each run, Pallas kernels for 4% -> 5%
where the time goes in v8:
time: 241 us; the launch traced here: 239 us
  starting transfers between devices  85.4 us (35%)
  blocking collectives  45.2 us (19%)
  waiting for transfers between devices  40.6 us (17%)
  local copies, waits for them, and re-layouts  16.4 us (7%)
  between operations  15.2 us (6%)
  Pallas kernels  13.1 us (5%)
  other arithmetic  12.1 us (5%)
  matrix products  10.9 us (5%)
    all_to_all x3, blocking collectives, exchange(): return lax.all_to_all(pieces, axis, split_axis=0, concat_axis=0, tiled=True)  45.2 us
    all_to_all x5, starting transfers between devices, exchange(): return lax.all_to_all(pieces, axis, split_axis=0, concat_axis=0, tiled=True)  18.4 us
    ppermute x3, starting transfers between devices, body(): rising = lax.ppermute(rising, Z, up)  18.4 us
    all_to_all x5, waiting for transfers between devices, exchange(): return lax.all_to_all(pieces, axis, split_axis=0, concat_axis=0, tiled=True)  16.5 us
    pallas_call x2, Pallas kernels, attend(): pl.pallas_call(functools.partial(attend_kernel, count=len(packets), start...  11.5 us
    ppermute x1, starting transfers between devices, body(): both = jnp.concatenate([mine, lax.ppermute(other, CORE, SWAP)], axis=0)  8.79 us
    dot_general x11, matrix products, contract(): lax.dot_general(left, right, (((left_dim,), (right_dim,)), ((), ())), pre...  7.45 us
    ppermute x1, starting transfers between devices, body(): falling = lax.ppermute(packet, Z, down)  7.2 us
  transfers between devices with their start and end apart: 22, of which 13 were waited for; matrix products, arithmetic and copies ran while one was open for 8% of the time, Pallas kernels for 5%

profile of v8, /device:TPU:1, one launch (start us, length us, event | category | flops | bytes accessed | tf_op | source)
XLA Modules:
  0.0 239.0 jit_solution(3329711947246004497)
XLA Ops:
  7.2 0.9 constant_dynamic-slice_fusion.5
  8.1 0.8 constant_dynamic-slice_fusion.3
  8.9 0.7 fusion.63
  9.7 0.7 fusion.62
  10.4 1.7 maximum_maximum_fusion.3
  12.1 8.8 %collective-permute-start = (bf16[128,384]{1,0:T(8,128)(2,1)S(1)}, bf16[128,384]{1,0:T(8,128)(2,1)S(1)}, u32[]{:S(2)}, u32[]{:S(2)}) collective-permute-start(bf16[128,384]{1,0:T(8,128)(2,1)S(1)} %pad_maximum_fusion.6), channel_id=1, source_target_pairs={{0,8},{8,0},{1,9},{9,1},{2,10},{10,2},{3,11},{11,3},{4,12},{12,4},... | collective-permute-start | bytes 294920 | tf_op jit(solution)/shard_map/ppermute | solution.py:232
  20.9 0.7 fusion.49
  21.8 0.7 fusion.32
  22.5 0.8 broadcast_in_dim.21
  23.3 3.5 %all-to-all-start = ((bf16[4,288,128]{2,1,0:T(8,128)(2,1)}), bf16[4,288,128]{2,1,0:T(8,128)(2,1)S(1)}, u32[]{:S(2)}, u32[]{:S(2)}) async-start(bf16[4,288,128]{2,1,0:T(8,128)(2,1)} %broadcast_in_dim.21), calls=%async_computation | async-start | bytes 589824 | tf_op jit(solution)/shard_map/all_to_all | solution.py:30
  26.8 1.9 collective-permute-start.1
  28.7 7.2 %collective-permute-start.2 = (bf16[256,256]{1,0:T(8,128)(2,1)S(1)}, bf16[256,256]{1,0:T(8,128)(2,1)S(1)}, u32[]{:S(2)}, u32[]{:S(2)}) collective-permute-start(bf16[256,256]{1,0:T(8,128)(2,1)S(1)} %slice.258.refs_0_), channel_id=1, source_target_pairs={{0,448},{64,0},{128,64},{192,128},{256,192},{320,256},{384,320},{4... | collective-permute-start | bytes 393224 | tf_op jit(solution)/shard_map/ppermute | solution.py:244
  35.9 3.0 %collective-permute-done.1.refs_1_ = bf16[256,256]{1,0:T(8,128)(2,1)S(1)} collective-permute-done((bf16[256,256]{1,0:T(8,128)(2,1)S(1)}, bf16[256,256]{1,0:T(8,128)(2,1)S(1)}, u32[]{:S(2)}, u32[]{:S(2)}) %collective-permute-start.1) | collective-permute-done | bytes 131104 | tf_op jit(solution)/shard_map/ppermute | solution.py:243
  39.5 4.4 %collective-permute-start.3 = (bf16[320,256]{1,0:T(8,128)(2,1)S(1)}, bf16[320,256]{1,0:T(8,128)(2,1)S(1)}, u32[]{:S(2)}, u32[]{:S(2)}) collective-permute-start(bf16[320,256]{1,0:T(8,128)(2,1)S(1)} %get-tuple-element.82), channel_id=1, source_target_pairs={{0,64},{64,128},{128,192},{192,256},{256,320},{320,384},{384,448},... | collective-permute-start | bytes 491528 | tf_op jit(solution)/shard_map/ppermute | solution.py:258
  43.9 3.0 %collective-permute-start.4 = (bf16[320,256]{1,0:T(8,128)(2,1)S(1)}, bf16[320,256]{1,0:T(8,128)(2,1)S(1)}, u32[]{:S(2)}, u32[]{:S(2)}) collective-permute-start(bf16[320,256]{1,0:T(8,128)(2,1)S(1)} %get-tuple-element.81), channel_id=1, source_target_pairs={{0,448},{64,0},{128,64},{192,128},{256,192},{320,256},{384,320},{4... | collective-permute-start | bytes 491528 | tf_op jit(solution)/shard_map/ppermute | solution.py:259
  46.9 1.2 collective-permute-done.3.refs_3_.refs_1_
  48.1 9.0 %collective-permute-start.5 = (bf16[320,256]{1,0:T(8,128)(2,1)S(1)}, bf16[320,256]{1,0:T(8,128)(2,1)S(1)}, u32[]{:S(2)}, u32[]{:S(2)}) collective-permute-start(bf16[320,256]{1,0:T(8,128)(2,1)S(1)} %collective-permute-done.3.refs_3_.refs_1_), channel_id=1, source_target_pairs={{0,64},{64,128},{128,192},{192,256},{256,320},{320,384},{384,448},... | collective-permute-start | bytes 491528 | tf_op jit(solution)/shard_map/ppermute | solution.py:258
  57.1 1.9 collective-permute-start.6
  59.0 3.7 %collective-permute-done.5.refs_5_.refs_3_ = bf16[320,256]{1,0:T(8,128)(2,1)S(1)} collective-permute-done((bf16[320,256]{1,0:T(8,128)(2,1)S(1)}, bf16[320,256]{1,0:T(8,128)(2,1)S(1)}, u32[]{:S(2)}, u32[]{:S(2)}) %collective-permute-start.5) | collective-permute-done | bytes 163872 | tf_op jit(solution)/shard_map/ppermute | solution.py:258
  62.8 5.0 %collective-permute-start.7 = (bf16[320,256]{1,0:T(8,128)(2,1)S(1)}, bf16[320,256]{1,0:T(8,128)(2,1)S(1)}, u32[]{:S(2)}, u32[]{:S(2)}) collective-permute-start(bf16[320,256]{1,0:T(8,128)(2,1)S(1)} %collective-permute-done.5.refs_5_.refs_3_), channel_id=1, source_target_pairs={{0,64},{64,128},{128,192},{192,256},{256,320},{320,384},{384,448},... | collective-permute-start | bytes 491528 | tf_op jit(solution)/shard_map/ppermute | solution.py:264
  67.8 2.9 %collective-permute-done.6.refs_6_.refs_4_ = bf16[320,256]{1,0:T(8,128)(2,1)S(1)} collective-permute-done((bf16[320,256]{1,0:T(8,128)(2,1)S(1)}, bf16[320,256]{1,0:T(8,128)(2,1)S(1)}, u32[]{:S(2)}, u32[]{:S(2)}) %collective-permute-start.6) | collective-permute-done | bytes 163872 | tf_op jit(solution)/shard_map/ppermute | solution.py:259
  70.7 1.9 collective-permute-start.8
  72.7 0.6 concatenate.110.spots
  73.4 6.4 %attend.2 = (f32[1024,128]{1,0:T(8,128)}, f32[1024,128]{1,0:T(8,128)}, f32[1024,128]{1,0:T(8,128)}) custom-call(s32[10]{0:T(128)} %concatenate.110.spots, bf16[4,288,128]{2,1,0:T(8,128)(2,1)} %copy-done.1, bf16[256,256]{1,0:T(8,128)(2,1)} %copy-done.12, bf16[256,256]{1,0:T(8,128)(2,1)} %copy-done.10, bf16[256,256]{1,0:T(8,128)(2,1)} %copy-done.11, ...), custom_call_target="tpu_custom_call" | custom-call | tf_op jit(solution)/shard_map/attend/pallas_call | solution.py:172
  79.9 5.8 %collective-permute-start.9 = (bf16[64,256]{1,0:T(8,128)(2,1)S(1)}, bf16[64,256]{1,0:T(8,128)(2,1)S(1)}, u32[]{:S(2)}, u32[]{:S(2)}) collective-permute-start(bf16[64,256]{1,0:T(8,128)(2,1)S(1)} %slice.219), channel_id=1, source_target_pairs={{0,64},{64,128},{128,192},{192,256},{256,320},{320,384},{384,448},... | collective-permute-start | bytes 98312 | tf_op jit(solution)/shard_map/ppermute | solution.py:276
  86.4 5.1 %attend.3 = bf16[4,256,256]{2,1,0:T(8,128)(2,1)} custom-call(s32[3]{0:T(128)} %pad_add_fusion.spots, bf16[4,288,128]{2,1,0:T(8,128)(2,1)} %copy-done.1, bf16[320,256]{1,0:T(8,128)(2,1)} %copy-done.4, f32[1024,128]{1,0:T(8,128)} %get-tuple-element.37.refs_1_, f32[1024,128]{1,0:T(8,128)} %get-tuple-element.38.refs_2_, f32[1024,128]{1,0:T(8,128)} %get-tuple-element.39.refs_3_), custom_call_target="tpu_custom_call" | custom-call | tf_op jit(solution)/shard_map/attend/pallas_call | solution.py:172
  91.4 3.5 %all-to-all-start.1 = ((bf16[4,256,256]{2,1,0:T(8,128)(2,1)}), bf16[4,256,256]{2,1,0:T(8,128)(2,1)S(1)}, u32[]{:S(2)}, u32[]{:S(2)}) async-start(bf16[4,256,256]{2,1,0:T(8,128)(2,1)} %attend.3), calls=%async_computation.1 | async-start | bytes 1048576 | tf_op jit(solution)/shard_map/all_to_all | solution.py:30
  95.6 7.0 %all-to-all-done.1 = bf16[4,256,256]{2,1,0:T(8,128)(2,1)S(1)} async-done(((bf16[4,256,256]{2,1,0:T(8,128)(2,1)}), bf16[4,256,256]{2,1,0:T(8,128)(2,1)S(1)}, u32[]{:S(2)}, u32[]{:S(2)}) %all-to-all-start.1) | async-done | bytes 524320 | tf_op jit(solution)/shard_map/all_to_all | solution.py:30
  103.8 4.6 %collective-permute-start.10 = (bf16[128,128]{1,0:T(8,128)(2,1)S(1)}, bf16[128,128]{1,0:T(8,128)(2,1)S(1)}, u32[]{:S(2)}, u32[]{:S(2)}) collective-permute-start(bf16[128,128]{1,0:T(8,128)(2,1)S(1)} %slice.267), channel_id=1, source_target_pairs={{0,8},{8,0},{1,9},{9,1},{2,10},{10,2},{3,11},{11,3},{4,12},{12,4},... | collective-permute-start | bytes 98312 | tf_op jit(solution)/shard_map/ppermute | solution.py:294
  109.1 1.6 in_place.1
  111.6 0.9 pad_maximum_fusion.1
  112.5 4.0 %all-to-all-start.2 = ((bf16[8,272,128]{2,1,0:T(8,128)(2,1)}), bf16[8,272,128]{2,1,0:T(8,128)(2,1)S(1)}, u32[]{:S(2)}, u32[]{:S(2)}) async-start(bf16[8,272,128]{2,1,0:T(8,128)(2,1)} %pad_maximum_fusion.1), calls=%async_computation.2 | async-start | bytes 1114112 | tf_op jit(solution)/shard_map/all_to_all | solution.py:30
  116.5 3.5 %collective-permute-start.11 = (bf16[128,512]{1,0:T(8,128)(2,1)S(1)}, bf16[128,512]{1,0:T(8,128)(2,1)}, u32[]{:S(2)}, u32[]{:S(2)}) collective-permute-start(bf16[128,512]{1,0:T(8,128)(2,1)S(1)} %copy-done.16), channel_id=1, source_target_pairs={{0,1},{1,0},{2,3},{3,2},{4,5},{5,4},{6,7},{7,6},{8,9},{9,8},{10,11... | collective-permute-start | bytes 393224 | tf_op jit(solution)/shard_map/ppermute | solution.py:230
  121.2 0.7 pad.25.clone
  122.4 0.8 dynamic_slice.28
  123.2 3.6 %all-to-all-done.2 = bf16[8,272,128]{2,1,0:T(8,128)(2,1)S(1)} async-done(((bf16[8,272,128]{2,1,0:T(8,128)(2,1)}), bf16[8,272,128]{2,1,0:T(8,128)(2,1)S(1)}, u32[]{:S(2)}, u32[]{:S(2)}) %all-to-all-start.2) | async-done | bytes 557088 | tf_op jit(solution)/shard_map/all_to_all | solution.py:30
  127.0 0.9 multiply_convert_fusion.4
  127.9 1.0 convolution_convert_fusion.2
  128.9 3.4 %all-to-all-start.3 = ((bf16[8,16,512]{2,1,0:T(8,128)(2,1)}), bf16[8,16,512]{2,1,0:T(8,128)(2,1)S(1)}, u32[]{:S(2)}, u32[]{:S(2)}) async-start(bf16[8,16,512]{2,1,0:T(8,128)(2,1)} %bitcast.22), calls=%async_computation.3 | async-start | bytes 262144 | tf_op jit(solution)/shard_map/all_to_all | solution.py:30
  132.2 1.5 fusion.57
  133.7 3.9 %all-gather.7.cloned.1.call-done = bf16[2048,256]{1,0:T(8,128)(2,1)} async-done(((bf16[512,256]{1,0:T(8,128)(2,1)}), bf16[2048,256]{1,0:T(8,128)(2,1)}) %all-gather.7.cloned.1.call-update) | async-done | bytes 1048592 | tf_op jit(solution)/shard_map/all_gather | solution.py:281
  137.7 4.9 %collective-permute-start.12 = (bf16[4,512,256]{2,1,0:T(8,128)(2,1)}, bf16[4,512,256]{2,1,0:T(8,128)(2,1)}, u32[]{:S(2)}, u32[]{:S(2)}) collective-permute-start(bf16[4,512,256]{2,1,0:T(8,128)(2,1)} %bitcast.126), channel_id=1, source_target_pairs={{0,8},{8,0},{1,9},{9,1},{2,10},{10,2},{3,11},{11,3},{4,12},{12,4},... | collective-permute-start | bytes 3145736 | tf_op jit(solution)/shard_map/ppermute | solution.py:317
  144.1 2.4 collective-permute-start.13
  146.4 0.8 maximum_maximum_fusion.4
  147.3 4.4 %collective-permute-done.13 = bf16[128,640]{1,0:T(8,128)(2,1)S(1)} collective-permute-done((bf16[128,640]{1,0:T(8,128)(2,1)S(1)}, bf16[128,640]{1,0:T(8,128)(2,1)S(1)}, u32[]{:S(2)}, u32[]{:S(2)}) %collective-permute-start.13) | collective-permute-done | bytes 163872 | tf_op jit(solution)/shard_map/ppermute | solution.py:339
  151.9 1.4 broadcast_select_fusion.1
  154.1 0.7 fusion.16
  154.8 1.5 fusion.1
  156.3 0.7 convolution_bitcast_fusion
  157.4 2.6 %collective-permute-start.14 = (bf16[128,640]{1,0:T(8,128)(2,1)S(1)}, bf16[128,640]{1,0:T(8,128)(2,1)S(1)}, u32[]{:S(2)}, u32[]{:S(2)}) collective-permute-start(bf16[128,640]{1,0:T(8,128)(2,1)S(1)} %slice.340), channel_id=1, source_target_pairs={{0,1},{1,0},{2,3},{3,2},{4,5},{5,4},{6,7},{7,6},{8,9},{9,8},{10,11... | collective-permute-start | bytes 491528 | tf_op jit(solution)/shard_map/ppermute | solution.py:346
  160.0 4.2 %collective-permute-done.14 = bf16[128,640]{1,0:T(8,128)(2,1)S(1)} collective-permute-done((bf16[128,640]{1,0:T(8,128)(2,1)S(1)}, bf16[128,640]{1,0:T(8,128)(2,1)S(1)}, u32[]{:S(2)}, u32[]{:S(2)}) %collective-permute-start.14) | collective-permute-done | bytes 163872 | tf_op jit(solution)/shard_map/ppermute | solution.py:346
  165.3 0.8 fusion.19
  166.2 4.1 %all-to-all-start.4 = ((bf16[8,64,512]{2,1,0:T(8,128)(2,1)}), bf16[8,64,512]{2,1,0:T(8,128)(2,1)}, u32[]{:S(2)}, u32[]{:S(2)}) async-start(bf16[8,64,512]{2,1,0:T(8,128)(2,1)} %fusion.19), calls=%async_computation.4 | async-start | bytes 1048576 | tf_op jit(solution)/shard_map/all_to_all | solution.py:30
  170.4 1.8 slice.241
  172.3 0.6 copy.103
  172.9 5.8 %all-to-all-done.4 = bf16[8,64,512]{2,1,0:T(8,128)(2,1)} async-done(((bf16[8,64,512]{2,1,0:T(8,128)(2,1)}), bf16[8,64,512]{2,1,0:T(8,128)(2,1)}, u32[]{:S(2)}, u32[]{:S(2)}) %all-to-all-start.4) | async-done | bytes 524320 | tf_op jit(solution)/shard_map/all_to_all | solution.py:30
  178.8 0.9 slice.278
  179.7 1.9 fusion.2
  181.6 0.9 convolution_convert_fusion.7
  182.5 0.9 fusion.7
  183.8 1.1 convert_reduce_fusion.1
  184.9 11.5 %all_to_all.40 = bf16[8,12,256]{2,1,0:T(8,128)(2,1)S(1)} all-to-all(bf16[8,12,256]{2,1,0:T(8,128)(2,1)S(1)} %convert_element_type.134), channel_id=1, replica_groups=mesh['seq_0'=8,'near'=2,'seq_1'=2,'seq_2'=2,'row_0'=4,'row_1'=2] {'near'..., dimensions={0} | all-to-all | bytes 98304 | tf_op jit(solution)/shard_map/all_to_all | solution.py:30
  196.5 23.3 %all_to_all.41 = bf16[8,12,256]{2,1,0:T(8,128)(2,1)S(1)} all-to-all(bf16[8,12,256]{2,1,0:T(8,128)(2,1)S(1)} %broadcast_in_dim.28), channel_id=1, replica_groups=mesh['seq_0'=8,'near'=2,'seq_1'=2,'seq_2'=2,'row_0'=4,'row_1'=2] {'seq_0'}, dimensions={0} | all-to-all | bytes 98304 | tf_op jit(solution)/shard_map/all_to_all | solution.py:30
  219.8 10.5 %all_to_all.42 = bf16[8,12,256]{2,1,0:T(8,128)(2,1)S(1)} all-to-all(bf16[8,12,256]{2,1,0:T(8,128)(2,1)S(1)} %broadcast_in_dim.29), channel_id=1, replica_groups=mesh['seq_0'=8,'near'=2,'seq_1'=2,'seq_2'=2,'row_0'=4,'row_1'=2] {'near'..., dimensions={0} | all-to-all | bytes 98304 | tf_op jit(solution)/shard_map/all_to_all | solution.py:30
  (177 shorter events, 13.0 us)
Async XLA Ops:
  7.2 103.6 %copy-start = (bf16[256,2048]{1,0:T(8,128)(2,1)S(1)}, bf16[256,2048]{1,0:T(8,128)(2,1)}, u32[]{:S(2)}) copy-start(bf16[256,2048]{1,0:T(8,128)(2,1)} %param.25) | copy-start | bytes 3145732
  7.2 72.7 %all-gather.5.cloned.1.call-start = ((), (), s32[]{:S(2)}) async-start(), calls=%async_computation.8 | async-start | bytes 2506752 | tf_op jit(solution)/shard_map/all_gather | solution.py:229
  12.1 9.7 %collective-permute-start = (bf16[128,384]{1,0:T(8,128)(2,1)S(1)}, bf16[128,384]{1,0:T(8,128)(2,1)S(1)}, u32[]{:S(2)}, u32[]{:S(2)}) collective-permute-start(bf16[128,384]{1,0:T(8,128)(2,1)S(1)} %pad_maximum_fusion.6), channel_id=1, source_target_pairs={{0,8},{8,0},{1,9},{9,1},{2,10},{10,2},{3,11},{11,3},{4,12},{12,4},... | collective-permute-start | bytes 294920 | tf_op jit(solution)/shard_map/ppermute | solution.py:232
  23.3 16.2 %all-to-all-start = ((bf16[4,288,128]{2,1,0:T(8,128)(2,1)}), bf16[4,288,128]{2,1,0:T(8,128)(2,1)S(1)}, u32[]{:S(2)}, u32[]{:S(2)}) async-start(bf16[4,288,128]{2,1,0:T(8,128)(2,1)} %broadcast_in_dim.21), calls=%async_computation | async-start | bytes 589824 | tf_op jit(solution)/shard_map/all_to_all | solution.py:30
  26.8 46.6 %copy-start.12 = (bf16[256,256]{1,0:T(8,128)(2,1)}, bf16[256,256]{1,0:T(8,128)(2,1)S(1)}, u32[]{:S(2)}) copy-start(bf16[256,256]{1,0:T(8,128)(2,1)S(1)} %slice.258.refs_0_) | copy-start | bytes 393220
  26.8 12.1 %collective-permute-start.1 = (bf16[256,256]{1,0:T(8,128)(2,1)S(1)}, bf16[256,256]{1,0:T(8,128)(2,1)S(1)}, u32[]{:S(2)}, u32[]{:S(2)}) collective-permute-start(bf16[256,256]{1,0:T(8,128)(2,1)S(1)} %slice.258.refs_0_), channel_id=1, source_target_pairs={{0,64},{64,128},{128,192},{192,256},{256,320},{320,384},{384,448},... | collective-permute-start | bytes 393224 | tf_op jit(solution)/shard_map/ppermute | solution.py:243
  28.7 10.7 %collective-permute-start.2 = (bf16[256,256]{1,0:T(8,128)(2,1)S(1)}, bf16[256,256]{1,0:T(8,128)(2,1)S(1)}, u32[]{:S(2)}, u32[]{:S(2)}) collective-permute-start(bf16[256,256]{1,0:T(8,128)(2,1)S(1)} %slice.258.refs_0_), channel_id=1, source_target_pairs={{0,448},{64,0},{128,64},{192,128},{256,192},{320,256},{384,320},{4... | collective-permute-start | bytes 393224 | tf_op jit(solution)/shard_map/ppermute | solution.py:244
  38.9 34.4 %copy-start.10 = (bf16[256,256]{1,0:T(8,128)(2,1)}, bf16[256,256]{1,0:T(8,128)(2,1)S(1)}, u32[]{:S(2)}) copy-start(bf16[256,256]{1,0:T(8,128)(2,1)S(1)} %collective-permute-done.1.refs_1_) | copy-start | bytes 393220
  39.4 33.9 %copy-start.11 = (bf16[256,256]{1,0:T(8,128)(2,1)}, bf16[256,256]{1,0:T(8,128)(2,1)S(1)}, u32[]{:S(2)}) copy-start(bf16[256,256]{1,0:T(8,128)(2,1)S(1)} %collective-permute-done.2.refs_2_) | copy-start | bytes 393220
  39.4 33.9 %copy-start.1 = (bf16[4,288,128]{2,1,0:T(8,128)(2,1)}, bf16[4,288,128]{2,1,0:T(8,128)(2,1)S(1)}, u32[]{:S(2)}) copy-start(bf16[4,288,128]{2,1,0:T(8,128)(2,1)S(1)} %all-to-all-done.queries) | copy-start | bytes 884740
  39.5 8.6 %collective-permute-start.3 = (bf16[320,256]{1,0:T(8,128)(2,1)S(1)}, bf16[320,256]{1,0:T(8,128)(2,1)S(1)}, u32[]{:S(2)}, u32[]{:S(2)}) collective-permute-start(bf16[320,256]{1,0:T(8,128)(2,1)S(1)} %get-tuple-element.82), channel_id=1, source_target_pairs={{0,64},{64,128},{128,192},{192,256},{256,320},{320,384},{384,448},... | collective-permute-start | bytes 491528 | tf_op jit(solution)/shard_map/ppermute | solution.py:258
  43.9 13.2 %collective-permute-start.4 = (bf16[320,256]{1,0:T(8,128)(2,1)S(1)}, bf16[320,256]{1,0:T(8,128)(2,1)S(1)}, u32[]{:S(2)}, u32[]{:S(2)}) collective-permute-start(bf16[320,256]{1,0:T(8,128)(2,1)S(1)} %get-tuple-element.81), channel_id=1, source_target_pairs={{0,448},{64,0},{128,64},{192,128},{256,192},{320,256},{384,320},{4... | collective-permute-start | bytes 491528 | tf_op jit(solution)/shard_map/ppermute | solution.py:259
  48.1 25.3 %copy-start.6 = (bf16[320,256]{1,0:T(8,128)(2,1)}, bf16[320,256]{1,0:T(8,128)(2,1)S(1)}, u32[]{:S(2)}) copy-start(bf16[320,256]{1,0:T(8,128)(2,1)S(1)} %collective-permute-done.3.refs_3_.refs_1_) | copy-start | bytes 491524
  48.1 14.7 %collective-permute-start.5 = (bf16[320,256]{1,0:T(8,128)(2,1)S(1)}, bf16[320,256]{1,0:T(8,128)(2,1)S(1)}, u32[]{:S(2)}, u32[]{:S(2)}) collective-permute-start(bf16[320,256]{1,0:T(8,128)(2,1)S(1)} %collective-permute-done.3.refs_3_.refs_1_), channel_id=1, source_target_pairs={{0,64},{64,128},{128,192},{192,256},{256,320},{320,384},{384,448},... | collective-permute-start | bytes 491528 | tf_op jit(solution)/shard_map/ppermute | solution.py:258
  57.1 16.3 %copy-start.7 = (bf16[320,256]{1,0:T(8,128)(2,1)}, bf16[320,256]{1,0:T(8,128)(2,1)S(1)}, u32[]{:S(2)}) copy-start(bf16[320,256]{1,0:T(8,128)(2,1)S(1)} %collective-permute-done.4.refs_4_.refs_2_) | copy-start | bytes 491524
  57.1 13.6 %collective-permute-start.6 = (bf16[320,256]{1,0:T(8,128)(2,1)S(1)}, bf16[320,256]{1,0:T(8,128)(2,1)S(1)}, u32[]{:S(2)}, u32[]{:S(2)}) collective-permute-start(bf16[320,256]{1,0:T(8,128)(2,1)S(1)} %collective-permute-done.4.refs_4_.refs_2_), channel_id=1, source_target_pairs={{0,448},{64,0},{128,64},{192,128},{256,192},{320,256},{384,320},{4... | collective-permute-start | bytes 491528 | tf_op jit(solution)/shard_map/ppermute | solution.py:259
  62.8 10.6 %copy-start.8 = (bf16[320,256]{1,0:T(8,128)(2,1)}, bf16[320,256]{1,0:T(8,128)(2,1)S(1)}, u32[]{:S(2)}) copy-start(bf16[320,256]{1,0:T(8,128)(2,1)S(1)} %collective-permute-done.5.refs_5_.refs_3_) | copy-start | bytes 491524
  62.8 17.1 %collective-permute-start.7 = (bf16[320,256]{1,0:T(8,128)(2,1)S(1)}, bf16[320,256]{1,0:T(8,128)(2,1)S(1)}, u32[]{:S(2)}, u32[]{:S(2)}) collective-permute-start(bf16[320,256]{1,0:T(8,128)(2,1)S(1)} %collective-permute-done.5.refs_5_.refs_3_), channel_id=1, source_target_pairs={{0,64},{64,128},{128,192},{192,256},{256,320},{320,384},{384,448},... | collective-permute-start | bytes 491528 | tf_op jit(solution)/shard_map/ppermute | solution.py:264
  70.7 2.7 %copy-start.5 = (bf16[320,256]{1,0:T(8,128)(2,1)}, bf16[320,256]{1,0:T(8,128)(2,1)S(1)}, u32[]{:S(2)}) copy-start(bf16[320,256]{1,0:T(8,128)(2,1)S(1)} %collective-permute-done.6.refs_6_.refs_4_) | copy-start | bytes 491524
  70.7 9.2 %collective-permute-start.8 = (bf16[64,256]{1,0:T(8,128)(2,1)S(1)}, bf16[64,256]{1,0:T(8,128)(2,1)S(1)}, u32[]{:S(2)}, u32[]{:S(2)}) collective-permute-start(bf16[64,256]{1,0:T(8,128)(2,1)S(1)} %slice.261), channel_id=1, source_target_pairs={{0,448},{64,0},{128,64},{192,128},{256,192},{320,256},{384,320},{4... | collective-permute-start | bytes 98312 | tf_op jit(solution)/shard_map/ppermute | solution.py:265
  79.8 22.8 %copy-start.24 = (bf16[64,256]{1,0:T(8,128)(2,1)}, bf16[64,256]{1,0:T(8,128)(2,1)S(1)}, u32[]{:S(2)}) copy-start(bf16[64,256]{1,0:T(8,128)(2,1)S(1)} %collective-permute-done.8.refs_6_) | copy-start | bytes 98308
  79.9 6.5 %copy-start.4 = (bf16[320,256]{1,0:T(8,128)(2,1)}, bf16[320,256]{1,0:T(8,128)(2,1)S(1)}, u32[]{:S(2)}) copy-start(bf16[320,256]{1,0:T(8,128)(2,1)S(1)} %collective-permute-done.7.refs_0_.refs_5_) | copy-start | bytes 491524
  79.9 11.5 %collective-permute-start.9 = (bf16[64,256]{1,0:T(8,128)(2,1)S(1)}, bf16[64,256]{1,0:T(8,128)(2,1)S(1)}, u32[]{:S(2)}, u32[]{:S(2)}) collective-permute-start(bf16[64,256]{1,0:T(8,128)(2,1)S(1)} %slice.219), channel_id=1, source_target_pairs={{0,64},{64,128},{128,192},{192,256},{256,320},{320,384},{384,448},... | collective-permute-start | bytes 98312 | tf_op jit(solution)/shard_map/ppermute | solution.py:276
  91.4 11.7 %copy-start.25 = (bf16[64,256]{1,0:T(8,128)(2,1)}, bf16[64,256]{1,0:T(8,128)(2,1)S(1)}, u32[]{:S(2)}) copy-start(bf16[64,256]{1,0:T(8,128)(2,1)S(1)} %collective-permute-done.9.refs_7_) | copy-start | bytes 98308
  91.4 11.2 %all-to-all-start.1 = ((bf16[4,256,256]{2,1,0:T(8,128)(2,1)}), bf16[4,256,256]{2,1,0:T(8,128)(2,1)S(1)}, u32[]{:S(2)}, u32[]{:S(2)}) async-start(bf16[4,256,256]{2,1,0:T(8,128)(2,1)} %attend.3), calls=%async_computation.1 | async-start | bytes 1048576 | tf_op jit(solution)/shard_map/all_to_all | solution.py:30
  94.9 42.7 %all-gather.7.cloned.1.call-start = ((), (), s32[]{:S(2)}) async-start(), calls=%async_computation.9 | async-start | bytes 1310720 | tf_op jit(solution)/shard_map/all_gather | solution.py:281
  103.8 6.9 %collective-permute-start.10 = (bf16[128,128]{1,0:T(8,128)(2,1)S(1)}, bf16[128,128]{1,0:T(8,128)(2,1)S(1)}, u32[]{:S(2)}, u32[]{:S(2)}) collective-permute-start(bf16[128,128]{1,0:T(8,128)(2,1)S(1)} %slice.267), channel_id=1, source_target_pairs={{0,8},{8,0},{1,9},{9,1},{2,10},{10,2},{3,11},{11,3},{4,12},{12,4},... | collective-permute-start | bytes 98312 | tf_op jit(solution)/shard_map/ppermute | solution.py:294
  109.1 2.4 copy-start.37
  110.8 1.8 copy-start.14
  110.8 1.7 copy-start.15
  111.1 5.4 %copy-start.16 = (bf16[128,512]{1,0:T(8,128)(2,1)S(1)}, bf16[128,512]{1,0:T(8,128)(2,1)}, u32[]{:S(2)}) copy-start(bf16[128,512]{1,0:T(8,128)(2,1)} %param.39) | copy-start | bytes 393220
  111.1 8.9 %copy-start.40 = (s32[128]{0:T(128)S(1)}, s32[128]{0:T(128)}, u32[]{:S(2)}) copy-start(s32[128]{0:T(128)} %param.23) | copy-start | bytes 1540
  111.1 9.1 %copy-start.30 = (bf16[8,512]{1,0:T(8,128)(2,1)S(1)}, bf16[8,512]{1,0:T(8,128)(2,1)}, u32[]{:S(2)}) copy-start(bf16[8,512]{1,0:T(8,128)(2,1)} %param.32) | copy-start | bytes 24580
  111.2 9.7 %copy-start.38 = (f32[8,16]{1,0:T(8,128)S(1)}, f32[8,16]{1,0:T(8,128)}, u32[]{:S(2)}) copy-start(f32[8,16]{1,0:T(8,128)} %param.38) | copy-start | bytes 1540
  111.5 15.5 %copy-start.39 = (f32[8,16]{1,0:T(8,128)S(1)}, f32[8,16]{1,0:T(8,128)}, u32[]{:S(2)}) copy-start(f32[8,16]{1,0:T(8,128)} %param.28) | copy-start | bytes 1540
  111.5 16.4 %copy-start.2 = (bf16[256,512]{1,0:T(8,128)(2,1)S(1)}, bf16[256,512]{1,0:T(8,128)(2,1)}, u32[]{:S(2)}) copy-start(bf16[256,512]{1,0:T(8,128)(2,1)} %param.29) | copy-start | bytes 786436
  111.5 16.4 %copy-start.17 = (bf16[128,256]{1,0:T(8,128)(2,1)S(1)}, bf16[128,256]{1,0:T(8,128)(2,1)}, u32[]{:S(2)}) copy-start(bf16[128,256]{1,0:T(8,128)(2,1)} %param.24) | copy-start | bytes 196612
  111.5 16.4 %copy-start.23 = (bf16[16,256]{1,0:T(8,128)(2,1)S(1)}, bf16[16,256]{1,0:T(8,128)(2,1)}, u32[]{:S(2)}) copy-start(bf16[16,256]{1,0:T(8,128)(2,1)} %param.27) | copy-start | bytes 24580
  112.5 30.1 %copy-start.13 = (bf16[256,512]{1,0:T(8,128)(2,1)S(1)}, bf16[256,512]{1,0:T(8,128)(2,1)}, u32[]{:S(2)}) copy-start(bf16[256,512]{1,0:T(8,128)(2,1)} %param.31) | copy-start | bytes 786436
  112.5 31.0 %copy-start.26 = (f32[512]{0:T(512)S(1)}, f32[512]{0:T(512)}, u32[]{:S(2)}) copy-start(f32[512]{0:T(512)} %param.33) | copy-start | bytes 6148
  112.5 14.3 %all-to-all-start.2 = ((bf16[8,272,128]{2,1,0:T(8,128)(2,1)}), bf16[8,272,128]{2,1,0:T(8,128)(2,1)S(1)}, u32[]{:S(2)}, u32[]{:S(2)}) async-start(bf16[8,272,128]{2,1,0:T(8,128)(2,1)} %pad_maximum_fusion.1), calls=%async_computation.2 | async-start | bytes 1114112 | tf_op jit(solution)/shard_map/all_to_all | solution.py:30
  116.5 27.1 %copy-start.18 = (bf16[512,16]{0,1:T(8,128)(2,1)S(1)}, bf16[512,16]{0,1:T(8,128)(2,1)}, u32[]{:S(2)}) copy-start(bf16[512,16]{0,1:T(8,128)(2,1)} %param.36) | copy-start | bytes 49156
  116.5 38.3 %collective-permute-start.11 = (bf16[128,512]{1,0:T(8,128)(2,1)S(1)}, bf16[128,512]{1,0:T(8,128)(2,1)}, u32[]{:S(2)}, u32[]{:S(2)}) collective-permute-start(bf16[128,512]{1,0:T(8,128)(2,1)S(1)} %copy-done.16), channel_id=1, source_target_pairs={{0,1},{1,0},{2,3},{3,2},{4,5},{5,4},{6,7},{7,6},{8,9},{9,8},{10,11... | collective-permute-start | bytes 393224 | tf_op jit(solution)/shard_map/ppermute | solution.py:230
  120.3 0.5 copy-start.33
  126.9 6.9 %copy-start.9 = (f32[272,128]{1,0:T(8,128)}, f32[272,128]{1,0:T(8,128)S(1)}, u32[]{:S(2)}) copy-start(f32[272,128]{1,0:T(8,128)S(1)} %convert_reduce_fusion) | copy-start | bytes 417796
  127.9 5.9 %copy-start.28 = (bf16[128,16]{0,1:T(8,128)(2,1)}, bf16[128,16]{0,1:T(8,128)(2,1)S(1)}, u32[]{:S(2)}) copy-start(bf16[128,16]{0,1:T(8,128)(2,1)S(1)} %get-tuple-element.91) | copy-start | bytes 12292
  128.9 8.9 %all-to-all-start.3 = ((bf16[8,16,512]{2,1,0:T(8,128)(2,1)}), bf16[8,16,512]{2,1,0:T(8,128)(2,1)S(1)}, u32[]{:S(2)}, u32[]{:S(2)}) async-start(bf16[8,16,512]{2,1,0:T(8,128)(2,1)} %bitcast.22), calls=%async_computation.3 | async-start | bytes 262144 | tf_op jit(solution)/shard_map/all_to_all | solution.py:30
  137.6 14.3 %copy-start.3 = (bf16[2048,256]{1,0:T(8,128)(2,1)S(1)}, bf16[2048,256]{1,0:T(8,128)(2,1)}, u32[]{:S(2)}) copy-start(bf16[2048,256]{1,0:T(8,128)(2,1)} %all-gather.7.cloned.1.call-done) | copy-start | bytes 3145732
  137.7 14.1 %collective-permute-start.12 = (bf16[4,512,256]{2,1,0:T(8,128)(2,1)}, bf16[4,512,256]{2,1,0:T(8,128)(2,1)}, u32[]{:S(2)}, u32[]{:S(2)}) collective-permute-start(bf16[4,512,256]{2,1,0:T(8,128)(2,1)} %bitcast.126), channel_id=1, source_target_pairs={{0,8},{8,0},{1,9},{9,1},{2,10},{10,2},{3,11},{11,3},{4,12},{12,4},... | collective-permute-start | bytes 3145736 | tf_op jit(solution)/shard_map/ppermute | solution.py:317
  143.0 0.6 copy-start.31
  144.1 7.7 %collective-permute-start.13 = (bf16[128,640]{1,0:T(8,128)(2,1)S(1)}, bf16[128,640]{1,0:T(8,128)(2,1)S(1)}, u32[]{:S(2)}, u32[]{:S(2)}) collective-permute-start(bf16[128,640]{1,0:T(8,128)(2,1)S(1)} %pad_maximum_fusion.5), channel_id=1, source_target_pairs={{0,1},{1,0},{2,3},{3,2},{4,5},{5,4},{6,7},{7,6},{8,9},{9,8},{10,11... | collective-permute-start | bytes 491528 | tf_op jit(solution)/shard_map/ppermute | solution.py:339
  153.4 0.7 copy-start.35
  157.0 7.4 %copy-start.27 = (f32[512]{0:T(512)S(1)}, f32[512]{0:T(512)}, u32[]{:S(2)}) copy-start(f32[512]{0:T(512)} %param.33) | copy-start | bytes 6148
  157.1 7.6 %copy-start.34 = (s32[128]{0:T(128)S(1)}, s32[128]{0:T(128)}, u32[]{:S(2)}) copy-start(s32[128]{0:T(128)} %copy-done.33) | copy-start | bytes 1540
  157.1 7.9 %copy-start.32 = (f32[128]{0:T(128)S(1)}, f32[128]{0:T(128)}, u32[]{:S(2)}) copy-start(f32[128]{0:T(128)} %copy-done.31) | copy-start | bytes 1540
  157.3 7.9 %copy-start.36 = (bf16[48]{0:T(256)(128)(2,1)S(1)}, bf16[48]{0:T(256)(128)(2,1)}, u32[]{:S(2)}) copy-start(bf16[48]{0:T(256)(128)(2,1)} %pad.22.clone) | copy-start | bytes 292
  157.4 6.8 %collective-permute-start.14 = (bf16[128,640]{1,0:T(8,128)(2,1)S(1)}, bf16[128,640]{1,0:T(8,128)(2,1)S(1)}, u32[]{:S(2)}, u32[]{:S(2)}) collective-permute-start(bf16[128,640]{1,0:T(8,128)(2,1)S(1)} %slice.340), channel_id=1, source_target_pairs={{0,1},{1,0},{2,3},{3,2},{4,5},{5,4},{6,7},{7,6},{8,9},{9,8},{10,11... | collective-permute-start | bytes 491528 | tf_op jit(solution)/shard_map/ppermute | solution.py:346
  166.2 12.6 %all-to-all-start.4 = ((bf16[8,64,512]{2,1,0:T(8,128)(2,1)}), bf16[8,64,512]{2,1,0:T(8,128)(2,1)}, u32[]{:S(2)}, u32[]{:S(2)}) async-start(bf16[8,64,512]{2,1,0:T(8,128)(2,1)} %fusion.19), calls=%async_computation.4 | async-start | bytes 1048576 | tf_op jit(solution)/shard_map/all_to_all | solution.py:30
  170.3 1.9 copy-start.19
  170.3 1.9 copy-start.20
  170.3 1.9 copy-start.21
  170.3 1.9 copy-start.22
  172.2 9.4 %copy-start.41 = (s32[128]{0:T(128)S(1)}, s32[128]{0:T(128)}, u32[]{:S(2)}) copy-start(s32[128]{0:T(128)} %param.23) | copy-start | bytes 1540
  172.2 11.2 %copy-start.29 = (bf16[128,16]{0,1:T(8,128)(2,1)S(1)}, bf16[128,16]{0,1:T(8,128)(2,1)}, u32[]{:S(2)}) copy-start(bf16[128,16]{0,1:T(8,128)(2,1)} %copy-done.28) | copy-start | bytes 12292
Sparse Core Ops, SparseCore 0:
  12.2 67.2 all-gather.4
  110.9 26.6 all-gather.6

commit v9 on v8

--- a/solution.py
+++ b/solution.py
@@ -77,13 +77,15 @@
     return jnp.concatenate([array[:, :RANK], array[:, RANK:]], axis=2)
 
 
-def attend_kernel(spots, queries, *refs, count, start, finish):
+def attend_kernel(spots, queries, *refs, count, start, hosted):
+    finish = hosted > 0
     packets, refs = refs[:count], refs[count:]
     blocks, rows = queries.shape[:2]
     half = rows // 2
     core = spots[0]
     state_in = () if start else refs[:3]
     refs = refs[len(state_in) :]
+    guests, refs = refs[:hosted], refs[hosted:]
 
     def inside(shape, dim):
         at = lax.broadcasted_iota(jnp.int32, shape, dim)
@@ -127,36 +129,19 @@
         low = level - high - middle
         lane = lax.broadcasted_iota(jnp.int32, (rows, HEAD), 1)
         level = jnp.where(lane < 32, high, jnp.where(lane < 64, middle, low))
-        refs[0][block, :, :HEAD] = (out / safe).astype(BF)
-        refs[0][block, :, HEAD:] = level.astype(BF)
-
-
-def in_place_kernel(spots, *refs):
-    out = refs[-1]
-    for index, piece in enumerate(refs[:-1]):
-        tall = piece.shape[0]
-        out[pl.ds(pl.multiple_of(spots[index] * tall, tall), tall), :] = piece[...]
-
-
-def in_place(spots, pieces, tall):
-    wide = pieces[0].shape[1]
-    count = len(pieces)
-    specs = [
-        pl.BlockSpec((tall, wide), functools.partial(lambda at, k: (at, 0), p.shape[0] // tall - 1))
-        for p in pieces
-    ]
-    return pl.pallas_call(
-        in_place_kernel,
-        grid=(1,),
-        in_specs=[pl.BlockSpec(memory_space=pltpu.SMEM)] + specs,
-        out_specs=pl.BlockSpec((count * tall, wide), lambda k: (0, 0)),
-        out_shape=jax.ShapeDtypeStruct((count * tall, wide), pieces[0].dtype),
-        name="in_place",
-    )(spots, *pieces)
-
-
-def attend(spots, queries, packets, state, finish, rows):
+        refs[0][block, :rows, :HEAD] = (out / safe).astype(BF)
+        refs[0][block, :rows, HEAD:] = level.astype(BF)
+        for index, guest in enumerate(guests):
+            extra = guest.shape[0]
+            spot = pl.multiple_of(rows + spots[2 + count + index] * extra, extra)
+            refs[0][block, pl.ds(spot, extra), :] = guest[...]
+
+
+def attend(spots, queries, packets, state, guests, rows):
     sides = queries.shape[0]
+    finish = len(guests) > 0
+    extra = guests[0].shape[0] - rows if finish else 0
+    tall = rows + extra * len(guests)
     blocks = sides if finish else 2
     block = pl.BlockSpec((blocks * rows, HEAD), lambda k: (k, 0))
     asked = pl.BlockSpec((blocks, rows, HEAD), lambda k: (k, 0, 0))
@@ -164,21 +149,22 @@
     start = state is None
     state = () if start else state
     if finish:
-        shapes = jax.ShapeDtypeStruct((sides, rows, 2 * HEAD), BF)
-        outs = pl.BlockSpec((blocks, rows, 2 * HEAD), lambda k: (k, 0, 0))
+        shapes = jax.ShapeDtypeStruct((sides, tall, 2 * HEAD), BF)
+        outs = pl.BlockSpec((blocks, tall, 2 * HEAD), lambda k: (k, 0, 0))
     else:
         shapes = (jax.ShapeDtypeStruct((sides * rows, HEAD), F32),) * 3
         outs = (block,) * 3
     return pl.pallas_call(
-        functools.partial(attend_kernel, count=len(packets), start=start, finish=finish),
+        functools.partial(attend_kernel, count=len(packets), start=start, hosted=len(guests)),
         grid=(sides // blocks,),
         in_specs=[pl.BlockSpec(memory_space=pltpu.SMEM), asked]
         + [whole] * len(packets)
-        + [block] * len(state),
+        + [block] * len(state)
+        + [pl.BlockSpec((extra, 2 * HEAD), lambda k: (rows // extra, 0))] * len(guests),
         out_specs=outs,
         out_shape=shapes,
         name="attend",
-    )(spots, queries, *packets, *state)
+    )(spots, queries, *packets, *state, *guests)
 
 
 def body(
@@ -232,53 +218,32 @@
     both = jnp.concatenate([mine, lax.ppermute(other, CORE, SWAP)], axis=0)
     chip_rows = 2 * rows
     packet = both[:, HEAD:]
-    halves = [hidden[:, k * HEAD : (k + 1) * HEAD] for k in range(units // HEAD)]
-    queries = to_everyone(jnp.concatenate([both[:, :HEAD], *halves], axis=0), QUAD)
+    packet = jnp.concatenate([packet, hidden], axis=0)
+    queries = to_everyone(both[:, :HEAD], QUAD)
     sides = lax.axis_size(QUAD)
-    tall = sides * 2 * share
 
     up = [(i, (i + 1) % ring) for i in range(ring)]
     down = [(i, (i - 1) % ring) for i in range(ring)]
 
-    rising = lax.ppermute(packet, Z, up)
-    falling = lax.ppermute(packet, Z, down)
-    held, at = [packet, rising, falling], [z, z - 1, z + 1]
-    rising, falling, queries = lax.optimization_barrier((rising, falling, queries))
-    riders = jnp.concatenate(
-        [
-            queries[:, chip_rows + k * 2 * share :][:, : 2 * share].reshape(tall, HEAD)
-            for k in range(units // HEAD)
-        ],
-        axis=1,
-    )
-    pieces, whose = [riders], [z]
-    rising = jnp.concatenate([rising, riders], axis=0)
-    falling = jnp.concatenate([falling, riders], axis=0)
-    for step in range(2, ring // 2):
+    rising = falling = packet
+    held, at = [packet], [z]
+    for step in range(1, ring // 2 + 1):
         rising = lax.ppermute(rising, Z, up)
-        falling = lax.ppermute(falling, Z, down)
-        held += [rising, falling]
-        at += [z - step, z + step]
-        pieces += [rising, falling]
-        whose += [z - step + 1, z + step - 1]
-    rising = lax.ppermute(rising, Z, up)
-    falling = lax.ppermute(falling[chip_rows:], Z, down)
-    held.append(rising)
-    at.append(z - ring // 2)
-    pieces.append(rising)
-    whose += [z - ring // 2 + 1, z + ring // 2 - 1, z - ring // 2]
+        held.append(rising)
+        at.append(z - step)
+        if step < ring // 2:
+            falling = lax.ppermute(falling, Z, down)
+            held.append(falling)
+            at.append(z + step)
+        if step == 1:
+            rising, falling, queries = lax.optimization_barrier((rising, falling, queries))
     at = [k % ring for k in at]
-    whose = jnp.stack([k % ring for k in whose]).astype(jnp.int32)
     spots = jnp.stack([z * sides] + [k * sides + near * 2 + far for k in at]).astype(jnp.int32)
     spots = jnp.concatenate([core.astype(jnp.int32)[None], spots])
-    state = attend(spots, queries, held[:-1], None, False, chip_rows)
-    state, last, weights, falling = lax.optimization_barrier((state, rising, weights, falling))
-    final = lax.ppermute(last[chip_rows:], Z, up)
-    spots = jnp.concatenate([spots[:2], spots[-1:]])
-    met = attend(spots, queries, [last], state, True, chip_rows)
-    met, final = lax.optimization_barrier((met, final))
-    pieces += [falling, final]
-    riders = lax.all_gather(in_place(whose, pieces, tall), LINE, axis=0, tiled=False)
+    state = attend(spots, queries, held[:-1], None, [], chip_rows)
+    state, last, weights = lax.optimization_barrier((state, held[-1], weights))
+    spots = jnp.concatenate([spots[:2], spots[-1:], jnp.stack(at).astype(jnp.int32)])
+    met = attend(spots, queries, [last], state, held[:-1] + [last], chip_rows)
 
     local_whole = weights[:, :width].reshape(-1, columns)
     up_whole = unfold(weights[:, width : width + 8])
@@ -286,7 +251,10 @@
     local_ups = unfold(weights[:, width + 8 :]).reshape(line, 2, RANK, units)
     local_ups = lax.dynamic_index_in_dim(local_ups, side, 1, keepdims=False)
 
-    met = exchange(met, QUAD).astype(F32)
+    met = exchange(met, QUAD)
+    riders = met[:, chip_rows:].reshape(-1, units)
+    riders = lax.all_gather(riders, LINE, axis=0, tiled=False)
+    met = met[:, :chip_rows].astype(F32)
     levels = met[:, :, 128:129] + met[:, :, 160:161] + met[:, :, 192:193]
     parts = jnp.exp(levels - jnp.max(levels, axis=0, keepdims=True))
     merged = (parts * met[:, :, :HEAD]).sum(axis=0) / parts.sum(axis=0)
@@ -315,9 +283,9 @@
     projected = total(projected).astype(BF)
 
     rest = lax.ppermute(riders, CORE, SWAP)
-    split = (line, columns // (2 * share), 2, 1, share, units)
-    riders = in_pair_order(riders.reshape(split), rest.reshape(split), core, 3)
-    riders = jnp.moveaxis(riders, 2, 0).reshape(2, line, columns, units)
+    split = (line, sides, ring, 2, 1, share, units)
+    riders = in_pair_order(riders.reshape(split), rest.reshape(split), core, 4)
+    riders = jnp.transpose(riders, (3, 0, 2, 1, 4, 5, 6)).reshape(2, line, columns, units)
     rows_in, rows_out = riders[0], riders[1]
     lanes = 128
     spare_rows = jnp.zeros((line, lanes - RANK, units), BF)

time: 241 us -> 238 us (0.988)
  blocking collectives: 45.2 us -> 62.5 us
  starting transfers between devices: 85.4 us -> 73.1 us
  waiting for transfers between devices: 40.6 us -> 35.8 us
  other arithmetic: 12.1 us -> 9.6 us
    all_to_all x3 -> x4, blocking collectives: 45.2 us -> 62.5 us  [exchange(): return lax.all_to_all(pieces, axis, split_axis=0, concat_axis=0, tiled=True)]
    ppermute x4 -> x0, starting transfers between devices: 16.9 us -> none  [the longest x1 7.2 us: body(): falling = lax.ppermute(packet, Z, down)]
    ppermute x2 -> x3, starting transfers between devices: 4.89 us -> 12.1 us  [body(): falling = lax.ppermute(falling, Z, down)]
    all_gather x1, waiting for transfers between devices: 0.02 us -> 4.7 us  [body(): weights = lax.all_gather(weights, ROW, axis=0, tiled=False)]
    all_to_all x5 -> x4, starting transfers between devices: 18.4 us -> 14.7 us  [exchange(): return lax.all_to_all(pieces, axis, split_axis=0, concat_axis=0, tiled=True)]
    ppermute x4 -> x0, waiting for transfers between devices: 3.5 us -> none  [the longest x1 2.99 us: body(): rising = lax.ppermute(packet, Z, up)]
    all_to_all x5 -> x4, waiting for transfers between devices: 16.5 us -> 13.1 us  [exchange(): return lax.all_to_all(pieces, axis, split_axis=0, concat_axis=0, tiled=True)]
    all_gather x1, waiting for transfers between devices: 3.86 us -> 1.15 us  [body(): riders = lax.all_gather(riders, LINE, axis=0, tiled=False)]
  transfers between devices with their start and end apart: 22 -> 19, of which waited for: 13 -> 14; matrix products, arithmetic and copies ran while one was open for 8% -> 7% of each run, Pallas kernels for 5% -> 3%
where the time goes in v9:
time: 238 us; the launch traced here: 236 us
  starting transfers between devices  73.1 us (31%)
  blocking collectives  62.5 us (26%)
  waiting for transfers between devices  35.8 us (15%)
  local copies, waits for them, and re-layouts  17.7 us (7%)
  between operations  15.2 us (6%)
  Pallas kernels  11.6 us (5%)
  matrix products  10.9 us (5%)
  other arithmetic  9.6 us (4%)
    all_to_all x4, blocking collectives, exchange(): return lax.all_to_all(pieces, axis, split_axis=0, concat_axis=0, tiled=True)  62.5 us
    ppermute x4, starting transfers between devices, body(): rising = lax.ppermute(rising, Z, up)  19.7 us
    all_to_all x4, starting transfers between devices, exchange(): return lax.all_to_all(pieces, axis, split_axis=0, concat_axis=0, tiled=True)  14.7 us
    all_to_all x4, waiting for transfers between devices, exchange(): return lax.all_to_all(pieces, axis, split_axis=0, concat_axis=0, tiled=True)  13.1 us
    ppermute x3, starting transfers between devices, body(): falling = lax.ppermute(falling, Z, down)  12.1 us
    pallas_call x2, Pallas kernels, attend(): pl.pallas_call(functools.partial(attend_kernel, count=len(packets), start...  11.6 us
    ppermute x1, starting transfers between devices, body(): both = jnp.concatenate([mine, lax.ppermute(other, CORE, SWAP)], axis=0)  8.79 us
    dot_general x11, matrix products, contract(): lax.dot_general(left, right, (((left_dim,), (right_dim,)), ((), ())), pre...  7.46 us
  transfers between devices with their start and end apart: 19, of which 14 were waited for; matrix products, arithmetic and copies ran while one was open for 7% of the time, Pallas kernels for 3%

profile of v9, /device:TPU:1, one launch (start us, length us, event | category | flops | bytes accessed | tf_op | source)
XLA Modules:
  0.0 236.4 jit_solution(12253603446081659077)
XLA Ops:
  7.3 0.9 constant_dynamic-slice_fusion.5
  8.1 0.8 constant_dynamic-slice_fusion.3
  9.0 0.7 fusion.57
  9.7 0.7 fusion.56
  10.4 1.7 maximum_maximum_fusion.3
  12.2 8.8 %collective-permute-start = (bf16[128,384]{1,0:T(8,128)(2,1)S(1)}, bf16[128,384]{1,0:T(8,128)(2,1)S(1)}, u32[]{:S(2)}, u32[]{:S(2)}) collective-permute-start(bf16[128,384]{1,0:T(8,128)(2,1)S(1)} %pad_maximum_fusion.6), channel_id=1, source_target_pairs={{0,8},{8,0},{1,9},{9,1},{2,10},{10,2},{3,11},{11,3},{4,12},{12,4},... | collective-permute-start | bytes 294920 | tf_op jit(solution)/shard_map/ppermute | solution.py:218
  21.0 0.9 collective-permute-done
  21.9 0.7 broadcast_in_dim.21
  22.6 3.4 %all-to-all-start = ((bf16[4,256,128]{2,1,0:T(8,128)(2,1)}), bf16[4,256,128]{2,1,0:T(8,128)(2,1)S(1)}, u32[]{:S(2)}, u32[]{:S(2)}) async-start(bf16[4,256,128]{2,1,0:T(8,128)(2,1)} %broadcast_in_dim.21), calls=%async_computation | async-start | bytes 524288 | tf_op jit(solution)/shard_map/all_to_all | solution.py:30
  26.2 1.9 collective-permute-start.1
  28.1 7.2 %collective-permute-start.2 = (bf16[272,256]{1,0:T(8,128)(2,1)S(1)}, bf16[272,256]{1,0:T(8,128)(2,1)S(1)}, u32[]{:S(2)}, u32[]{:S(2)}) collective-permute-start(bf16[272,256]{1,0:T(8,128)(2,1)S(1)} %pad_maximum_fusion.5.refs_0_.refs_4_), channel_id=1, source_target_pairs={{0,448},{64,0},{128,64},{192,128},{256,192},{320,256},{384,320},{4... | collective-permute-start | bytes 417800 | tf_op jit(solution)/shard_map/ppermute | solution.py:235
  35.3 2.6 %collective-permute-done.1.refs_1_.refs_5_ = bf16[272,256]{1,0:T(8,128)(2,1)S(1)} collective-permute-done((bf16[272,256]{1,0:T(8,128)(2,1)S(1)}, bf16[272,256]{1,0:T(8,128)(2,1)S(1)}, u32[]{:S(2)}, u32[]{:S(2)}) %collective-permute-start.1) | collective-permute-done | bytes 139296 | tf_op jit(solution)/shard_map/ppermute | solution.py:231
  37.9 1.2 collective-permute-done.2.refs_2_.refs_6_
  39.1 4.4 %collective-permute-start.3 = (bf16[272,256]{1,0:T(8,128)(2,1)S(1)}, bf16[272,256]{1,0:T(8,128)(2,1)S(1)}, u32[]{:S(2)}, u32[]{:S(2)}) collective-permute-start(bf16[272,256]{1,0:T(8,128)(2,1)S(1)} %collective-permute-done.1.refs_1_.refs_5_), channel_id=1, source_target_pairs={{0,64},{64,128},{128,192},{192,256},{256,320},{320,384},{384,448},... | collective-permute-start | bytes 417800 | tf_op jit(solution)/shard_map/ppermute | solution.py:231
  43.5 3.0 %collective-permute-start.4 = (bf16[272,256]{1,0:T(8,128)(2,1)S(1)}, bf16[272,256]{1,0:T(8,128)(2,1)S(1)}, u32[]{:S(2)}, u32[]{:S(2)}) collective-permute-start(bf16[272,256]{1,0:T(8,128)(2,1)S(1)} %collective-permute-done.2.refs_2_.refs_6_), channel_id=1, source_target_pairs={{0,448},{64,0},{128,64},{192,128},{256,192},{320,256},{384,320},{4... | collective-permute-start | bytes 417800 | tf_op jit(solution)/shard_map/ppermute | solution.py:235
  47.0 8.3 %collective-permute-start.5 = (bf16[272,256]{1,0:T(8,128)(2,1)S(1)}, bf16[272,256]{1,0:T(8,128)(2,1)S(1)}, u32[]{:S(2)}, u32[]{:S(2)}) collective-permute-start(bf16[272,256]{1,0:T(8,128)(2,1)S(1)} %collective-permute-done.3.refs_3_.refs_7_), channel_id=1, source_target_pairs={{0,64},{64,128},{128,192},{192,256},{256,320},{320,384},{384,448},... | collective-permute-start | bytes 417800 | tf_op jit(solution)/shard_map/ppermute | solution.py:231
  55.4 1.9 collective-permute-start.6
  57.3 3.7 %collective-permute-done.5.refs_5_.refs_9_ = bf16[272,256]{1,0:T(8,128)(2,1)S(1)} collective-permute-done((bf16[272,256]{1,0:T(8,128)(2,1)S(1)}, bf16[272,256]{1,0:T(8,128)(2,1)S(1)}, u32[]{:S(2)}, u32[]{:S(2)}) %collective-permute-start.5) | collective-permute-done | bytes 139296 | tf_op jit(solution)/shard_map/ppermute | solution.py:231
  61.0 5.0 %collective-permute-start.7 = (bf16[272,256]{1,0:T(8,128)(2,1)S(1)}, bf16[272,256]{1,0:T(8,128)(2,1)S(1)}, u32[]{:S(2)}, u32[]{:S(2)}) collective-permute-start(bf16[272,256]{1,0:T(8,128)(2,1)S(1)} %collective-permute-done.5.refs_5_.refs_9_), channel_id=1, source_target_pairs={{0,64},{64,128},{128,192},{192,256},{256,320},{320,384},{384,448},... | collective-permute-start | bytes 417800 | tf_op jit(solution)/shard_map/ppermute | solution.py:231
  66.1 0.7 concatenate.97.spots
  67.9 0.6 copy-done.10
  68.5 6.4 %attend.2 = (f32[1024,128]{1,0:T(8,128)}, f32[1024,128]{1,0:T(8,128)}, f32[1024,128]{1,0:T(8,128)}) custom-call(s32[10]{0:T(128)} %concatenate.97.spots, bf16[4,256,128]{2,1,0:T(8,128)(2,1)} %copy-done.2, bf16[272,256]{1,0:T(8,128)(2,1)} %copy-done.3, bf16[272,256]{1,0:T(8,128)(2,1)} %copy-done.5, bf16[272,256]{1,0:T(8,128)(2,1)} %copy-done.6, ...), custom_call_target="tpu_custom_call" | custom-call | tf_op jit(solution)/shard_map/attend/pallas_call | solution.py:157
  74.9 4.7 %all-gather.6.cloned.1.call-done = bf16[2176,512]{1,0:T(8,128)(2,1)} async-done(((bf16[272,512]{1,0:T(8,128)(2,1)}), bf16[2176,512]{1,0:T(8,128)(2,1)}) %all-gather.6.cloned.1.call-update) | async-done | bytes 2228240 | tf_op jit(solution)/shard_map/all_gather | solution.py:215
  79.6 5.3 %attend.3 = bf16[4,384,256]{2,1,0:T(8,128)(2,1)} custom-call(s32[11]{0:T(128)} %concatenate.92.spots, bf16[4,256,128]{2,1,0:T(8,128)(2,1)} %copy-done.2, bf16[272,256]{1,0:T(8,128)(2,1)} %copy-done.11, f32[1024,128]{1,0:T(8,128)} %get-tuple-element.34.refs_1_, f32[1024,128]{1,0:T(8,128)} %get-tuple-element.35.refs_2_, ...), custom_call_target="tpu_custom_call" | custom-call | tf_op jit(solution)/shard_map/attend/pallas_call | solution.py:157
  84.9 16.0 %all_to_all.40 = bf16[4,384,256]{2,1,0:T(8,128)(2,1)S(1)} all-to-all(bf16[4,384,256]{2,1,0:T(8,128)(2,1)} %attend.3), channel_id=1, replica_groups=mesh['seq_0'=8,'near'=2,'seq_1'=2,'seq_2'=2,'row_0'=4,'row_1'=2] {'near'..., dimensions={0} | all-to-all | bytes 1572864 | tf_op jit(solution)/shard_map/all_to_all | solution.py:30
  102.1 4.4 %collective-permute-start.8 = (bf16[128,128]{1,0:T(8,128)(2,1)S(1)}, bf16[128,128]{1,0:T(8,128)(2,1)S(1)}, u32[]{:S(2)}, u32[]{:S(2)}) collective-permute-start(bf16[128,128]{1,0:T(8,128)(2,1)S(1)} %slice.247), channel_id=1, source_target_pairs={{0,8},{8,0},{1,9},{9,1},{2,10},{10,2},{3,11},{11,3},{4,12},{12,4},... | collective-permute-start | bytes 98312 | tf_op jit(solution)/shard_map/ppermute | solution.py:262
  106.5 0.7 slice.250
  108.2 0.9 pad_maximum_fusion.1
  109.1 3.7 %all-to-all-start.2 = ((bf16[8,272,128]{2,1,0:T(8,128)(2,1)}), bf16[8,272,128]{2,1,0:T(8,128)(2,1)S(1)}, u32[]{:S(2)}, u32[]{:S(2)}) async-start(bf16[8,272,128]{2,1,0:T(8,128)(2,1)} %pad_maximum_fusion.1), calls=%async_computation.2 | async-start | bytes 1114112 | tf_op jit(solution)/shard_map/all_to_all | solution.py:30
  112.8 3.4 %collective-permute-start.9 = (bf16[128,512]{1,0:T(8,128)(2,1)S(1)}, bf16[128,512]{1,0:T(8,128)(2,1)}, u32[]{:S(2)}, u32[]{:S(2)}) collective-permute-start(bf16[128,512]{1,0:T(8,128)(2,1)S(1)} %copy-done.16), channel_id=1, source_target_pairs={{0,1},{1,0},{2,3},{3,2},{4,5},{5,4},{6,7},{7,6},{8,9},{9,8},{10,11... | collective-permute-start | bytes 393224 | tf_op jit(solution)/shard_map/ppermute | solution.py:216
  117.4 0.7 pad.25.clone
  118.6 0.8 dynamic_slice.28
  119.4 3.2 %all-to-all-done.2 = bf16[8,272,128]{2,1,0:T(8,128)(2,1)S(1)} async-done(((bf16[8,272,128]{2,1,0:T(8,128)(2,1)}), bf16[8,272,128]{2,1,0:T(8,128)(2,1)S(1)}, u32[]{:S(2)}, u32[]{:S(2)}) %all-to-all-start.2) | async-done | bytes 557088 | tf_op jit(solution)/shard_map/all_to_all | solution.py:30
  122.8 0.9 multiply_convert_fusion.4
  123.7 1.0 convolution_convert_fusion.2
  124.7 3.4 %all-to-all-start.3 = ((bf16[8,16,512]{2,1,0:T(8,128)(2,1)}), bf16[8,16,512]{2,1,0:T(8,128)(2,1)S(1)}, u32[]{:S(2)}, u32[]{:S(2)}) async-start(bf16[8,16,512]{2,1,0:T(8,128)(2,1)} %bitcast.28), calls=%async_computation.3 | async-start | bytes 262144 | tf_op jit(solution)/shard_map/all_to_all | solution.py:30
  128.1 1.5 fusion.52
  129.6 4.2 %all-to-all-done.3 = bf16[8,16,512]{2,1,0:T(8,128)(2,1)S(1)} async-done(((bf16[8,16,512]{2,1,0:T(8,128)(2,1)}), bf16[8,16,512]{2,1,0:T(8,128)(2,1)S(1)}, u32[]{:S(2)}, u32[]{:S(2)}) %all-to-all-start.3) | async-done | bytes 131104 | tf_op jit(solution)/shard_map/all_to_all | solution.py:30
  133.8 1.2 all-gather.4.cloned.1.call-done
  134.9 4.0 %collective-permute-start.10 = (bf16[4,512,256]{2,1,0:T(8,128)(2,1)}, bf16[4,512,256]{2,1,0:T(8,128)(2,1)}, u32[]{:S(2)}, u32[]{:S(2)}) collective-permute-start(bf16[4,512,256]{2,1,0:T(8,128)(2,1)} %all-gather.4.cloned.1.call-done), channel_id=1, source_target_pairs={{0,8},{8,0},{1,9},{9,1},{2,10},{10,2},{3,11},{11,3},{4,12},{12,4},... | collective-permute-start | bytes 3145736 | tf_op jit(solution)/shard_map/ppermute | solution.py:285
  140.4 2.9 %collective-permute-start.11 = (bf16[128,640]{1,0:T(8,128)(2,1)S(1)}, bf16[128,640]{1,0:T(8,128)(2,1)S(1)}, u32[]{:S(2)}, u32[]{:S(2)}) collective-permute-start(bf16[128,640]{1,0:T(8,128)(2,1)S(1)} %pad_maximum_fusion.4), channel_id=1, source_target_pairs={{0,1},{1,0},{2,3},{3,2},{4,5},{5,4},{6,7},{7,6},{8,9},{9,8},{10,11... | collective-permute-start | bytes 491528 | tf_op jit(solution)/shard_map/ppermute | solution.py:307
  143.3 0.8 maximum_maximum_fusion.4
  144.2 3.9 %collective-permute-done.11 = bf16[128,640]{1,0:T(8,128)(2,1)S(1)} collective-permute-done((bf16[128,640]{1,0:T(8,128)(2,1)S(1)}, bf16[128,640]{1,0:T(8,128)(2,1)S(1)}, u32[]{:S(2)}, u32[]{:S(2)}) %collective-permute-start.11) | collective-permute-done | bytes 163872 | tf_op jit(solution)/shard_map/ppermute | solution.py:307
  148.2 1.4 broadcast_select_fusion.1
  150.5 0.7 fusion.16
  151.2 1.5 fusion.1
  152.8 0.7 convolution_bitcast_fusion
  153.8 3.1 %collective-permute-start.12 = (bf16[128,640]{1,0:T(8,128)(2,1)S(1)}, bf16[128,640]{1,0:T(8,128)(2,1)S(1)}, u32[]{:S(2)}, u32[]{:S(2)}) collective-permute-start(bf16[128,640]{1,0:T(8,128)(2,1)S(1)} %slice.316), channel_id=1, source_target_pairs={{0,1},{1,0},{2,3},{3,2},{4,5},{5,4},{6,7},{7,6},{8,9},{9,8},{10,11... | collective-permute-start | bytes 491528 | tf_op jit(solution)/shard_map/ppermute | solution.py:314
  157.0 3.6 %collective-permute-done.12 = bf16[128,640]{1,0:T(8,128)(2,1)S(1)} collective-permute-done((bf16[128,640]{1,0:T(8,128)(2,1)S(1)}, bf16[128,640]{1,0:T(8,128)(2,1)S(1)}, u32[]{:S(2)}, u32[]{:S(2)}) %collective-permute-start.12) | collective-permute-done | bytes 163872 | tf_op jit(solution)/shard_map/ppermute | solution.py:314
  161.7 0.8 fusion.19
  162.6 4.1 %all-to-all-start.4 = ((bf16[8,64,512]{2,1,0:T(8,128)(2,1)}), bf16[8,64,512]{2,1,0:T(8,128)(2,1)}, u32[]{:S(2)}, u32[]{:S(2)}) async-start(bf16[8,64,512]{2,1,0:T(8,128)(2,1)} %fusion.19), calls=%async_computation.4 | async-start | bytes 1048576 | tf_op jit(solution)/shard_map/all_to_all | solution.py:30
  166.8 1.8 slice.223
  168.7 0.6 copy.103
  169.3 5.7 %all-to-all-done.4 = bf16[8,64,512]{2,1,0:T(8,128)(2,1)} async-done(((bf16[8,64,512]{2,1,0:T(8,128)(2,1)}), bf16[8,64,512]{2,1,0:T(8,128)(2,1)}, u32[]{:S(2)}, u32[]{:S(2)}) %all-to-all-start.4) | async-done | bytes 524320 | tf_op jit(solution)/shard_map/all_to_all | solution.py:30
  175.0 0.9 slice.259
  175.9 1.9 fusion.2
  177.8 0.9 convolution_convert_fusion.7
  178.7 0.9 fusion.7
  180.0 1.1 convert_reduce_fusion.1
  181.2 13.1 %all_to_all.41 = bf16[8,12,256]{2,1,0:T(8,128)(2,1)S(1)} all-to-all(bf16[8,12,256]{2,1,0:T(8,128)(2,1)S(1)} %convert_element_type.134), channel_id=1, replica_groups=mesh['seq_0'=8,'near'=2,'seq_1'=2,'seq_2'=2,'row_0'=4,'row_1'=2] {'near'..., dimensions={0} | all-to-all | bytes 98304 | tf_op jit(solution)/shard_map/all_to_all | solution.py:30
  194.3 22.9 %all_to_all.42 = bf16[8,12,256]{2,1,0:T(8,128)(2,1)S(1)} all-to-all(bf16[8,12,256]{2,1,0:T(8,128)(2,1)S(1)} %broadcast_in_dim.28), channel_id=1, replica_groups=mesh['seq_0'=8,'near'=2,'seq_1'=2,'seq_2'=2,'row_0'=4,'row_1'=2] {'seq_0'}, dimensions={0} | all-to-all | bytes 98304 | tf_op jit(solution)/shard_map/all_to_all | solution.py:30
  217.2 10.5 %all_to_all.43 = bf16[8,12,256]{2,1,0:T(8,128)(2,1)S(1)} all-to-all(bf16[8,12,256]{2,1,0:T(8,128)(2,1)S(1)} %broadcast_in_dim.29), channel_id=1, replica_groups=mesh['seq_0'=8,'near'=2,'seq_1'=2,'seq_2'=2,'row_0'=4,'row_1'=2] {'near'..., dimensions={0} | all-to-all | bytes 98304 | tf_op jit(solution)/shard_map/all_to_all | solution.py:30
  227.7 0.6 fusion.55
  229.0 0.6 maximum_bitcast_fusion.3
  (166 shorter events, 10.7 us)
Async XLA Ops:
  7.2 100.2 %copy-start = (bf16[256,2048]{1,0:T(8,128)(2,1)S(1)}, bf16[256,2048]{1,0:T(8,128)(2,1)}, u32[]{:S(2)}) copy-start(bf16[256,2048]{1,0:T(8,128)(2,1)} %param.25) | copy-start | bytes 3145732
  7.2 19.0 %copy-start.29 = (bf16[256,8]{0,1:T(8,128)(2,1)S(1)}, bf16[256,8]{0,1:T(8,128)(2,1)}, u32[]{:S(2)}) copy-start(bf16[256,8]{0,1:T(8,128)(2,1)} %param.35) | copy-start | bytes 12292
  7.2 19.0 %copy-start.30 = (bf16[256,8]{0,1:T(8,128)(2,1)S(1)}, bf16[256,8]{0,1:T(8,128)(2,1)}, u32[]{:S(2)}) copy-start(bf16[256,8]{0,1:T(8,128)(2,1)} %param.34) | copy-start | bytes 12292
  7.2 72.4 %all-gather.6.cloned.1.call-start = ((), (), s32[]{:S(2)}) async-start(), calls=%async_computation.9 | async-start | bytes 2506752 | tf_op jit(solution)/shard_map/all_gather | solution.py:215
  12.2 9.7 %collective-permute-start = (bf16[128,384]{1,0:T(8,128)(2,1)S(1)}, bf16[128,384]{1,0:T(8,128)(2,1)S(1)}, u32[]{:S(2)}, u32[]{:S(2)}) collective-permute-start(bf16[128,384]{1,0:T(8,128)(2,1)S(1)} %pad_maximum_fusion.6), channel_id=1, source_target_pairs={{0,8},{8,0},{1,9},{9,1},{2,10},{10,2},{3,11},{11,3},{4,12},{12,4},... | collective-permute-start | bytes 294920 | tf_op jit(solution)/shard_map/ppermute | solution.py:218
  22.6 16.5 %all-to-all-start = ((bf16[4,256,128]{2,1,0:T(8,128)(2,1)}), bf16[4,256,128]{2,1,0:T(8,128)(2,1)S(1)}, u32[]{:S(2)}, u32[]{:S(2)}) async-start(bf16[4,256,128]{2,1,0:T(8,128)(2,1)} %broadcast_in_dim.21), calls=%async_computation | async-start | bytes 524288 | tf_op jit(solution)/shard_map/all_to_all | solution.py:30
  26.0 108.9 %all-gather.4.cloned.1.call-start = ((), (), s32[]{:S(2)}) async-start(), calls=%async_computation.8 | async-start | bytes 1310720 | tf_op jit(solution)/shard_map/all_gather | solution.py:256
  26.2 41.6 %copy-start.3 = (bf16[272,256]{1,0:T(8,128)(2,1)}, bf16[272,256]{1,0:T(8,128)(2,1)S(1)}, u32[]{:S(2)}) copy-start(bf16[272,256]{1,0:T(8,128)(2,1)S(1)} %pad_maximum_fusion.5.refs_0_.refs_4_) | copy-start | bytes 417796
  26.2 11.7 %collective-permute-start.1 = (bf16[272,256]{1,0:T(8,128)(2,1)S(1)}, bf16[272,256]{1,0:T(8,128)(2,1)S(1)}, u32[]{:S(2)}, u32[]{:S(2)}) collective-permute-start(bf16[272,256]{1,0:T(8,128)(2,1)S(1)} %pad_maximum_fusion.5.refs_0_.refs_4_), channel_id=1, source_target_pairs={{0,64},{64,128},{128,192},{192,256},{256,320},{320,384},{384,448},... | collective-permute-start | bytes 417800 | tf_op jit(solution)/shard_map/ppermute | solution.py:231
  28.1 11.0 %collective-permute-start.2 = (bf16[272,256]{1,0:T(8,128)(2,1)S(1)}, bf16[272,256]{1,0:T(8,128)(2,1)S(1)}, u32[]{:S(2)}, u32[]{:S(2)}) collective-permute-start(bf16[272,256]{1,0:T(8,128)(2,1)S(1)} %pad_maximum_fusion.5.refs_0_.refs_4_), channel_id=1, source_target_pairs={{0,448},{64,0},{128,64},{192,128},{256,192},{320,256},{384,320},{4... | collective-permute-start | bytes 417800 | tf_op jit(solution)/shard_map/ppermute | solution.py:235
  37.9 29.9 %copy-start.5 = (bf16[272,256]{1,0:T(8,128)(2,1)}, bf16[272,256]{1,0:T(8,128)(2,1)S(1)}, u32[]{:S(2)}) copy-start(bf16[272,256]{1,0:T(8,128)(2,1)S(1)} %collective-permute-done.1.refs_1_.refs_5_) | copy-start | bytes 417796
  39.1 28.7 %copy-start.6 = (bf16[272,256]{1,0:T(8,128)(2,1)}, bf16[272,256]{1,0:T(8,128)(2,1)S(1)}, u32[]{:S(2)}) copy-start(bf16[272,256]{1,0:T(8,128)(2,1)S(1)} %collective-permute-done.2.refs_2_.refs_6_) | copy-start | bytes 417796
  39.1 28.7 %copy-start.2 = (bf16[4,256,128]{2,1,0:T(8,128)(2,1)}, bf16[4,256,128]{2,1,0:T(8,128)(2,1)S(1)}, u32[]{:S(2)}) copy-start(bf16[4,256,128]{2,1,0:T(8,128)(2,1)S(1)} %all-to-all-done.queries) | copy-start | bytes 786436
  39.1 7.9 %collective-permute-start.3 = (bf16[272,256]{1,0:T(8,128)(2,1)S(1)}, bf16[272,256]{1,0:T(8,128)(2,1)S(1)}, u32[]{:S(2)}, u32[]{:S(2)}) collective-permute-start(bf16[272,256]{1,0:T(8,128)(2,1)S(1)} %collective-permute-done.1.refs_1_.refs_5_), channel_id=1, source_target_pairs={{0,64},{64,128},{128,192},{192,256},{256,320},{320,384},{384,448},... | collective-permute-start | bytes 417800 | tf_op jit(solution)/shard_map/ppermute | solution.py:231
  43.5 11.8 %collective-permute-start.4 = (bf16[272,256]{1,0:T(8,128)(2,1)S(1)}, bf16[272,256]{1,0:T(8,128)(2,1)S(1)}, u32[]{:S(2)}, u32[]{:S(2)}) collective-permute-start(bf16[272,256]{1,0:T(8,128)(2,1)S(1)} %collective-permute-done.2.refs_2_.refs_6_), channel_id=1, source_target_pairs={{0,448},{64,0},{128,64},{192,128},{256,192},{320,256},{384,320},{4... | collective-permute-start | bytes 417800 | tf_op jit(solution)/shard_map/ppermute | solution.py:235
  47.0 20.8 %copy-start.7 = (bf16[272,256]{1,0:T(8,128)(2,1)}, bf16[272,256]{1,0:T(8,128)(2,1)S(1)}, u32[]{:S(2)}) copy-start(bf16[272,256]{1,0:T(8,128)(2,1)S(1)} %collective-permute-done.3.refs_3_.refs_7_) | copy-start | bytes 417796
  47.0 14.0 %collective-permute-start.5 = (bf16[272,256]{1,0:T(8,128)(2,1)S(1)}, bf16[272,256]{1,0:T(8,128)(2,1)S(1)}, u32[]{:S(2)}, u32[]{:S(2)}) collective-permute-start(bf16[272,256]{1,0:T(8,128)(2,1)S(1)} %collective-permute-done.3.refs_3_.refs_7_), channel_id=1, source_target_pairs={{0,64},{64,128},{128,192},{192,256},{256,320},{320,384},{384,448},... | collective-permute-start | bytes 417800 | tf_op jit(solution)/shard_map/ppermute | solution.py:231
  55.4 12.5 %copy-start.8 = (bf16[272,256]{1,0:T(8,128)(2,1)}, bf16[272,256]{1,0:T(8,128)(2,1)S(1)}, u32[]{:S(2)}) copy-start(bf16[272,256]{1,0:T(8,128)(2,1)S(1)} %collective-permute-done.4.refs_4_.refs_8_) | copy-start | bytes 417796
  55.4 12.4 %collective-permute-start.6 = (bf16[272,256]{1,0:T(8,128)(2,1)S(1)}, bf16[272,256]{1,0:T(8,128)(2,1)S(1)}, u32[]{:S(2)}, u32[]{:S(2)}) collective-permute-start(bf16[272,256]{1,0:T(8,128)(2,1)S(1)} %collective-permute-done.4.refs_4_.refs_8_), channel_id=1, source_target_pairs={{0,448},{64,0},{128,64},{192,128},{256,192},{320,256},{384,320},{4... | collective-permute-start | bytes 417800 | tf_op jit(solution)/shard_map/ppermute | solution.py:235
  61.0 6.8 %copy-start.9 = (bf16[272,256]{1,0:T(8,128)(2,1)}, bf16[272,256]{1,0:T(8,128)(2,1)S(1)}, u32[]{:S(2)}) copy-start(bf16[272,256]{1,0:T(8,128)(2,1)S(1)} %collective-permute-done.5.refs_5_.refs_9_) | copy-start | bytes 417796
  61.0 13.9 %collective-permute-start.7 = (bf16[272,256]{1,0:T(8,128)(2,1)S(1)}, bf16[272,256]{1,0:T(8,128)(2,1)S(1)}, u32[]{:S(2)}, u32[]{:S(2)}) collective-permute-start(bf16[272,256]{1,0:T(8,128)(2,1)S(1)} %collective-permute-done.5.refs_5_.refs_9_), channel_id=1, source_target_pairs={{0,64},{64,128},{128,192},{192,256},{256,320},{320,384},{384,448},... | collective-permute-start | bytes 417800 | tf_op jit(solution)/shard_map/ppermute | solution.py:231
  67.9 0.7 copy-start.10
  74.9 4.7 %copy-start.11 = (bf16[272,256]{1,0:T(8,128)(2,1)}, bf16[272,256]{1,0:T(8,128)(2,1)S(1)}, u32[]{:S(2)}) copy-start(bf16[272,256]{1,0:T(8,128)(2,1)S(1)} %collective-permute-done.7.refs_0_.refs_11_) | copy-start | bytes 417796
  102.0 6.0 %copy-start.37 = (bf16[256,16]{0,1:T(8,128)(2,1)S(1)}, bf16[256,16]{0,1:T(8,128)(2,1)}, u32[]{:S(2)}) copy-start(bf16[256,16]{0,1:T(8,128)(2,1)} %param.26) | copy-start | bytes 24580
  102.1 5.2 %collective-permute-start.8 = (bf16[128,128]{1,0:T(8,128)(2,1)S(1)}, bf16[128,128]{1,0:T(8,128)(2,1)S(1)}, u32[]{:S(2)}, u32[]{:S(2)}) collective-permute-start(bf16[128,128]{1,0:T(8,128)(2,1)S(1)} %slice.247), channel_id=1, source_target_pairs={{0,8},{8,0},{1,9},{9,1},{2,10},{10,2},{3,11},{11,3},{4,12},{12,4},... | collective-permute-start | bytes 98312 | tf_op jit(solution)/shard_map/ppermute | solution.py:262
  107.3 1.7 copy-start.14
  107.3 1.7 copy-start.15
  107.7 5.1 %copy-start.16 = (bf16[128,512]{1,0:T(8,128)(2,1)S(1)}, bf16[128,512]{1,0:T(8,128)(2,1)}, u32[]{:S(2)}) copy-start(bf16[128,512]{1,0:T(8,128)(2,1)} %param.39) | copy-start | bytes 393220
  107.7 8.5 %copy-start.40 = (s32[128]{0:T(128)S(1)}, s32[128]{0:T(128)}, u32[]{:S(2)}) copy-start(s32[128]{0:T(128)} %param.23) | copy-start | bytes 1540
  107.7 8.7 %copy-start.28 = (bf16[8,512]{1,0:T(8,128)(2,1)S(1)}, bf16[8,512]{1,0:T(8,128)(2,1)}, u32[]{:S(2)}) copy-start(bf16[8,512]{1,0:T(8,128)(2,1)} %param.32) | copy-start | bytes 24580
  107.7 9.3 %copy-start.38 = (f32[8,16]{1,0:T(8,128)S(1)}, f32[8,16]{1,0:T(8,128)}, u32[]{:S(2)}) copy-start(f32[8,16]{1,0:T(8,128)} %param.38) | copy-start | bytes 1540
  108.0 14.8 %copy-start.39 = (f32[8,16]{1,0:T(8,128)S(1)}, f32[8,16]{1,0:T(8,128)}, u32[]{:S(2)}) copy-start(f32[8,16]{1,0:T(8,128)} %param.28) | copy-start | bytes 1540
  108.0 15.7 %copy-start.1 = (bf16[256,512]{1,0:T(8,128)(2,1)S(1)}, bf16[256,512]{1,0:T(8,128)(2,1)}, u32[]{:S(2)}) copy-start(bf16[256,512]{1,0:T(8,128)(2,1)} %param.29) | copy-start | bytes 786436
  108.0 15.6 %copy-start.17 = (bf16[128,256]{1,0:T(8,128)(2,1)S(1)}, bf16[128,256]{1,0:T(8,128)(2,1)}, u32[]{:S(2)}) copy-start(bf16[128,256]{1,0:T(8,128)(2,1)} %param.24) | copy-start | bytes 196612
  108.0 15.6 %copy-start.23 = (bf16[16,256]{1,0:T(8,128)(2,1)S(1)}, bf16[16,256]{1,0:T(8,128)(2,1)}, u32[]{:S(2)}) copy-start(bf16[16,256]{1,0:T(8,128)(2,1)} %param.27) | copy-start | bytes 24580
  109.1 30.0 %copy-start.13 = (bf16[256,512]{1,0:T(8,128)(2,1)S(1)}, bf16[256,512]{1,0:T(8,128)(2,1)}, u32[]{:S(2)}) copy-start(bf16[256,512]{1,0:T(8,128)(2,1)} %param.31) | copy-start | bytes 786436
  109.1 30.8 %copy-start.24 = (f32[512]{0:T(512)S(1)}, f32[512]{0:T(512)}, u32[]{:S(2)}) copy-start(f32[512]{0:T(512)} %param.33) | copy-start | bytes 6148
  109.1 13.5 %all-to-all-start.2 = ((bf16[8,272,128]{2,1,0:T(8,128)(2,1)}), bf16[8,272,128]{2,1,0:T(8,128)(2,1)S(1)}, u32[]{:S(2)}, u32[]{:S(2)}) async-start(bf16[8,272,128]{2,1,0:T(8,128)(2,1)} %pad_maximum_fusion.1), calls=%async_computation.2 | async-start | bytes 1114112 | tf_op jit(solution)/shard_map/all_to_all | solution.py:30
  112.8 27.2 %copy-start.18 = (bf16[512,16]{0,1:T(8,128)(2,1)S(1)}, bf16[512,16]{0,1:T(8,128)(2,1)}, u32[]{:S(2)}) copy-start(bf16[512,16]{0,1:T(8,128)(2,1)} %param.36) | copy-start | bytes 49156
  112.8 38.4 %collective-permute-start.9 = (bf16[128,512]{1,0:T(8,128)(2,1)S(1)}, bf16[128,512]{1,0:T(8,128)(2,1)}, u32[]{:S(2)}, u32[]{:S(2)}) collective-permute-start(bf16[128,512]{1,0:T(8,128)(2,1)S(1)} %copy-done.16), channel_id=1, source_target_pairs={{0,1},{1,0},{2,3},{3,2},{4,5},{5,4},{6,7},{7,6},{8,9},{9,8},{10,11... | collective-permute-start | bytes 393224 | tf_op jit(solution)/shard_map/ppermute | solution.py:216
  116.4 0.6 copy-start.33
  122.7 11.1 %copy-start.12 = (f32[272,128]{1,0:T(8,128)}, f32[272,128]{1,0:T(8,128)S(1)}, u32[]{:S(2)}) copy-start(f32[272,128]{1,0:T(8,128)S(1)} %convert_reduce_fusion) | copy-start | bytes 417796
  123.7 1.0 copy-start.26
  124.7 9.1 %all-to-all-start.3 = ((bf16[8,16,512]{2,1,0:T(8,128)(2,1)}), bf16[8,16,512]{2,1,0:T(8,128)(2,1)S(1)}, u32[]{:S(2)}, u32[]{:S(2)}) async-start(bf16[8,16,512]{2,1,0:T(8,128)(2,1)} %bitcast.28), calls=%async_computation.3 | async-start | bytes 262144 | tf_op jit(solution)/shard_map/all_to_all | solution.py:30
  134.9 13.3 %copy-start.4 = (bf16[4,512,256]{2,1,0:T(8,128)(2,1)S(1)}, bf16[4,512,256]{2,1,0:T(8,128)(2,1)}, u32[]{:S(2)}) copy-start(bf16[4,512,256]{2,1,0:T(8,128)(2,1)} %all-gather.4.cloned.1.call-done) | copy-start | bytes 3145732
  134.9 13.3 %collective-permute-start.10 = (bf16[4,512,256]{2,1,0:T(8,128)(2,1)}, bf16[4,512,256]{2,1,0:T(8,128)(2,1)}, u32[]{:S(2)}, u32[]{:S(2)}) collective-permute-start(bf16[4,512,256]{2,1,0:T(8,128)(2,1)} %all-gather.4.cloned.1.call-done), channel_id=1, source_target_pairs={{0,8},{8,0},{1,9},{9,1},{2,10},{10,2},{3,11},{11,3},{4,12},{12,4},... | collective-permute-start | bytes 3145736 | tf_op jit(solution)/shard_map/ppermute | solution.py:285
  139.3 0.5 copy-start.31
  140.4 7.7 %collective-permute-start.11 = (bf16[128,640]{1,0:T(8,128)(2,1)S(1)}, bf16[128,640]{1,0:T(8,128)(2,1)S(1)}, u32[]{:S(2)}, u32[]{:S(2)}) collective-permute-start(bf16[128,640]{1,0:T(8,128)(2,1)S(1)} %pad_maximum_fusion.4), channel_id=1, source_target_pairs={{0,1},{1,0},{2,3},{3,2},{4,5},{5,4},{6,7},{7,6},{8,9},{9,8},{10,11... | collective-permute-start | bytes 491528 | tf_op jit(solution)/shard_map/ppermute | solution.py:307
  149.8 0.7 copy-start.35
  153.5 7.4 %copy-start.25 = (f32[512]{0:T(512)S(1)}, f32[512]{0:T(512)}, u32[]{:S(2)}) copy-start(f32[512]{0:T(512)} %param.33) | copy-start | bytes 6148
  153.5 7.6 %copy-start.34 = (s32[128]{0:T(128)S(1)}, s32[128]{0:T(128)}, u32[]{:S(2)}) copy-start(s32[128]{0:T(128)} %copy-done.33) | copy-start | bytes 1540
  153.5 7.9 %copy-start.32 = (f32[128]{0:T(128)S(1)}, f32[128]{0:T(128)}, u32[]{:S(2)}) copy-start(f32[128]{0:T(128)} %copy-done.31) | copy-start | bytes 1540
  153.8 7.9 %copy-start.36 = (bf16[48]{0:T(256)(128)(2,1)S(1)}, bf16[48]{0:T(256)(128)(2,1)}, u32[]{:S(2)}) copy-start(bf16[48]{0:T(256)(128)(2,1)} %pad.22.clone) | copy-start | bytes 292
  153.8 6.8 %collective-permute-start.12 = (bf16[128,640]{1,0:T(8,128)(2,1)S(1)}, bf16[128,640]{1,0:T(8,128)(2,1)S(1)}, u32[]{:S(2)}, u32[]{:S(2)}) collective-permute-start(bf16[128,640]{1,0:T(8,128)(2,1)S(1)} %slice.316), channel_id=1, source_target_pairs={{0,1},{1,0},{2,3},{3,2},{4,5},{5,4},{6,7},{7,6},{8,9},{9,8},{10,11... | collective-permute-start | bytes 491528 | tf_op jit(solution)/shard_map/ppermute | solution.py:314
  162.6 12.4 %all-to-all-start.4 = ((bf16[8,64,512]{2,1,0:T(8,128)(2,1)}), bf16[8,64,512]{2,1,0:T(8,128)(2,1)}, u32[]{:S(2)}, u32[]{:S(2)}) async-start(bf16[8,64,512]{2,1,0:T(8,128)(2,1)} %fusion.19), calls=%async_computation.4 | async-start | bytes 1048576 | tf_op jit(solution)/shard_map/all_to_all | solution.py:30
  166.7 1.9 copy-start.19
  166.7 1.9 copy-start.20
  166.8 1.9 copy-start.21
  166.8 1.9 copy-start.22
  168.6 9.2 %copy-start.41 = (s32[128]{0:T(128)S(1)}, s32[128]{0:T(128)}, u32[]{:S(2)}) copy-start(s32[128]{0:T(128)} %param.23) | copy-start | bytes 1540
  168.6 11.1 %copy-start.27 = (bf16[128,16]{0,1:T(8,128)(2,1)S(1)}, bf16[128,16]{0,1:T(8,128)(2,1)}, u32[]{:S(2)}) copy-start(bf16[128,16]{0,1:T(8,128)(2,1)} %copy-done.26) | copy-start | bytes 12292
Sparse Core Ops, SparseCore 0:
  12.3 67.2 all-gather.5
  107.3 27.5 all-gather.3

commit v10 on v9

--- a/solution.py
+++ b/solution.py
@@ -123,17 +123,19 @@
         mass = jnp.sum(mass, axis=1, keepdims=True)
         safe = jnp.where(mass > 0, mass, 1.0)
         level = jnp.where(mass > 0, top + jnp.log(safe), -1e30)
-        level = jnp.broadcast_to(level, (rows, HEAD))
+        level = jnp.transpose(jnp.broadcast_to(level, (rows, HEAD)))[:16]
         high = level.astype(BF).astype(F32)
         middle = (level - high).astype(BF).astype(F32)
         low = level - high - middle
-        lane = lax.broadcasted_iota(jnp.int32, (rows, HEAD), 1)
-        level = jnp.where(lane < 32, high, jnp.where(lane < 64, middle, low))
-        refs[0][block, :rows, :HEAD] = (out / safe).astype(BF)
-        refs[0][block, :rows, HEAD:] = level.astype(BF)
+        line = lax.broadcasted_iota(jnp.int32, level.shape, 0)
+        level = jnp.where(line == 0, high, jnp.where(line == 1, middle, low))
+        out = (out / safe).astype(BF)
+        refs[0][block, :half, :HEAD] = out[:half]
+        refs[0][block, :half, HEAD:] = out[half:]
+        refs[0][block, half : half + 16, :] = level.astype(BF)
         for index, guest in enumerate(guests):
             extra = guest.shape[0]
-            spot = pl.multiple_of(rows + spots[2 + count + index] * extra, extra)
+            spot = pl.multiple_of(half + 16 + spots[2 + count + index] * extra, extra)
             refs[0][block, pl.ds(spot, extra), :] = guest[...]
 
 
@@ -141,7 +143,7 @@
     sides = queries.shape[0]
     finish = len(guests) > 0
     extra = guests[0].shape[0] - rows if finish else 0
-    tall = rows + extra * len(guests)
+    tall = rows // 2 + 16 + extra * len(guests)
     blocks = sides if finish else 2
     block = pl.BlockSpec((blocks * rows, HEAD), lambda k: (k, 0))
     asked = pl.BlockSpec((blocks, rows, HEAD), lambda k: (k, 0, 0))
@@ -241,26 +243,27 @@
     spots = jnp.stack([z * sides] + [k * sides + near * 2 + far for k in at]).astype(jnp.int32)
     spots = jnp.concatenate([core.astype(jnp.int32)[None], spots])
     state = attend(spots, queries, held[:-1], None, [], chip_rows)
-    state, last, weights = lax.optimization_barrier((state, held[-1], weights))
+    state, last = lax.optimization_barrier((state, held[-1]))
     spots = jnp.concatenate([spots[:2], spots[-1:], jnp.stack(at).astype(jnp.int32)])
     met = attend(spots, queries, [last], state, held[:-1] + [last], chip_rows)
+
+    met = exchange(met, QUAD)
+    riders = met[:, rows + 16 :].reshape(-1, units)
+    riders = lax.all_gather(riders, LINE, axis=0, tiled=False)
+    levels = met[:, rows : rows + 3].astype(F32).sum(axis=1)[:, :, None]
+    met = jnp.concatenate([met[:, :rows, :HEAD], met[:, :rows, HEAD:]], axis=1).astype(F32)
+    parts = jnp.exp(levels - jnp.max(levels, axis=0, keepdims=True))
+    merged = (parts * met).sum(axis=0) / parts.sum(axis=0)
+    merged = merged.astype(BF)
+    merged, weights = lax.optimization_barrier((merged, weights))
+    partner = lax.ppermute(merged[rows:], CORE, SWAP)
+    attended = in_pair_order(merged[:rows], partner, core, 1)
 
     local_whole = weights[:, :width].reshape(-1, columns)
     up_whole = unfold(weights[:, width : width + 8])
     up_whole = jnp.transpose(up_whole, (1, 0, 2)).reshape(RANK, -1)
     local_ups = unfold(weights[:, width + 8 :]).reshape(line, 2, RANK, units)
     local_ups = lax.dynamic_index_in_dim(local_ups, side, 1, keepdims=False)
-
-    met = exchange(met, QUAD)
-    riders = met[:, chip_rows:].reshape(-1, units)
-    riders = lax.all_gather(riders, LINE, axis=0, tiled=False)
-    met = met[:, :chip_rows].astype(F32)
-    levels = met[:, :, 128:129] + met[:, :, 160:161] + met[:, :, 192:193]
-    parts = jnp.exp(levels - jnp.max(levels, axis=0, keepdims=True))
-    merged = (parts * met[:, :, :HEAD]).sum(axis=0) / parts.sum(axis=0)
-    merged = merged.astype(BF)
-    partner = lax.ppermute(merged[rows:], CORE, SWAP)
-    attended = in_pair_order(merged[:rows], partner, core, 1)
 
     task_scales = select_rows(global_scales, patch_tasks)
     part = contract(output_weight, attended, 0, 1).astype(BF).reshape(row_count, width, rows)

time: 238 us -> 231 us (0.971)
  blocking collectives: 62.5 us -> 57.2 us
  waiting for transfers between devices: 35.8 us -> 32.2 us
    all_to_all x4, blocking collectives: 62.5 us -> 57.2 us  [exchange(): return lax.all_to_all(pieces, axis, split_axis=0, concat_axis=0, tiled=True)]
    all_gather x1, waiting for transfers between devices: 4.7 us -> 0.02 us  [body(): weights = lax.all_gather(weights, ROW, axis=0, tiled=False)]
  transfers between devices with their start and end apart: 19 -> 19, of which waited for: 14 -> 12; matrix products, arithmetic and copies ran while one was open for 7% -> 9% of each run, Pallas kernels for 3% -> 5%
where the time goes in v10:
time: 231 us; the launch traced here: 229 us
  starting transfers between devices  73.4 us (32%)
  blocking collectives  57.2 us (25%)
  waiting for transfers between devices  32.2 us (14%)
  local copies, waits for them, and re-layouts  18.4 us (8%)
  between operations  16.6 us (7%)
  Pallas kernels  11.9 us (5%)
  matrix products  10.9 us (5%)
  other arithmetic  8.75 us (4%)
    all_to_all x4, blocking collectives, exchange(): return lax.all_to_all(pieces, axis, split_axis=0, concat_axis=0, tiled=True)  57.2 us
    ppermute x4, starting transfers between devices, body(): rising = lax.ppermute(rising, Z, up)  19 us
    all_to_all x4, starting transfers between devices, exchange(): return lax.all_to_all(pieces, axis, split_axis=0, concat_axis=0, tiled=True)  15.3 us
    all_to_all x4, waiting for transfers between devices, exchange(): return lax.all_to_all(pieces, axis, split_axis=0, concat_axis=0, tiled=True)  12.9 us
    ppermute x3, starting transfers between devices, body(): falling = lax.ppermute(falling, Z, down)  12.2 us
    pallas_call x2, Pallas kernels, attend(): pl.pallas_call(functools.partial(attend_kernel, count=len(packets), start...  11.9 us
    ppermute x1, starting transfers between devices, body(): both = jnp.concatenate([mine, lax.ppermute(other, CORE, SWAP)], axis=0)  8.79 us
    dot_general x11, matrix products, contract(): lax.dot_general(left, right, (((left_dim,), (right_dim,)), ((), ())), pre...  7.46 us
  transfers between devices with their start and end apart: 19, of which 12 were waited for; matrix products, arithmetic and copies ran while one was open for 9% of the time, Pallas kernels for 5%

profile of v10, /device:TPU:1, one launch (start us, length us, event | category | flops | bytes accessed | tf_op | source)
XLA Modules:
  0.0 229.3 jit_solution(9507020628289456178)
XLA Ops:
  8.1 0.9 constant_dynamic-slice_fusion.5
  8.9 0.8 constant_dynamic-slice_fusion.3
  9.8 8.8 %collective-permute-start = (bf16[128,384]{1,0:T(8,128)(2,1)S(1)}, bf16[128,384]{1,0:T(8,128)(2,1)S(1)}, u32[]{:S(2)}, u32[]{:S(2)}) collective-permute-start(bf16[128,384]{1,0:T(8,128)(2,1)S(1)} %pad_maximum_fusion.6), channel_id=1, source_target_pairs={{0,8},{8,0},{1,9},{9,1},{2,10},{10,2},{3,11},{11,3},{4,12},{12,4},... | collective-permute-start | bytes 294920 | tf_op jit(solution)/shard_map/ppermute | solution.py:220
  18.6 0.7 fusion.55
  19.3 0.7 fusion.54
  20.1 1.7 maximum_maximum_fusion.3
  21.8 0.8 broadcast_in_dim.21
  22.5 3.4 %all-to-all-start = ((bf16[4,256,128]{2,1,0:T(8,128)(2,1)}), bf16[4,256,128]{2,1,0:T(8,128)(2,1)S(1)}, u32[]{:S(2)}, u32[]{:S(2)}) async-start(bf16[4,256,128]{2,1,0:T(8,128)(2,1)} %broadcast_in_dim.21), calls=%async_computation | async-start | bytes 524288 | tf_op jit(solution)/shard_map/all_to_all | solution.py:30
  26.1 1.9 collective-permute-start.1
  28.0 7.2 %collective-permute-start.2 = (bf16[272,256]{1,0:T(8,128)(2,1)S(1)}, bf16[272,256]{1,0:T(8,128)(2,1)S(1)}, u32[]{:S(2)}, u32[]{:S(2)}) collective-permute-start(bf16[272,256]{1,0:T(8,128)(2,1)S(1)} %pad_maximum_fusion.5.refs_0_.refs_4_), channel_id=1, source_target_pairs={{0,448},{64,0},{128,64},{192,128},{256,192},{320,256},{384,320},{4... | collective-permute-start | bytes 417800 | tf_op jit(solution)/shard_map/ppermute | solution.py:237
  35.2 3.0 %collective-permute-done.1.refs_1_.refs_5_ = bf16[272,256]{1,0:T(8,128)(2,1)S(1)} collective-permute-done((bf16[272,256]{1,0:T(8,128)(2,1)S(1)}, bf16[272,256]{1,0:T(8,128)(2,1)S(1)}, u32[]{:S(2)}, u32[]{:S(2)}) %collective-permute-start.1) | collective-permute-done | bytes 139296 | tf_op jit(solution)/shard_map/ppermute | solution.py:233
  38.3 1.1 collective-permute-done.2.refs_2_.refs_6_
  39.4 4.3 %collective-permute-start.3 = (bf16[272,256]{1,0:T(8,128)(2,1)S(1)}, bf16[272,256]{1,0:T(8,128)(2,1)S(1)}, u32[]{:S(2)}, u32[]{:S(2)}) collective-permute-start(bf16[272,256]{1,0:T(8,128)(2,1)S(1)} %collective-permute-done.1.refs_1_.refs_5_), channel_id=1, source_target_pairs={{0,64},{64,128},{128,192},{192,256},{256,320},{320,384},{384,448},... | collective-permute-start | bytes 417800 | tf_op jit(solution)/shard_map/ppermute | solution.py:233
  43.6 3.1 %collective-permute-start.4 = (bf16[272,256]{1,0:T(8,128)(2,1)S(1)}, bf16[272,256]{1,0:T(8,128)(2,1)S(1)}, u32[]{:S(2)}, u32[]{:S(2)}) collective-permute-start(bf16[272,256]{1,0:T(8,128)(2,1)S(1)} %collective-permute-done.2.refs_2_.refs_6_), channel_id=1, source_target_pairs={{0,448},{64,0},{128,64},{192,128},{256,192},{320,256},{384,320},{4... | collective-permute-start | bytes 417800 | tf_op jit(solution)/shard_map/ppermute | solution.py:237
  46.8 0.9 collective-permute-done.3.refs_3_.refs_7_
  47.7 7.8 %collective-permute-start.5 = (bf16[272,256]{1,0:T(8,128)(2,1)S(1)}, bf16[272,256]{1,0:T(8,128)(2,1)S(1)}, u32[]{:S(2)}, u32[]{:S(2)}) collective-permute-start(bf16[272,256]{1,0:T(8,128)(2,1)S(1)} %collective-permute-done.3.refs_3_.refs_7_), channel_id=1, source_target_pairs={{0,64},{64,128},{128,192},{192,256},{256,320},{320,384},{384,448},... | collective-permute-start | bytes 417800 | tf_op jit(solution)/shard_map/ppermute | solution.py:233
  55.5 1.9 collective-permute-start.6
  57.4 3.4 %collective-permute-done.5.refs_5_.refs_9_ = bf16[272,256]{1,0:T(8,128)(2,1)S(1)} collective-permute-done((bf16[272,256]{1,0:T(8,128)(2,1)S(1)}, bf16[272,256]{1,0:T(8,128)(2,1)S(1)}, u32[]{:S(2)}, u32[]{:S(2)}) %collective-permute-start.5) | collective-permute-done | bytes 139296 | tf_op jit(solution)/shard_map/ppermute | solution.py:233
  60.8 5.1 %collective-permute-start.7 = (bf16[272,256]{1,0:T(8,128)(2,1)S(1)}, bf16[272,256]{1,0:T(8,128)(2,1)S(1)}, u32[]{:S(2)}, u32[]{:S(2)}) collective-permute-start(bf16[272,256]{1,0:T(8,128)(2,1)S(1)} %collective-permute-done.5.refs_5_.refs_9_), channel_id=1, source_target_pairs={{0,64},{64,128},{128,192},{192,256},{256,320},{320,384},{384,448},... | collective-permute-start | bytes 417800 | tf_op jit(solution)/shard_map/ppermute | solution.py:233
  66.0 0.6 concatenate.100.spots
  66.6 0.6 concatenate.95.spots
  67.2 1.6 collective-permute-done.6.refs_6_.refs_10_
  68.9 0.7 copy-done.10
  69.5 6.4 %attend.2 = (f32[1024,128]{1,0:T(8,128)}, f32[1024,128]{1,0:T(8,128)}, f32[1024,128]{1,0:T(8,128)}) custom-call(s32[10]{0:T(128)} %concatenate.100.spots, bf16[4,256,128]{2,1,0:T(8,128)(2,1)} %copy-done.2, bf16[272,256]{1,0:T(8,128)(2,1)} %copy-done.3, bf16[272,256]{1,0:T(8,128)(2,1)} %copy-done.5, bf16[272,256]{1,0:T(8,128)(2,1)} %copy-done.6, ...), custom_call_target="tpu_custom_call" | custom-call | tf_op jit(solution)/shard_map/attend/pallas_call | solution.py:159
  75.9 0.6 copy-done.11
  76.6 5.5 %attend.3 = bf16[4,272,256]{2,1,0:T(8,128)(2,1)} custom-call(s32[11]{0:T(128)} %concatenate.95.spots, bf16[4,256,128]{2,1,0:T(8,128)(2,1)} %copy-done.2, bf16[272,256]{1,0:T(8,128)(2,1)} %copy-done.11, f32[1024,128]{1,0:T(8,128)} %get-tuple-element.32.refs_1_, f32[1024,128]{1,0:T(8,128)} %get-tuple-element.33.refs_2_, ...), custom_call_target="tpu_custom_call" | custom-call | tf_op jit(solution)/shard_map/attend/pallas_call | solution.py:159
  82.1 12.6 %all_to_all.40 = bf16[4,272,256]{2,1,0:T(8,128)(2,1)S(1)} all-to-all(bf16[4,272,256]{2,1,0:T(8,128)(2,1)} %attend.3), channel_id=1, replica_groups=mesh['seq_0'=8,'near'=2,'seq_1'=2,'seq_2'=2,'row_0'=4,'row_1'=2] {'near'..., dimensions={0} | all-to-all | bytes 1114112 | tf_op jit(solution)/shard_map/all_to_all | solution.py:30
  95.1 4.4 %collective-permute-start.8 = (bf16[128,128]{1,0:T(8,128)(2,1)S(1)}, bf16[128,128]{1,0:T(8,128)(2,1)S(1)}, u32[]{:S(2)}, u32[]{:S(2)}) collective-permute-start(bf16[128,128]{1,0:T(8,128)(2,1)S(1)} %slice.198), channel_id=1, source_target_pairs={{0,8},{8,0},{1,9},{9,1},{2,10},{10,2},{3,11},{11,3},{4,12},{12,4},... | collective-permute-start | bytes 98312 | tf_op jit(solution)/shard_map/ppermute | solution.py:259
  99.5 0.7 slice.238
  101.2 0.9 pad_maximum_fusion.1
  102.1 4.2 %all-to-all-start.2 = ((bf16[8,272,128]{2,1,0:T(8,128)(2,1)}), bf16[8,272,128]{2,1,0:T(8,128)(2,1)S(1)}, u32[]{:S(2)}, u32[]{:S(2)}) async-start(bf16[8,272,128]{2,1,0:T(8,128)(2,1)} %pad_maximum_fusion.1), calls=%async_computation.2 | async-start | bytes 1114112 | tf_op jit(solution)/shard_map/all_to_all | solution.py:30
  106.3 3.5 %collective-permute-start.9 = (bf16[128,512]{1,0:T(8,128)(2,1)S(1)}, bf16[128,512]{1,0:T(8,128)(2,1)}, u32[]{:S(2)}, u32[]{:S(2)}) collective-permute-start(bf16[128,512]{1,0:T(8,128)(2,1)S(1)} %copy-done.16), channel_id=1, source_target_pairs={{0,1},{1,0},{2,3},{3,2},{4,5},{5,4},{6,7},{7,6},{8,9},{9,8},{10,11... | collective-permute-start | bytes 393224 | tf_op jit(solution)/shard_map/ppermute | solution.py:218
  111.0 0.7 pad.25.clone
  112.3 0.8 dynamic_slice.28
  113.0 2.9 %all-to-all-done.2 = bf16[8,272,128]{2,1,0:T(8,128)(2,1)S(1)} async-done(((bf16[8,272,128]{2,1,0:T(8,128)(2,1)}), bf16[8,272,128]{2,1,0:T(8,128)(2,1)S(1)}, u32[]{:S(2)}, u32[]{:S(2)}) %all-to-all-start.2) | async-done | bytes 557088 | tf_op jit(solution)/shard_map/all_to_all | solution.py:30
  116.1 0.9 multiply_convert_fusion.4
  117.0 1.0 convolution_convert_fusion.2
  118.0 3.5 %all-to-all-start.3 = ((bf16[8,16,512]{2,1,0:T(8,128)(2,1)}), bf16[8,16,512]{2,1,0:T(8,128)(2,1)S(1)}, u32[]{:S(2)}, u32[]{:S(2)}) async-start(bf16[8,16,512]{2,1,0:T(8,128)(2,1)} %bitcast.28), calls=%async_computation.3 | async-start | bytes 262144 | tf_op jit(solution)/shard_map/all_to_all | solution.py:30
  121.5 1.5 fusion.49
  123.0 4.2 %all-to-all-done.3 = bf16[8,16,512]{2,1,0:T(8,128)(2,1)S(1)} async-done(((bf16[8,16,512]{2,1,0:T(8,128)(2,1)}), bf16[8,16,512]{2,1,0:T(8,128)(2,1)S(1)}, u32[]{:S(2)}, u32[]{:S(2)}) %all-to-all-start.3) | async-done | bytes 131104 | tf_op jit(solution)/shard_map/all_to_all | solution.py:30
  127.5 5.4 %collective-permute-start.10 = (bf16[4,512,256]{2,1,0:T(8,128)(2,1)}, bf16[4,512,256]{2,1,0:T(8,128)(2,1)}, u32[]{:S(2)}, u32[]{:S(2)}) collective-permute-start(bf16[4,512,256]{2,1,0:T(8,128)(2,1)} %all-gather.4.cloned.1.call-done), channel_id=1, source_target_pairs={{0,8},{8,0},{1,9},{9,1},{2,10},{10,2},{3,11},{11,3},{4,12},{12,4},... | collective-permute-start | bytes 3145736 | tf_op jit(solution)/shard_map/ppermute | solution.py:288
  134.3 2.4 %collective-permute-start.11 = (bf16[128,640]{1,0:T(8,128)(2,1)S(1)}, bf16[128,640]{1,0:T(8,128)(2,1)S(1)}, u32[]{:S(2)}, u32[]{:S(2)}) collective-permute-start(bf16[128,640]{1,0:T(8,128)(2,1)S(1)} %pad_maximum_fusion.4), channel_id=1, source_target_pairs={{0,1},{1,0},{2,3},{3,2},{4,5},{5,4},{6,7},{7,6},{8,9},{9,8},{10,11... | collective-permute-start | bytes 491528 | tf_op jit(solution)/shard_map/ppermute | solution.py:310
  136.7 0.8 maximum_maximum_fusion.4
  137.6 4.4 %collective-permute-done.11 = bf16[128,640]{1,0:T(8,128)(2,1)S(1)} collective-permute-done((bf16[128,640]{1,0:T(8,128)(2,1)S(1)}, bf16[128,640]{1,0:T(8,128)(2,1)S(1)}, u32[]{:S(2)}, u32[]{:S(2)}) %collective-permute-start.11) | collective-permute-done | bytes 163872 | tf_op jit(solution)/shard_map/ppermute | solution.py:310
  142.1 1.4 broadcast_select_fusion.1
  144.5 0.7 fusion.16
  145.2 1.5 fusion.1
  146.7 0.7 convolution_bitcast_fusion
  147.8 2.4 %collective-permute-start.12 = (bf16[128,640]{1,0:T(8,128)(2,1)S(1)}, bf16[128,640]{1,0:T(8,128)(2,1)S(1)}, u32[]{:S(2)}, u32[]{:S(2)}) collective-permute-start(bf16[128,640]{1,0:T(8,128)(2,1)S(1)} %slice.296), channel_id=1, source_target_pairs={{0,1},{1,0},{2,3},{3,2},{4,5},{5,4},{6,7},{7,6},{8,9},{9,8},{10,11... | collective-permute-start | bytes 491528 | tf_op jit(solution)/shard_map/ppermute | solution.py:317
  150.2 4.4 %collective-permute-done.12 = bf16[128,640]{1,0:T(8,128)(2,1)S(1)} collective-permute-done((bf16[128,640]{1,0:T(8,128)(2,1)S(1)}, bf16[128,640]{1,0:T(8,128)(2,1)S(1)}, u32[]{:S(2)}, u32[]{:S(2)}) %collective-permute-start.12) | collective-permute-done | bytes 163872 | tf_op jit(solution)/shard_map/ppermute | solution.py:317
  155.7 0.8 fusion.19
  156.6 4.1 %all-to-all-start.4 = ((bf16[8,64,512]{2,1,0:T(8,128)(2,1)}), bf16[8,64,512]{2,1,0:T(8,128)(2,1)}, u32[]{:S(2)}, u32[]{:S(2)}) async-start(bf16[8,64,512]{2,1,0:T(8,128)(2,1)} %fusion.19), calls=%async_computation.4 | async-start | bytes 1048576 | tf_op jit(solution)/shard_map/all_to_all | solution.py:30
  160.8 1.8 slice.215
  162.7 0.6 copy.103
  163.3 5.9 %all-to-all-done.4 = bf16[8,64,512]{2,1,0:T(8,128)(2,1)} async-done(((bf16[8,64,512]{2,1,0:T(8,128)(2,1)}), bf16[8,64,512]{2,1,0:T(8,128)(2,1)}, u32[]{:S(2)}, u32[]{:S(2)}) %all-to-all-start.4) | async-done | bytes 524320 | tf_op jit(solution)/shard_map/all_to_all | solution.py:30
  169.2 0.9 slice.247
  170.1 1.9 fusion.2
  172.0 0.9 convolution_convert_fusion.7
  172.9 0.9 fusion.7
  174.2 1.1 convert_reduce_fusion.1
  175.3 11.3 %all_to_all.41 = bf16[8,12,256]{2,1,0:T(8,128)(2,1)S(1)} all-to-all(bf16[8,12,256]{2,1,0:T(8,128)(2,1)S(1)} %convert_element_type.138), channel_id=1, replica_groups=mesh['seq_0'=8,'near'=2,'seq_1'=2,'seq_2'=2,'row_0'=4,'row_1'=2] {'near'..., dimensions={0} | all-to-all | bytes 98304 | tf_op jit(solution)/shard_map/all_to_all | solution.py:30
  186.7 22.8 %all_to_all.42 = bf16[8,12,256]{2,1,0:T(8,128)(2,1)S(1)} all-to-all(bf16[8,12,256]{2,1,0:T(8,128)(2,1)S(1)} %broadcast_in_dim.28), channel_id=1, replica_groups=mesh['seq_0'=8,'near'=2,'seq_1'=2,'seq_2'=2,'row_0'=4,'row_1'=2] {'seq_0'}, dimensions={0} | all-to-all | bytes 98304 | tf_op jit(solution)/shard_map/all_to_all | solution.py:30
  209.5 10.5 %all_to_all.43 = bf16[8,12,256]{2,1,0:T(8,128)(2,1)S(1)} all-to-all(bf16[8,12,256]{2,1,0:T(8,128)(2,1)S(1)} %broadcast_in_dim.29), channel_id=1, replica_groups=mesh['seq_0'=8,'near'=2,'seq_1'=2,'seq_2'=2,'row_0'=4,'row_1'=2] {'near'..., dimensions={0} | all-to-all | bytes 98304 | tf_op jit(solution)/shard_map/all_to_all | solution.py:30
  220.0 0.6 fusion.53
  (167 shorter events, 9.4 us)
Async XLA Ops:
  8.0 92.4 %copy-start = (bf16[256,2048]{1,0:T(8,128)(2,1)S(1)}, bf16[256,2048]{1,0:T(8,128)(2,1)}, u32[]{:S(2)}) copy-start(bf16[256,2048]{1,0:T(8,128)(2,1)} %param.25) | copy-start | bytes 3145732
  8.0 18.0 %copy-start.29 = (bf16[256,8]{0,1:T(8,128)(2,1)S(1)}, bf16[256,8]{0,1:T(8,128)(2,1)}, u32[]{:S(2)}) copy-start(bf16[256,8]{0,1:T(8,128)(2,1)} %param.35) | copy-start | bytes 12292
  8.0 18.0 %copy-start.30 = (bf16[256,8]{0,1:T(8,128)(2,1)S(1)}, bf16[256,8]{0,1:T(8,128)(2,1)}, u32[]{:S(2)}) copy-start(bf16[256,8]{0,1:T(8,128)(2,1)} %param.34) | copy-start | bytes 12292
  8.0 87.1 %all-gather.6.cloned.1.call-start = ((), (), s32[]{:S(2)}) async-start(), calls=%async_computation.9 | async-start | bytes 2506752 | tf_op jit(solution)/shard_map/all_gather | solution.py:217
  9.8 12.0 %collective-permute-start = (bf16[128,384]{1,0:T(8,128)(2,1)S(1)}, bf16[128,384]{1,0:T(8,128)(2,1)S(1)}, u32[]{:S(2)}, u32[]{:S(2)}) collective-permute-start(bf16[128,384]{1,0:T(8,128)(2,1)S(1)} %pad_maximum_fusion.6), channel_id=1, source_target_pairs={{0,8},{8,0},{1,9},{9,1},{2,10},{10,2},{3,11},{11,3},{4,12},{12,4},... | collective-permute-start | bytes 294920 | tf_op jit(solution)/shard_map/ppermute | solution.py:220
  22.5 16.8 %all-to-all-start = ((bf16[4,256,128]{2,1,0:T(8,128)(2,1)}), bf16[4,256,128]{2,1,0:T(8,128)(2,1)S(1)}, u32[]{:S(2)}, u32[]{:S(2)}) async-start(bf16[4,256,128]{2,1,0:T(8,128)(2,1)} %broadcast_in_dim.21), calls=%async_computation | async-start | bytes 524288 | tf_op jit(solution)/shard_map/all_to_all | solution.py:30
  26.0 101.5 %all-gather.4.cloned.1.call-start = ((), (), s32[]{:S(2)}) async-start(), calls=%async_computation.8 | async-start | bytes 1310720 | tf_op jit(solution)/shard_map/all_gather | solution.py:252
  26.1 42.7 %copy-start.3 = (bf16[272,256]{1,0:T(8,128)(2,1)}, bf16[272,256]{1,0:T(8,128)(2,1)S(1)}, u32[]{:S(2)}) copy-start(bf16[272,256]{1,0:T(8,128)(2,1)S(1)} %pad_maximum_fusion.5.refs_0_.refs_4_) | copy-start | bytes 417796
  26.1 12.2 %collective-permute-start.1 = (bf16[272,256]{1,0:T(8,128)(2,1)S(1)}, bf16[272,256]{1,0:T(8,128)(2,1)S(1)}, u32[]{:S(2)}, u32[]{:S(2)}) collective-permute-start(bf16[272,256]{1,0:T(8,128)(2,1)S(1)} %pad_maximum_fusion.5.refs_0_.refs_4_), channel_id=1, source_target_pairs={{0,64},{64,128},{128,192},{192,256},{256,320},{320,384},{384,448},... | collective-permute-start | bytes 417800 | tf_op jit(solution)/shard_map/ppermute | solution.py:233
  28.0 11.3 %collective-permute-start.2 = (bf16[272,256]{1,0:T(8,128)(2,1)S(1)}, bf16[272,256]{1,0:T(8,128)(2,1)S(1)}, u32[]{:S(2)}, u32[]{:S(2)}) collective-permute-start(bf16[272,256]{1,0:T(8,128)(2,1)S(1)} %pad_maximum_fusion.5.refs_0_.refs_4_), channel_id=1, source_target_pairs={{0,448},{64,0},{128,64},{192,128},{256,192},{320,256},{384,320},{4... | collective-permute-start | bytes 417800 | tf_op jit(solution)/shard_map/ppermute | solution.py:237
  38.3 30.5 %copy-start.5 = (bf16[272,256]{1,0:T(8,128)(2,1)}, bf16[272,256]{1,0:T(8,128)(2,1)S(1)}, u32[]{:S(2)}) copy-start(bf16[272,256]{1,0:T(8,128)(2,1)S(1)} %collective-permute-done.1.refs_1_.refs_5_) | copy-start | bytes 417796
  39.4 29.5 %copy-start.6 = (bf16[272,256]{1,0:T(8,128)(2,1)}, bf16[272,256]{1,0:T(8,128)(2,1)S(1)}, u32[]{:S(2)}) copy-start(bf16[272,256]{1,0:T(8,128)(2,1)S(1)} %collective-permute-done.2.refs_2_.refs_6_) | copy-start | bytes 417796
  39.4 29.5 %copy-start.2 = (bf16[4,256,128]{2,1,0:T(8,128)(2,1)}, bf16[4,256,128]{2,1,0:T(8,128)(2,1)S(1)}, u32[]{:S(2)}) copy-start(bf16[4,256,128]{2,1,0:T(8,128)(2,1)S(1)} %all-to-all-done.queries) | copy-start | bytes 786436
  39.4 8.3 %collective-permute-start.3 = (bf16[272,256]{1,0:T(8,128)(2,1)S(1)}, bf16[272,256]{1,0:T(8,128)(2,1)S(1)}, u32[]{:S(2)}, u32[]{:S(2)}) collective-permute-start(bf16[272,256]{1,0:T(8,128)(2,1)S(1)} %collective-permute-done.1.refs_1_.refs_5_), channel_id=1, source_target_pairs={{0,64},{64,128},{128,192},{192,256},{256,320},{320,384},{384,448},... | collective-permute-start | bytes 417800 | tf_op jit(solution)/shard_map/ppermute | solution.py:233
  43.6 11.8 %collective-permute-start.4 = (bf16[272,256]{1,0:T(8,128)(2,1)S(1)}, bf16[272,256]{1,0:T(8,128)(2,1)S(1)}, u32[]{:S(2)}, u32[]{:S(2)}) collective-permute-start(bf16[272,256]{1,0:T(8,128)(2,1)S(1)} %collective-permute-done.2.refs_2_.refs_6_), channel_id=1, source_target_pairs={{0,448},{64,0},{128,64},{192,128},{256,192},{320,256},{384,320},{4... | collective-permute-start | bytes 417800 | tf_op jit(solution)/shard_map/ppermute | solution.py:237
  47.7 21.2 %copy-start.7 = (bf16[272,256]{1,0:T(8,128)(2,1)}, bf16[272,256]{1,0:T(8,128)(2,1)S(1)}, u32[]{:S(2)}) copy-start(bf16[272,256]{1,0:T(8,128)(2,1)S(1)} %collective-permute-done.3.refs_3_.refs_7_) | copy-start | bytes 417796
  47.7 13.1 %collective-permute-start.5 = (bf16[272,256]{1,0:T(8,128)(2,1)S(1)}, bf16[272,256]{1,0:T(8,128)(2,1)S(1)}, u32[]{:S(2)}, u32[]{:S(2)}) collective-permute-start(bf16[272,256]{1,0:T(8,128)(2,1)S(1)} %collective-permute-done.3.refs_3_.refs_7_), channel_id=1, source_target_pairs={{0,64},{64,128},{128,192},{192,256},{256,320},{320,384},{384,448},... | collective-permute-start | bytes 417800 | tf_op jit(solution)/shard_map/ppermute | solution.py:233
  55.5 13.4 %copy-start.8 = (bf16[272,256]{1,0:T(8,128)(2,1)}, bf16[272,256]{1,0:T(8,128)(2,1)S(1)}, u32[]{:S(2)}) copy-start(bf16[272,256]{1,0:T(8,128)(2,1)S(1)} %collective-permute-done.4.refs_4_.refs_8_) | copy-start | bytes 417796
  55.5 13.3 %collective-permute-start.6 = (bf16[272,256]{1,0:T(8,128)(2,1)S(1)}, bf16[272,256]{1,0:T(8,128)(2,1)S(1)}, u32[]{:S(2)}, u32[]{:S(2)}) collective-permute-start(bf16[272,256]{1,0:T(8,128)(2,1)S(1)} %collective-permute-done.4.refs_4_.refs_8_), channel_id=1, source_target_pairs={{0,448},{64,0},{128,64},{192,128},{256,192},{320,256},{384,320},{4... | collective-permute-start | bytes 417800 | tf_op jit(solution)/shard_map/ppermute | solution.py:237
  60.8 8.1 %copy-start.9 = (bf16[272,256]{1,0:T(8,128)(2,1)}, bf16[272,256]{1,0:T(8,128)(2,1)S(1)}, u32[]{:S(2)}) copy-start(bf16[272,256]{1,0:T(8,128)(2,1)S(1)} %collective-permute-done.5.refs_5_.refs_9_) | copy-start | bytes 417796
  60.8 15.1 %collective-permute-start.7 = (bf16[272,256]{1,0:T(8,128)(2,1)S(1)}, bf16[272,256]{1,0:T(8,128)(2,1)S(1)}, u32[]{:S(2)}, u32[]{:S(2)}) collective-permute-start(bf16[272,256]{1,0:T(8,128)(2,1)S(1)} %collective-permute-done.5.refs_5_.refs_9_), channel_id=1, source_target_pairs={{0,64},{64,128},{128,192},{192,256},{256,320},{320,384},{384,448},... | collective-permute-start | bytes 417800 | tf_op jit(solution)/shard_map/ppermute | solution.py:233
  68.9 0.7 copy-start.10
  75.9 0.7 copy-start.11
  94.8 6.3 %copy-start.37 = (bf16[256,16]{0,1:T(8,128)(2,1)S(1)}, bf16[256,16]{0,1:T(8,128)(2,1)}, u32[]{:S(2)}) copy-start(bf16[256,16]{0,1:T(8,128)(2,1)} %param.26) | copy-start | bytes 24580
  95.1 5.2 %collective-permute-start.8 = (bf16[128,128]{1,0:T(8,128)(2,1)S(1)}, bf16[128,128]{1,0:T(8,128)(2,1)S(1)}, u32[]{:S(2)}, u32[]{:S(2)}) collective-permute-start(bf16[128,128]{1,0:T(8,128)(2,1)S(1)} %slice.198), channel_id=1, source_target_pairs={{0,8},{8,0},{1,9},{9,1},{2,10},{10,2},{3,11},{11,3},{4,12},{12,4},... | collective-permute-start | bytes 98312 | tf_op jit(solution)/shard_map/ppermute | solution.py:259
  100.4 1.7 copy-start.14
  100.4 1.7 copy-start.15
  100.7 5.6 %copy-start.16 = (bf16[128,512]{1,0:T(8,128)(2,1)S(1)}, bf16[128,512]{1,0:T(8,128)(2,1)}, u32[]{:S(2)}) copy-start(bf16[128,512]{1,0:T(8,128)(2,1)} %param.39) | copy-start | bytes 393220
  100.7 9.1 %copy-start.40 = (s32[128]{0:T(128)S(1)}, s32[128]{0:T(128)}, u32[]{:S(2)}) copy-start(s32[128]{0:T(128)} %param.23) | copy-start | bytes 1540
  100.7 9.3 %copy-start.28 = (bf16[8,512]{1,0:T(8,128)(2,1)S(1)}, bf16[8,512]{1,0:T(8,128)(2,1)}, u32[]{:S(2)}) copy-start(bf16[8,512]{1,0:T(8,128)(2,1)} %param.32) | copy-start | bytes 24580
  100.8 9.9 %copy-start.38 = (f32[8,16]{1,0:T(8,128)S(1)}, f32[8,16]{1,0:T(8,128)}, u32[]{:S(2)}) copy-start(f32[8,16]{1,0:T(8,128)} %param.38) | copy-start | bytes 1540
  101.1 15.1 %copy-start.39 = (f32[8,16]{1,0:T(8,128)S(1)}, f32[8,16]{1,0:T(8,128)}, u32[]{:S(2)}) copy-start(f32[8,16]{1,0:T(8,128)} %param.28) | copy-start | bytes 1540
  101.1 15.9 %copy-start.1 = (bf16[256,512]{1,0:T(8,128)(2,1)S(1)}, bf16[256,512]{1,0:T(8,128)(2,1)}, u32[]{:S(2)}) copy-start(bf16[256,512]{1,0:T(8,128)(2,1)} %param.29) | copy-start | bytes 786436
  101.1 15.9 %copy-start.17 = (bf16[128,256]{1,0:T(8,128)(2,1)S(1)}, bf16[128,256]{1,0:T(8,128)(2,1)}, u32[]{:S(2)}) copy-start(bf16[128,256]{1,0:T(8,128)(2,1)} %param.24) | copy-start | bytes 196612
  101.1 15.9 %copy-start.23 = (bf16[16,256]{1,0:T(8,128)(2,1)S(1)}, bf16[16,256]{1,0:T(8,128)(2,1)}, u32[]{:S(2)}) copy-start(bf16[16,256]{1,0:T(8,128)(2,1)} %param.27) | copy-start | bytes 24580
  102.1 30.9 %copy-start.13 = (bf16[256,512]{1,0:T(8,128)(2,1)S(1)}, bf16[256,512]{1,0:T(8,128)(2,1)}, u32[]{:S(2)}) copy-start(bf16[256,512]{1,0:T(8,128)(2,1)} %param.31) | copy-start | bytes 786436
  102.1 31.7 %copy-start.24 = (f32[512]{0:T(512)S(1)}, f32[512]{0:T(512)}, u32[]{:S(2)}) copy-start(f32[512]{0:T(512)} %param.33) | copy-start | bytes 6148
  102.1 13.8 %all-to-all-start.2 = ((bf16[8,272,128]{2,1,0:T(8,128)(2,1)}), bf16[8,272,128]{2,1,0:T(8,128)(2,1)S(1)}, u32[]{:S(2)}, u32[]{:S(2)}) async-start(bf16[8,272,128]{2,1,0:T(8,128)(2,1)} %pad_maximum_fusion.1), calls=%async_computation.2 | async-start | bytes 1114112 | tf_op jit(solution)/shard_map/all_to_all | solution.py:30
  106.3 27.6 %copy-start.18 = (bf16[512,16]{0,1:T(8,128)(2,1)S(1)}, bf16[512,16]{0,1:T(8,128)(2,1)}, u32[]{:S(2)}) copy-start(bf16[512,16]{0,1:T(8,128)(2,1)} %param.36) | copy-start | bytes 49156
  106.3 38.9 %collective-permute-start.9 = (bf16[128,512]{1,0:T(8,128)(2,1)S(1)}, bf16[128,512]{1,0:T(8,128)(2,1)}, u32[]{:S(2)}, u32[]{:S(2)}) collective-permute-start(bf16[128,512]{1,0:T(8,128)(2,1)S(1)} %copy-done.16), channel_id=1, source_target_pairs={{0,1},{1,0},{2,3},{3,2},{4,5},{5,4},{6,7},{7,6},{8,9},{9,8},{10,11... | collective-permute-start | bytes 393224 | tf_op jit(solution)/shard_map/ppermute | solution.py:218
  110.1 0.6 copy-start.33
  116.0 11.2 %copy-start.12 = (f32[272,128]{1,0:T(8,128)}, f32[272,128]{1,0:T(8,128)S(1)}, u32[]{:S(2)}) copy-start(f32[272,128]{1,0:T(8,128)S(1)} %convert_reduce_fusion) | copy-start | bytes 417796
  117.0 1.0 copy-start.26
  118.0 9.2 %all-to-all-start.3 = ((bf16[8,16,512]{2,1,0:T(8,128)(2,1)}), bf16[8,16,512]{2,1,0:T(8,128)(2,1)S(1)}, u32[]{:S(2)}, u32[]{:S(2)}) async-start(bf16[8,16,512]{2,1,0:T(8,128)(2,1)} %bitcast.28), calls=%async_computation.3 | async-start | bytes 262144 | tf_op jit(solution)/shard_map/all_to_all | solution.py:30
  127.5 14.7 %copy-start.4 = (bf16[4,512,256]{2,1,0:T(8,128)(2,1)S(1)}, bf16[4,512,256]{2,1,0:T(8,128)(2,1)}, u32[]{:S(2)}) copy-start(bf16[4,512,256]{2,1,0:T(8,128)(2,1)} %all-gather.4.cloned.1.call-done) | copy-start | bytes 3145732
  127.5 14.7 %collective-permute-start.10 = (bf16[4,512,256]{2,1,0:T(8,128)(2,1)}, bf16[4,512,256]{2,1,0:T(8,128)(2,1)}, u32[]{:S(2)}, u32[]{:S(2)}) collective-permute-start(bf16[4,512,256]{2,1,0:T(8,128)(2,1)} %all-gather.4.cloned.1.call-done), channel_id=1, source_target_pairs={{0,8},{8,0},{1,9},{9,1},{2,10},{10,2},{3,11},{11,3},{4,12},{12,4},... | collective-permute-start | bytes 3145736 | tf_op jit(solution)/shard_map/ppermute | solution.py:288
  133.3 0.5 copy-start.31
  134.3 7.7 %collective-permute-start.11 = (bf16[128,640]{1,0:T(8,128)(2,1)S(1)}, bf16[128,640]{1,0:T(8,128)(2,1)S(1)}, u32[]{:S(2)}, u32[]{:S(2)}) collective-permute-start(bf16[128,640]{1,0:T(8,128)(2,1)S(1)} %pad_maximum_fusion.4), channel_id=1, source_target_pairs={{0,1},{1,0},{2,3},{3,2},{4,5},{5,4},{6,7},{7,6},{8,9},{9,8},{10,11... | collective-permute-start | bytes 491528 | tf_op jit(solution)/shard_map/ppermute | solution.py:310
  143.8 0.7 copy-start.35
  147.4 7.4 %copy-start.25 = (f32[512]{0:T(512)S(1)}, f32[512]{0:T(512)}, u32[]{:S(2)}) copy-start(f32[512]{0:T(512)} %param.33) | copy-start | bytes 6148
  147.4 7.6 %copy-start.34 = (s32[128]{0:T(128)S(1)}, s32[128]{0:T(128)}, u32[]{:S(2)}) copy-start(s32[128]{0:T(128)} %copy-done.33) | copy-start | bytes 1540
  147.5 7.9 %copy-start.32 = (f32[128]{0:T(128)S(1)}, f32[128]{0:T(128)}, u32[]{:S(2)}) copy-start(f32[128]{0:T(128)} %copy-done.31) | copy-start | bytes 1540
  147.7 7.9 %copy-start.36 = (bf16[48]{0:T(256)(128)(2,1)S(1)}, bf16[48]{0:T(256)(128)(2,1)}, u32[]{:S(2)}) copy-start(bf16[48]{0:T(256)(128)(2,1)} %pad.22.clone) | copy-start | bytes 292
  147.8 6.8 %collective-permute-start.12 = (bf16[128,640]{1,0:T(8,128)(2,1)S(1)}, bf16[128,640]{1,0:T(8,128)(2,1)S(1)}, u32[]{:S(2)}, u32[]{:S(2)}) collective-permute-start(bf16[128,640]{1,0:T(8,128)(2,1)S(1)} %slice.296), channel_id=1, source_target_pairs={{0,1},{1,0},{2,3},{3,2},{4,5},{5,4},{6,7},{7,6},{8,9},{9,8},{10,11... | collective-permute-start | bytes 491528 | tf_op jit(solution)/shard_map/ppermute | solution.py:317
  156.6 12.6 %all-to-all-start.4 = ((bf16[8,64,512]{2,1,0:T(8,128)(2,1)}), bf16[8,64,512]{2,1,0:T(8,128)(2,1)}, u32[]{:S(2)}, u32[]{:S(2)}) async-start(bf16[8,64,512]{2,1,0:T(8,128)(2,1)} %fusion.19), calls=%async_computation.4 | async-start | bytes 1048576 | tf_op jit(solution)/shard_map/all_to_all | solution.py:30
  160.7 1.9 copy-start.19
  160.7 1.9 copy-start.20
  160.7 1.9 copy-start.21
  160.7 1.9 copy-start.22
  162.6 9.4 %copy-start.41 = (s32[128]{0:T(128)S(1)}, s32[128]{0:T(128)}, u32[]{:S(2)}) copy-start(s32[128]{0:T(128)} %param.23) | copy-start | bytes 1540
  162.6 11.2 %copy-start.27 = (bf16[128,16]{0,1:T(8,128)(2,1)S(1)}, bf16[128,16]{0,1:T(8,128)(2,1)}, u32[]{:S(2)}) copy-start(bf16[128,16]{0,1:T(8,128)(2,1)} %copy-done.26) | copy-start | bytes 12292
Sparse Core Ops, SparseCore 0:
  21.9 60.5 all-gather.5
Sparse Core Ops, SparseCore 1:
  100.3 27.0 all-gather.3

commit v11 on v10

--- a/solution.py
+++ b/solution.py
@@ -18,7 +18,7 @@
 SEQ = ("seq_0", "near", "seq_1", "seq_2")
 Z, NEAR, FAR, CORE = SEQ
 QUAD = (NEAR, FAR)
-EIGHT = (NEAR, FAR, CORE)
+CHIPS = (FAR, CORE)
 LINE, SIDE = ROW
 SEQ_ROW = SEQ + ROW
 SWAP = [(0, 1), (1, 0)]
@@ -363,10 +363,10 @@
         ]
     ).astype(BF)
     shape = packed.shape
-    pieces = packed.reshape(lax.axis_size(EIGHT), -1, shape[1])
-    pieces = total(exchange(pieces, EIGHT)).astype(BF)
-    pieces = total(to_everyone(pieces, Z)).astype(BF)
-    packed = to_everyone(pieces, EIGHT).reshape(shape).astype(F32)
+    pieces = packed.reshape(lax.axis_size(CHIPS), -1, shape[1])
+    pieces = total(exchange(pieces, CHIPS)).astype(BF)
+    pieces = total(to_everyone(pieces, (Z, NEAR))).astype(BF)
+    packed = to_everyone(pieces, CHIPS).reshape(shape).astype(F32)
     return (
         jnp.transpose(packed[:16]),
         packed[16:32],

time: 231 us -> 232 us (level)
  no operation moved by 1% of the time
where the time goes in v11:
time: 232 us; the launch traced here: 230 us
  starting transfers between devices  73.4 us (32%)
  blocking collectives  58.3 us (25%)
  waiting for transfers between devices  32.2 us (14%)
  local copies, waits for them, and re-layouts  18.4 us (8%)
  between operations  16.6 us (7%)
  Pallas kernels  11.9 us (5%)
  matrix products  10.9 us (5%)
  other arithmetic  8.74 us (4%)
    all_to_all x4, blocking collectives, exchange(): return lax.all_to_all(pieces, axis, split_axis=0, concat_axis=0, tiled=True)  58.3 us
    ppermute x4, starting transfers between devices, body(): rising = lax.ppermute(rising, Z, up)  19 us
    all_to_all x4, starting transfers between devices, exchange(): return lax.all_to_all(pieces, axis, split_axis=0, concat_axis=0, tiled=True)  15.3 us
    all_to_all x4, waiting for transfers between devices, exchange(): return lax.all_to_all(pieces, axis, split_axis=0, concat_axis=0, tiled=True)  12.9 us
    ppermute x3, starting transfers between devices, body(): falling = lax.ppermute(falling, Z, down)  12.2 us
    pallas_call x2, Pallas kernels, attend(): pl.pallas_call(functools.partial(attend_kernel, count=len(packets), start...  11.9 us
    ppermute x1, starting transfers between devices, body(): both = jnp.concatenate([mine, lax.ppermute(other, CORE, SWAP)], axis=0)  8.79 us
    dot_general x11, matrix products, contract(): lax.dot_general(left, right, (((left_dim,), (right_dim,)), ((), ())), pre...  7.46 us
  transfers between devices with their start and end apart: 19, of which 12 were waited for; matrix products, arithmetic and copies ran while one was open for 9% of the time, Pallas kernels for 5%

profile of v11, /device:TPU:1, one launch (start us, length us, event | category | flops | bytes accessed | tf_op | source)
XLA Modules:
  0.0 230.4 jit_solution(18197736117769514378)
XLA Ops:
  8.1 0.9 constant_dynamic-slice_fusion.5
  8.9 0.8 constant_dynamic-slice_fusion.3
  9.8 8.8 %collective-permute-start = (bf16[128,384]{1,0:T(8,128)(2,1)S(1)}, bf16[128,384]{1,0:T(8,128)(2,1)S(1)}, u32[]{:S(2)}, u32[]{:S(2)}) collective-permute-start(bf16[128,384]{1,0:T(8,128)(2,1)S(1)} %pad_maximum_fusion.6), channel_id=1, source_target_pairs={{0,8},{8,0},{1,9},{9,1},{2,10},{10,2},{3,11},{11,3},{4,12},{12,4},... | collective-permute-start | bytes 294920 | tf_op jit(solution)/shard_map/ppermute | solution.py:220
  18.6 0.7 fusion.55
  19.3 0.7 fusion.54
  20.1 1.7 maximum_maximum_fusion.3
  21.8 0.8 broadcast_in_dim.21
  22.5 3.4 %all-to-all-start = ((bf16[4,256,128]{2,1,0:T(8,128)(2,1)}), bf16[4,256,128]{2,1,0:T(8,128)(2,1)S(1)}, u32[]{:S(2)}, u32[]{:S(2)}) async-start(bf16[4,256,128]{2,1,0:T(8,128)(2,1)} %broadcast_in_dim.21), calls=%async_computation | async-start | bytes 524288 | tf_op jit(solution)/shard_map/all_to_all | solution.py:30
  26.1 1.9 collective-permute-start.1
  28.0 7.2 %collective-permute-start.2 = (bf16[272,256]{1,0:T(8,128)(2,1)S(1)}, bf16[272,256]{1,0:T(8,128)(2,1)S(1)}, u32[]{:S(2)}, u32[]{:S(2)}) collective-permute-start(bf16[272,256]{1,0:T(8,128)(2,1)S(1)} %pad_maximum_fusion.5.refs_0_.refs_4_), channel_id=1, source_target_pairs={{0,448},{64,0},{128,64},{192,128},{256,192},{320,256},{384,320},{4... | collective-permute-start | bytes 417800 | tf_op jit(solution)/shard_map/ppermute | solution.py:237
  35.2 3.0 %collective-permute-done.1.refs_1_.refs_5_ = bf16[272,256]{1,0:T(8,128)(2,1)S(1)} collective-permute-done((bf16[272,256]{1,0:T(8,128)(2,1)S(1)}, bf16[272,256]{1,0:T(8,128)(2,1)S(1)}, u32[]{:S(2)}, u32[]{:S(2)}) %collective-permute-start.1) | collective-permute-done | bytes 139296 | tf_op jit(solution)/shard_map/ppermute | solution.py:233
  38.3 1.1 collective-permute-done.2.refs_2_.refs_6_
  39.4 4.3 %collective-permute-start.3 = (bf16[272,256]{1,0:T(8,128)(2,1)S(1)}, bf16[272,256]{1,0:T(8,128)(2,1)S(1)}, u32[]{:S(2)}, u32[]{:S(2)}) collective-permute-start(bf16[272,256]{1,0:T(8,128)(2,1)S(1)} %collective-permute-done.1.refs_1_.refs_5_), channel_id=1, source_target_pairs={{0,64},{64,128},{128,192},{192,256},{256,320},{320,384},{384,448},... | collective-permute-start | bytes 417800 | tf_op jit(solution)/shard_map/ppermute | solution.py:233
  43.6 3.1 %collective-permute-start.4 = (bf16[272,256]{1,0:T(8,128)(2,1)S(1)}, bf16[272,256]{1,0:T(8,128)(2,1)S(1)}, u32[]{:S(2)}, u32[]{:S(2)}) collective-permute-start(bf16[272,256]{1,0:T(8,128)(2,1)S(1)} %collective-permute-done.2.refs_2_.refs_6_), channel_id=1, source_target_pairs={{0,448},{64,0},{128,64},{192,128},{256,192},{320,256},{384,320},{4... | collective-permute-start | bytes 417800 | tf_op jit(solution)/shard_map/ppermute | solution.py:237
  46.8 0.9 collective-permute-done.3.refs_3_.refs_7_
  47.7 7.8 %collective-permute-start.5 = (bf16[272,256]{1,0:T(8,128)(2,1)S(1)}, bf16[272,256]{1,0:T(8,128)(2,1)S(1)}, u32[]{:S(2)}, u32[]{:S(2)}) collective-permute-start(bf16[272,256]{1,0:T(8,128)(2,1)S(1)} %collective-permute-done.3.refs_3_.refs_7_), channel_id=1, source_target_pairs={{0,64},{64,128},{128,192},{192,256},{256,320},{320,384},{384,448},... | collective-permute-start | bytes 417800 | tf_op jit(solution)/shard_map/ppermute | solution.py:233
  55.5 1.9 collective-permute-start.6
  57.4 3.4 %collective-permute-done.5.refs_5_.refs_9_ = bf16[272,256]{1,0:T(8,128)(2,1)S(1)} collective-permute-done((bf16[272,256]{1,0:T(8,128)(2,1)S(1)}, bf16[272,256]{1,0:T(8,128)(2,1)S(1)}, u32[]{:S(2)}, u32[]{:S(2)}) %collective-permute-start.5) | collective-permute-done | bytes 139296 | tf_op jit(solution)/shard_map/ppermute | solution.py:233
  60.8 5.1 %collective-permute-start.7 = (bf16[272,256]{1,0:T(8,128)(2,1)S(1)}, bf16[272,256]{1,0:T(8,128)(2,1)S(1)}, u32[]{:S(2)}, u32[]{:S(2)}) collective-permute-start(bf16[272,256]{1,0:T(8,128)(2,1)S(1)} %collective-permute-done.5.refs_5_.refs_9_), channel_id=1, source_target_pairs={{0,64},{64,128},{128,192},{192,256},{256,320},{320,384},{384,448},... | collective-permute-start | bytes 417800 | tf_op jit(solution)/shard_map/ppermute | solution.py:233
  66.0 0.6 concatenate.100.spots
  66.6 0.6 concatenate.95.spots
  67.2 1.6 collective-permute-done.6.refs_6_.refs_10_
  68.9 0.7 copy-done.10
  69.5 6.4 %attend.2 = (f32[1024,128]{1,0:T(8,128)}, f32[1024,128]{1,0:T(8,128)}, f32[1024,128]{1,0:T(8,128)}) custom-call(s32[10]{0:T(128)} %concatenate.100.spots, bf16[4,256,128]{2,1,0:T(8,128)(2,1)} %copy-done.2, bf16[272,256]{1,0:T(8,128)(2,1)} %copy-done.3, bf16[272,256]{1,0:T(8,128)(2,1)} %copy-done.5, bf16[272,256]{1,0:T(8,128)(2,1)} %copy-done.6, ...), custom_call_target="tpu_custom_call" | custom-call | tf_op jit(solution)/shard_map/attend/pallas_call | solution.py:159
  75.9 0.6 copy-done.11
  76.6 5.5 %attend.3 = bf16[4,272,256]{2,1,0:T(8,128)(2,1)} custom-call(s32[11]{0:T(128)} %concatenate.95.spots, bf16[4,256,128]{2,1,0:T(8,128)(2,1)} %copy-done.2, bf16[272,256]{1,0:T(8,128)(2,1)} %copy-done.11, f32[1024,128]{1,0:T(8,128)} %get-tuple-element.32.refs_1_, f32[1024,128]{1,0:T(8,128)} %get-tuple-element.33.refs_2_, ...), custom_call_target="tpu_custom_call" | custom-call | tf_op jit(solution)/shard_map/attend/pallas_call | solution.py:159
  82.1 12.6 %all_to_all.40 = bf16[4,272,256]{2,1,0:T(8,128)(2,1)S(1)} all-to-all(bf16[4,272,256]{2,1,0:T(8,128)(2,1)} %attend.3), channel_id=1, replica_groups=mesh['seq_0'=8,'near'=2,'seq_1'=2,'seq_2'=2,'row_0'=4,'row_1'=2] {'near'..., dimensions={0} | all-to-all | bytes 1114112 | tf_op jit(solution)/shard_map/all_to_all | solution.py:30
  95.1 4.4 %collective-permute-start.8 = (bf16[128,128]{1,0:T(8,128)(2,1)S(1)}, bf16[128,128]{1,0:T(8,128)(2,1)S(1)}, u32[]{:S(2)}, u32[]{:S(2)}) collective-permute-start(bf16[128,128]{1,0:T(8,128)(2,1)S(1)} %slice.198), channel_id=1, source_target_pairs={{0,8},{8,0},{1,9},{9,1},{2,10},{10,2},{3,11},{11,3},{4,12},{12,4},... | collective-permute-start | bytes 98312 | tf_op jit(solution)/shard_map/ppermute | solution.py:259
  99.5 0.7 slice.238
  101.2 0.9 pad_maximum_fusion.1
  102.1 4.2 %all-to-all-start.2 = ((bf16[8,272,128]{2,1,0:T(8,128)(2,1)}), bf16[8,272,128]{2,1,0:T(8,128)(2,1)S(1)}, u32[]{:S(2)}, u32[]{:S(2)}) async-start(bf16[8,272,128]{2,1,0:T(8,128)(2,1)} %pad_maximum_fusion.1), calls=%async_computation.2 | async-start | bytes 1114112 | tf_op jit(solution)/shard_map/all_to_all | solution.py:30
  106.3 3.5 %collective-permute-start.9 = (bf16[128,512]{1,0:T(8,128)(2,1)S(1)}, bf16[128,512]{1,0:T(8,128)(2,1)}, u32[]{:S(2)}, u32[]{:S(2)}) collective-permute-start(bf16[128,512]{1,0:T(8,128)(2,1)S(1)} %copy-done.16), channel_id=1, source_target_pairs={{0,1},{1,0},{2,3},{3,2},{4,5},{5,4},{6,7},{7,6},{8,9},{9,8},{10,11... | collective-permute-start | bytes 393224 | tf_op jit(solution)/shard_map/ppermute | solution.py:218
  111.0 0.7 pad.25.clone
  112.3 0.8 dynamic_slice.28
  113.0 2.9 %all-to-all-done.2 = bf16[8,272,128]{2,1,0:T(8,128)(2,1)S(1)} async-done(((bf16[8,272,128]{2,1,0:T(8,128)(2,1)}), bf16[8,272,128]{2,1,0:T(8,128)(2,1)S(1)}, u32[]{:S(2)}, u32[]{:S(2)}) %all-to-all-start.2) | async-done | bytes 557088 | tf_op jit(solution)/shard_map/all_to_all | solution.py:30
  116.1 0.9 multiply_convert_fusion.4
  117.0 1.0 convolution_convert_fusion.2
  118.0 3.5 %all-to-all-start.3 = ((bf16[8,16,512]{2,1,0:T(8,128)(2,1)}), bf16[8,16,512]{2,1,0:T(8,128)(2,1)S(1)}, u32[]{:S(2)}, u32[]{:S(2)}) async-start(bf16[8,16,512]{2,1,0:T(8,128)(2,1)} %bitcast.28), calls=%async_computation.3 | async-start | bytes 262144 | tf_op jit(solution)/shard_map/all_to_all | solution.py:30
  121.5 1.5 fusion.49
  123.0 4.2 %all-to-all-done.3 = bf16[8,16,512]{2,1,0:T(8,128)(2,1)S(1)} async-done(((bf16[8,16,512]{2,1,0:T(8,128)(2,1)}), bf16[8,16,512]{2,1,0:T(8,128)(2,1)S(1)}, u32[]{:S(2)}, u32[]{:S(2)}) %all-to-all-start.3) | async-done | bytes 131104 | tf_op jit(solution)/shard_map/all_to_all | solution.py:30
  127.5 5.4 %collective-permute-start.10 = (bf16[4,512,256]{2,1,0:T(8,128)(2,1)}, bf16[4,512,256]{2,1,0:T(8,128)(2,1)}, u32[]{:S(2)}, u32[]{:S(2)}) collective-permute-start(bf16[4,512,256]{2,1,0:T(8,128)(2,1)} %all-gather.4.cloned.1.call-done), channel_id=1, source_target_pairs={{0,8},{8,0},{1,9},{9,1},{2,10},{10,2},{3,11},{11,3},{4,12},{12,4},... | collective-permute-start | bytes 3145736 | tf_op jit(solution)/shard_map/ppermute | solution.py:288
  134.3 2.4 %collective-permute-start.11 = (bf16[128,640]{1,0:T(8,128)(2,1)S(1)}, bf16[128,640]{1,0:T(8,128)(2,1)S(1)}, u32[]{:S(2)}, u32[]{:S(2)}) collective-permute-start(bf16[128,640]{1,0:T(8,128)(2,1)S(1)} %pad_maximum_fusion.4), channel_id=1, source_target_pairs={{0,1},{1,0},{2,3},{3,2},{4,5},{5,4},{6,7},{7,6},{8,9},{9,8},{10,11... | collective-permute-start | bytes 491528 | tf_op jit(solution)/shard_map/ppermute | solution.py:310
  136.7 0.8 maximum_maximum_fusion.4
  137.6 4.4 %collective-permute-done.11 = bf16[128,640]{1,0:T(8,128)(2,1)S(1)} collective-permute-done((bf16[128,640]{1,0:T(8,128)(2,1)S(1)}, bf16[128,640]{1,0:T(8,128)(2,1)S(1)}, u32[]{:S(2)}, u32[]{:S(2)}) %collective-permute-start.11) | collective-permute-done | bytes 163872 | tf_op jit(solution)/shard_map/ppermute | solution.py:310
  142.1 1.4 broadcast_select_fusion.1
  144.5 0.7 fusion.16
  145.2 1.5 fusion.1
  146.7 0.7 convolution_bitcast_fusion
  147.8 2.4 %collective-permute-start.12 = (bf16[128,640]{1,0:T(8,128)(2,1)S(1)}, bf16[128,640]{1,0:T(8,128)(2,1)S(1)}, u32[]{:S(2)}, u32[]{:S(2)}) collective-permute-start(bf16[128,640]{1,0:T(8,128)(2,1)S(1)} %slice.296), channel_id=1, source_target_pairs={{0,1},{1,0},{2,3},{3,2},{4,5},{5,4},{6,7},{7,6},{8,9},{9,8},{10,11... | collective-permute-start | bytes 491528 | tf_op jit(solution)/shard_map/ppermute | solution.py:317
  150.2 4.4 %collective-permute-done.12 = bf16[128,640]{1,0:T(8,128)(2,1)S(1)} collective-permute-done((bf16[128,640]{1,0:T(8,128)(2,1)S(1)}, bf16[128,640]{1,0:T(8,128)(2,1)S(1)}, u32[]{:S(2)}, u32[]{:S(2)}) %collective-permute-start.12) | collective-permute-done | bytes 163872 | tf_op jit(solution)/shard_map/ppermute | solution.py:317
  155.7 0.8 fusion.19
  156.6 4.1 %all-to-all-start.4 = ((bf16[8,64,512]{2,1,0:T(8,128)(2,1)}), bf16[8,64,512]{2,1,0:T(8,128)(2,1)}, u32[]{:S(2)}, u32[]{:S(2)}) async-start(bf16[8,64,512]{2,1,0:T(8,128)(2,1)} %fusion.19), calls=%async_computation.4 | async-start | bytes 1048576 | tf_op jit(solution)/shard_map/all_to_all | solution.py:30
  160.8 1.8 slice.215
  162.7 0.6 copy.89
  163.3 5.9 %all-to-all-done.4 = bf16[8,64,512]{2,1,0:T(8,128)(2,1)} async-done(((bf16[8,64,512]{2,1,0:T(8,128)(2,1)}), bf16[8,64,512]{2,1,0:T(8,128)(2,1)}, u32[]{:S(2)}, u32[]{:S(2)}) %all-to-all-start.4) | async-done | bytes 524320 | tf_op jit(solution)/shard_map/all_to_all | solution.py:30
  169.2 0.9 slice.247
  170.1 1.9 fusion.2
  172.0 0.9 convolution_convert_fusion.7
  172.9 0.9 fusion.7
  174.2 1.1 convert_reduce_fusion.1
  175.3 9.7 %all_to_all.41 = bf16[4,24,256]{2,1,0:T(8,128)(2,1)S(1)} all-to-all(bf16[4,24,256]{2,1,0:T(8,128)(2,1)S(1)} %bitcast.135), channel_id=1, replica_groups=mesh['seq_0'=8,'near'=2,'seq_1'=2,'seq_2'=2,'row_0'=4,'row_1'=2] {'seq_1..., dimensions={0} | all-to-all | bytes 98304 | tf_op jit(solution)/shard_map/all_to_all | solution.py:30
  185.0 24.0 %all_to_all.42 = bf16[16,24,256]{2,1,0:T(8,128)(2,1)S(1)} all-to-all(bf16[16,24,256]{2,1,0:T(8,128)(2,1)S(1)} %broadcast_in_dim.28), channel_id=1, replica_groups=mesh['seq_0'=8,'near'=2,'seq_1'=2,'seq_2'=2,'row_0'=4,'row_1'=2] {'seq_0..., dimensions={0} | all-to-all | bytes 393216 | tf_op jit(solution)/shard_map/all_to_all | solution.py:30
  209.1 12.1 %all_to_all.43 = bf16[4,24,256]{2,1,0:T(8,128)(2,1)S(1)} all-to-all(bf16[4,24,256]{2,1,0:T(8,128)(2,1)S(1)} %broadcast_in_dim.29), channel_id=1, replica_groups=mesh['seq_0'=8,'near'=2,'seq_1'=2,'seq_2'=2,'row_0'=4,'row_1'=2] {'seq_1..., dimensions={0} | all-to-all | bytes 98304 | tf_op jit(solution)/shard_map/all_to_all | solution.py:30
  221.2 0.6 fusion.53
  (166 shorter events, 9.4 us)
Async XLA Ops:
  8.0 92.4 %copy-start = (bf16[256,2048]{1,0:T(8,128)(2,1)S(1)}, bf16[256,2048]{1,0:T(8,128)(2,1)}, u32[]{:S(2)}) copy-start(bf16[256,2048]{1,0:T(8,128)(2,1)} %param.25) | copy-start | bytes 3145732
  8.0 18.0 %copy-start.29 = (bf16[256,8]{0,1:T(8,128)(2,1)S(1)}, bf16[256,8]{0,1:T(8,128)(2,1)}, u32[]{:S(2)}) copy-start(bf16[256,8]{0,1:T(8,128)(2,1)} %param.35) | copy-start | bytes 12292
  8.0 18.0 %copy-start.30 = (bf16[256,8]{0,1:T(8,128)(2,1)S(1)}, bf16[256,8]{0,1:T(8,128)(2,1)}, u32[]{:S(2)}) copy-start(bf16[256,8]{0,1:T(8,128)(2,1)} %param.34) | copy-start | bytes 12292
  8.0 87.1 %all-gather.6.cloned.1.call-start = ((), (), s32[]{:S(2)}) async-start(), calls=%async_computation.9 | async-start | bytes 2506752 | tf_op jit(solution)/shard_map/all_gather | solution.py:217
  9.8 12.0 %collective-permute-start = (bf16[128,384]{1,0:T(8,128)(2,1)S(1)}, bf16[128,384]{1,0:T(8,128)(2,1)S(1)}, u32[]{:S(2)}, u32[]{:S(2)}) collective-permute-start(bf16[128,384]{1,0:T(8,128)(2,1)S(1)} %pad_maximum_fusion.6), channel_id=1, source_target_pairs={{0,8},{8,0},{1,9},{9,1},{2,10},{10,2},{3,11},{11,3},{4,12},{12,4},... | collective-permute-start | bytes 294920 | tf_op jit(solution)/shard_map/ppermute | solution.py:220
  22.5 16.8 %all-to-all-start = ((bf16[4,256,128]{2,1,0:T(8,128)(2,1)}), bf16[4,256,128]{2,1,0:T(8,128)(2,1)S(1)}, u32[]{:S(2)}, u32[]{:S(2)}) async-start(bf16[4,256,128]{2,1,0:T(8,128)(2,1)} %broadcast_in_dim.21), calls=%async_computation | async-start | bytes 524288 | tf_op jit(solution)/shard_map/all_to_all | solution.py:30
  26.0 101.5 %all-gather.4.cloned.1.call-start = ((), (), s32[]{:S(2)}) async-start(), calls=%async_computation.8 | async-start | bytes 1310720 | tf_op jit(solution)/shard_map/all_gather | solution.py:252
  26.1 42.7 %copy-start.3 = (bf16[272,256]{1,0:T(8,128)(2,1)}, bf16[272,256]{1,0:T(8,128)(2,1)S(1)}, u32[]{:S(2)}) copy-start(bf16[272,256]{1,0:T(8,128)(2,1)S(1)} %pad_maximum_fusion.5.refs_0_.refs_4_) | copy-start | bytes 417796
  26.1 12.2 %collective-permute-start.1 = (bf16[272,256]{1,0:T(8,128)(2,1)S(1)}, bf16[272,256]{1,0:T(8,128)(2,1)S(1)}, u32[]{:S(2)}, u32[]{:S(2)}) collective-permute-start(bf16[272,256]{1,0:T(8,128)(2,1)S(1)} %pad_maximum_fusion.5.refs_0_.refs_4_), channel_id=1, source_target_pairs={{0,64},{64,128},{128,192},{192,256},{256,320},{320,384},{384,448},... | collective-permute-start | bytes 417800 | tf_op jit(solution)/shard_map/ppermute | solution.py:233
  28.0 11.3 %collective-permute-start.2 = (bf16[272,256]{1,0:T(8,128)(2,1)S(1)}, bf16[272,256]{1,0:T(8,128)(2,1)S(1)}, u32[]{:S(2)}, u32[]{:S(2)}) collective-permute-start(bf16[272,256]{1,0:T(8,128)(2,1)S(1)} %pad_maximum_fusion.5.refs_0_.refs_4_), channel_id=1, source_target_pairs={{0,448},{64,0},{128,64},{192,128},{256,192},{320,256},{384,320},{4... | collective-permute-start | bytes 417800 | tf_op jit(solution)/shard_map/ppermute | solution.py:237
  38.3 30.5 %copy-start.5 = (bf16[272,256]{1,0:T(8,128)(2,1)}, bf16[272,256]{1,0:T(8,128)(2,1)S(1)}, u32[]{:S(2)}) copy-start(bf16[272,256]{1,0:T(8,128)(2,1)S(1)} %collective-permute-done.1.refs_1_.refs_5_) | copy-start | bytes 417796
  39.4 29.5 %copy-start.6 = (bf16[272,256]{1,0:T(8,128)(2,1)}, bf16[272,256]{1,0:T(8,128)(2,1)S(1)}, u32[]{:S(2)}) copy-start(bf16[272,256]{1,0:T(8,128)(2,1)S(1)} %collective-permute-done.2.refs_2_.refs_6_) | copy-start | bytes 417796
  39.4 29.5 %copy-start.2 = (bf16[4,256,128]{2,1,0:T(8,128)(2,1)}, bf16[4,256,128]{2,1,0:T(8,128)(2,1)S(1)}, u32[]{:S(2)}) copy-start(bf16[4,256,128]{2,1,0:T(8,128)(2,1)S(1)} %all-to-all-done.queries) | copy-start | bytes 786436
  39.4 8.3 %collective-permute-start.3 = (bf16[272,256]{1,0:T(8,128)(2,1)S(1)}, bf16[272,256]{1,0:T(8,128)(2,1)S(1)}, u32[]{:S(2)}, u32[]{:S(2)}) collective-permute-start(bf16[272,256]{1,0:T(8,128)(2,1)S(1)} %collective-permute-done.1.refs_1_.refs_5_), channel_id=1, source_target_pairs={{0,64},{64,128},{128,192},{192,256},{256,320},{320,384},{384,448},... | collective-permute-start | bytes 417800 | tf_op jit(solution)/shard_map/ppermute | solution.py:233
  43.6 11.8 %collective-permute-start.4 = (bf16[272,256]{1,0:T(8,128)(2,1)S(1)}, bf16[272,256]{1,0:T(8,128)(2,1)S(1)}, u32[]{:S(2)}, u32[]{:S(2)}) collective-permute-start(bf16[272,256]{1,0:T(8,128)(2,1)S(1)} %collective-permute-done.2.refs_2_.refs_6_), channel_id=1, source_target_pairs={{0,448},{64,0},{128,64},{192,128},{256,192},{320,256},{384,320},{4... | collective-permute-start | bytes 417800 | tf_op jit(solution)/shard_map/ppermute | solution.py:237
  47.7 21.2 %copy-start.7 = (bf16[272,256]{1,0:T(8,128)(2,1)}, bf16[272,256]{1,0:T(8,128)(2,1)S(1)}, u32[]{:S(2)}) copy-start(bf16[272,256]{1,0:T(8,128)(2,1)S(1)} %collective-permute-done.3.refs_3_.refs_7_) | copy-start | bytes 417796
  47.7 13.1 %collective-permute-start.5 = (bf16[272,256]{1,0:T(8,128)(2,1)S(1)}, bf16[272,256]{1,0:T(8,128)(2,1)S(1)}, u32[]{:S(2)}, u32[]{:S(2)}) collective-permute-start(bf16[272,256]{1,0:T(8,128)(2,1)S(1)} %collective-permute-done.3.refs_3_.refs_7_), channel_id=1, source_target_pairs={{0,64},{64,128},{128,192},{192,256},{256,320},{320,384},{384,448},... | collective-permute-start | bytes 417800 | tf_op jit(solution)/shard_map/ppermute | solution.py:233
  55.5 13.4 %copy-start.8 = (bf16[272,256]{1,0:T(8,128)(2,1)}, bf16[272,256]{1,0:T(8,128)(2,1)S(1)}, u32[]{:S(2)}) copy-start(bf16[272,256]{1,0:T(8,128)(2,1)S(1)} %collective-permute-done.4.refs_4_.refs_8_) | copy-start | bytes 417796
  55.5 13.3 %collective-permute-start.6 = (bf16[272,256]{1,0:T(8,128)(2,1)S(1)}, bf16[272,256]{1,0:T(8,128)(2,1)S(1)}, u32[]{:S(2)}, u32[]{:S(2)}) collective-permute-start(bf16[272,256]{1,0:T(8,128)(2,1)S(1)} %collective-permute-done.4.refs_4_.refs_8_), channel_id=1, source_target_pairs={{0,448},{64,0},{128,64},{192,128},{256,192},{320,256},{384,320},{4... | collective-permute-start | bytes 417800 | tf_op jit(solution)/shard_map/ppermute | solution.py:237
  60.8 8.1 %copy-start.9 = (bf16[272,256]{1,0:T(8,128)(2,1)}, bf16[272,256]{1,0:T(8,128)(2,1)S(1)}, u32[]{:S(2)}) copy-start(bf16[272,256]{1,0:T(8,128)(2,1)S(1)} %collective-permute-done.5.refs_5_.refs_9_) | copy-start | bytes 417796
  60.8 15.1 %collective-permute-start.7 = (bf16[272,256]{1,0:T(8,128)(2,1)S(1)}, bf16[272,256]{1,0:T(8,128)(2,1)S(1)}, u32[]{:S(2)}, u32[]{:S(2)}) collective-permute-start(bf16[272,256]{1,0:T(8,128)(2,1)S(1)} %collective-permute-done.5.refs_5_.refs_9_), channel_id=1, source_target_pairs={{0,64},{64,128},{128,192},{192,256},{256,320},{320,384},{384,448},... | collective-permute-start | bytes 417800 | tf_op jit(solution)/shard_map/ppermute | solution.py:233
  68.9 0.7 copy-start.10
  75.9 0.7 copy-start.11
  94.8 6.3 %copy-start.37 = (bf16[256,16]{0,1:T(8,128)(2,1)S(1)}, bf16[256,16]{0,1:T(8,128)(2,1)}, u32[]{:S(2)}) copy-start(bf16[256,16]{0,1:T(8,128)(2,1)} %param.26) | copy-start | bytes 24580
  95.1 5.2 %collective-permute-start.8 = (bf16[128,128]{1,0:T(8,128)(2,1)S(1)}, bf16[128,128]{1,0:T(8,128)(2,1)S(1)}, u32[]{:S(2)}, u32[]{:S(2)}) collective-permute-start(bf16[128,128]{1,0:T(8,128)(2,1)S(1)} %slice.198), channel_id=1, source_target_pairs={{0,8},{8,0},{1,9},{9,1},{2,10},{10,2},{3,11},{11,3},{4,12},{12,4},... | collective-permute-start | bytes 98312 | tf_op jit(solution)/shard_map/ppermute | solution.py:259
  100.4 1.7 copy-start.14
  100.4 1.7 copy-start.15
  100.7 5.6 %copy-start.16 = (bf16[128,512]{1,0:T(8,128)(2,1)S(1)}, bf16[128,512]{1,0:T(8,128)(2,1)}, u32[]{:S(2)}) copy-start(bf16[128,512]{1,0:T(8,128)(2,1)} %param.39) | copy-start | bytes 393220
  100.7 9.1 %copy-start.40 = (s32[128]{0:T(128)S(1)}, s32[128]{0:T(128)}, u32[]{:S(2)}) copy-start(s32[128]{0:T(128)} %param.23) | copy-start | bytes 1540
  100.7 9.3 %copy-start.28 = (bf16[8,512]{1,0:T(8,128)(2,1)S(1)}, bf16[8,512]{1,0:T(8,128)(2,1)}, u32[]{:S(2)}) copy-start(bf16[8,512]{1,0:T(8,128)(2,1)} %param.32) | copy-start | bytes 24580
  100.8 9.9 %copy-start.38 = (f32[8,16]{1,0:T(8,128)S(1)}, f32[8,16]{1,0:T(8,128)}, u32[]{:S(2)}) copy-start(f32[8,16]{1,0:T(8,128)} %param.38) | copy-start | bytes 1540
  101.1 15.1 %copy-start.39 = (f32[8,16]{1,0:T(8,128)S(1)}, f32[8,16]{1,0:T(8,128)}, u32[]{:S(2)}) copy-start(f32[8,16]{1,0:T(8,128)} %param.28) | copy-start | bytes 1540
  101.1 15.9 %copy-start.1 = (bf16[256,512]{1,0:T(8,128)(2,1)S(1)}, bf16[256,512]{1,0:T(8,128)(2,1)}, u32[]{:S(2)}) copy-start(bf16[256,512]{1,0:T(8,128)(2,1)} %param.29) | copy-start | bytes 786436
  101.1 15.9 %copy-start.17 = (bf16[128,256]{1,0:T(8,128)(2,1)S(1)}, bf16[128,256]{1,0:T(8,128)(2,1)}, u32[]{:S(2)}) copy-start(bf16[128,256]{1,0:T(8,128)(2,1)} %param.24) | copy-start | bytes 196612
  101.1 15.9 %copy-start.23 = (bf16[16,256]{1,0:T(8,128)(2,1)S(1)}, bf16[16,256]{1,0:T(8,128)(2,1)}, u32[]{:S(2)}) copy-start(bf16[16,256]{1,0:T(8,128)(2,1)} %param.27) | copy-start | bytes 24580
  102.1 30.9 %copy-start.13 = (bf16[256,512]{1,0:T(8,128)(2,1)S(1)}, bf16[256,512]{1,0:T(8,128)(2,1)}, u32[]{:S(2)}) copy-start(bf16[256,512]{1,0:T(8,128)(2,1)} %param.31) | copy-start | bytes 786436
  102.1 31.7 %copy-start.24 = (f32[512]{0:T(512)S(1)}, f32[512]{0:T(512)}, u32[]{:S(2)}) copy-start(f32[512]{0:T(512)} %param.33) | copy-start | bytes 6148
  102.1 13.8 %all-to-all-start.2 = ((bf16[8,272,128]{2,1,0:T(8,128)(2,1)}), bf16[8,272,128]{2,1,0:T(8,128)(2,1)S(1)}, u32[]{:S(2)}, u32[]{:S(2)}) async-start(bf16[8,272,128]{2,1,0:T(8,128)(2,1)} %pad_maximum_fusion.1), calls=%async_computation.2 | async-start | bytes 1114112 | tf_op jit(solution)/shard_map/all_to_all | solution.py:30
  106.3 27.6 %copy-start.18 = (bf16[512,16]{0,1:T(8,128)(2,1)S(1)}, bf16[512,16]{0,1:T(8,128)(2,1)}, u32[]{:S(2)}) copy-start(bf16[512,16]{0,1:T(8,128)(2,1)} %param.36) | copy-start | bytes 49156
  106.3 38.9 %collective-permute-start.9 = (bf16[128,512]{1,0:T(8,128)(2,1)S(1)}, bf16[128,512]{1,0:T(8,128)(2,1)}, u32[]{:S(2)}, u32[]{:S(2)}) collective-permute-start(bf16[128,512]{1,0:T(8,128)(2,1)S(1)} %copy-done.16), channel_id=1, source_target_pairs={{0,1},{1,0},{2,3},{3,2},{4,5},{5,4},{6,7},{7,6},{8,9},{9,8},{10,11... | collective-permute-start | bytes 393224 | tf_op jit(solution)/shard_map/ppermute | solution.py:218
  110.1 0.6 copy-start.33
  116.0 11.2 %copy-start.12 = (f32[272,128]{1,0:T(8,128)}, f32[272,128]{1,0:T(8,128)S(1)}, u32[]{:S(2)}) copy-start(f32[272,128]{1,0:T(8,128)S(1)} %convert_reduce_fusion) | copy-start | bytes 417796
  117.0 1.0 copy-start.26
  118.0 9.2 %all-to-all-start.3 = ((bf16[8,16,512]{2,1,0:T(8,128)(2,1)}), bf16[8,16,512]{2,1,0:T(8,128)(2,1)S(1)}, u32[]{:S(2)}, u32[]{:S(2)}) async-start(bf16[8,16,512]{2,1,0:T(8,128)(2,1)} %bitcast.28), calls=%async_computation.3 | async-start | bytes 262144 | tf_op jit(solution)/shard_map/all_to_all | solution.py:30
  127.5 14.7 %copy-start.4 = (bf16[4,512,256]{2,1,0:T(8,128)(2,1)S(1)}, bf16[4,512,256]{2,1,0:T(8,128)(2,1)}, u32[]{:S(2)}) copy-start(bf16[4,512,256]{2,1,0:T(8,128)(2,1)} %all-gather.4.cloned.1.call-done) | copy-start | bytes 3145732
  127.5 14.7 %collective-permute-start.10 = (bf16[4,512,256]{2,1,0:T(8,128)(2,1)}, bf16[4,512,256]{2,1,0:T(8,128)(2,1)}, u32[]{:S(2)}, u32[]{:S(2)}) collective-permute-start(bf16[4,512,256]{2,1,0:T(8,128)(2,1)} %all-gather.4.cloned.1.call-done), channel_id=1, source_target_pairs={{0,8},{8,0},{1,9},{9,1},{2,10},{10,2},{3,11},{11,3},{4,12},{12,4},... | collective-permute-start | bytes 3145736 | tf_op jit(solution)/shard_map/ppermute | solution.py:288
  133.3 0.5 copy-start.31
  134.3 7.7 %collective-permute-start.11 = (bf16[128,640]{1,0:T(8,128)(2,1)S(1)}, bf16[128,640]{1,0:T(8,128)(2,1)S(1)}, u32[]{:S(2)}, u32[]{:S(2)}) collective-permute-start(bf16[128,640]{1,0:T(8,128)(2,1)S(1)} %pad_maximum_fusion.4), channel_id=1, source_target_pairs={{0,1},{1,0},{2,3},{3,2},{4,5},{5,4},{6,7},{7,6},{8,9},{9,8},{10,11... | collective-permute-start | bytes 491528 | tf_op jit(solution)/shard_map/ppermute | solution.py:310
  143.8 0.7 copy-start.35
  147.4 7.4 %copy-start.25 = (f32[512]{0:T(512)S(1)}, f32[512]{0:T(512)}, u32[]{:S(2)}) copy-start(f32[512]{0:T(512)} %param.33) | copy-start | bytes 6148
  147.4 7.6 %copy-start.34 = (s32[128]{0:T(128)S(1)}, s32[128]{0:T(128)}, u32[]{:S(2)}) copy-start(s32[128]{0:T(128)} %copy-done.33) | copy-start | bytes 1540
  147.5 7.9 %copy-start.32 = (f32[128]{0:T(128)S(1)}, f32[128]{0:T(128)}, u32[]{:S(2)}) copy-start(f32[128]{0:T(128)} %copy-done.31) | copy-start | bytes 1540
  147.7 7.9 %copy-start.36 = (bf16[48]{0:T(256)(128)(2,1)S(1)}, bf16[48]{0:T(256)(128)(2,1)}, u32[]{:S(2)}) copy-start(bf16[48]{0:T(256)(128)(2,1)} %pad.22.clone) | copy-start | bytes 292
  147.8 6.8 %collective-permute-start.12 = (bf16[128,640]{1,0:T(8,128)(2,1)S(1)}, bf16[128,640]{1,0:T(8,128)(2,1)S(1)}, u32[]{:S(2)}, u32[]{:S(2)}) collective-permute-start(bf16[128,640]{1,0:T(8,128)(2,1)S(1)} %slice.296), channel_id=1, source_target_pairs={{0,1},{1,0},{2,3},{3,2},{4,5},{5,4},{6,7},{7,6},{8,9},{9,8},{10,11... | collective-permute-start | bytes 491528 | tf_op jit(solution)/shard_map/ppermute | solution.py:317
  156.6 12.6 %all-to-all-start.4 = ((bf16[8,64,512]{2,1,0:T(8,128)(2,1)}), bf16[8,64,512]{2,1,0:T(8,128)(2,1)}, u32[]{:S(2)}, u32[]{:S(2)}) async-start(bf16[8,64,512]{2,1,0:T(8,128)(2,1)} %fusion.19), calls=%async_computation.4 | async-start | bytes 1048576 | tf_op jit(solution)/shard_map/all_to_all | solution.py:30
  160.7 1.9 copy-start.19
  160.7 1.9 copy-start.20
  160.7 1.9 copy-start.21
  160.7 1.9 copy-start.22
  162.6 9.4 %copy-start.41 = (s32[128]{0:T(128)S(1)}, s32[128]{0:T(128)}, u32[]{:S(2)}) copy-start(s32[128]{0:T(128)} %param.23) | copy-start | bytes 1540
  162.6 11.2 %copy-start.27 = (bf16[128,16]{0,1:T(8,128)(2,1)S(1)}, bf16[128,16]{0,1:T(8,128)(2,1)}, u32[]{:S(2)}) copy-start(bf16[128,16]{0,1:T(8,128)(2,1)} %copy-done.26) | copy-start | bytes 12292
Sparse Core Ops, SparseCore 0:
  21.9 60.5 all-gather.5
Sparse Core Ops, SparseCore 1:
  100.3 27.0 all-gather.3
